TPU v7x, 32 devices: a whole 2x2x4 slice. The times are simulated.
32 devices in a mesh: gz: 4 (over z), gy: 2 (over x), gx: 4 (over y, core).
Axes of the slice: x: 2, y: 2, z: 4, core: 2. Of those that a mesh axis runs over, the one named last changes fastest.
Arguments:
- fields: float32 [5, 128, 32, 512], P(None, 'gz', 'gy', 'gx'), may hold values from -6 to 6
- diffusivity: float32 [128, 32, 512], P('gz', 'gy', 'gx'), may hold values from 0.01 to 0.08
- courant: float32 [5, 3], replicated, may hold values from 0.03 to 0.1
- tf_center: float32 [16], replicated, may hold values from -1.5 to 1.5
- tf_sharp: float32 [16], replicated, may hold values from 0.5 to 4
- tf_gain: float32 [16], replicated, may hold values from 0.01 to 0.12
- tf_color: float32 [3, 16], replicated, may hold values from 0.2 to 1
- tile_mask: int32 [4, 16, 32, 4], P('gz', None, 'gy', 'gx'), may hold values from 0 to 1, as said below
- tile_perm: int32 [2, 4, 256], P('gy', 'gx'), may hold values from 0 to 255, each once within a row
Outputs:
- advanced: float32 [5, 128, 32, 512], P(None, 'gz', 'gy', 'gx')
- picture: float32 [2, 4, 256, 4, 128], P('gy', 'gx', 'gz')
Inputs may be any that keep to these rules, and one draw needn't show every extreme that they name: `tile_mask`: 1 marks an active tile; the share of active tiles differs from slab to slab.
All inputs are finite; a program needn't handle non-finite values.
Results may differ from a plain program's by a relative error of at most 0.0001.
Values sent between devices are 32-bit elements; how exact they have to be, the bound alone decides.
No kernel may reach another device: no remote copies, remote signals or barrier semaphores. Data moves between devices by JAX's collectives and lax.ppermute only.
A program may use at most 64 MiB of HBM per device.

v0:
```python
import jax
import jax.numpy as jnp
from jax import lax
from jax.sharding import PartitionSpec as P


def extended(cells, sides, width):
    for axis, dim in sides:
        count = lax.axis_size(axis)
        ends = count - 1
        head = lax.slice_in_dim(cells, 0, width, axis=dim)
        tail = lax.slice_in_dim(cells, cells.shape[dim] - width, cells.shape[dim], axis=dim)
        cells = jnp.concatenate(
            [
                lax.ppermute(tail, axis, [(i, (i + 1) % count) for i in range(ends)]),
                cells,
                lax.ppermute(head, axis, [((i + 1) % count, i) for i in range(ends)]),
            ],
            axis=dim,
        )
    return cells


def inner(source, leading, axis_pos, offset):
    picks = [slice(None)] * leading + [slice(1, -1)] * 3
    length = source.shape[leading + axis_pos]
    picks[leading + axis_pos] = slice(1 + offset, length - 1 + offset)
    return source[tuple(picks)]


def advance(padded, kappa_pad, courant):
    center = inner(padded, 1, 0, 0)
    kappa_mid = inner(kappa_pad, 0, 0, 0)
    result = center
    for axis_pos in range(3):
        upper = inner(padded, 1, axis_pos, 1)
        lower = inner(padded, 1, axis_pos, -1)
        kappa_up = inner(kappa_pad, 0, axis_pos, 1)
        kappa_down = inner(kappa_pad, 0, axis_pos, -1)
        speed = courant[:, axis_pos][:, None, None, None]
        result = (
            result
            + 0.5 * (kappa_mid + kappa_up) * (upper - center)
            + 0.5 * (kappa_mid + kappa_down) * (lower - center)
            - speed * (center - lower)
        )
    return result


def inside(position, total, length):
    start = position * length - 1
    cells = start + jnp.arange(length + 2, dtype=jnp.int32)
    return ((cells >= 0) & (cells < length * total)).astype(jnp.float32)


def over(front, back):
    front_alpha = front[:, 3:4]
    color = front[:, :3] + (1.0 - front_alpha) * back[:, :3]
    alpha = front_alpha + (1.0 - front_alpha) * back[:, 3:4]
    return jnp.concatenate([color, alpha], 1)


def fold_slabs(received):
    result = received[0]
    for slab in range(1, received.shape[0]):
        result = over(result, received[slab])
    return result


def shards(
    fields, diffusivity, courant, tf_center, tf_sharp, tf_gain, tf_color, tile_mask, tile_perm
):
    nfield, depth_len, rows_len, cols_len = fields.shape
    stacked = jnp.concatenate([fields, diffusivity[None]], 0)
    padded = extended(stacked, (("gz", 1), ("gy", 2), ("gx", 3)), 2)
    kappa_pad = padded[nfield]
    widened = advance(padded[:nfield], kappa_pad, courant)
    valid_z = inside(lax.axis_index("gz"), lax.axis_size("gz"), depth_len)
    valid_y = inside(lax.axis_index("gy"), lax.axis_size("gy"), rows_len)
    valid_x = inside(lax.axis_index("gx"), lax.axis_size("gx"), cols_len)
    valid = valid_z[:, None, None] * valid_y[None, :, None] * valid_x[None, None, :]
    widened = widened * valid[None]
    state = advance(widened, inner(kappa_pad, 0, 0, 0), courant)
    scalar = state[0]
    spad = extended(scalar, (("gz", 0), ("gy", 1), ("gx", 2)), 1)
    grad_z = 0.5 * (spad[2:, 1:-1, 1:-1] - spad[:-2, 1:-1, 1:-1])
    grad_y = 0.5 * (spad[1:-1, 2:, 1:-1] - spad[1:-1, :-2, 1:-1])
    grad_x = 0.5 * (spad[1:-1, 1:-1, 2:] - spad[1:-1, 1:-1, :-2])
    shade = 0.35 + 0.65 * jnp.abs(0.64 * grad_z + 0.6 * grad_y + 0.48 * grad_x) / jnp.sqrt(
        grad_z * grad_z + grad_y * grad_y + grad_x * grad_x + 1.0
    )
    modul = 1.0 + 0.5 * jnp.tanh(state[4])
    bases = shade[None] * jax.nn.sigmoid(state[1:4])
    steps_idx = jnp.arange(depth_len, dtype=jnp.int32)
    earlier = (steps_idx[:, None] > steps_idx[None, :]).astype(jnp.float32)

    def render(items):
        center, sharp, gain, color = items
        depth = gain * jnp.exp(-sharp * (scalar - center) ** 2) * modul
        before = jnp.einsum("wz,zyx->wyx", earlier, depth, precision=lax.Precision.HIGHEST)
        weight = jnp.exp(-before) * (1.0 - jnp.exp(-depth))
        colors = jnp.sum(weight[None] * bases, axis=1) * color[:, None, None]
        alpha = 1.0 - jnp.exp(-jnp.sum(depth, axis=0))
        return jnp.transpose(jnp.concatenate([colors, alpha[None]], 0), (1, 0, 2))

    rendered = lax.map(render, (tf_center, tf_sharp, tf_gain, tf_color.T))
    cover = tile_mask[0].astype(jnp.float32)[..., None]
    tiles = (rendered * cover).reshape(-1, 4, cols_len)
    order = tile_perm[0, 0]
    count = lax.axis_size("gz")
    per_owner = tiles.shape[0] // count
    grouped = tiles[order].reshape(count, per_owner, 4, cols_len)
    composed = fold_slabs(lax.all_to_all(grouped, "gz", split_axis=0, concat_axis=0, tiled=True))
    picture = composed.reshape(1, 1, per_owner, 4, cols_len)
    return (state, picture)


def solution(mesh):
    return jax.shard_map(
        shards,
        mesh=mesh,
        in_specs=(
            P(None, "gz", "gy", "gx"),
            P("gz", "gy", "gx"),
            P(),
            P(),
            P(),
            P(),
            P(),
            P("gz", None, "gy", "gx"),
            P("gy", "gx", None),
        ),
        out_specs=(P(None, "gz", "gy", "gx"), P("gy", "gx", "gz", None, None)),
        check_vma=False,
    )
```

profile of v0, /device:TPU:6, one launch (start us, length us, event | category | flops | bytes accessed | tf_op | source)
XLA Modules:
  0.0 218.6 jit_solution(6006665853479157277)
XLA Ops:
  1.7 3.5 %collective-permute-start = (f32[6,2,16,128]{3,2,1,0:T(8,128)S(1)}, f32[6,2,16,128]{3,2,1,0:T(8,128)S(1)}, u32[]{:S(2)}, u32[]{:S(2)}) collective-permute-start(f32[6,2,16,128]{3,2,1,0:T(8,128)S(1)} %get-tuple-element.148), channel_id=1, source_target_pairs={{0,8},{8,16},{16,24},{1,9},{9,17},{17,25},{2,10},{10,18},{18,26},{... | collective-permute-start | bytes 294920 | tf_op jit(solution)/shard_map/ppermute | solution.py:15
  5.2 1.3 collective-permute-start.1
  7.4 4.3 %collective-permute-done.1 = f32[6,2,16,128]{3,2,1,0:T(8,128)S(1)} collective-permute-done((f32[6,2,16,128]{3,2,1,0:T(8,128)S(1)}, f32[6,2,16,128]{3,2,1,0:T(8,128)S(1)}, u32[]{:S(2)}, u32[]{:S(2)}) %collective-permute-start.1) | collective-permute-done | bytes 98336 | tf_op jit(solution)/shard_map/ppermute | solution.py:17
  11.8 1.6 pad_maximum_fusion.36
  13.4 1.3 collective-permute-start.2
  14.7 4.6 %collective-permute-start.3 = (f32[6,36,2,128]{3,2,1,0:T(2,128)S(1)}, f32[6,36,2,128]{3,2,1,0:T(2,128)S(1)}, u32[]{:S(2)}, u32[]{:S(2)}) collective-permute-start(f32[6,36,2,128]{3,2,1,0:T(2,128)S(1)} %get-tuple-element.147), channel_id=1, source_target_pairs={{4,0},{5,1},{6,2},{7,3},{12,8},{13,9},{14,10},{15,11},{20,16},{21,... | collective-permute-start | bytes 663560 | tf_op jit(solution)/shard_map/ppermute | solution.py:17
  19.5 1.8 collective-permute-done.2
  21.2 1.5 collective-permute-done.3
  23.1 3.2 %fusion.66 = (f32[6,36,20,2]{3,2,1,0:T(8,128)}, f32[6,36,20,2]{3,2,1,0:T(8,128)}) fusion(f32[6,36,20,128]{3,2,1,0:T(8,128)S(1)} %pad_maximum_fusion.13), kind=kLoop, calls=%fused_computation.163 | loop fusion | bytes 138240 | tf_op jit(solution)/shard_map/slice | solution.py:12
  26.3 2.7 %copy.44 = f32[6,36,20,2]{1,3,2,0:T(2,128)S(1)} copy(f32[6,36,20,2]{3,2,1,0:T(8,128)} %get-tuple-element.144) | data formatting | bytes 69120 | tf_op jit(solution)/shard_map/slice | solution.py:12
  29.0 1.9 collective-permute-start.4
  30.9 2.7 %copy.45 = f32[6,36,20,2]{1,3,2,0:T(2,128)S(1)} copy(f32[6,36,20,2]{3,2,1,0:T(8,128)} %get-tuple-element.145) | data formatting | bytes 69120 | tf_op jit(solution)/shard_map/slice | solution.py:11
  33.6 3.8 %collective-permute-start.5 = (f32[6,36,20,2]{1,3,2,0:T(2,128)S(1)}, f32[6,36,20,2]{1,3,2,0:T(2,128)}, u32[]{:S(2)}, u32[]{:S(2)}) collective-permute-start(f32[6,36,20,2]{1,3,2,0:T(2,128)S(1)} %copy.45), channel_id=1, source_target_pairs={{1,0},{2,1},{3,2},{5,4},{6,5},{7,6},{9,8},{10,9},{11,10},{13,12},{... | collective-permute-start | bytes 103688 | tf_op jit(solution)/shard_map/ppermute | solution.py:17
  37.5 2.6 %copy.46 = f32[6,36,20,2]{3,2,1,0:T(8,128)} copy(f32[6,36,20,2]{1,3,2,0:T(2,128)S(1)} %collective-permute-done.4) | data formatting | bytes 69120 | tf_op jit(solution)/shard_map/ppermute | solution.py:15
  40.1 3.6 %copy.47 = f32[6,36,20,2]{3,2,1,0:T(8,128)} copy(f32[6,36,20,2]{1,3,2,0:T(2,128)} %collective-permute-done.5) | data formatting | bytes 69120 | tf_op jit(solution)/shard_map/ppermute | solution.py:17
  43.7 8.0 %pad_maximum_fusion = f32[6,36,20,132]{3,2,1,0:T(8,128)S(1)} fusion(f32[6,36,20,2]{3,2,1,0:T(8,128)} %copy.47, f32[6,36,2,128]{3,2,1,0:T(2,128)S(1)} %collective-permute-done.3, f32[6,2,16,128]{3,2,1,0:T(8,128)S(1)} %collective-permute-done.1, f32[1,32,16,128]{3,2,1,0:T(8,128)S(1)} %bitcast.78, f32[5,32,16,128]{3,2,1,0:T(8,128)S(1)} %copy-done, ...), kind=kLoop, calls=%fused_computation.18 | loop fusion | flops 3991680 | bytes 4561920 | tf_op jit(solution)/shard_map/concatenate | solution.py:13
  51.8 1.4 fusion.41
  53.1 1.7 fusion.57
  55.5 13.5 %fusion.15 = f32[5,34,18,130]{3,2,1,0:T(8,128)S(1)} fusion(f32[6,36,20,2]{3,2,1,0:T(8,128)S(1)} %copy-done.2, f32[6,36,2,128]{3,2,1,0:T(2,128)} %copy-done.5, f32[6,36,2,128]{3,2,1,0:T(2,128)S(1)} %collective-permute-done.2, f32[6,2,16,128]{3,2,1,0:T(8,128)} %copy-done.7, f32[6,2,16,128]{3,2,1,0:T(8,128)} %copy-done.6, f32[1,32,16,128]{3,2,1,0:T(8,128)S(1)} %bitcast.79, ...), kind=kLoop, calls=%fused_computation.31 | loop fusion | flops 15912000 | bytes 14055900 | tf_op jit(solution)/shard_map/mul | solution.py:82
  69.0 3.9 %fusion.27 = f32[5,32,16,128]{3,2,1,0:T(8,128)S(1)} fusion(f32[5,34,18,130]{3,2,1,0:T(8,128)S(1)} %fusion.15, f32[5]{0:T(128)S(1)} %get-tuple-element.176, f32[32,16,128]{2,1,0:T(8,128)} %get-tuple-element.159, f32[32,16,128]{2,1,0:T(8,128)} %get-tuple-element.158, f32[5]{0:T(128)S(1)} %get-tuple-element.177, f32[32,16,128]{2,1,0:T(8,128)} %get-tuple-element.155, ...), kind=kLoop, calls=%fused_computation.52 | loop fusion | flops 8847360 | bytes 12058684 | tf_op jit(solution)/shard_map/sub | solution.py:42
  72.9 1.4 collective-permute-start.6
  74.4 4.5 %collective-permute-start.7 = (f32[1,16,128]{2,1,0:T(8,128)S(1)}, f32[1,16,128]{2,1,0:T(8,128)S(1)}, u32[]{:S(2)}, u32[]{:S(2)}) collective-permute-start(f32[1,16,128]{2,1,0:T(8,128)S(1)} %get-tuple-element.150), channel_id=1, source_target_pairs={{0,8},{8,16},{16,24},{1,9},{9,17},{17,25},{2,10},{10,18},{18,26},{... | collective-permute-start | bytes 24584 | tf_op jit(solution)/shard_map/ppermute | solution.py:15
  80.3 4.4 %collective-permute-start.8 = (f32[34,1,128]{2,1,0:T(1,128)S(1)}, f32[34,1,128]{2,1,0:T(1,128)S(1)}, u32[]{:S(2)}, u32[]{:S(2)}) collective-permute-start(f32[34,1,128]{2,1,0:T(1,128)S(1)} %get-tuple-element.173), channel_id=1, source_target_pairs={{4,0},{5,1},{6,2},{7,3},{12,8},{13,9},{14,10},{15,11},{20,16},{21,... | collective-permute-start | bytes 52232 | tf_op jit(solution)/shard_map/ppermute | solution.py:17
  84.7 1.3 collective-permute-start.9
  86.1 4.2 %collective-permute-done.9 = f32[34,1,128]{2,1,0:T(1,128)S(1)} collective-permute-done((f32[34,1,128]{2,1,0:T(1,128)S(1)}, f32[34,1,128]{2,1,0:T(1,128)S(1)}, u32[]{:S(2)}, u32[]{:S(2)}) %collective-permute-start.9) | collective-permute-done | bytes 17440 | tf_op jit(solution)/shard_map/ppermute | solution.py:15
  91.4 1.9 collective-permute-start.10
  93.3 2.6 %collective-permute-start.11 = (f32[34,18,1]{2,1,0:T(8,128)}, f32[34,18,1]{2,1,0:T(8,128)}, u32[]{:S(2)}, u32[]{:S(2)}) collective-permute-start(f32[34,18,1]{2,1,0:T(8,128)} %get-tuple-element.171), channel_id=1, source_target_pairs={{0,1},{1,2},{2,3},{4,5},{5,6},{6,7},{8,9},{9,10},{10,11},{12,13},{... | collective-permute-start | bytes 7352 | tf_op jit(solution)/shard_map/ppermute | solution.py:15
  96.3 2.9 %collective-permute-done.10 = f32[34,18,1]{2,1,0:T(8,128)S(1)} collective-permute-done((f32[34,18,1]{2,1,0:T(8,128)}, f32[34,18,1]{2,1,0:T(8,128)S(1)}, u32[]{:S(2)}, u32[]{:S(2)}) %collective-permute-start.10) | collective-permute-done | bytes 2480 | tf_op jit(solution)/shard_map/ppermute | solution.py:17
  99.2 3.8 %collective-permute-done.11 = f32[34,18,1]{2,1,0:T(8,128)} collective-permute-done((f32[34,18,1]{2,1,0:T(8,128)}, f32[34,18,1]{2,1,0:T(8,128)}, u32[]{:S(2)}, u32[]{:S(2)}) %collective-permute-start.11) | collective-permute-done | bytes 2480 | tf_op jit(solution)/shard_map/ppermute | solution.py:15
  103.0 1.4 multiply_add_fusion
  104.7 95.7 %while.11 = (s32[]{:T(128)}, f32[16,16,4,128]{3,1,0,2:T(8,128)S(1)}, f32[16]{0:T(128)S(1)}, f32[16]{0:T(128)S(1)}, f32[16]{0:T(128)S(1)}, /*index=5*/f32[32,16,1...) while((s32[]{:T(128)}, ...), condition=%wide.region_3.4_spmd.clone, body=%wide.region_0.3_spmd.clone.sunk | while | flops 26882052 | bytes 3047637 | solution.py:106
  107.3 1.7 fusion.75
  109.3 1.3 fusion.74
  113.3 1.7 fusion.75
  115.3 1.3 fusion.74
  119.2 1.7 fusion.75
  121.3 1.3 fusion.74
  125.2 1.7 fusion.75
  127.3 1.3 fusion.74
  131.2 1.7 fusion.75
  133.2 1.3 fusion.74
  137.2 1.7 fusion.75
  139.2 1.3 fusion.74
  143.2 1.7 fusion.75
  145.2 1.3 fusion.74
  149.1 1.7 fusion.75
  151.2 1.3 fusion.74
  155.1 1.7 fusion.75
  157.2 1.3 fusion.74
  161.1 1.7 fusion.75
  163.1 1.3 fusion.74
  167.1 1.7 fusion.75
  169.1 1.3 fusion.74
  173.1 1.7 fusion.75
  175.1 1.3 fusion.74
  179.0 1.7 fusion.75
  181.1 1.3 fusion.74
  185.0 1.7 fusion.75
  187.1 1.3 fusion.74
  191.0 1.7 fusion.75
  193.0 1.3 fusion.74
  197.0 1.7 fusion.75
  199.0 1.3 fusion.74
  201.8 15.7 %all_to_all.5 = f32[4,64,4,128]{3,2,1,0:T(4,128)S(1)} all-to-all(f32[4,64,4,128]{3,2,1,0:T(4,128)S(1)} %bitcast.80), channel_id=1, replica_groups=mesh['gz'=4,'gy'=2,'gx'=4] {'gz'}, dimensions={0} | all-to-all | bytes 1048576 | tf_op jit(solution)/shard_map/all_to_all | solution.py:113
  (211 shorter events, 44.3 us)
Async XLA Ops:
  0.6 22.1 %copy-start.3 = (f32[32,16,128]{2,1,0:T(8,128)S(1)}, f32[32,16,128]{2,1,0:T(8,128)}, u32[]{:S(2)}) copy-start(f32[32,16,128]{2,1,0:T(8,128)} %param.12) | copy-start | bytes 786436
  0.6 22.1 %copy-start = (f32[5,32,16,128]{3,2,1,0:T(8,128)S(1)}, f32[5,32,16,128]{3,2,1,0:T(8,128)}, u32[]{:S(2)}) copy-start(f32[5,32,16,128]{3,2,1,0:T(8,128)} %param.11) | copy-start | bytes 3932164
  1.7 5.7 %collective-permute-start = (f32[6,2,16,128]{3,2,1,0:T(8,128)S(1)}, f32[6,2,16,128]{3,2,1,0:T(8,128)S(1)}, u32[]{:S(2)}, u32[]{:S(2)}) collective-permute-start(f32[6,2,16,128]{3,2,1,0:T(8,128)S(1)} %get-tuple-element.148), channel_id=1, source_target_pairs={{0,8},{8,16},{16,24},{1,9},{9,17},{17,25},{2,10},{10,18},{18,26},{... | collective-permute-start | bytes 294920 | tf_op jit(solution)/shard_map/ppermute | solution.py:15
  5.2 6.5 %collective-permute-start.1 = (f32[6,2,16,128]{3,2,1,0:T(8,128)S(1)}, f32[6,2,16,128]{3,2,1,0:T(8,128)S(1)}, u32[]{:S(2)}, u32[]{:S(2)}) collective-permute-start(f32[6,2,16,128]{3,2,1,0:T(8,128)S(1)} %get-tuple-element.149), channel_id=1, source_target_pairs={{8,0},{16,8},{24,16},{9,1},{17,9},{25,17},{10,2},{18,10},{26,18},{... | collective-permute-start | bytes 294920 | tf_op jit(solution)/shard_map/ppermute | solution.py:17
  7.4 36.2 %copy-start.6 = (f32[6,2,16,128]{3,2,1,0:T(8,128)}, f32[6,2,16,128]{3,2,1,0:T(8,128)S(1)}, u32[]{:S(2)}) copy-start(f32[6,2,16,128]{3,2,1,0:T(8,128)S(1)} %collective-permute-done) | copy-start | bytes 294916
  11.8 31.9 %copy-start.7 = (f32[6,2,16,128]{3,2,1,0:T(8,128)}, f32[6,2,16,128]{3,2,1,0:T(8,128)S(1)}, u32[]{:S(2)}) copy-start(f32[6,2,16,128]{3,2,1,0:T(8,128)S(1)} %collective-permute-done.1) | copy-start | bytes 294916
  13.4 7.8 %collective-permute-start.2 = (f32[6,36,2,128]{3,2,1,0:T(2,128)S(1)}, f32[6,36,2,128]{3,2,1,0:T(2,128)S(1)}, u32[]{:S(2)}, u32[]{:S(2)}) collective-permute-start(f32[6,36,2,128]{3,2,1,0:T(2,128)S(1)} %get-tuple-element.146), channel_id=1, source_target_pairs={{0,4},{1,5},{2,6},{3,7},{8,12},{9,13},{10,14},{11,15},{16,20},{17,... | collective-permute-start | bytes 663560 | tf_op jit(solution)/shard_map/ppermute | solution.py:15
  14.7 8.0 %collective-permute-start.3 = (f32[6,36,2,128]{3,2,1,0:T(2,128)S(1)}, f32[6,36,2,128]{3,2,1,0:T(2,128)S(1)}, u32[]{:S(2)}, u32[]{:S(2)}) collective-permute-start(f32[6,36,2,128]{3,2,1,0:T(2,128)S(1)} %get-tuple-element.147), channel_id=1, source_target_pairs={{4,0},{5,1},{6,2},{7,3},{12,8},{13,9},{14,10},{15,11},{20,16},{21,... | collective-permute-start | bytes 663560 | tf_op jit(solution)/shard_map/ppermute | solution.py:17
  22.7 21.0 %copy-start.5 = (f32[6,36,2,128]{3,2,1,0:T(2,128)}, f32[6,36,2,128]{3,2,1,0:T(2,128)S(1)}, u32[]{:S(2)}) copy-start(f32[6,36,2,128]{3,2,1,0:T(2,128)S(1)} %collective-permute-done.3) | copy-start | bytes 663556
  26.3 11.1 %copy-start.10 = (f32[5,3]{0,1:T(4,128)S(1)}, f32[5,3]{0,1:T(4,128)}, u32[]{:S(2)}) copy-start(f32[5,3]{0,1:T(4,128)} %param.13) | copy-start | bytes 184
  29.0 8.5 %collective-permute-start.4 = (f32[6,36,20,2]{1,3,2,0:T(2,128)S(1)}, f32[6,36,20,2]{1,3,2,0:T(2,128)S(1)}, u32[]{:S(2)}, u32[]{:S(2)}) collective-permute-start(f32[6,36,20,2]{1,3,2,0:T(2,128)S(1)} %copy.44), channel_id=1, source_target_pairs={{0,1},{1,2},{2,3},{4,5},{5,6},{6,7},{8,9},{9,10},{10,11},{12,13},{... | collective-permute-start | bytes 103688 | tf_op jit(solution)/shard_map/ppermute | solution.py:15
  33.6 6.5 %collective-permute-start.5 = (f32[6,36,20,2]{1,3,2,0:T(2,128)S(1)}, f32[6,36,20,2]{1,3,2,0:T(2,128)}, u32[]{:S(2)}, u32[]{:S(2)}) collective-permute-start(f32[6,36,20,2]{1,3,2,0:T(2,128)S(1)} %copy.45), channel_id=1, source_target_pairs={{1,0},{2,1},{3,2},{5,4},{6,5},{7,6},{9,8},{10,9},{11,10},{13,12},{... | collective-permute-start | bytes 103688 | tf_op jit(solution)/shard_map/ppermute | solution.py:17
  51.7 3.0 %copy-start.2 = (f32[6,36,20,2]{3,2,1,0:T(8,128)S(1)}, f32[6,36,20,2]{3,2,1,0:T(8,128)}, u32[]{:S(2)}) copy-start(f32[6,36,20,2]{3,2,1,0:T(8,128)} %copy.47) | copy-start | bytes 103684
  53.1 2.4 %copy-start.1 = (f32[6,36,20,2]{3,2,1,0:T(8,128)S(1)}, f32[6,36,20,2]{3,2,1,0:T(8,128)}, u32[]{:S(2)}) copy-start(f32[6,36,20,2]{3,2,1,0:T(8,128)} %copy.46) | copy-start | bytes 103684
  69.0 17.0 %copy-start.11 = (s32[1,1,256]{2,1,0:T(1,128)S(1)}, s32[1,1,256]{2,1,0:T(1,128)}, u32[]{:S(2)}) copy-start(s32[1,1,256]{2,1,0:T(1,128)} %param.19) | copy-start | bytes 3076
  69.0 27.0 %copy-start.9 = (f32[3,16]{1,0:T(4,128)S(1)}, f32[3,16]{1,0:T(4,128)}, u32[]{:S(2)}) copy-start(f32[3,16]{1,0:T(4,128)} %param.17) | copy-start | bytes 580
  69.0 27.1 %copy-start.8 = (s32[1,16,16,1]{2,3,1,0:T(1,128)S(1)}, s32[1,16,16,1]{2,3,1,0:T(1,128)}, u32[]{:S(2)}) copy-start(s32[1,16,16,1]{2,3,1,0:T(1,128)} %param.18) | copy-start | bytes 3076
  72.9 31.8 %copy-start.4 = (f32[5,32,16,128]{3,2,1,0:T(8,128)}, f32[5,32,16,128]{3,2,1,0:T(8,128)S(1)}, u32[]{:S(2)}) copy-start(f32[5,32,16,128]{3,2,1,0:T(8,128)S(1)} %fusion.27) | copy-start | bytes 3932164
  72.9 31.8 %copy-start.12 = (f32[16]{0:T(128)S(1)}, f32[16]{0:T(128)}, u32[]{:S(2)}) copy-start(f32[16]{0:T(128)} %param.16) | copy-start | bytes 196
  72.9 31.8 %copy-start.13 = (f32[16]{0:T(128)S(1)}, f32[16]{0:T(128)}, u32[]{:S(2)}) copy-start(f32[16]{0:T(128)} %param.15) | copy-start | bytes 196
  72.9 31.8 %copy-start.14 = (f32[16]{0:T(128)S(1)}, f32[16]{0:T(128)}, u32[]{:S(2)}) copy-start(f32[16]{0:T(128)} %param.14) | copy-start | bytes 196
  72.9 6.0 %collective-permute-start.6 = (f32[1,16,128]{2,1,0:T(8,128)S(1)}, f32[1,16,128]{2,1,0:T(8,128)S(1)}, u32[]{:S(2)}, u32[]{:S(2)}) collective-permute-start(f32[1,16,128]{2,1,0:T(8,128)S(1)} %get-tuple-element.151), channel_id=1, source_target_pairs={{8,0},{16,8},{24,16},{9,1},{17,9},{25,17},{10,2},{18,10},{26,18},{... | collective-permute-start | bytes 24584 | tf_op jit(solution)/shard_map/ppermute | solution.py:17
  74.4 5.9 %collective-permute-start.7 = (f32[1,16,128]{2,1,0:T(8,128)S(1)}, f32[1,16,128]{2,1,0:T(8,128)S(1)}, u32[]{:S(2)}, u32[]{:S(2)}) collective-permute-start(f32[1,16,128]{2,1,0:T(8,128)S(1)} %get-tuple-element.150), channel_id=1, source_target_pairs={{0,8},{8,16},{16,24},{1,9},{9,17},{17,25},{2,10},{10,18},{18,26},{... | collective-permute-start | bytes 24584 | tf_op jit(solution)/shard_map/ppermute | solution.py:15
  80.3 5.8 %collective-permute-start.8 = (f32[34,1,128]{2,1,0:T(1,128)S(1)}, f32[34,1,128]{2,1,0:T(1,128)S(1)}, u32[]{:S(2)}, u32[]{:S(2)}) collective-permute-start(f32[34,1,128]{2,1,0:T(1,128)S(1)} %get-tuple-element.173), channel_id=1, source_target_pairs={{4,0},{5,1},{6,2},{7,3},{12,8},{13,9},{14,10},{15,11},{20,16},{21,... | collective-permute-start | bytes 52232 | tf_op jit(solution)/shard_map/ppermute | solution.py:17
  84.7 5.6 %collective-permute-start.9 = (f32[34,1,128]{2,1,0:T(1,128)S(1)}, f32[34,1,128]{2,1,0:T(1,128)S(1)}, u32[]{:S(2)}, u32[]{:S(2)}) collective-permute-start(f32[34,1,128]{2,1,0:T(1,128)S(1)} %get-tuple-element.172), channel_id=1, source_target_pairs={{0,4},{1,5},{2,6},{3,7},{8,12},{9,13},{10,14},{11,15},{16,20},{17,... | collective-permute-start | bytes 52232 | tf_op jit(solution)/shard_map/ppermute | solution.py:15
  91.4 7.8 %collective-permute-start.10 = (f32[34,18,1]{2,1,0:T(8,128)}, f32[34,18,1]{2,1,0:T(8,128)S(1)}, u32[]{:S(2)}, u32[]{:S(2)}) collective-permute-start(f32[34,18,1]{2,1,0:T(8,128)} %get-tuple-element.170), channel_id=1, source_target_pairs={{1,0},{2,1},{3,2},{5,4},{6,5},{7,6},{9,8},{10,9},{11,10},{13,12},{... | collective-permute-start | bytes 7352 | tf_op jit(solution)/shard_map/ppermute | solution.py:17
  93.3 9.7 %collective-permute-start.11 = (f32[34,18,1]{2,1,0:T(8,128)}, f32[34,18,1]{2,1,0:T(8,128)}, u32[]{:S(2)}, u32[]{:S(2)}) collective-permute-start(f32[34,18,1]{2,1,0:T(8,128)} %get-tuple-element.171), channel_id=1, source_target_pairs={{0,1},{1,2},{2,3},{4,5},{5,6},{6,7},{8,9},{9,10},{10,11},{12,13},{... | collective-permute-start | bytes 7352 | tf_op jit(solution)/shard_map/ppermute | solution.py:15
where the time goes:
time: 220 us; the launch traced here: 219 us
  other arithmetic  58.3 us (26%)
  local copies, waits for them, and re-layouts  51.1 us (23%)
  starting transfers between devices  32.6 us (15%)
  matrix products  27.3 us (12%)
  waiting for transfers between devices  20.6 us (9%)
  blocking collectives  15.7 us (7%)
  loops' own time  12 us (5%)
    dynamic_slice x48, local copies, waits for them, and re-layouts, shards(): rendered = lax.map(render, (tf_center, tf_sharp, tf_gain, tf_color.T))  30.1 us
    dot_general x16, matrix products, render(): jnp.einsum('wz,zyx->wyx', earlier, depth, precision=lax.Precision.HIGHEST)  27.3 us
    reduce_sum x16, other arithmetic, render(): alpha = 1.0 - jnp.exp(-jnp.sum(depth, axis=0))  21.1 us
    ppermute x6, starting transfers between devices, extended(): lax.ppermute(head, axis, [((i + 1) % count, i) for i in range(ends)])  17.4 us
    all_to_all x1, blocking collectives, shards(): lax.all_to_all(grouped, 'gz', split_axis=0, concat_axis=0, tiled=True)  15.7 us
    ppermute x6, starting transfers between devices, extended(): lax.ppermute(tail, axis, [(i, (i + 1) % count) for i in range(ends)])  15.2 us
    mul x1, other arithmetic, shards(): widened = widened * valid[None]  13.5 us
    another operation x1, loops' own time, shards(): rendered = lax.map(render, (tf_center, tf_sharp, tf_gain, tf_color.T))  12 us
  transfers between devices with their start and end apart: 12, of which 9 were waited for; matrix products, arithmetic and copies ran while one was open for 3% of the time, Pallas kernels for 0%

commit v1 on v0

--- a/solution.py
+++ b/solution.py
@@ -1,6 +1,8 @@
 import jax
 import jax.numpy as jnp
 from jax import lax
+from jax.experimental import pallas as pl
+from jax.experimental.pallas import tpu as pltpu
 from jax.sharding import PartitionSpec as P
 
 
@@ -53,18 +55,95 @@
     return ((cells >= 0) & (cells < length * total)).astype(jnp.float32)
 
 
-def over(front, back):
-    front_alpha = front[:, 3:4]
-    color = front[:, :3] + (1.0 - front_alpha) * back[:, :3]
-    alpha = front_alpha + (1.0 - front_alpha) * back[:, 3:4]
-    return jnp.concatenate([color, alpha], 1)
-
-
-def fold_slabs(received):
-    result = received[0]
-    for slab in range(1, received.shape[0]):
-        result = over(result, received[slab])
-    return result
+LOG2E = 1.4426950408889634
+
+
+def march_kernel(
+    center_ref, sharp_ref, gain_ref, color_ref, mask_ref, order_ref, s_ref, modul_ref, base_ref,
+    out_ref, tile_ref,
+):
+    depth_len, rows, lanes = s_ref.shape
+    ntf = center_ref.shape[0]
+    chunk = 4 if ntf % 4 == 0 else 1
+    sub = 8
+    halves = rows // sub
+
+    @pl.loop(0, (ntf // chunk) * halves)
+    def _(step):
+        first = (step // halves) * chunk
+        row = pl.multiple_of((step % halves) * sub, sub)
+        shape = (sub, lanes)
+        mid = [jnp.full(shape, center_ref[first + j], jnp.float32) for j in range(chunk)]
+        bend = [jnp.full(shape, sharp_ref[first + j] * -LOG2E, jnp.float32) for j in range(chunk)]
+        dense = [jnp.full(shape, gain_ref[first + j] * -LOG2E, jnp.float32) for j in range(chunk)]
+        passed = [jnp.ones(shape, jnp.float32)] * chunk
+        total = [jnp.zeros(shape, jnp.float32)] * chunk
+        acc = [[jnp.zeros(shape, jnp.float32)] * 3 for _ in range(chunk)]
+        for z in range(depth_len):
+            s = s_ref[z, pl.ds(row, sub), :]
+            modul = modul_ref[z, pl.ds(row, sub), :]
+            base = [base_ref[k, z, pl.ds(row, sub), :] for k in range(3)]
+            for j in range(chunk):
+                diff = s - mid[j]
+                total[j] = total[j] + modul * jnp.exp2(diff * diff * bend[j])
+                after = jnp.exp2(total[j] * dense[j])
+                weight = passed[j] - after
+                passed[j] = after
+                acc[j] = [acc[j][k] + weight * base[k] for k in range(3)]
+        for j in range(chunk):
+            start = ((first + j) * rows + row) * 4
+            for k in range(3):
+                tile_ref[pl.ds(start + k, sub, stride=4), :] = acc[j][k] * color_ref[k, first + j]
+            tile_ref[pl.ds(start + 3, sub, stride=4), :] = 1.0 - passed[j]
+
+    @pl.loop(0, order_ref.shape[0], unroll=8)
+    def _(slot):
+        tile = order_ref[slot]
+        cover = mask_ref[tile].astype(jnp.float32)
+        out_ref[slot] = tile_ref[pl.ds(pl.multiple_of(tile * 4, 4), 4), :] * cover
+
+
+def march(center, sharp, gain, color, mask, order, s, modul, base):
+    lanes = s.shape[-1]
+    smem = pl.BlockSpec(memory_space=pltpu.SMEM)
+    vmem = pl.BlockSpec(memory_space=pltpu.VMEM)
+    return pl.pallas_call(
+        march_kernel,
+        out_shape=jax.ShapeDtypeStruct((order.shape[0], 4, lanes), jnp.float32),
+        in_specs=[smem] * 6 + [vmem] * 3,
+        out_specs=vmem,
+        scratch_shapes=[pltpu.VMEM((order.shape[0] * 4, lanes), jnp.float32)],
+        compiler_params=pltpu.CompilerParams(vmem_limit_bytes=32 * 1024 * 1024),
+        name="march",
+    )(center, sharp, gain, color, mask, order, s, modul, base)
+
+
+def compose_kernel(part_ref, out_ref):
+    slabs, rows, _ = part_ref.shape
+
+    @pl.loop(0, rows // 32)
+    def _(step):
+        def load(slab, k):
+            return part_ref[slab, pl.ds(step * 32 + k, 8, stride=4), :]
+
+        acc = [load(0, k) for k in range(4)]
+        for slab in range(1, slabs):
+            clear = 1.0 - acc[3]
+            acc = [acc[k] + clear * load(slab, k) for k in range(4)]
+        for k in range(4):
+            out_ref[pl.ds(step * 32 + k, 8, stride=4), :] = acc[k]
+
+
+def compose(parts):
+    vmem = pl.BlockSpec(memory_space=pltpu.VMEM)
+    return pl.pallas_call(
+        compose_kernel,
+        out_shape=jax.ShapeDtypeStruct(parts.shape[1:], jnp.float32),
+        in_specs=[vmem],
+        out_specs=vmem,
+        compiler_params=pltpu.CompilerParams(vmem_limit_bytes=32 * 1024 * 1024),
+        name="compose",
+    )(parts)
 
 
 def shards(
@@ -91,26 +170,14 @@
     )
     modul = 1.0 + 0.5 * jnp.tanh(state[4])
     bases = shade[None] * jax.nn.sigmoid(state[1:4])
-    steps_idx = jnp.arange(depth_len, dtype=jnp.int32)
-    earlier = (steps_idx[:, None] > steps_idx[None, :]).astype(jnp.float32)
-
-    def render(items):
-        center, sharp, gain, color = items
-        depth = gain * jnp.exp(-sharp * (scalar - center) ** 2) * modul
-        before = jnp.einsum("wz,zyx->wyx", earlier, depth, precision=lax.Precision.HIGHEST)
-        weight = jnp.exp(-before) * (1.0 - jnp.exp(-depth))
-        colors = jnp.sum(weight[None] * bases, axis=1) * color[:, None, None]
-        alpha = 1.0 - jnp.exp(-jnp.sum(depth, axis=0))
-        return jnp.transpose(jnp.concatenate([colors, alpha[None]], 0), (1, 0, 2))
-
-    rendered = lax.map(render, (tf_center, tf_sharp, tf_gain, tf_color.T))
-    cover = tile_mask[0].astype(jnp.float32)[..., None]
-    tiles = (rendered * cover).reshape(-1, 4, cols_len)
+    count = lax.axis_size("gz")
     order = tile_perm[0, 0]
-    count = lax.axis_size("gz")
-    per_owner = tiles.shape[0] // count
-    grouped = tiles[order].reshape(count, per_owner, 4, cols_len)
-    composed = fold_slabs(lax.all_to_all(grouped, "gz", split_axis=0, concat_axis=0, tiled=True))
+    per_owner = order.shape[0] // count
+    tiles = march(
+        tf_center, tf_sharp, tf_gain, tf_color, tile_mask[0].reshape(-1), order, scalar, modul, bases
+    )
+    grouped = tiles.reshape(count, per_owner * 4, cols_len)
+    composed = compose(lax.all_to_all(grouped, "gz", split_axis=0, concat_axis=0, tiled=True))
     picture = composed.reshape(1, 1, per_owner, 4, cols_len)
     return (state, picture)
 

time: 220 us -> 124 us (0.56)
  local copies, waits for them, and re-layouts: 51.1 us -> 17.1 us
  matrix products: 27.3 us -> 0 us
  other arithmetic: 58.3 us -> 33.2 us
  loops' own time: 12 us -> 0 us
  Pallas kernels: 0 us -> 4.24 us
    dynamic_slice x48 -> x0, local copies, waits for them, and re-layouts: 30.1 us -> none  [shards(): rendered = lax.map(render, (tf_center, tf_sharp, tf_gain, tf_color.T))]
    dot_general x16 -> x0, matrix products: 27.3 us -> none  [render(): jnp.einsum('wz,zyx->wyx', earlier, depth, precision=lax.Precision.HIGHEST)]
    reduce_sum x32 -> x0, other arithmetic: 22.2 us -> none  [the longest x16 21.1 us: render(): alpha = 1.0 - jnp.exp(-jnp.sum(depth, axis=0))]
    another operation x1 -> x0, loops' own time: 12 us -> none  [shards(): rendered = lax.map(render, (tf_center, tf_sharp, tf_gain, tf_color.T))]
    pallas_call x0 -> x2, Pallas kernels: none -> 4.24 us  [the longest x1 3.5 us: march(): pl.pallas_call(march_kernel, out_shape=jax.ShapeDtypeStruct((order.shape[...]
    mul x32 -> x0, local copies, waits for them, and re-layouts: 2.71 us -> none  [the longest x16 2.52 us: render(): weight = jnp.exp(-before) * (1.0 - jnp.exp(-depth))]
  transfers between devices with their start and end apart: 12 -> 12, of which waited for: 9 -> 9; matrix products, arithmetic and copies ran while one was open for 3% -> 6% of each run, Pallas kernels for 0% -> 0%
where the time goes in v1:
time: 124 us; the launch traced here: 123 us
  other arithmetic  33.2 us (27%)
  starting transfers between devices  32.4 us (26%)
  waiting for transfers between devices  19.6 us (16%)
  local copies, waits for them, and re-layouts  17.1 us (14%)
  blocking collectives  15.7 us (13%)
  Pallas kernels  4.24 us (3%)
    ppermute x6, starting transfers between devices, extended(): lax.ppermute(head, axis, [((i + 1) % count, i) for i in range(ends)])  17.4 us
    all_to_all x1, blocking collectives, shards(): lax.all_to_all(grouped, 'gz', split_axis=0, concat_axis=0, tiled=True)  15.7 us
    ppermute x6, starting transfers between devices, extended(): lax.ppermute(tail, axis, [(i, (i + 1) % count) for i in range(ends)])  15 us
    mul x1, other arithmetic, shards(): widened = widened * valid[None]  13.5 us
    ppermute x6, waiting for transfers between devices, extended(): lax.ppermute(tail, axis, [(i, (i + 1) % count) for i in range(ends)])  11.5 us
    concatenate x4, other arithmetic, extended(): jnp.concatenate([lax.ppermute(tail, axis, [(i, (i + 1) % count) for i in...  8.48 us
    ppermute x6, waiting for transfers between devices, extended(): lax.ppermute(head, axis, [((i + 1) % count, i) for i in range(ends)])  8.07 us
    slice x3, local copies, waits for them, and re-layouts, extended(): lax.slice_in_dim(cells, cells.shape[dim] - width, cells.shape[dim], axis=...  5.88 us
  transfers between devices with their start and end apart: 12, of which 9 were waited for; matrix products, arithmetic and copies ran while one was open for 6% of the time, Pallas kernels for 0%

profile of v1, /device:TPU:6, one launch (start us, length us, event | category | flops | bytes accessed | tf_op | source)
XLA Modules:
  0.0 123.2 jit_solution(17430146529068679276)
XLA Ops:
  0.6 0.0 copy-start.8
  0.6 0.0 copy-start.5
  0.7 1.1 pad_maximum_fusion.38
  1.7 3.5 %collective-permute-start = (f32[6,2,16,128]{3,2,1,0:T(8,128)S(1)}, f32[6,2,16,128]{3,2,1,0:T(8,128)S(1)}, u32[]{:S(2)}, u32[]{:S(2)}) collective-permute-start(f32[6,2,16,128]{3,2,1,0:T(8,128)S(1)} %get-tuple-element.6), channel_id=1, source_target_pairs={{0,8},{8,16},{16,24},{1,9},{9,17},{17,25},{2,10},{10,18},{18,26},{... | collective-permute-start | bytes 294920 | tf_op jit(solution)/shard_map/ppermute | solution.py:17
  5.2 1.3 %collective-permute-start.1 = (f32[6,2,16,128]{3,2,1,0:T(8,128)S(1)}, f32[6,2,16,128]{3,2,1,0:T(8,128)S(1)}, u32[]{:S(2)}, u32[]{:S(2)}) collective-permute-start(f32[6,2,16,128]{3,2,1,0:T(8,128)S(1)} %get-tuple-element.7), channel_id=1, source_target_pairs={{8,0},{16,8},{24,16},{9,1},{17,9},{25,17},{10,2},{18,10},{26,18},{... | collective-permute-start | bytes 294920 | tf_op jit(solution)/shard_map/ppermute | solution.py:19
  6.6 0.1 broadcast_multiply_fusion.1
  6.7 0.8 collective-permute-done
  7.4 4.3 %collective-permute-done.1 = f32[6,2,16,128]{3,2,1,0:T(8,128)S(1)} collective-permute-done((f32[6,2,16,128]{3,2,1,0:T(8,128)S(1)}, f32[6,2,16,128]{3,2,1,0:T(8,128)S(1)}, u32[]{:S(2)}, u32[]{:S(2)}) %collective-permute-start.1) | collective-permute-done | bytes 98336 | tf_op jit(solution)/shard_map/ppermute | solution.py:19
  11.8 1.6 %pad_maximum_fusion.36 = (f32[6,36,2,128]{3,2,1,0:T(2,128)S(1)}, f32[6,36,2,128]{3,2,1,0:T(2,128)S(1)}) fusion(f32[6,2,16,128]{3,2,1,0:T(8,128)S(1)} %collective-permute-done.1, f32[6,2,16,128]{3,2,1,0:T(8,128)S(1)} %collective-permute-done, f32[1,32,16,128]{3,2,1,0:T(8,128)} %bitcast.24, f32[5,32,16,128]{3,2,1,0:T(8,128)} %param.9), kind=kLoop, calls=%fused_computation.107 | loop fusion | flops 331776 | bytes 2211840 | tf_op jit(solution)/shard_map/slice | solution.py:14
  13.4 1.3 %collective-permute-start.2 = (f32[6,36,2,128]{3,2,1,0:T(2,128)S(1)}, f32[6,36,2,128]{3,2,1,0:T(2,128)S(1)}, u32[]{:S(2)}, u32[]{:S(2)}) collective-permute-start(f32[6,36,2,128]{3,2,1,0:T(2,128)S(1)} %get-tuple-element.4), channel_id=1, source_target_pairs={{0,4},{1,5},{2,6},{3,7},{8,12},{9,13},{10,14},{11,15},{16,20},{17,... | collective-permute-start | bytes 663560 | tf_op jit(solution)/shard_map/ppermute | solution.py:17
  14.7 4.6 %collective-permute-start.3 = (f32[6,36,2,128]{3,2,1,0:T(2,128)S(1)}, f32[6,36,2,128]{3,2,1,0:T(2,128)S(1)}, u32[]{:S(2)}, u32[]{:S(2)}) collective-permute-start(f32[6,36,2,128]{3,2,1,0:T(2,128)S(1)} %get-tuple-element.5), channel_id=1, source_target_pairs={{4,0},{5,1},{6,2},{7,3},{12,8},{13,9},{14,10},{15,11},{20,16},{21,... | collective-permute-start | bytes 663560 | tf_op jit(solution)/shard_map/ppermute | solution.py:19
  19.3 0.2 broadcast_multiply_fusion
  19.5 1.8 %collective-permute-done.2 = f32[6,36,2,128]{3,2,1,0:T(2,128)S(1)} collective-permute-done((f32[6,36,2,128]{3,2,1,0:T(2,128)S(1)}, f32[6,36,2,128]{3,2,1,0:T(2,128)S(1)}, u32[]{:S(2)}, u32[]{:S(2)}) %collective-permute-start.2) | collective-permute-done | bytes 221216 | tf_op jit(solution)/shard_map/ppermute | solution.py:17
  21.2 1.5 %collective-permute-done.3 = f32[6,36,2,128]{3,2,1,0:T(2,128)S(1)} collective-permute-done((f32[6,36,2,128]{3,2,1,0:T(2,128)S(1)}, f32[6,36,2,128]{3,2,1,0:T(2,128)S(1)}, u32[]{:S(2)}, u32[]{:S(2)}) %collective-permute-start.3) | collective-permute-done | bytes 221216 | tf_op jit(solution)/shard_map/ppermute | solution.py:19
  22.7 0.0 copy-done.8
  22.7 0.0 copy-done.5
  22.7 0.4 pad_maximum_fusion.13
  23.1 3.2 %fusion.48 = (f32[6,36,20,2]{3,2,1,0:T(8,128)}, f32[6,36,20,2]{3,2,1,0:T(8,128)}) fusion(f32[6,36,20,128]{3,2,1,0:T(8,128)S(1)} %pad_maximum_fusion.13), kind=kLoop, calls=%fused_computation.122 | loop fusion | bytes 138240 | tf_op jit(solution)/shard_map/slice | solution.py:14
  26.3 2.7 %copy.11 = f32[6,36,20,2]{1,3,2,0:T(2,128)S(1)} copy(f32[6,36,20,2]{3,2,1,0:T(8,128)} %get-tuple-element.2) | data formatting | bytes 69120 | tf_op jit(solution)/shard_map/slice | solution.py:14
  29.0 1.9 %collective-permute-start.4 = (f32[6,36,20,2]{1,3,2,0:T(2,128)S(1)}, f32[6,36,20,2]{1,3,2,0:T(2,128)S(1)}, u32[]{:S(2)}, u32[]{:S(2)}) collective-permute-start(f32[6,36,20,2]{1,3,2,0:T(2,128)S(1)} %copy.11), channel_id=1, source_target_pairs={{0,1},{1,2},{2,3},{4,5},{5,6},{6,7},{8,9},{9,10},{10,11},{12,13},{... | collective-permute-start | bytes 103688 | tf_op jit(solution)/shard_map/ppermute | solution.py:17
  30.9 2.7 %copy.12 = f32[6,36,20,2]{1,3,2,0:T(2,128)S(1)} copy(f32[6,36,20,2]{3,2,1,0:T(8,128)} %get-tuple-element.3) | data formatting | bytes 69120 | tf_op jit(solution)/shard_map/slice | solution.py:13
  33.6 3.8 %collective-permute-start.5 = (f32[6,36,20,2]{1,3,2,0:T(2,128)S(1)}, f32[6,36,20,2]{1,3,2,0:T(2,128)}, u32[]{:S(2)}, u32[]{:S(2)}) collective-permute-start(f32[6,36,20,2]{1,3,2,0:T(2,128)S(1)} %copy.12), channel_id=1, source_target_pairs={{1,0},{2,1},{3,2},{5,4},{6,5},{7,6},{9,8},{10,9},{11,10},{13,12},{... | collective-permute-start | bytes 103688 | tf_op jit(solution)/shard_map/ppermute | solution.py:19
  37.4 0.0 copy-done.14
  37.5 0.0 collective-permute-done.4
  37.5 2.6 %copy.13 = f32[6,36,20,2]{3,2,1,0:T(8,128)} copy(f32[6,36,20,2]{1,3,2,0:T(2,128)S(1)} %collective-permute-done.4) | data formatting | bytes 69120 | tf_op jit(solution)/shard_map/ppermute | solution.py:17
  40.1 0.0 collective-permute-done.5
  40.1 3.6 %copy.14 = f32[6,36,20,2]{3,2,1,0:T(8,128)} copy(f32[6,36,20,2]{1,3,2,0:T(2,128)} %collective-permute-done.5) | data formatting | bytes 69120 | tf_op jit(solution)/shard_map/ppermute | solution.py:19
  43.7 8.0 %pad_maximum_fusion = f32[6,36,20,132]{3,2,1,0:T(8,128)S(1)} fusion(f32[6,36,20,2]{3,2,1,0:T(8,128)} %copy.14, f32[6,36,2,128]{3,2,1,0:T(2,128)S(1)} %collective-permute-done.3, f32[6,2,16,128]{3,2,1,0:T(8,128)S(1)} %collective-permute-done.1, f32[1,32,16,128]{3,2,1,0:T(8,128)S(1)} %bitcast.26, f32[5,32,16,128]{3,2,1,0:T(8,128)S(1)} %copy-done.5, ...), kind=kLoop, calls=%fused_computation | loop fusion | flops 3991680 | bytes 4561920 | tf_op jit(solution)/shard_map/concatenate | solution.py:15
  51.7 0.1 slice_bitcast_fusion
  51.7 0.0 copy-start.7
  51.7 1.4 %fusion.31 = (f32[34,18,130]{2,1,0:T(8,128)S(1)}, f32[34,18,130]{2,1,0:T(8,128)S(1)}, f32[34,18,130]{2,1,0:T(8,128)S(1)}, f32[34,18,130]{2,1,0:T(8,128)S(1)}, f3...) fusion(f32[36,20,132]{2,1,0:T(8,128)S(1)} %slice_bitcast_fusion), kind=kLoop, calls=%fused_computation.57 | loop fusion | flops 954720 | bytes 4137120 | tf_op jit(solution)/shard_map/mul | solution.py:45
  53.1 1.7 %fusion.47 = (f32[32,16,128]{2,1,0:T(8,128)}, f32[32,16,128]{2,1,0:T(8,128)}, f32[32,16,128]{2,1,0:T(8,128)}, f32[32,16,128]{2,1,0:T(8,128)}, f32[32,16,128]{2,1,0:T(8,128)}, /*index=5*/f32[32,16,128]{2,1,0:T(8,128)}) fusion(f32[36,20,132]{2,1,0:T(8,128)S(1)} %slice_bitcast_fusion), kind=kLoop, calls=%fused_computation.102 | loop fusion | flops 786432 | bytes 3407872 | tf_op jit(solution)/shard_map/mul | solution.py:45
  54.8 0.7 copy-done.6
  55.5 13.5 %fusion.5 = f32[5,34,18,130]{3,2,1,0:T(8,128)S(1)} fusion(f32[6,36,20,2]{3,2,1,0:T(8,128)S(1)} %copy-done.7, f32[6,36,2,128]{3,2,1,0:T(2,128)} %copy-done.10, f32[6,36,2,128]{3,2,1,0:T(2,128)S(1)} %collective-permute-done.2, f32[6,2,16,128]{3,2,1,0:T(8,128)} %copy-done.12, f32[6,2,16,128]{3,2,1,0:T(8,128)} %copy-done.11, f32[1,32,16,128]{3,2,1,0:T(8,128)S(1)} %bitcast.27, ...), kind=kLoop, calls=%fused_computation.13 | loop fusion | flops 15912000 | bytes 14055900 | tf_op jit(solution)/shard_map/mul | solution.py:161
  69.0 0.0 copy-start.13
  69.0 3.9 %fusion.17 = f32[5,32,16,128]{3,2,1,0:T(8,128)S(1)} fusion(f32[5,34,18,130]{3,2,1,0:T(8,128)S(1)} %fusion.5, f32[5]{0:T(128)S(1)} %get-tuple-element.29, f32[32,16,128]{2,1,0:T(8,128)} %get-tuple-element.17, f32[32,16,128]{2,1,0:T(8,128)} %get-tuple-element.16, f32[5]{0:T(128)S(1)} %get-tuple-element.30, f32[32,16,128]{2,1,0:T(8,128)} %get-tuple-element.13, ...), kind=kLoop, calls=%fused_computation.34 | loop fusion | flops 8847360 | bytes 12058684 | tf_op jit(solution)/shard_map/sub | solution.py:44
  72.9 0.0 copy-start.9
  72.9 0.0 copy-start
  72.9 0.0 copy-start.1
  72.9 0.0 copy-start.2
  72.9 0.0 copy-start.3
  72.9 0.0 copy-start.4
  72.9 1.4 %collective-permute-start.6 = (f32[1,16,128]{2,1,0:T(8,128)S(1)}, f32[1,16,128]{2,1,0:T(8,128)S(1)}, u32[]{:S(2)}, u32[]{:S(2)}) collective-permute-start(f32[1,16,128]{2,1,0:T(8,128)S(1)} %get-tuple-element.9), channel_id=1, source_target_pairs={{8,0},{16,8},{24,16},{9,1},{17,9},{25,17},{10,2},{18,10},{26,18},{... | collective-permute-start | bytes 24584 | tf_op jit(solution)/shard_map/ppermute | solution.py:19
  74.4 4.5 %collective-permute-start.7 = (f32[1,16,128]{2,1,0:T(8,128)S(1)}, f32[1,16,128]{2,1,0:T(8,128)S(1)}, u32[]{:S(2)}, u32[]{:S(2)}) collective-permute-start(f32[1,16,128]{2,1,0:T(8,128)S(1)} %get-tuple-element.8), channel_id=1, source_target_pairs={{0,8},{8,16},{16,24},{1,9},{9,17},{17,25},{2,10},{10,18},{18,26},{... | collective-permute-start | bytes 24584 | tf_op jit(solution)/shard_map/ppermute | solution.py:17
  79.0 0.0 collective-permute-done.6
  79.0 1.3 %collective-permute-done.7 = f32[1,16,128]{2,1,0:T(8,128)S(1)} collective-permute-done((f32[1,16,128]{2,1,0:T(8,128)S(1)}, f32[1,16,128]{2,1,0:T(8,128)S(1)}, u32[]{:S(2)}, u32[]{:S(2)}) %collective-permute-start.7) | collective-permute-done | bytes 8224 | tf_op jit(solution)/shard_map/ppermute | solution.py:17
  80.3 4.4 %collective-permute-start.8 = (f32[34,1,128]{2,1,0:T(1,128)S(1)}, f32[34,1,128]{2,1,0:T(1,128)S(1)}, u32[]{:S(2)}, u32[]{:S(2)}) collective-permute-start(f32[34,1,128]{2,1,0:T(1,128)S(1)} %get-tuple-element.27), channel_id=1, source_target_pairs={{4,0},{5,1},{6,2},{7,3},{12,8},{13,9},{14,10},{15,11},{20,16},{21,... | collective-permute-start | bytes 52232 | tf_op jit(solution)/shard_map/ppermute | solution.py:19
  84.7 1.3 %collective-permute-start.9 = (f32[34,1,128]{2,1,0:T(1,128)S(1)}, f32[34,1,128]{2,1,0:T(1,128)S(1)}, u32[]{:S(2)}, u32[]{:S(2)}) collective-permute-start(f32[34,1,128]{2,1,0:T(1,128)S(1)} %get-tuple-element.26), channel_id=1, source_target_pairs={{0,4},{1,5},{2,6},{3,7},{8,12},{9,13},{10,14},{11,15},{16,20},{17,... | collective-permute-start | bytes 52232 | tf_op jit(solution)/shard_map/ppermute | solution.py:17
  86.0 0.1 collective-permute-done.8
  86.1 4.2 %collective-permute-done.9 = f32[34,1,128]{2,1,0:T(1,128)S(1)} collective-permute-done((f32[34,1,128]{2,1,0:T(1,128)S(1)}, f32[34,1,128]{2,1,0:T(1,128)S(1)}, u32[]{:S(2)}, u32[]{:S(2)}) %collective-permute-start.9) | collective-permute-done | bytes 17440 | tf_op jit(solution)/shard_map/ppermute | solution.py:17
  90.3 0.1 pad_maximum_fusion.14
  90.4 0.9 fusion.49
  91.3 1.9 %collective-permute-start.10 = (f32[34,18,1]{2,1,0:T(8,128)}, f32[34,18,1]{2,1,0:T(8,128)S(1)}, u32[]{:S(2)}, u32[]{:S(2)}) collective-permute-start(f32[34,18,1]{2,1,0:T(8,128)} %get-tuple-element.24), channel_id=1, source_target_pairs={{1,0},{2,1},{3,2},{5,4},{6,5},{7,6},{9,8},{10,9},{11,10},{13,12},{... | collective-permute-start | bytes 7352 | tf_op jit(solution)/shard_map/ppermute | solution.py:19
  93.2 2.4 %collective-permute-start.11 = (f32[34,18,1]{2,1,0:T(8,128)S(1)}, f32[34,18,1]{2,1,0:T(8,128)S(1)}, u32[]{:S(2)}, u32[]{:S(2)}) collective-permute-start(f32[34,18,1]{2,1,0:T(8,128)S(1)} %get-tuple-element.25), channel_id=1, source_target_pairs={{0,1},{1,2},{2,3},{4,5},{5,6},{6,7},{8,9},{9,10},{10,11},{12,13},{... | collective-permute-start | bytes 7352 | tf_op jit(solution)/shard_map/ppermute | solution.py:17
  95.6 0.5 broadcast.138
  96.2 0.7 reduce.3
  96.8 0.1 reshape_squeeze.3.mask_ref
  96.9 2.1 %collective-permute-done.10 = f32[34,18,1]{2,1,0:T(8,128)S(1)} collective-permute-done((f32[34,18,1]{2,1,0:T(8,128)}, f32[34,18,1]{2,1,0:T(8,128)S(1)}, u32[]{:S(2)}, u32[]{:S(2)}) %collective-permute-start.10) | collective-permute-done | bytes 2480 | tf_op jit(solution)/shard_map/ppermute | solution.py:19
  99.1 3.5 %collective-permute-done.11 = f32[34,18,1]{2,1,0:T(8,128)S(1)} collective-permute-done((f32[34,18,1]{2,1,0:T(8,128)S(1)}, f32[34,18,1]{2,1,0:T(8,128)S(1)}, u32[]{:S(2)}, u32[]{:S(2)}) %collective-permute-start.11) | collective-permute-done | bytes 2480 | tf_op jit(solution)/shard_map/ppermute | solution.py:17
  102.6 0.4 multiply_add_fusion
  103.0 0.2 fusion.35.base_ref
  103.3 3.5 %march.1 = f32[256,4,128]{2,1,0:T(4,128)S(1)} custom-call(f32[16]{0:T(128)S(1)} %copy-done.2, f32[16]{0:T(128)S(1)} %copy-done.3, f32[16]{0:T(128)S(1)} %copy-done.4, f32[3,16]{1,0:T(4,128)S(1)} %copy-done, s32[256]{0:T(256)S(1)} %reshape_squeeze.3.mask_ref, s32[256]{0:T(256)S(1)} %bitcast.22, f32[32,16,128]{2,1,0:T(8,128)S(1)} %get-tuple-element.11.s_ref, ...), custom_call_target="tpu_custom_call" | custom-call | tf_op jit(solution)/shard_map/march/pallas_call | solution.py:110
  106.8 15.7 %all_to_all.5.part_ref = f32[4,256,128]{2,1,0:T(8,128)S(1)} all-to-all(f32[4,256,128]{2,1,0:T(8,128)S(1)} %bitcast.21), channel_id=1, replica_groups=mesh['gz'=4,'gy'=2,'gx'=4] {'gz'}, dimensions={0} | all-to-all | bytes 1048576 | tf_op jit(solution)/shard_map/all_to_all | solution.py:180
  122.5 0.7 compose.1
  (23 shorter events, 0.1 us)
Async XLA Ops:
  0.6 22.1 %copy-start.8 = (f32[32,16,128]{2,1,0:T(8,128)S(1)}, f32[32,16,128]{2,1,0:T(8,128)}, u32[]{:S(2)}) copy-start(f32[32,16,128]{2,1,0:T(8,128)} %param.10) | copy-start | bytes 786436
  0.6 22.1 %copy-start.5 = (f32[5,32,16,128]{3,2,1,0:T(8,128)S(1)}, f32[5,32,16,128]{3,2,1,0:T(8,128)}, u32[]{:S(2)}) copy-start(f32[5,32,16,128]{3,2,1,0:T(8,128)} %param.9) | copy-start | bytes 3932164
  1.7 5.7 %collective-permute-start = (f32[6,2,16,128]{3,2,1,0:T(8,128)S(1)}, f32[6,2,16,128]{3,2,1,0:T(8,128)S(1)}, u32[]{:S(2)}, u32[]{:S(2)}) collective-permute-start(f32[6,2,16,128]{3,2,1,0:T(8,128)S(1)} %get-tuple-element.6), channel_id=1, source_target_pairs={{0,8},{8,16},{16,24},{1,9},{9,17},{17,25},{2,10},{10,18},{18,26},{... | collective-permute-start | bytes 294920 | tf_op jit(solution)/shard_map/ppermute | solution.py:17
  5.2 6.5 %collective-permute-start.1 = (f32[6,2,16,128]{3,2,1,0:T(8,128)S(1)}, f32[6,2,16,128]{3,2,1,0:T(8,128)S(1)}, u32[]{:S(2)}, u32[]{:S(2)}) collective-permute-start(f32[6,2,16,128]{3,2,1,0:T(8,128)S(1)} %get-tuple-element.7), channel_id=1, source_target_pairs={{8,0},{16,8},{24,16},{9,1},{17,9},{25,17},{10,2},{18,10},{26,18},{... | collective-permute-start | bytes 294920 | tf_op jit(solution)/shard_map/ppermute | solution.py:19
  7.4 36.2 %copy-start.11 = (f32[6,2,16,128]{3,2,1,0:T(8,128)}, f32[6,2,16,128]{3,2,1,0:T(8,128)S(1)}, u32[]{:S(2)}) copy-start(f32[6,2,16,128]{3,2,1,0:T(8,128)S(1)} %collective-permute-done) | copy-start | bytes 294916
  11.8 31.9 %copy-start.12 = (f32[6,2,16,128]{3,2,1,0:T(8,128)}, f32[6,2,16,128]{3,2,1,0:T(8,128)S(1)}, u32[]{:S(2)}) copy-start(f32[6,2,16,128]{3,2,1,0:T(8,128)S(1)} %collective-permute-done.1) | copy-start | bytes 294916
  13.4 7.8 %collective-permute-start.2 = (f32[6,36,2,128]{3,2,1,0:T(2,128)S(1)}, f32[6,36,2,128]{3,2,1,0:T(2,128)S(1)}, u32[]{:S(2)}, u32[]{:S(2)}) collective-permute-start(f32[6,36,2,128]{3,2,1,0:T(2,128)S(1)} %get-tuple-element.4), channel_id=1, source_target_pairs={{0,4},{1,5},{2,6},{3,7},{8,12},{9,13},{10,14},{11,15},{16,20},{17,... | collective-permute-start | bytes 663560 | tf_op jit(solution)/shard_map/ppermute | solution.py:17
  14.7 8.0 %collective-permute-start.3 = (f32[6,36,2,128]{3,2,1,0:T(2,128)S(1)}, f32[6,36,2,128]{3,2,1,0:T(2,128)S(1)}, u32[]{:S(2)}, u32[]{:S(2)}) collective-permute-start(f32[6,36,2,128]{3,2,1,0:T(2,128)S(1)} %get-tuple-element.5), channel_id=1, source_target_pairs={{4,0},{5,1},{6,2},{7,3},{12,8},{13,9},{14,10},{15,11},{20,16},{21,... | collective-permute-start | bytes 663560 | tf_op jit(solution)/shard_map/ppermute | solution.py:19
  22.7 21.0 %copy-start.10 = (f32[6,36,2,128]{3,2,1,0:T(2,128)}, f32[6,36,2,128]{3,2,1,0:T(2,128)S(1)}, u32[]{:S(2)}) copy-start(f32[6,36,2,128]{3,2,1,0:T(2,128)S(1)} %collective-permute-done.3) | copy-start | bytes 663556
  26.3 11.1 %copy-start.14 = (f32[5,3]{0,1:T(4,128)S(1)}, f32[5,3]{0,1:T(4,128)}, u32[]{:S(2)}) copy-start(f32[5,3]{0,1:T(4,128)} %param.11) | copy-start | bytes 184
  29.0 8.5 %collective-permute-start.4 = (f32[6,36,20,2]{1,3,2,0:T(2,128)S(1)}, f32[6,36,20,2]{1,3,2,0:T(2,128)S(1)}, u32[]{:S(2)}, u32[]{:S(2)}) collective-permute-start(f32[6,36,20,2]{1,3,2,0:T(2,128)S(1)} %copy.11), channel_id=1, source_target_pairs={{0,1},{1,2},{2,3},{4,5},{5,6},{6,7},{8,9},{9,10},{10,11},{12,13},{... | collective-permute-start | bytes 103688 | tf_op jit(solution)/shard_map/ppermute | solution.py:17
  33.6 6.5 %collective-permute-start.5 = (f32[6,36,20,2]{1,3,2,0:T(2,128)S(1)}, f32[6,36,20,2]{1,3,2,0:T(2,128)}, u32[]{:S(2)}, u32[]{:S(2)}) collective-permute-start(f32[6,36,20,2]{1,3,2,0:T(2,128)S(1)} %copy.12), channel_id=1, source_target_pairs={{1,0},{2,1},{3,2},{5,4},{6,5},{7,6},{9,8},{10,9},{11,10},{13,12},{... | collective-permute-start | bytes 103688 | tf_op jit(solution)/shard_map/ppermute | solution.py:19
  51.7 3.1 %copy-start.7 = (f32[6,36,20,2]{3,2,1,0:T(8,128)S(1)}, f32[6,36,20,2]{3,2,1,0:T(8,128)}, u32[]{:S(2)}) copy-start(f32[6,36,20,2]{3,2,1,0:T(8,128)} %copy.14) | copy-start | bytes 103684
  53.1 2.4 %copy-start.6 = (f32[6,36,20,2]{3,2,1,0:T(8,128)S(1)}, f32[6,36,20,2]{3,2,1,0:T(8,128)}, u32[]{:S(2)}) copy-start(f32[6,36,20,2]{3,2,1,0:T(8,128)} %copy.13) | copy-start | bytes 103684
  69.0 27.2 %copy-start.13 = (s32[1,16,16,1]{2,3,1,0:T(1,128)S(1)}, s32[1,16,16,1]{2,3,1,0:T(1,128)}, u32[]{:S(2)}) copy-start(s32[1,16,16,1]{2,3,1,0:T(1,128)} %param.16) | copy-start | bytes 3076
  72.9 33.9 %copy-start.9 = (f32[5,32,16,128]{3,2,1,0:T(8,128)}, f32[5,32,16,128]{3,2,1,0:T(8,128)S(1)}, u32[]{:S(2)}) copy-start(f32[5,32,16,128]{3,2,1,0:T(8,128)S(1)} %fusion.17) | copy-start | bytes 3932164
  72.9 30.4 %copy-start = (f32[3,16]{1,0:T(4,128)S(1)}, f32[3,16]{1,0:T(4,128)}, u32[]{:S(2)}) copy-start(f32[3,16]{1,0:T(4,128)} %color_ref.1) | copy-start | bytes 580
  72.9 30.4 %copy-start.1 = (s32[1,1,256]{2,1,0:T(1,128)S(1)}, s32[1,1,256]{2,1,0:T(1,128)}, u32[]{:S(2)}) copy-start(s32[1,1,256]{2,1,0:T(1,128)} %param.17) | copy-start | bytes 3076
  72.9 30.4 %copy-start.2 = (f32[16]{0:T(128)S(1)}, f32[16]{0:T(128)}, u32[]{:S(2)}) copy-start(f32[16]{0:T(128)} %center_ref.1) | copy-start | bytes 196
  72.9 30.4 %copy-start.3 = (f32[16]{0:T(128)S(1)}, f32[16]{0:T(128)}, u32[]{:S(2)}) copy-start(f32[16]{0:T(128)} %sharp_ref.1) | copy-start | bytes 196
  72.9 30.4 %copy-start.4 = (f32[16]{0:T(128)S(1)}, f32[16]{0:T(128)}, u32[]{:S(2)}) copy-start(f32[16]{0:T(128)} %gain_ref.1) | copy-start | bytes 196
  72.9 6.0 %collective-permute-start.6 = (f32[1,16,128]{2,1,0:T(8,128)S(1)}, f32[1,16,128]{2,1,0:T(8,128)S(1)}, u32[]{:S(2)}, u32[]{:S(2)}) collective-permute-start(f32[1,16,128]{2,1,0:T(8,128)S(1)} %get-tuple-element.9), channel_id=1, source_target_pairs={{8,0},{16,8},{24,16},{9,1},{17,9},{25,17},{10,2},{18,10},{26,18},{... | collective-permute-start | bytes 24584 | tf_op jit(solution)/shard_map/ppermute | solution.py:19
  74.4 5.9 %collective-permute-start.7 = (f32[1,16,128]{2,1,0:T(8,128)S(1)}, f32[1,16,128]{2,1,0:T(8,128)S(1)}, u32[]{:S(2)}, u32[]{:S(2)}) collective-permute-start(f32[1,16,128]{2,1,0:T(8,128)S(1)} %get-tuple-element.8), channel_id=1, source_target_pairs={{0,8},{8,16},{16,24},{1,9},{9,17},{17,25},{2,10},{10,18},{18,26},{... | collective-permute-start | bytes 24584 | tf_op jit(solution)/shard_map/ppermute | solution.py:17
  80.3 5.8 %collective-permute-start.8 = (f32[34,1,128]{2,1,0:T(1,128)S(1)}, f32[34,1,128]{2,1,0:T(1,128)S(1)}, u32[]{:S(2)}, u32[]{:S(2)}) collective-permute-start(f32[34,1,128]{2,1,0:T(1,128)S(1)} %get-tuple-element.27), channel_id=1, source_target_pairs={{4,0},{5,1},{6,2},{7,3},{12,8},{13,9},{14,10},{15,11},{20,16},{21,... | collective-permute-start | bytes 52232 | tf_op jit(solution)/shard_map/ppermute | solution.py:19
  84.7 5.6 %collective-permute-start.9 = (f32[34,1,128]{2,1,0:T(1,128)S(1)}, f32[34,1,128]{2,1,0:T(1,128)S(1)}, u32[]{:S(2)}, u32[]{:S(2)}) collective-permute-start(f32[34,1,128]{2,1,0:T(1,128)S(1)} %get-tuple-element.26), channel_id=1, source_target_pairs={{0,4},{1,5},{2,6},{3,7},{8,12},{9,13},{10,14},{11,15},{16,20},{17,... | collective-permute-start | bytes 52232 | tf_op jit(solution)/shard_map/ppermute | solution.py:17
  91.3 7.8 %collective-permute-start.10 = (f32[34,18,1]{2,1,0:T(8,128)}, f32[34,18,1]{2,1,0:T(8,128)S(1)}, u32[]{:S(2)}, u32[]{:S(2)}) collective-permute-start(f32[34,18,1]{2,1,0:T(8,128)} %get-tuple-element.24), channel_id=1, source_target_pairs={{1,0},{2,1},{3,2},{5,4},{6,5},{7,6},{9,8},{10,9},{11,10},{13,12},{... | collective-permute-start | bytes 7352 | tf_op jit(solution)/shard_map/ppermute | solution.py:19
  93.2 9.4 %collective-permute-start.11 = (f32[34,18,1]{2,1,0:T(8,128)S(1)}, f32[34,18,1]{2,1,0:T(8,128)S(1)}, u32[]{:S(2)}, u32[]{:S(2)}) collective-permute-start(f32[34,18,1]{2,1,0:T(8,128)S(1)} %get-tuple-element.25), channel_id=1, source_target_pairs={{0,1},{1,2},{2,3},{4,5},{5,6},{6,7},{8,9},{9,10},{10,11},{12,13},{... | collective-permute-start | bytes 7352 | tf_op jit(solution)/shard_map/ppermute | solution.py:17

commit v2 on v1

v2 whole, which is shorter than its diff:
```python
import jax
import jax.numpy as jnp
from jax import lax
from jax.experimental import pallas as pl
from jax.experimental.pallas import tpu as pltpu
from jax.sharding import PartitionSpec as P

LOG2E = 1.4426950408889634
W = 3
SUB = 8
F32 = jnp.float32


def reach(field, nfield):
    return W if field in (0, nfield) else W - 1


def tiles_of(first, last):
    return [min(start, last - SUB) for start in range(first, last, SUB)]


def z_plan(nfield):
    plan, at = [], 0
    for field in range(nfield + 1):
        plan.append((field, at, reach(field, nfield)))
        at += reach(field, nfield)
    return plan, at


def y_plan(nfield, depth_len):
    plan, at = [], 0
    for field in range(nfield + 1):
        wide = reach(field, nfield)
        for away in range(1, wide + 1):
            extra = wide - away
            plan.append((field, away, -extra, depth_len + 2 * extra, at))
            at += depth_len + 2 * extra
    return plan, at + (-at) % SUB


def source_plane(refs, field, z):
    fields_ref, kappa_ref, zlo_ref, zhi_ref = refs
    nfield, depth_len = fields_ref.shape[:2]
    _, at, wide = z_plan(nfield)[0][field]
    if z < 0:
        return zlo_ref.at[at + wide + z]
    if z >= depth_len:
        return zhi_ref.at[at + z - depth_len]
    return kappa_ref.at[z] if field == nfield else fields_ref.at[field, z]


def pack_rows_kernel(fields_ref, kappa_ref, zlo_ref, zhi_ref, lo_ref, hi_ref):
    refs = (fields_ref, kappa_ref, zlo_ref, zhi_ref)
    nfield, depth_len, rows, lanes = fields_ref.shape
    flat_fields = fields_ref.reshape(nfield * depth_len * rows, lanes)
    flat_kappa = kappa_ref.reshape(depth_len * rows, lanes)
    plan, used = y_plan(nfield, depth_len)
    for out_ref, top in ((lo_ref, True), (hi_ref, False)):
        for field, away, first, length, at in plan:
            row = away - 1 if top else rows - away
            for z in list(range(first, 0)) + list(range(depth_len, first + length)):
                out_ref[at + z - first, :] = source_plane(refs, field, z)[row, :]
            flat, base = (flat_kappa, 0) if field == nfield else (flat_fields, field * depth_len * rows)
            for z in range(0, depth_len, SUB):
                out_ref[pl.ds(at - first + z, SUB), :] = flat[
                    pl.ds(base + z * rows + row, SUB, stride=rows), :
                ]
        spare = plan[-1][3] + plan[-1][4]
        if used > spare:
            out_ref[spare:used, :] = jnp.zeros((used - spare, lanes), F32)


def assemble(refs, ylo_ref, yhi_ref, flags_ref, pad_ref):
    fields_ref, kappa_ref, zlo_ref, zhi_ref = refs
    nfield, depth_len, rows, lanes = fields_ref.shape
    planes, pitch = depth_len + 2 * W, rows + 8

    @pl.loop(0, depth_len)
    def _(z):
        for field in range(nfield + 1):
            for r in range(0, rows, SUB):
                value = kappa_ref[z, r : r + SUB, :] if field == nfield else fields_ref[field, z, r : r + SUB, :]
                pad_ref[field * planes + W + z, W + r : W + r + SUB, :] = value

    for field, at, wide in z_plan(nfield)[0]:
        for k in range(wide):
            for r in range(0, rows, SUB):
                pad_ref[field * planes + W - wide + k, W + r : W + r + SUB, :] = zlo_ref[at + k, r : r + SUB, :]
                pad_ref[field * planes + W + depth_len + k, W + r : W + r + SUB, :] = zhi_ref[at + k, r : r + SUB, :]
    flat = pad_ref.reshape((nfield + 1) * planes * pitch, lanes)
    low, high = flags_ref[2], flags_ref[3]
    for field, away, first, length, at in y_plan(nfield, depth_len)[0]:
        for ref, flag, row in ((ylo_ref, low, W - away), (yhi_ref, high, W + rows + away - 1)):
            for start in tiles_of(0, length):
                flat[pl.ds((field * planes + W + first + start) * pitch + row, SUB, stride=pitch), :] = (
                    ref[pl.ds(at + start, SUB), :] * flag
                )


def clear_pad(pad_ref):
    @pl.loop(0, pad_ref.shape[0])
    def _(plane):
        pad_ref[plane] = jnp.zeros(pad_ref.shape[1:], F32)


def pack_columns_kernel(
    flags_ref, fields_ref, kappa_ref, zlo_ref, zhi_ref, ylo_ref, yhi_ref, lo_ref, hi_ref, pad_ref
):
    refs = (fields_ref, kappa_ref, zlo_ref, zhi_ref)
    nfield, depth_len, rows, lanes = fields_ref.shape
    planes, pitch = depth_len + 2 * W, rows + 8
    clear_pad(pad_ref)
    assemble(refs, ylo_ref, yhi_ref, flags_ref, pad_ref)
    lane = lax.broadcasted_iota(jnp.int32, (SUB, lanes), 1)

    @pl.loop(0, nfield + 1)
    def _(field):
        for r in range(0, pitch, SUB):

            def body(zi, carry):
                low, high = carry
                value = pad_ref[field * planes + zi, r : r + SUB, :]
                mine = (lane >= W * zi) & (lane < W * zi + W)
                low = jnp.where(mine, pltpu.roll(value, W * zi, 1), low)
                high = jnp.where(mine, pltpu.roll(value, lax.rem(W * zi + W, lanes), 1), high)
                return low, high

            zero = jnp.zeros((SUB, lanes), F32)
            low, high = lax.fori_loop(0, planes, body, (zero, zero), unroll=planes)
            lo_ref[field, r : r + SUB, :] = low
            hi_ref[field, r : r + SUB, :] = high


def stencil(u, coefs, ups, downs, speeds):
    total = u
    for axis in range(3):
        k_up, k_down = coefs[axis]
        total = total + k_up * (ups[axis] - u) + (k_down + speeds[axis]) * (downs[axis] - u)
    return total


def side_neighbours(near, own, is_left, lanes, col):
    first, second = (near, own) if is_left else (own, near)
    first_up = jnp.where(col == W - 1, pltpu.roll(second, W - 1, 1), pltpu.roll(first, lanes - 1, 1))
    first_down = pltpu.roll(first, 1, 1)
    second_up = pltpu.roll(second, lanes - 1, 1)
    second_down = jnp.where(col == 0, pltpu.roll(first, lanes - (W - 1), 1), pltpu.roll(second, 1, 1))
    pair = ((first_up, first_down), (second_up, second_down))
    return pair if is_left else (pair[1], pair[0])


def main_kernel(
    flags_ref, courant_ref, center_ref, sharp_ref, gain_ref, color_ref, mask_ref, order_ref,
    fields_ref, kappa_ref, zlo_ref, zhi_ref, ylo_ref, yhi_ref, xlo_ref, xhi_ref, ownlo_ref, ownhi_ref,
    state_ref, out_ref,
    pad_ref, next_ref, last_ref, side_ref, edge_ref, base_ref, tile_ref,
):
    refs = (fields_ref, kappa_ref, zlo_ref, zhi_ref)
    nfield, depth_len, rows, lanes = fields_ref.shape
    planes, pitch = depth_len + 2 * W, rows + 8
    clear_pad(pad_ref)
    assemble(refs, ylo_ref, yhi_ref, flags_ref, pad_ref)
    lane = lax.broadcasted_iota(jnp.int32, (SUB, lanes), 1)
    sub = lax.broadcasted_iota(jnp.int32, (SUB, lanes), 0)
    zi_of = lane // W
    col = lane - zi_of * W
    flag = [flags_ref[i] for i in range(6)]
    speed = [[courant_ref[f, a] for a in range(3)] for f in range(nfield)]

    def row_mask(r):
        y = sub + (r - W)
        return jnp.where(y < 0, flag[2], jnp.where(y >= rows, flag[3], 1.0))

    def lane_z_mask():
        return jnp.where(zi_of < W, flag[0], jnp.where(zi_of >= W + depth_len, flag[1], 1.0))

    sides = ((xlo_ref, ownlo_ref, True, flag[4]), (xhi_ref, ownhi_ref, False, flag[5]))
    for side, (near_ref, own_ref, _, _) in enumerate(sides):
        for field in range(nfield + 1):
            side_ref[0, side, 0, field] = near_ref[field]
            side_ref[0, side, 1, field] = own_ref[field]

    def edges(level, field):
        for r in range(0, pitch, SUB):
            left = side_ref[level, 0, 0, field, r : r + SUB, :]
            right = side_ref[level, 1, 0, field, r : r + SUB, :]
            edge_ref[level, field, r : r + SUB, :] = jnp.where(col == W - 1, left, pltpu.roll(right, 1, 1))

    def side_step(level, count, r):
        zmask = lane_z_mask() * row_mask(r)
        for side, (_, _, is_left, present) in enumerate(sides):
            def get(block, field, dr=0, lvl=level):
                return side_ref[lvl, side, block, field, r + dr : r + dr + SUB, :]

            blocks = (0, 1)
            kx = side_neighbours(get(0, nfield, 0, 0), get(1, nfield, 0, 0), is_left, lanes, col)
            coefs = []
            for block in blocks:
                k = get(block, nfield, 0, 0)
                coefs.append(
                    [
                        (0.5 * (k + pltpu.roll(k, lanes - W, 1)), 0.5 * (k + pltpu.roll(k, W, 1))),
                        (0.5 * (k + get(block, nfield, 1, 0)), 0.5 * (k + get(block, nfield, -1, 0))),
                        (0.5 * (k + kx[block][0]), 0.5 * (k + kx[block][1])),
                    ]
                )
            for field in range(count):
                ux = side_neighbours(get(0, field), get(1, field), is_left, lanes, col)
                for block in blocks:
                    u = get(block, field)
                    ups = (pltpu.roll(u, lanes - W, 1), get(block, field, 1), ux[block][0])
                    downs = (pltpu.roll(u, W, 1), get(block, field, -1), ux[block][1])
                    value = stencil(u, coefs[block], ups, downs, speed[field])
                    side_ref[level + 1, side, block, field, r : r + SUB, :] = (
                        value * (zmask * present) if block == 0 else value * zmask
                    )

    def along_x(value, zi, edge):
        turned = pltpu.roll(edge, lax.rem(2 * lanes - 2 - W * zi, lanes), 1)
        up = jnp.where(lane == lanes - 1, turned, pltpu.roll(value, lanes - 1, 1))
        down = jnp.where(lane == 0, turned, pltpu.roll(value, 1, 1))
        return up, down

    def kappa_coefs(zi, r):
        plane = nfield * planes + zi
        k = pad_ref[plane, r : r + SUB, :]
        up, down = along_x(k, zi, edge_ref[0, nfield, r : r + SUB, :])
        half = 0.5 * k
        return [
            (half + 0.5 * pad_ref[plane + 1, r : r + SUB, :], half + 0.5 * pad_ref[plane - 1, r : r + SUB, :]),
            (half + 0.5 * pad_ref[plane, r + 1 : r + 1 + SUB, :], half + 0.5 * pad_ref[plane, r - 1 : r - 1 + SUB, :]),
            (half + 0.5 * up, half + 0.5 * down),
        ]

    def step_value(src_ref, level, field, zi, r, coefs):
        plane = field * planes + zi
        u = src_ref[plane, r : r + SUB, :]
        x_up, x_down = along_x(u, zi, edge_ref[level, field, r : r + SUB, :])
        ups = (src_ref[plane + 1, r : r + SUB, :], src_ref[plane, r + 1 : r + 1 + SUB, :], x_up)
        downs = (src_ref[plane - 1, r : r + SUB, :], src_ref[plane, r - 1 : r - 1 + SUB, :], x_down)
        return stencil(u, coefs, ups, downs, speed[field])

    def depth_mask(zi):
        return jnp.where(zi < W, flag[0], jnp.where(zi >= W + depth_len, flag[1], 1.0))

    for field in range(nfield + 1):
        edges(0, field)
    for r in tiles_of(1, rows + 2 * W - 1):
        side_step(0, nfield, r)
    for field in range(nfield):
        edges(1, field)
    for r in tiles_of(2, rows + 2 * W - 2):
        side_step(1, 1, r)
    edges(2, 0)

    @pl.loop(1, planes - 1)
    def _(zi):
        zmask = depth_mask(zi)
        for r in tiles_of(1, rows + 2 * W - 1):
            mask = row_mask(r) * zmask
            coefs = kappa_coefs(zi, r)
            for field in range(nfield):
                next_ref[field * planes + zi, r : r + SUB, :] = mask * step_value(
                    pad_ref, 0, field, zi, r, coefs
                )

    @pl.loop(2, planes - 2)
    def _(zi):
        zmask = depth_mask(zi)
        for r in tiles_of(2, rows + 2 * W - 2):
            value = step_value(next_ref, 1, 0, zi, r, kappa_coefs(zi, r))
            last_ref[zi, r : r + SUB, :] = value * (row_mask(r) * zmask)

    @pl.loop(0, depth_len)
    def _(z):
        zi = z + W
        for r in range(W, W + rows, SUB):
            coefs = kappa_coefs(zi, r)
            s = last_ref[zi, r : r + SUB, :]
            state_ref[0, z, r - W : r - W + SUB, :] = s
            x_up, x_down = along_x(s, zi, edge_ref[2, 0, r : r + SUB, :])
            g_z = 0.5 * (last_ref[zi + 1, r : r + SUB, :] - last_ref[zi - 1, r : r + SUB, :])
            g_y = 0.5 * (last_ref[zi, r + 1 : r + 1 + SUB, :] - last_ref[zi, r - 1 : r - 1 + SUB, :])
            g_x = 0.5 * (x_up - x_down)
            shade = 0.35 + 0.65 * jnp.abs(0.64 * g_z + 0.6 * g_y + 0.48 * g_x) * lax.rsqrt(
                g_z * g_z + g_y * g_y + g_x * g_x + 1.0
            )
            for field in range(1, nfield):
                value = step_value(next_ref, 1, field, zi, r, coefs)
                state_ref[field, z, r - W : r - W + SUB, :] = value
                if field <= 3:
                    base_ref[field, z, r - W : r - W + SUB, :] = shade * (0.5 + 0.5 * jnp.tanh(0.5 * value))
                if field == 4:
                    base_ref[0, z, r - W : r - W + SUB, :] = 1.0 + 0.5 * jnp.tanh(value)

    ntf = center_ref.shape[0]
    chunk = 4 if ntf % 4 == 0 else 1
    halves = rows // SUB

    @pl.loop(0, (ntf // chunk) * halves)
    def _(step):
        first = (step // halves) * chunk
        row = pl.multiple_of((step % halves) * SUB, SUB)
        shape = (SUB, lanes)
        mid = [jnp.full(shape, center_ref[first + j], jnp.float32) for j in range(chunk)]
        bend = [jnp.full(shape, sharp_ref[first + j] * -LOG2E, jnp.float32) for j in range(chunk)]
        dense = [jnp.full(shape, gain_ref[first + j] * -LOG2E, jnp.float32) for j in range(chunk)]
        passed = [jnp.ones(shape, jnp.float32)] * chunk
        total = [jnp.zeros(shape, jnp.float32)] * chunk
        acc = [[jnp.zeros(shape, jnp.float32)] * 3 for _ in range(chunk)]
        for z in range(depth_len):
            s = state_ref[0, z, pl.ds(row, SUB), :]
            modul = base_ref[0, z, pl.ds(row, SUB), :]
            base = [base_ref[k + 1, z, pl.ds(row, SUB), :] for k in range(3)]
            for j in range(chunk):
                diff = s - mid[j]
                total[j] = total[j] + modul * jnp.exp2(diff * diff * bend[j])
                after = jnp.exp2(total[j] * dense[j])
                weight = passed[j] - after
                passed[j] = after
                acc[j] = [acc[j][k] + weight * base[k] for k in range(3)]
        for j in range(chunk):
            start = ((first + j) * rows + row) * 4
            for k in range(3):
                tile_ref[pl.ds(start + k, SUB, stride=4), :] = acc[j][k] * color_ref[k, first + j]
            tile_ref[pl.ds(start + 3, SUB, stride=4), :] = 1.0 - passed[j]

    @pl.loop(0, order_ref.shape[0], unroll=8)
    def _(slot):
        tile = order_ref[slot]
        cover = mask_ref[tile].astype(jnp.float32)
        out_ref[slot] = tile_ref[pl.ds(pl.multiple_of(tile * 4, 4), 4), :] * cover


def compose_kernel(part_ref, out_ref):
    slabs, rows, _ = part_ref.shape

    @pl.loop(0, rows // 32)
    def _(step):
        def load(slab, k):
            return part_ref[slab, pl.ds(step * 32 + k, 8, stride=4), :]

        acc = [load(0, k) for k in range(4)]
        for slab in range(1, slabs):
            clear = 1.0 - acc[3]
            acc = [acc[k] + clear * load(slab, k) for k in range(4)]
        for k in range(4):
            out_ref[pl.ds(step * 32 + k, 8, stride=4), :] = acc[k]


def compose(parts):
    vmem = pl.BlockSpec(memory_space=pltpu.VMEM)
    return pl.pallas_call(
        compose_kernel,
        out_shape=jax.ShapeDtypeStruct(parts.shape[1:], jnp.float32),
        in_specs=[vmem],
        out_specs=vmem,
        compiler_params=pltpu.CompilerParams(vmem_limit_bytes=32 * 1024 * 1024),
        name="compose",
    )(parts)


def shift(message, axis, up):
    count = lax.axis_size(axis)
    pairs = [(i, i + 1) if up else (i + 1, i) for i in range(count - 1)]
    return lax.ppermute(message, axis, pairs)


def present(axis):
    here = lax.axis_index(axis)
    return [(here > 0).astype(F32), (here < lax.axis_size(axis) - 1).astype(F32)]


def shards(
    fields, diffusivity, courant, tf_center, tf_sharp, tf_gain, tf_color, tile_mask, tile_perm
):
    nfield, depth_len, rows_len, cols_len = fields.shape
    planes, pitch = depth_len + 2 * W, rows_len + 8
    smem = pl.BlockSpec(memory_space=pltpu.SMEM)
    vmem = pl.BlockSpec(memory_space=pltpu.VMEM)
    params = pltpu.CompilerParams(vmem_limit_bytes=40 * 1024 * 1024)

    def array(*shape):
        return jax.ShapeDtypeStruct(shape, F32)

    flags = jnp.stack(present("gz") + present("gy") + present("gx"))

    def z_faces(low):
        faces = []
        for field in range(nfield + 1):
            wide = reach(field, nfield)
            source = diffusivity if field == nfield else fields[field]
            faces.append(source[:wide] if low else source[depth_len - wide :])
        return jnp.concatenate(faces, 0)

    zlo = shift(z_faces(False), "gz", True)
    zhi = shift(z_faces(True), "gz", False)
    used = y_plan(nfield, depth_len)[1]
    send_lo, send_hi = pl.pallas_call(
        pack_rows_kernel,
        out_shape=(array(used, cols_len), array(used, cols_len)),
        in_specs=[vmem] * 4,
        out_specs=(vmem, vmem),
        compiler_params=params,
        name="pack_rows",
    )(fields, diffusivity, zlo, zhi)
    if lax.axis_size("gy") == 2:
        mine = jnp.where(lax.axis_index("gy") == 0, send_hi, send_lo)
        ylo = yhi = lax.ppermute(mine, "gy", [(0, 1), (1, 0)])
    else:
        ylo = shift(send_hi, "gy", True)
        yhi = shift(send_lo, "gy", False)
    pad = pltpu.VMEM(((nfield + 1) * planes, pitch, cols_len), F32)
    own_lo, own_hi = pl.pallas_call(
        pack_columns_kernel,
        out_shape=(array(nfield + 1, pitch, cols_len),) * 2,
        in_specs=[smem] + [vmem] * 6,
        out_specs=(vmem, vmem),
        scratch_shapes=[pad],
        compiler_params=params,
        name="pack_columns",
    )(flags, fields, diffusivity, zlo, zhi, ylo, yhi)
    xlo = shift(own_hi, "gx", True)
    xhi = shift(own_lo, "gx", False)
    count = lax.axis_size("gz")
    order = tile_perm[0, 0]
    per_owner = order.shape[0] // count
    state, tiles = pl.pallas_call(
        main_kernel,
        out_shape=(array(*fields.shape), array(order.shape[0], 4, cols_len)),
        in_specs=[smem] * 8 + [vmem] * 10,
        out_specs=(vmem, vmem),
        scratch_shapes=[
            pad,
            pltpu.VMEM((nfield * planes, pitch, cols_len), F32),
            pltpu.VMEM((planes, pitch, cols_len), F32),
            pltpu.VMEM((3, 2, 2, nfield + 1, pitch, cols_len), F32),
            pltpu.VMEM((3, nfield + 1, pitch, cols_len), F32),
            pltpu.VMEM((4, depth_len, rows_len, cols_len), F32),
            pltpu.VMEM((order.shape[0] * 4, cols_len), F32),
        ],
        compiler_params=params,
        name="step_and_march",
    )(
        flags, courant, tf_center, tf_sharp, tf_gain, tf_color, tile_mask[0].reshape(-1), order,
        fields, diffusivity, zlo, zhi, ylo, yhi, xlo, xhi, own_lo, own_hi,
    )
    grouped = tiles.reshape(count, per_owner * 4, cols_len)
    composed = compose(lax.all_to_all(grouped, "gz", split_axis=0, concat_axis=0, tiled=True))
    picture = composed.reshape(1, 1, per_owner, 4, cols_len)
    return (state, picture)


def solution(mesh):
    return jax.shard_map(
        shards,
        mesh=mesh,
        in_specs=(
            P(None, "gz", "gy", "gx"),
            P("gz", "gy", "gx"),
            P(),
            P(),
            P(),
            P(),
            P(),
            P("gz", None, "gy", "gx"),
            P("gy", "gx", None),
        ),
        out_specs=(P(None, "gz", "gy", "gx"), P("gy", "gx", "gz", None, None)),
        check_vma=False,
    )
```

time: 124 us -> 75 us (0.60)
  the two profiles are of different devices: /device:TPU:6 before, /device:TPU:1 now
where the time goes in v2:
time: 75 us; the launch traced here: 74.1 us
  Pallas kernels  23.7 us (32%)
  blocking collectives  17.9 us (24%)
  starting transfers between devices  15 us (20%)
  waiting for transfers between devices  8.44 us (11%)
  local copies, waits for them, and re-layouts  7.62 us (10%)
  between operations  0.79 us (1%)
    pallas_call x1, Pallas kernels, shards(): pl.pallas_call(main_kernel, out_shape=(array(*fields.shape), array(order....  18.7 us
    all_to_all x1, blocking collectives, shards(): lax.all_to_all(grouped, 'gz', split_axis=0, concat_axis=0, tiled=True)  17.9 us
    ppermute x4, starting transfers between devices, shift(): return lax.ppermute(message, axis, pairs)  13.5 us
    unnamed x29, local copies, waits for them, and re-layouts  6.68 us
    ppermute x1, waiting for transfers between devices, shards(): ylo = yhi = lax.ppermute(mine, 'gy', [(0, 1), (1, 0)])  4.31 us
    ppermute x4, waiting for transfers between devices, shift(): return lax.ppermute(message, axis, pairs)  4.13 us
    pallas_call x1, Pallas kernels, shards(): pl.pallas_call(pack_columns_kernel, out_shape=(array(nfield + 1, pitch, c...  4.03 us
  transfers between devices with their start and end apart: 5, of which 4 were waited for; matrix products, arithmetic and copies ran while one was open for 2% of the time, Pallas kernels for 0%

profile of v2, /device:TPU:1, one launch (start us, length us, event | category | flops | bytes accessed | tf_op | source)
XLA Modules:
  0.0 74.1 jit_solution(15188019225561623133)
XLA Ops:
  0.6 0.8 %constant_dynamic-update-slice_fusion.11 = (f32[14,16,128]{2,1,0:T(8,128)S(1)}, f32[14,16,128]{2,1,0:T(8,128)S(1)}) fusion(f32[5,32,16,128]{3,2,1,0:T(8,128)} %fields_ref.5), kind=kLoop, calls=%fused_computation.12 | loop fusion | bytes 98304
  1.4 0.7 constant_dynamic-update-slice_fusion.10
  2.1 0.0 copy-start.3
  2.1 0.8 %constant_dynamic-update-slice_fusion.9 = (f32[14,16,128]{2,1,0:T(8,128)S(1)}, f32[14,16,128]{2,1,0:T(8,128)S(1)}) fusion(f32[14,16,128]{2,1,0:T(8,128)S(1)} %get-tuple-element.20, f32[5,32,16,128]{3,2,1,0:T(8,128)} %fields_ref.5, f32[14,16,128]{2,1,0:T(8,128)S(1)} %get-tuple-element.21), kind=kLoop, calls=%fused_computation.10 | loop fusion | bytes 65536
  2.9 0.7 constant_dynamic-update-slice_fusion.8
  3.7 0.7 constant_dynamic-update-slice_fusion.7
  4.4 0.8 %constant_dynamic-update-slice_fusion.6 = (f32[14,16,128]{2,1,0:T(8,128)S(1)}, f32[14,16,128]{2,1,0:T(8,128)S(1)}) fusion(f32[14,16,128]{2,1,0:T(8,128)S(1)} %get-tuple-element.14, f32[32,16,128]{2,1,0:T(8,128)} %kappa_ref.5, f32[14,16,128]{2,1,0:T(8,128)S(1)} %get-tuple-element.15), kind=kLoop, calls=%fused_computation.7 | loop fusion | bytes 98304 | tf_op jit(solution)/shard_map/concatenate | solution.py:394
  5.1 1.3 %collective-permute-start.1 = (f32[14,16,128]{2,1,0:T(8,128)S(1)}, f32[14,16,128]{2,1,0:T(8,128)S(1)}, u32[]{:S(2)}, u32[]{:S(2)}) collective-permute-start(f32[14,16,128]{2,1,0:T(8,128)S(1)} %get-tuple-element.24), channel_id=1, source_target_pairs={{8,0},{16,8},{24,16},{9,1},{17,9},{25,17},{10,2},{18,10},{26,18},{... | collective-permute-start | bytes 344072 | tf_op jit(solution)/shard_map/ppermute | solution.py:366
  6.4 4.7 %collective-permute-start = (f32[14,16,128]{2,1,0:T(8,128)S(1)}, f32[14,16,128]{2,1,0:T(8,128)S(1)}, u32[]{:S(2)}, u32[]{:S(2)}) collective-permute-start(f32[14,16,128]{2,1,0:T(8,128)S(1)} %get-tuple-element.25), channel_id=1, source_target_pairs={{0,8},{8,16},{16,24},{1,9},{9,17},{17,25},{2,10},{10,18},{18,26},{... | collective-permute-start | bytes 344072 | tf_op jit(solution)/shard_map/ppermute | solution.py:366
  11.1 0.9 %collective-permute-done.1.zhi_ref = f32[14,16,128]{2,1,0:T(8,128)S(1)} collective-permute-done((f32[14,16,128]{2,1,0:T(8,128)S(1)}, f32[14,16,128]{2,1,0:T(8,128)S(1)}, u32[]{:S(2)}, u32[]{:S(2)}) %collective-permute-start.1) | collective-permute-done | bytes 114720 | tf_op jit(solution)/shard_map/ppermute | solution.py:366
  12.0 0.8 %collective-permute-done.zlo_ref = f32[14,16,128]{2,1,0:T(8,128)S(1)} collective-permute-done((f32[14,16,128]{2,1,0:T(8,128)S(1)}, f32[14,16,128]{2,1,0:T(8,128)S(1)}, u32[]{:S(2)}, u32[]{:S(2)}) %collective-permute-start) | collective-permute-done | bytes 114720 | tf_op jit(solution)/shard_map/ppermute | solution.py:366
  12.9 0.0 copy-start
  12.9 1.3 %copy-done = f32[5,32,16,128]{3,2,1,0:T(8,128)S(1)} copy-done((f32[5,32,16,128]{3,2,1,0:T(8,128)S(1)}, f32[5,32,16,128]{3,2,1,0:T(8,128)}, u32[]{:S(2)}) %copy-start) | copy-done | bytes 1310744
  14.2 0.0 copy-start.2
  14.2 0.9 %copy-done.2 = f32[32,16,128]{2,1,0:T(8,128)S(1)} copy-done((f32[32,16,128]{2,1,0:T(8,128)S(1)}, f32[32,16,128]{2,1,0:T(8,128)}, u32[]{:S(2)}) %copy-start.2) | copy-done | bytes 262168
  15.1 0.0 copy-start.1
  15.1 0.2 pack_rows.1
  15.3 0.0 copy-start.10
  15.4 0.0 copy-start.9
  15.4 0.0 copy-start.4
  15.4 0.0 copy-start.5
  15.4 0.0 copy-start.6
  15.4 0.0 copy-start.7
  15.4 0.0 copy-start.8
  15.4 1.4 %collective-permute-start.2 = (f32[472,128]{1,0:T(8,128)S(1)}, f32[472,128]{1,0:T(8,128)S(1)}, u32[]{:S(2)}, u32[]{:S(2)}) collective-permute-start(f32[472,128]{1,0:T(8,128)S(1)} %broadcast_select_fusion), channel_id=1, source_target_pairs={{0,4},{4,0},{1,5},{5,1},{2,6},{6,2},{3,7},{7,3},{8,12},{12,8},{9,1... | collective-permute-start | bytes 725000 | tf_op jit(solution)/shard_map/ppermute | solution.py:409
  16.9 0.1 stack.35
  17.0 4.3 %collective-permute-done.2.ylo_ref.yhi_ref = f32[472,128]{1,0:T(8,128)S(1)} collective-permute-done((f32[472,128]{1,0:T(8,128)S(1)}, f32[472,128]{1,0:T(8,128)S(1)}, u32[]{:S(2)}, u32[]{:S(2)}) %collective-permute-start.2) | collective-permute-done | bytes 241696 | tf_op jit(solution)/shard_map/ppermute | solution.py:409
  21.3 0.0 copy-done.3
  21.3 0.0 copy-done.1
  21.3 4.0 %pack_columns.1 = (f32[6,24,128]{2,1,0:T(8,128)S(1)}, f32[6,24,128]{2,1,0:T(8,128)S(1)}) custom-call(f32[6]{0:T(128)S(1)} %stack.36.flags_ref, f32[5,32,16,128]{3,2,1,0:T(8,128)S(1)} %copy-done.1, f32[32,16,128]{2,1,0:T(8,128)S(1)} %copy-done.3, f32[14,16,128]{2,1,0:T(8,128)S(1)} %collective-permute-done.zlo_ref, ...), custom_call_target="tpu_custom_call" | custom-call | tf_op jit(solution)/shard_map/pack_columns/pallas_call | solution.py:414
  25.3 5.7 %collective-permute-start.3 = (f32[6,24,128]{2,1,0:T(8,128)S(1)}, f32[6,24,128]{2,1,0:T(8,128)S(1)}, u32[]{:S(2)}, u32[]{:S(2)}) collective-permute-start(f32[6,24,128]{2,1,0:T(8,128)S(1)} %get-tuple-element.10.ownhi_ref), channel_id=1, source_target_pairs={{0,1},{1,2},{2,3},{4,5},{5,6},{6,7},{8,9},{9,10},{10,11},{12,13},{... | collective-permute-start | bytes 221192 | tf_op jit(solution)/shard_map/ppermute | solution.py:366
  31.0 1.9 %collective-permute-start.4 = (f32[6,24,128]{2,1,0:T(8,128)S(1)}, f32[6,24,128]{2,1,0:T(8,128)S(1)}, u32[]{:S(2)}, u32[]{:S(2)}) collective-permute-start(f32[6,24,128]{2,1,0:T(8,128)S(1)} %get-tuple-element.11.ownlo_ref), channel_id=1, source_target_pairs={{1,0},{2,1},{3,2},{5,4},{6,5},{7,6},{9,8},{10,9},{11,10},{13,12},{... | collective-permute-start | bytes 221192 | tf_op jit(solution)/shard_map/ppermute | solution.py:366
  33.0 0.0 copy-done.10
  33.0 0.1 copy.11.courant_ref
  33.1 0.5 broadcast.3
  33.6 0.0 copy-done.9
  33.6 0.7 reduce.3
  34.2 0.1 reshape_squeeze.3.mask_ref
  34.3 0.0 collective-permute-done.3.xlo_ref
  34.3 2.4 %collective-permute-done.4.xhi_ref = f32[6,24,128]{2,1,0:T(8,128)S(1)} collective-permute-done((f32[6,24,128]{2,1,0:T(8,128)S(1)}, f32[6,24,128]{2,1,0:T(8,128)S(1)}, u32[]{:S(2)}, u32[]{:S(2)}) %collective-permute-start.4) | collective-permute-done | bytes 73760 | tf_op jit(solution)/shard_map/ppermute | solution.py:366
  36.7 0.0 copy-done.4
  36.7 0.0 copy-done.5
  36.7 0.0 copy-done.6
  36.7 0.0 copy-done.7
  36.7 0.0 copy-done.8
  36.7 18.7 %step_and_march.1 = (f32[5,32,16,128]{3,2,1,0:T(8,128)}, f32[256,4,128]{2,1,0:T(4,128)S(1)}) custom-call(f32[6]{0:T(128)S(1)} %stack.36.flags_ref, f32[5,3]{1,0:T(8,128)S(1)} %copy.11.courant_ref, f32[16]{0:T(128)S(1)} %copy-done.6, f32[16]{0:T(128)S(1)} %copy-done.7, f32[16]{0:T(128)S(1)} %copy-done.8, f32[3,16]{1,0:T(4,128)S(1)} %copy-done.4, ...), custom_call_target="tpu_custom_call" | custom-call | tf_op jit(solution)/shard_map/step_and_march/pallas_call | solution.py:428
  55.5 17.9 %all_to_all.5.part_ref = f32[4,256,128]{2,1,0:T(8,128)S(1)} all-to-all(f32[4,256,128]{2,1,0:T(8,128)S(1)} %bitcast.30), channel_id=1, replica_groups=mesh['gz'=4,'gy'=2,'gx'=4] {'gz'}, dimensions={0} | all-to-all | bytes 1048576 | tf_op jit(solution)/shard_map/all_to_all | solution.py:449
  73.4 0.7 %compose.1 = f32[256,128]{1,0:T(8,128)} custom-call(f32[4,256,128]{2,1,0:T(8,128)S(1)} %all_to_all.5.part_ref), custom_call_target="tpu_custom_call" | custom-call | tf_op jit(solution)/shard_map/compose/pallas_call | solution.py:353
  (2 shorter events, 0.0 us)
Async XLA Ops:
  2.1 19.2 %copy-start.3 = (f32[32,16,128]{2,1,0:T(8,128)S(1)}, f32[32,16,128]{2,1,0:T(8,128)}, u32[]{:S(2)}) copy-start(f32[32,16,128]{2,1,0:T(8,128)} %kappa_ref.5) | copy-start | bytes 786436
  5.1 6.9 %collective-permute-start.1 = (f32[14,16,128]{2,1,0:T(8,128)S(1)}, f32[14,16,128]{2,1,0:T(8,128)S(1)}, u32[]{:S(2)}, u32[]{:S(2)}) collective-permute-start(f32[14,16,128]{2,1,0:T(8,128)S(1)} %get-tuple-element.24), channel_id=1, source_target_pairs={{8,0},{16,8},{24,16},{9,1},{17,9},{25,17},{10,2},{18,10},{26,18},{... | collective-permute-start | bytes 344072 | tf_op jit(solution)/shard_map/ppermute | solution.py:366
  6.4 6.4 %collective-permute-start = (f32[14,16,128]{2,1,0:T(8,128)S(1)}, f32[14,16,128]{2,1,0:T(8,128)S(1)}, u32[]{:S(2)}, u32[]{:S(2)}) collective-permute-start(f32[14,16,128]{2,1,0:T(8,128)S(1)} %get-tuple-element.25), channel_id=1, source_target_pairs={{0,8},{8,16},{16,24},{1,9},{9,17},{17,25},{2,10},{10,18},{18,26},{... | collective-permute-start | bytes 344072 | tf_op jit(solution)/shard_map/ppermute | solution.py:366
  12.9 1.3 %copy-start = (f32[5,32,16,128]{3,2,1,0:T(8,128)S(1)}, f32[5,32,16,128]{3,2,1,0:T(8,128)}, u32[]{:S(2)}) copy-start(f32[5,32,16,128]{3,2,1,0:T(8,128)} %fields_ref.5) | copy-start | bytes 3932164
  14.2 0.9 %copy-start.2 = (f32[32,16,128]{2,1,0:T(8,128)S(1)}, f32[32,16,128]{2,1,0:T(8,128)}, u32[]{:S(2)}) copy-start(f32[32,16,128]{2,1,0:T(8,128)} %kappa_ref.5) | copy-start | bytes 786436
  15.1 6.1 %copy-start.1 = (f32[5,32,16,128]{3,2,1,0:T(8,128)S(1)}, f32[5,32,16,128]{3,2,1,0:T(8,128)}, u32[]{:S(2)}) copy-start(f32[5,32,16,128]{3,2,1,0:T(8,128)} %fields_ref.5) | copy-start | bytes 3932164
  15.3 17.6 %copy-start.10 = (f32[5,3]{0,1:T(4,128)S(1)}, f32[5,3]{0,1:T(4,128)}, u32[]{:S(2)}) copy-start(f32[5,3]{0,1:T(4,128)} %param.11) | copy-start | bytes 184
  15.4 18.2 %copy-start.9 = (s32[1,16,16,1]{2,3,1,0:T(1,128)S(1)}, s32[1,16,16,1]{2,3,1,0:T(1,128)}, u32[]{:S(2)}) copy-start(s32[1,16,16,1]{2,3,1,0:T(1,128)} %param.16) | copy-start | bytes 3076
  15.4 21.3 %copy-start.4 = (f32[3,16]{1,0:T(4,128)S(1)}, f32[3,16]{1,0:T(4,128)}, u32[]{:S(2)}) copy-start(f32[3,16]{1,0:T(4,128)} %color_ref.1) | copy-start | bytes 580
  15.4 21.3 %copy-start.5 = (s32[1,1,256]{2,1,0:T(1,128)S(1)}, s32[1,1,256]{2,1,0:T(1,128)}, u32[]{:S(2)}) copy-start(s32[1,1,256]{2,1,0:T(1,128)} %param.17) | copy-start | bytes 3076
  15.4 21.3 %copy-start.6 = (f32[16]{0:T(128)S(1)}, f32[16]{0:T(128)}, u32[]{:S(2)}) copy-start(f32[16]{0:T(128)} %center_ref.1) | copy-start | bytes 196
  15.4 21.3 %copy-start.7 = (f32[16]{0:T(128)S(1)}, f32[16]{0:T(128)}, u32[]{:S(2)}) copy-start(f32[16]{0:T(128)} %sharp_ref.1) | copy-start | bytes 196
  15.4 21.3 %copy-start.8 = (f32[16]{0:T(128)S(1)}, f32[16]{0:T(128)}, u32[]{:S(2)}) copy-start(f32[16]{0:T(128)} %gain_ref.1) | copy-start | bytes 196
  15.4 5.9 %collective-permute-start.2 = (f32[472,128]{1,0:T(8,128)S(1)}, f32[472,128]{1,0:T(8,128)S(1)}, u32[]{:S(2)}, u32[]{:S(2)}) collective-permute-start(f32[472,128]{1,0:T(8,128)S(1)} %broadcast_select_fusion), channel_id=1, source_target_pairs={{0,4},{4,0},{1,5},{5,1},{2,6},{6,2},{3,7},{7,3},{8,12},{12,8},{9,1... | collective-permute-start | bytes 725000 | tf_op jit(solution)/shard_map/ppermute | solution.py:409
  25.3 9.0 %collective-permute-start.3 = (f32[6,24,128]{2,1,0:T(8,128)S(1)}, f32[6,24,128]{2,1,0:T(8,128)S(1)}, u32[]{:S(2)}, u32[]{:S(2)}) collective-permute-start(f32[6,24,128]{2,1,0:T(8,128)S(1)} %get-tuple-element.10.ownhi_ref), channel_id=1, source_target_pairs={{0,1},{1,2},{2,3},{4,5},{5,6},{6,7},{8,9},{9,10},{10,11},{12,13},{... | collective-permute-start | bytes 221192 | tf_op jit(solution)/shard_map/ppermute | solution.py:366
  31.0 5.7 %collective-permute-start.4 = (f32[6,24,128]{2,1,0:T(8,128)S(1)}, f32[6,24,128]{2,1,0:T(8,128)S(1)}, u32[]{:S(2)}, u32[]{:S(2)}) collective-permute-start(f32[6,24,128]{2,1,0:T(8,128)S(1)} %get-tuple-element.11.ownlo_ref), channel_id=1, source_target_pairs={{1,0},{2,1},{3,2},{5,4},{6,5},{7,6},{9,8},{10,9},{11,10},{13,12},{... | collective-permute-start | bytes 221192 | tf_op jit(solution)/shard_map/ppermute | solution.py:366

commit v3 on v2

v3 whole, which is shorter than its diff:
```python
import jax
import jax.numpy as jnp
from jax import lax
from jax.experimental import pallas as pl
from jax.experimental.pallas import tpu as pltpu
from jax.sharding import PartitionSpec as P

LOG2E = 1.4426950408889634
W = 3
SUB = 8
F32 = jnp.float32


def reach(field, nfield):
    return W if field in (0, nfield) else W - 1


def tiles_of(first, last):
    return [min(start, last - SUB) for start in range(first, last, SUB)]


def z_plan(nfield):
    plan, at = [], 0
    for field in range(nfield + 1):
        plan.append((field, at, reach(field, nfield)))
        at += reach(field, nfield)
    return plan, at


def y_plan(nfield, depth_len):
    plan, at = [], 0
    for field in range(nfield + 1):
        wide = reach(field, nfield)
        for away in range(1, wide + 1):
            extra = wide - away
            plan.append((field, away, -extra, depth_len + 2 * extra, at))
            at += depth_len + 2 * extra
    return plan, at + (-at) % SUB


def pack_planes_kernel(fields_ref, kappa_ref, lo_ref, hi_ref):
    nfield, depth_len = fields_ref.shape[:2]
    for field, at, wide in z_plan(nfield)[0]:
        source = kappa_ref if field == nfield else fields_ref.at[field]
        for k in range(wide):
            lo_ref[at + k] = source[k]
            hi_ref[at + k] = source[depth_len - wide + k]


def source_plane(refs, field, z):
    fields_ref, kappa_ref, zlo_ref, zhi_ref = refs
    nfield, depth_len = fields_ref.shape[:2]
    _, at, wide = z_plan(nfield)[0][field]
    if z < 0:
        return zlo_ref.at[at + wide + z]
    if z >= depth_len:
        return zhi_ref.at[at + z - depth_len]
    return kappa_ref.at[z] if field == nfield else fields_ref.at[field, z]


def pack_rows_kernel(fields_ref, kappa_ref, zlo_ref, zhi_ref, lo_ref, hi_ref):
    refs = (fields_ref, kappa_ref, zlo_ref, zhi_ref)
    nfield, depth_len, rows, lanes = fields_ref.shape
    flat_fields = fields_ref.reshape(nfield * depth_len * rows, lanes)
    flat_kappa = kappa_ref.reshape(depth_len * rows, lanes)
    plan, used = y_plan(nfield, depth_len)
    for out_ref, top in ((lo_ref, True), (hi_ref, False)):
        for field, away, first, length, at in plan:
            row = away - 1 if top else rows - away
            for z in list(range(first, 0)) + list(range(depth_len, first + length)):
                out_ref[at + z - first, :] = source_plane(refs, field, z)[row, :]
            flat, base = (flat_kappa, 0) if field == nfield else (flat_fields, field * depth_len * rows)
            for z in range(0, depth_len, SUB):
                out_ref[pl.ds(at - first + z, SUB), :] = flat[
                    pl.ds(base + z * rows + row, SUB, stride=rows), :
                ]
        spare = plan[-1][3] + plan[-1][4]
        if used > spare:
            out_ref[spare:used, :] = jnp.zeros((used - spare, lanes), F32)


def assemble(refs, ylo_ref, yhi_ref, flags_ref, pad_ref):
    fields_ref, kappa_ref, zlo_ref, zhi_ref = refs
    nfield, depth_len, rows, lanes = fields_ref.shape
    planes, pitch = depth_len + 2 * W, rows + SUB
    halo = jnp.zeros((SUB, lanes), F32)

    @pl.loop(0, depth_len)
    def _(z):
        for field in range(nfield + 1):
            plane = field * planes + W + z
            pad_ref[plane, :rows, :] = kappa_ref[z] if field == nfield else fields_ref[field, z]
            pad_ref[plane, rows:, :] = halo

    for field, at, wide in z_plan(nfield)[0]:
        for k in range(W):
            below, above = field * planes + W - 1 - k, field * planes + W + depth_len + k
            if k < wide:
                pad_ref[below, :rows, :] = zlo_ref[at + wide - 1 - k]
                pad_ref[above, :rows, :] = zhi_ref[at + k]
            for plane in (below, above):
                if k >= wide:
                    pad_ref[plane, :rows, :] = jnp.zeros((rows, lanes), F32)
                pad_ref[plane, rows:, :] = halo
    flat = pad_ref.reshape((nfield + 1) * planes * pitch, lanes)
    low, high = flags_ref[2], flags_ref[3]
    for field, away, first, length, at in y_plan(nfield, depth_len)[0]:
        for ref, flag, row in ((ylo_ref, low, pitch - away), (yhi_ref, high, rows + away - 1)):
            for start in tiles_of(0, length):
                flat[pl.ds((field * planes + W + first + start) * pitch + row, SUB, stride=pitch), :] = (
                    ref[pl.ds(at + start, SUB), :] * flag
                )


def pack_columns_kernel(
    flags_ref, fields_ref, kappa_ref, zlo_ref, zhi_ref, ylo_ref, yhi_ref, lo_ref, hi_ref, pad_ref
):
    refs = (fields_ref, kappa_ref, zlo_ref, zhi_ref)
    nfield, depth_len, rows, lanes = fields_ref.shape
    planes, pitch = depth_len + 2 * W, rows + SUB
    assemble(refs, ylo_ref, yhi_ref, flags_ref, pad_ref)
    lane = lax.broadcasted_iota(jnp.int32, (pitch, lanes), 1)
    group = (nfield + 1) // 2

    for start in range(0, nfield + 1, group):

        def body(zi, carry):
            mine = (lane >= W * zi) & (lane < W * zi + W)
            fresh = []
            for field in range(start, start + group):
                low, high = carry[field - start]
                value = pad_ref[field * planes + zi]
                low = jnp.where(mine, pltpu.roll(value, W * zi, 1), low)
                high = jnp.where(mine, pltpu.roll(value, lax.rem(W * zi + W, lanes), 1), high)
                fresh.append((low, high))
            return tuple(fresh)

        zero = jnp.zeros((pitch, lanes), F32)
        done = lax.fori_loop(0, planes, body, ((zero, zero),) * group)
        for field in range(start, start + group):
            lo_ref[field], hi_ref[field] = done[field - start]


def stencil(u, coefs, ups, downs, speeds):
    total = (coefs[3] - (speeds[0] + speeds[1] + speeds[2])) * u
    for axis in range(3):
        k_up, k_down = coefs[axis]
        total = total + k_up * ups[axis] + (k_down + speeds[axis]) * downs[axis]
    return total


def weights(k, ups, downs):
    half = 0.5 * k
    coefs = [(half + 0.5 * ups[a], half + 0.5 * downs[a]) for a in range(3)]
    rest = 1.0
    for up, down in coefs:
        rest = rest - (up + down)
    return coefs + [rest]


def side_neighbours(near, own, is_left, lanes, col):
    first, second = (near, own) if is_left else (own, near)
    first_up = jnp.where(col == W - 1, pltpu.roll(second, W - 1, 1), pltpu.roll(first, lanes - 1, 1))
    first_down = pltpu.roll(first, 1, 1)
    second_up = pltpu.roll(second, lanes - 1, 1)
    second_down = jnp.where(col == 0, pltpu.roll(first, lanes - (W - 1), 1), pltpu.roll(second, 1, 1))
    pair = ((first_up, first_down), (second_up, second_down))
    return pair if is_left else (pair[1], pair[0])


def main_kernel(
    flags_ref, courant_ref, center_ref, sharp_ref, gain_ref, color_ref, mask_ref, order_ref,
    pad_ref, xlo_ref, xhi_ref, ownlo_ref, ownhi_ref,
    state_ref, out_ref,
    next_ref, last_ref, side_ref, edge_ref, base_ref, tile_ref,
):
    nfield, depth_len, rows, lanes = state_ref.shape
    planes, pitch = depth_len + 2 * W, rows + SUB
    lane = lax.broadcasted_iota(jnp.int32, (pitch, lanes), 1)
    r = lax.broadcasted_iota(jnp.int32, (pitch, lanes), 0)
    zi_of = lane // W
    col = lane - zi_of * W
    flag = [flags_ref[i] for i in range(6)]
    speed = [[courant_ref[f, a] for a in range(3)] for f in range(nfield)]
    row_mask = jnp.where(r < rows, 1.0, jnp.where(r < rows + SUB // 2, flag[3], flag[2]))

    def along_y(value):
        return pltpu.roll(value, pitch - 1, 0), pltpu.roll(value, 1, 0)

    sides = ((xlo_ref, ownlo_ref, True, flag[4]), (xhi_ref, ownhi_ref, False, flag[5]))

    def block_of(level, side, block, field):
        if level == 0 or field == nfield:
            return sides[side][block][field]
        return side_ref[level - 1, side, block, field]

    def edges(level, field):
        left, right = block_of(level, 0, 0, field), block_of(level, 1, 0, field)
        edge_ref[level, field] = jnp.where(col == W - 1, left, pltpu.roll(right, 1, 1))

    def side_step(level, count):
        zmask = row_mask * jnp.where(
            zi_of < W, flag[0], jnp.where(zi_of >= W + depth_len, flag[1], 1.0)
        )
        for side, (_, _, is_left, present) in enumerate(sides):
            blocks = (0, 1) if level == 0 else (0,)

            def around(lvl, field):
                pair = [block_of(lvl, side, block, field) for block in (0, 1)]
                x = side_neighbours(pair[0], pair[1], is_left, lanes, col)
                found = []
                for block in blocks:
                    value = pair[block]
                    y_up, y_down = along_y(value)
                    ups = (pltpu.roll(value, lanes - W, 1), y_up, x[block][0])
                    downs = (pltpu.roll(value, W, 1), y_down, x[block][1])
                    found.append((value, ups, downs))
                return found

            coefs = [weights(*found) for found in around(0, nfield)]
            for field in range(count):
                for block, (u, ups, downs) in zip(blocks, around(level, field)):
                    value = stencil(u, coefs[block], ups, downs, speed[field])
                    side_ref[level, side, block, field] = value * (zmask * present if block == 0 else zmask)

    def along_x(value, zi, edge):
        n = value.shape[0]
        turned = pltpu.roll(edge, lax.rem(2 * lanes - 2 - W * zi, lanes), 1)
        up = jnp.where(lane[:n] == lanes - 1, turned, pltpu.roll(value, lanes - 1, 1))
        down = jnp.where(lane[:n] == 0, turned, pltpu.roll(value, 1, 1))
        return up, down

    def around(src_ref, level, field, zi, n):
        plane = field * planes + zi
        whole = src_ref[plane]
        value = whole[:n]
        y_up, y_down = along_y(whole)
        x_up, x_down = along_x(value, zi, edge_ref[level, field, :n, :])
        return (
            value,
            (src_ref[plane + 1, :n, :], y_up[:n], x_up),
            (src_ref[plane - 1, :n, :], y_down[:n], x_down),
        )

    def step_value(src_ref, level, field, zi, n, coefs):
        u, ups, downs = around(src_ref, level, field, zi, n)
        return stencil(u, coefs, ups, downs, speed[field])

    def depth_mask(zi):
        return jnp.where(zi < W, flag[0], jnp.where(zi >= W + depth_len, flag[1], 1.0))

    for field in range(nfield + 1):
        edges(0, field)
    side_step(0, nfield)
    for field in range(nfield):
        edges(1, field)
    side_step(1, 1)
    edges(2, 0)

    @pl.loop(1, planes - 1)
    def _(zi):
        mask = row_mask * depth_mask(zi)
        coefs = weights(*around(pad_ref, 0, nfield, zi, pitch))
        for field in range(nfield):
            next_ref[field * planes + zi] = mask * step_value(pad_ref, 0, field, zi, pitch, coefs)

    @pl.loop(2, planes - 2)
    def _(zi):
        coefs = weights(*around(pad_ref, 0, nfield, zi, pitch))
        last_ref[zi] = step_value(next_ref, 1, 0, zi, pitch, coefs) * (row_mask * depth_mask(zi))

    @pl.loop(0, depth_len)
    def _(z):
        zi = z + W
        coefs = weights(*around(pad_ref, 0, nfield, zi, rows))
        s, ups, downs = around(last_ref, 2, 0, zi, rows)
        state_ref[0, z] = s
        g_z, g_y, g_x = [0.5 * (ups[a] - downs[a]) for a in range(3)]
        shade = 0.35 + 0.65 * jnp.abs(0.64 * g_z + 0.6 * g_y + 0.48 * g_x) * lax.rsqrt(
            g_z * g_z + g_y * g_y + g_x * g_x + 1.0
        )
        for field in range(1, nfield):
            value = step_value(next_ref, 1, field, zi, rows, coefs)
            state_ref[field, z] = value
            if field <= 3:
                base_ref[field, z] = shade * (0.5 + 0.5 * jnp.tanh(0.5 * value))
            if field == 4:
                base_ref[0, z] = 1.0 + 0.5 * jnp.tanh(value)

    ntf = center_ref.shape[0]
    chunk = 4 if ntf % 4 == 0 else 1
    halves = rows // SUB

    @pl.loop(0, (ntf // chunk) * halves)
    def _(step):
        first = (step // halves) * chunk
        row = pl.multiple_of((step % halves) * SUB, SUB)
        shape = (SUB, lanes)
        mid = [jnp.full(shape, center_ref[first + j], jnp.float32) for j in range(chunk)]
        bend = [jnp.full(shape, sharp_ref[first + j] * -LOG2E, jnp.float32) for j in range(chunk)]
        dense = [jnp.full(shape, gain_ref[first + j] * -LOG2E, jnp.float32) for j in range(chunk)]
        passed = [jnp.ones(shape, jnp.float32)] * chunk
        total = [jnp.zeros(shape, jnp.float32)] * chunk
        acc = [[jnp.zeros(shape, jnp.float32)] * 3 for _ in range(chunk)]
        for z in range(depth_len):
            s = state_ref[0, z, pl.ds(row, SUB), :]
            modul = base_ref[0, z, pl.ds(row, SUB), :]
            base = [base_ref[k + 1, z, pl.ds(row, SUB), :] for k in range(3)]
            for j in range(chunk):
                diff = s - mid[j]
                total[j] = total[j] + modul * jnp.exp2(diff * diff * bend[j])
                after = jnp.exp2(total[j] * dense[j])
                weight = passed[j] - after
                passed[j] = after
                acc[j] = [acc[j][k] + weight * base[k] for k in range(3)]
        for j in range(chunk):
            start = ((first + j) * rows + row) * 4
            for k in range(3):
                tile_ref[pl.ds(start + k, SUB, stride=4), :] = acc[j][k] * color_ref[k, first + j]
            tile_ref[pl.ds(start + 3, SUB, stride=4), :] = 1.0 - passed[j]

    @pl.loop(0, order_ref.shape[0], unroll=8)
    def _(slot):
        tile = order_ref[slot]
        cover = mask_ref[tile].astype(jnp.float32)
        out_ref[slot] = tile_ref[pl.ds(pl.multiple_of(tile * 4, 4), 4), :] * cover


def compose_kernel(part_ref, out_ref):
    slabs, rows, _ = part_ref.shape

    @pl.loop(0, rows // 32)
    def _(step):
        def load(slab, k):
            return part_ref[slab, pl.ds(step * 32 + k, 8, stride=4), :]

        acc = [load(0, k) for k in range(4)]
        for slab in range(1, slabs):
            clear = 1.0 - acc[3]
            acc = [acc[k] + clear * load(slab, k) for k in range(4)]
        for k in range(4):
            out_ref[pl.ds(step * 32 + k, 8, stride=4), :] = acc[k]


def compose(parts):
    vmem = pl.BlockSpec(memory_space=pltpu.VMEM)
    return pl.pallas_call(
        compose_kernel,
        out_shape=jax.ShapeDtypeStruct(parts.shape[1:], jnp.float32),
        in_specs=[vmem],
        out_specs=vmem,
        compiler_params=pltpu.CompilerParams(vmem_limit_bytes=16 * 1024 * 1024),
        name="compose",
    )(parts)


def shift(message, axis, up):
    count = lax.axis_size(axis)
    pairs = [(i, i + 1) if up else (i + 1, i) for i in range(count - 1)]
    return lax.ppermute(message, axis, pairs)


def present(axis):
    here = lax.axis_index(axis)
    return [(here > 0).astype(F32), (here < lax.axis_size(axis) - 1).astype(F32)]


def shards(
    fields, diffusivity, courant, tf_center, tf_sharp, tf_gain, tf_color, tile_mask, tile_perm
):
    nfield, depth_len, rows_len, cols_len = fields.shape
    planes, pitch = depth_len + 2 * W, rows_len + SUB
    smem = pl.BlockSpec(memory_space=pltpu.SMEM)
    vmem = pl.BlockSpec(memory_space=pltpu.VMEM)
    params = pltpu.CompilerParams(vmem_limit_bytes=16 * 1024 * 1024)

    def array(*shape):
        return jax.ShapeDtypeStruct(shape, F32)

    flags = jnp.stack(present("gz") + present("gy") + present("gx"))

    faces = z_plan(nfield)[1]
    face_lo, face_hi = pl.pallas_call(
        pack_planes_kernel,
        out_shape=(array(faces, rows_len, cols_len),) * 2,
        in_specs=[vmem] * 2,
        out_specs=(vmem, vmem),
        compiler_params=params,
        name="pack_planes",
    )(fields, diffusivity)
    zlo = shift(face_hi, "gz", True)
    zhi = shift(face_lo, "gz", False)
    used = y_plan(nfield, depth_len)[1]
    send_lo, send_hi = pl.pallas_call(
        pack_rows_kernel,
        out_shape=(array(used, cols_len), array(used, cols_len)),
        in_specs=[vmem] * 4,
        out_specs=(vmem, vmem),
        compiler_params=params,
        name="pack_rows",
    )(fields, diffusivity, zlo, zhi)
    if lax.axis_size("gy") == 2:
        mine = jnp.where(lax.axis_index("gy") == 0, send_hi, send_lo)
        ylo = yhi = lax.ppermute(mine, "gy", [(0, 1), (1, 0)])
    else:
        ylo = shift(send_hi, "gy", True)
        yhi = shift(send_lo, "gy", False)
    own_lo, own_hi, pad = pl.pallas_call(
        pack_columns_kernel,
        out_shape=(array(nfield + 1, pitch, cols_len),) * 2
        + (array((nfield + 1) * planes, pitch, cols_len),),
        in_specs=[smem] + [vmem] * 6,
        out_specs=(vmem,) * 3,
        compiler_params=params,
        name="pack_columns",
    )(flags, fields, diffusivity, zlo, zhi, ylo, yhi)
    xlo = shift(own_hi, "gx", True)
    xhi = shift(own_lo, "gx", False)
    count = lax.axis_size("gz")
    order = tile_perm[0, 0]
    per_owner = order.shape[0] // count
    state, tiles = pl.pallas_call(
        main_kernel,
        out_shape=(array(*fields.shape), array(order.shape[0], 4, cols_len)),
        in_specs=[smem] * 8 + [vmem] * 5,
        out_specs=(vmem, vmem),
        scratch_shapes=[
            pltpu.VMEM((nfield * planes, pitch, cols_len), F32),
            pltpu.VMEM((planes, pitch, cols_len), F32),
            pltpu.VMEM((2, 2, 2, nfield, pitch, cols_len), F32),
            pltpu.VMEM((3, nfield + 1, pitch, cols_len), F32),
            pltpu.VMEM((4, depth_len, rows_len, cols_len), F32),
            pltpu.VMEM((order.shape[0] * 4, cols_len), F32),
        ],
        compiler_params=params,
        name="step_and_march",
    )(
        flags, courant, tf_center, tf_sharp, tf_gain, tf_color, tile_mask[0].reshape(-1), order,
        pad, xlo, xhi, own_lo, own_hi,
    )
    grouped = tiles.reshape(count, per_owner * 4, cols_len)
    composed = compose(lax.all_to_all(grouped, "gz", split_axis=0, concat_axis=0, tiled=True))
    picture = composed.reshape(1, 1, per_owner, 4, cols_len)
    return (state, picture)


def solution(mesh):
    return jax.shard_map(
        shards,
        mesh=mesh,
        in_specs=(
            P(None, "gz", "gy", "gx"),
            P("gz", "gy", "gx"),
            P(),
            P(),
            P(),
            P(),
            P(),
            P("gz", None, "gy", "gx"),
            P("gy", "gx", None),
        ),
        out_specs=(P(None, "gz", "gy", "gx"), P("gy", "gx", "gz", None, None)),
        check_vma=False,
    )
```

time: 75 us -> 75 us (level)
  the two profiles are of different devices: /device:TPU:1 before, /device:TPU:0 now
where the time goes in v3:
time: 75 us; the launch traced here: 74 us
  Pallas kernels  25.1 us (33%)
  blocking collectives  18.2 us (24%)
  waiting for transfers between devices  12.2 us (16%)
  starting transfers between devices  10.5 us (14%)
  local copies, waits for them, and re-layouts  6.44 us (9%)
  between operations  0.82 us (1%)
    all_to_all x1, blocking collectives, shards(): lax.all_to_all(grouped, 'gz', split_axis=0, concat_axis=0, tiled=True)  18.2 us
    pallas_call x1, Pallas kernels, shards(): pl.pallas_call(main_kernel, out_shape=(array(*fields.shape), array(order....  16.7 us
    ppermute x4, starting transfers between devices, shift(): return lax.ppermute(message, axis, pairs)  8.93 us
    ppermute x4, waiting for transfers between devices, shift(): return lax.ppermute(message, axis, pairs)  7.61 us
    pallas_call x1, Pallas kernels, shards(): pl.pallas_call(pack_columns_kernel, out_shape=(array(nfield + 1, pitch, c...  7.46 us
    unnamed x28, local copies, waits for them, and re-layouts  6.26 us
    ppermute x1, waiting for transfers between devices, shards(): ylo = yhi = lax.ppermute(mine, 'gy', [(0, 1), (1, 0)])  4.57 us
    ppermute x1, starting transfers between devices, shards(): ylo = yhi = lax.ppermute(mine, 'gy', [(0, 1), (1, 0)])  1.56 us
  transfers between devices with their start and end apart: 5, of which 4 were waited for; matrix products, arithmetic and copies ran while one was open for 2% of the time, Pallas kernels for 0%

profile of v3, /device:TPU:0, one launch (start us, length us, event | category | flops | bytes accessed | tf_op | source)
XLA Modules:
  0.0 74.0 jit_solution(1331861697017718412)
XLA Ops:
  0.6 0.0 copy-start
  0.6 1.3 %copy-done = f32[5,32,16,128]{3,2,1,0:T(8,128)S(1)} copy-done((f32[5,32,16,128]{3,2,1,0:T(8,128)S(1)}, f32[5,32,16,128]{3,2,1,0:T(8,128)}, u32[]{:S(2)}) %copy-start) | copy-done | bytes 1310744
  1.9 0.0 copy-start.4
  1.9 0.9 %copy-done.4 = f32[32,16,128]{2,1,0:T(8,128)S(1)} copy-done((f32[32,16,128]{2,1,0:T(8,128)S(1)}, f32[32,16,128]{2,1,0:T(8,128)}, u32[]{:S(2)}) %copy-start.4) | copy-done | bytes 262168
  2.9 0.0 copy-start.1
  2.9 0.0 copy-start.5
  2.9 5.1 %collective-permute-start = (f32[14,16,128]{2,1,0:T(8,128)S(1)}, f32[14,16,128]{2,1,0:T(8,128)S(1)}, u32[]{:S(2)}, u32[]{:S(2)}) collective-permute-start(f32[14,16,128]{2,1,0:T(8,128)S(1)} %get-tuple-element.11), channel_id=1, source_target_pairs={{0,8},{8,16},{16,24},{1,9},{9,17},{17,25},{2,10},{10,18},{18,26},{... | collective-permute-start | bytes 344072 | tf_op jit(solution)/shard_map/ppermute | solution.py:360
  8.0 1.3 %collective-permute-start.1 = (f32[14,16,128]{2,1,0:T(8,128)S(1)}, f32[14,16,128]{2,1,0:T(8,128)S(1)}, u32[]{:S(2)}, u32[]{:S(2)}) collective-permute-start(f32[14,16,128]{2,1,0:T(8,128)S(1)} %get-tuple-element.12), channel_id=1, source_target_pairs={{8,0},{16,8},{24,16},{9,1},{17,9},{25,17},{10,2},{18,10},{26,18},{... | collective-permute-start | bytes 344072 | tf_op jit(solution)/shard_map/ppermute | solution.py:360
  9.3 1.1 %collective-permute-done.zlo_ref = f32[14,16,128]{2,1,0:T(8,128)S(1)} collective-permute-done((f32[14,16,128]{2,1,0:T(8,128)S(1)}, f32[14,16,128]{2,1,0:T(8,128)S(1)}, u32[]{:S(2)}, u32[]{:S(2)}) %collective-permute-start) | collective-permute-done | bytes 114720 | tf_op jit(solution)/shard_map/ppermute | solution.py:360
  10.4 4.3 %collective-permute-done.1.zhi_ref = f32[14,16,128]{2,1,0:T(8,128)S(1)} collective-permute-done((f32[14,16,128]{2,1,0:T(8,128)S(1)}, f32[14,16,128]{2,1,0:T(8,128)S(1)}, u32[]{:S(2)}, u32[]{:S(2)}) %collective-permute-start.1) | collective-permute-done | bytes 114720 | tf_op jit(solution)/shard_map/ppermute | solution.py:360
  14.7 0.0 copy-done.1
  14.7 0.0 copy-done.5
  14.7 0.2 pack_rows.1
  14.9 0.0 copy-start.12
  14.9 0.0 copy-start.11
  14.9 0.0 copy-start.6
  14.9 0.0 copy-start.7
  14.9 0.0 copy-start.8
  14.9 0.0 copy-start.9
  15.0 0.0 copy-start.10
  15.0 1.6 %collective-permute-start.2 = (f32[472,128]{1,0:T(8,128)S(1)}, f32[472,128]{1,0:T(8,128)S(1)}, u32[]{:S(2)}, u32[]{:S(2)}) collective-permute-start(f32[472,128]{1,0:T(8,128)S(1)} %broadcast_select_fusion), channel_id=1, source_target_pairs={{0,4},{4,0},{1,5},{5,1},{2,6},{6,2},{3,7},{7,3},{8,12},{12,8},{9,1... | collective-permute-start | bytes 725000 | tf_op jit(solution)/shard_map/ppermute | solution.py:404
  16.5 0.1 stack.35
  16.6 4.6 %collective-permute-done.2.ylo_ref.yhi_ref = f32[472,128]{1,0:T(8,128)S(1)} collective-permute-done((f32[472,128]{1,0:T(8,128)S(1)}, f32[472,128]{1,0:T(8,128)S(1)}, u32[]{:S(2)}, u32[]{:S(2)}) %collective-permute-start.2) | collective-permute-done | bytes 241696 | tf_op jit(solution)/shard_map/ppermute | solution.py:404
  21.2 7.5 %pack_columns.1 = (f32[6,24,128]{2,1,0:T(8,128)S(1)}, f32[6,24,128]{2,1,0:T(8,128)S(1)}, f32[228,24,128]{2,1,0:T(8,128)S(1)}) custom-call(f32[6]{0:T(128)S(1)} %stack.36.flags_ref, f32[5,32,16,128]{3,2,1,0:T(8,128)S(1)} %copy-done.1, f32[32,16,128]{2,1,0:T(8,128)S(1)} %copy-done.5, f32[14,16,128]{2,1,0:T(8,128)S(1)} %collective-permute-done.zlo_ref, ...), custom_call_target="tpu_custom_call" | custom-call | tf_op jit(solution)/shard_map/pack_columns/pallas_call | solution.py:408
  28.7 0.0 copy-start.2
  28.7 1.6 %copy-done.2 = f32[228,24,128]{2,1,0:T(8,128)} copy-done((f32[228,24,128]{2,1,0:T(8,128)}, f32[228,24,128]{2,1,0:T(8,128)S(1)}, u32[]{:S(2)}) %copy-start.2) | copy-done | bytes 2801688
  30.3 1.3 %collective-permute-start.3 = (f32[6,24,128]{2,1,0:T(8,128)S(1)}, f32[6,24,128]{2,1,0:T(8,128)S(1)}, u32[]{:S(2)}, u32[]{:S(2)}) collective-permute-start(f32[6,24,128]{2,1,0:T(8,128)S(1)} %get-tuple-element.16.ownhi_ref), channel_id=1, source_target_pairs={{0,1},{1,2},{2,3},{4,5},{5,6},{6,7},{8,9},{9,10},{10,11},{12,13},{... | collective-permute-start | bytes 221192 | tf_op jit(solution)/shard_map/ppermute | solution.py:360
  31.5 1.3 %collective-permute-start.4 = (f32[6,24,128]{2,1,0:T(8,128)S(1)}, f32[6,24,128]{2,1,0:T(8,128)S(1)}, u32[]{:S(2)}, u32[]{:S(2)}) collective-permute-start(f32[6,24,128]{2,1,0:T(8,128)S(1)} %get-tuple-element.17.ownlo_ref), channel_id=1, source_target_pairs={{1,0},{2,1},{3,2},{5,4},{6,5},{7,6},{9,8},{10,9},{11,10},{13,12},{... | collective-permute-start | bytes 221192 | tf_op jit(solution)/shard_map/ppermute | solution.py:360
  32.8 0.0 copy-done.12
  32.9 0.1 copy.11.courant_ref
  32.9 0.5 broadcast.3
  33.5 0.0 copy-done.11
  33.5 0.7 reduce.3
  34.1 0.1 reshape_squeeze.3.mask_ref
  34.2 0.0 collective-permute-done.3.xlo_ref
  34.2 2.2 %collective-permute-done.4.xhi_ref = f32[6,24,128]{2,1,0:T(8,128)S(1)} collective-permute-done((f32[6,24,128]{2,1,0:T(8,128)S(1)}, f32[6,24,128]{2,1,0:T(8,128)S(1)}, u32[]{:S(2)}, u32[]{:S(2)}) %collective-permute-start.4) | collective-permute-done | bytes 73760 | tf_op jit(solution)/shard_map/ppermute | solution.py:360
  36.5 0.0 copy-done.6
  36.5 0.0 copy-done.7
  36.5 0.0 copy-done.8
  36.5 0.0 copy-done.9
  36.5 0.0 copy-done.10
  36.5 0.0 copy-start.3
  36.5 1.8 %copy-done.3 = f32[228,24,128]{2,1,0:T(8,128)S(1)} copy-done((f32[228,24,128]{2,1,0:T(8,128)S(1)}, f32[228,24,128]{2,1,0:T(8,128)}, u32[]{:S(2)}) %copy-start.3) | copy-done | bytes 2801688
  38.3 16.7 %step_and_march.1 = (f32[5,32,16,128]{3,2,1,0:T(8,128)}, f32[256,4,128]{2,1,0:T(4,128)S(1)}) custom-call(f32[6]{0:T(128)S(1)} %stack.36.flags_ref, f32[5,3]{1,0:T(8,128)S(1)} %copy.11.courant_ref, f32[16]{0:T(128)S(1)} %copy-done.8, f32[16]{0:T(128)S(1)} %copy-done.9, f32[16]{0:T(128)S(1)} %copy-done.10, f32[3,16]{1,0:T(4,128)S(1)} %copy-done.6, ...), custom_call_target="tpu_custom_call" | custom-call | tf_op jit(solution)/shard_map/step_and_march/pallas_call | solution.py:422
  55.0 18.2 %all_to_all.5.part_ref = f32[4,256,128]{2,1,0:T(8,128)S(1)} all-to-all(f32[4,256,128]{2,1,0:T(8,128)S(1)} %bitcast.10), channel_id=1, replica_groups=mesh['gz'=4,'gy'=2,'gx'=4] {'gz'}, dimensions={0} | all-to-all | bytes 1048576 | tf_op jit(solution)/shard_map/all_to_all | solution.py:442
  73.2 0.7 %compose.1 = f32[256,128]{1,0:T(8,128)} custom-call(f32[4,256,128]{2,1,0:T(8,128)S(1)} %all_to_all.5.part_ref), custom_call_target="tpu_custom_call" | custom-call | tf_op jit(solution)/shard_map/compose/pallas_call | solution.py:347
  (3 shorter events, 0.1 us)
Async XLA Ops:
  0.6 1.3 %copy-start = (f32[5,32,16,128]{3,2,1,0:T(8,128)S(1)}, f32[5,32,16,128]{3,2,1,0:T(8,128)}, u32[]{:S(2)}) copy-start(f32[5,32,16,128]{3,2,1,0:T(8,128)} %fields_ref.5) | copy-start | bytes 3932164
  1.9 0.9 %copy-start.4 = (f32[32,16,128]{2,1,0:T(8,128)S(1)}, f32[32,16,128]{2,1,0:T(8,128)}, u32[]{:S(2)}) copy-start(f32[32,16,128]{2,1,0:T(8,128)} %kappa_ref.5) | copy-start | bytes 786436
  2.9 11.8 %copy-start.1 = (f32[5,32,16,128]{3,2,1,0:T(8,128)S(1)}, f32[5,32,16,128]{3,2,1,0:T(8,128)}, u32[]{:S(2)}) copy-start(f32[5,32,16,128]{3,2,1,0:T(8,128)} %fields_ref.5) | copy-start | bytes 3932164
  2.9 11.8 %copy-start.5 = (f32[32,16,128]{2,1,0:T(8,128)S(1)}, f32[32,16,128]{2,1,0:T(8,128)}, u32[]{:S(2)}) copy-start(f32[32,16,128]{2,1,0:T(8,128)} %kappa_ref.5) | copy-start | bytes 786436
  2.9 7.5 %collective-permute-start = (f32[14,16,128]{2,1,0:T(8,128)S(1)}, f32[14,16,128]{2,1,0:T(8,128)S(1)}, u32[]{:S(2)}, u32[]{:S(2)}) collective-permute-start(f32[14,16,128]{2,1,0:T(8,128)S(1)} %get-tuple-element.11), channel_id=1, source_target_pairs={{0,8},{8,16},{16,24},{1,9},{9,17},{17,25},{2,10},{10,18},{18,26},{... | collective-permute-start | bytes 344072 | tf_op jit(solution)/shard_map/ppermute | solution.py:360
  8.0 6.7 %collective-permute-start.1 = (f32[14,16,128]{2,1,0:T(8,128)S(1)}, f32[14,16,128]{2,1,0:T(8,128)S(1)}, u32[]{:S(2)}, u32[]{:S(2)}) collective-permute-start(f32[14,16,128]{2,1,0:T(8,128)S(1)} %get-tuple-element.12), channel_id=1, source_target_pairs={{8,0},{16,8},{24,16},{9,1},{17,9},{25,17},{10,2},{18,10},{26,18},{... | collective-permute-start | bytes 344072 | tf_op jit(solution)/shard_map/ppermute | solution.py:360
  14.9 18.0 %copy-start.12 = (f32[5,3]{0,1:T(4,128)S(1)}, f32[5,3]{0,1:T(4,128)}, u32[]{:S(2)}) copy-start(f32[5,3]{0,1:T(4,128)} %param.11) | copy-start | bytes 184
  14.9 18.6 %copy-start.11 = (s32[1,16,16,1]{2,3,1,0:T(1,128)S(1)}, s32[1,16,16,1]{2,3,1,0:T(1,128)}, u32[]{:S(2)}) copy-start(s32[1,16,16,1]{2,3,1,0:T(1,128)} %param.16) | copy-start | bytes 3076
  14.9 21.5 %copy-start.6 = (f32[3,16]{1,0:T(4,128)S(1)}, f32[3,16]{1,0:T(4,128)}, u32[]{:S(2)}) copy-start(f32[3,16]{1,0:T(4,128)} %color_ref.1) | copy-start | bytes 580
  14.9 21.5 %copy-start.7 = (s32[1,1,256]{2,1,0:T(1,128)S(1)}, s32[1,1,256]{2,1,0:T(1,128)}, u32[]{:S(2)}) copy-start(s32[1,1,256]{2,1,0:T(1,128)} %param.17) | copy-start | bytes 3076
  14.9 21.5 %copy-start.8 = (f32[16]{0:T(128)S(1)}, f32[16]{0:T(128)}, u32[]{:S(2)}) copy-start(f32[16]{0:T(128)} %center_ref.1) | copy-start | bytes 196
  14.9 21.5 %copy-start.9 = (f32[16]{0:T(128)S(1)}, f32[16]{0:T(128)}, u32[]{:S(2)}) copy-start(f32[16]{0:T(128)} %sharp_ref.1) | copy-start | bytes 196
  15.0 21.5 %copy-start.10 = (f32[16]{0:T(128)S(1)}, f32[16]{0:T(128)}, u32[]{:S(2)}) copy-start(f32[16]{0:T(128)} %gain_ref.1) | copy-start | bytes 196
  15.0 6.2 %collective-permute-start.2 = (f32[472,128]{1,0:T(8,128)S(1)}, f32[472,128]{1,0:T(8,128)S(1)}, u32[]{:S(2)}, u32[]{:S(2)}) collective-permute-start(f32[472,128]{1,0:T(8,128)S(1)} %broadcast_select_fusion), channel_id=1, source_target_pairs={{0,4},{4,0},{1,5},{5,1},{2,6},{6,2},{3,7},{7,3},{8,12},{12,8},{9,1... | collective-permute-start | bytes 725000 | tf_op jit(solution)/shard_map/ppermute | solution.py:404
  28.7 1.6 %copy-start.2 = (f32[228,24,128]{2,1,0:T(8,128)}, f32[228,24,128]{2,1,0:T(8,128)S(1)}, u32[]{:S(2)}) copy-start(f32[228,24,128]{2,1,0:T(8,128)S(1)} %get-tuple-element.15.pad_ref) | copy-start | bytes 8404996
  30.3 4.0 %collective-permute-start.3 = (f32[6,24,128]{2,1,0:T(8,128)S(1)}, f32[6,24,128]{2,1,0:T(8,128)S(1)}, u32[]{:S(2)}, u32[]{:S(2)}) collective-permute-start(f32[6,24,128]{2,1,0:T(8,128)S(1)} %get-tuple-element.16.ownhi_ref), channel_id=1, source_target_pairs={{0,1},{1,2},{2,3},{4,5},{5,6},{6,7},{8,9},{9,10},{10,11},{12,13},{... | collective-permute-start | bytes 221192 | tf_op jit(solution)/shard_map/ppermute | solution.py:360
  31.5 4.9 %collective-permute-start.4 = (f32[6,24,128]{2,1,0:T(8,128)S(1)}, f32[6,24,128]{2,1,0:T(8,128)S(1)}, u32[]{:S(2)}, u32[]{:S(2)}) collective-permute-start(f32[6,24,128]{2,1,0:T(8,128)S(1)} %get-tuple-element.17.ownlo_ref), channel_id=1, source_target_pairs={{1,0},{2,1},{3,2},{5,4},{6,5},{7,6},{9,8},{10,9},{11,10},{13,12},{... | collective-permute-start | bytes 221192 | tf_op jit(solution)/shard_map/ppermute | solution.py:360
  36.5 1.8 %copy-start.3 = (f32[228,24,128]{2,1,0:T(8,128)S(1)}, f32[228,24,128]{2,1,0:T(8,128)}, u32[]{:S(2)}) copy-start(f32[228,24,128]{2,1,0:T(8,128)} %copy-done.2) | copy-start | bytes 8404996

commit v4 on v3

--- a/solution.py
+++ b/solution.py
@@ -38,13 +38,25 @@
     return plan, at + (-at) % SUB
 
 
-def pack_planes_kernel(fields_ref, kappa_ref, lo_ref, hi_ref):
+def pack_planes_kernel(fields_ref, kappa_ref, lo_ref, hi_ref, sems):
     nfield, depth_len = fields_ref.shape[:2]
+    copies = []
     for field, at, wide in z_plan(nfield)[0]:
         source = kappa_ref if field == nfield else fields_ref.at[field]
-        for k in range(wide):
-            lo_ref[at + k] = source[k]
-            hi_ref[at + k] = source[depth_len - wide + k]
+        for first, target in ((0, lo_ref), (depth_len - wide, hi_ref)):
+            copies.append(
+                pltpu.make_async_copy(
+                    source.at[pl.ds(first, wide)], target.at[pl.ds(at, wide)], sems.at[len(copies)]
+                )
+            )
+    for copy in copies:
+        copy.start()
+    for copy in copies:
+        copy.wait()
+
+
+def steps(count, most):
+    return max(k for k in range(1, most + 1) if count % k == 0)
 
 
 def source_plane(refs, field, z):
@@ -85,7 +97,7 @@
     planes, pitch = depth_len + 2 * W, rows + SUB
     halo = jnp.zeros((SUB, lanes), F32)
 
-    @pl.loop(0, depth_len)
+    @pl.loop(0, depth_len, unroll=steps(depth_len, 4))
     def _(z):
         for field in range(nfield + 1):
             plane = field * planes + W + z
@@ -119,26 +131,18 @@
     nfield, depth_len, rows, lanes = fields_ref.shape
     planes, pitch = depth_len + 2 * W, rows + SUB
     assemble(refs, ylo_ref, yhi_ref, flags_ref, pad_ref)
-    lane = lax.broadcasted_iota(jnp.int32, (pitch, lanes), 1)
-    group = (nfield + 1) // 2
-
-    for start in range(0, nfield + 1, group):
-
-        def body(zi, carry):
+    lane = lax.broadcasted_iota(jnp.int32, (1, lanes), 1)
+
+    @pl.loop(0, nfield + 1)
+    def _(field):
+        low = high = jnp.zeros((pitch, lanes), F32)
+        for zi in range(planes):
             mine = (lane >= W * zi) & (lane < W * zi + W)
-            fresh = []
-            for field in range(start, start + group):
-                low, high = carry[field - start]
-                value = pad_ref[field * planes + zi]
-                low = jnp.where(mine, pltpu.roll(value, W * zi, 1), low)
-                high = jnp.where(mine, pltpu.roll(value, lax.rem(W * zi + W, lanes), 1), high)
-                fresh.append((low, high))
-            return tuple(fresh)
-
-        zero = jnp.zeros((pitch, lanes), F32)
-        done = lax.fori_loop(0, planes, body, ((zero, zero),) * group)
-        for field in range(start, start + group):
-            lo_ref[field], hi_ref[field] = done[field - start]
+            value = pad_ref[field * planes + zi]
+            low = jnp.where(mine, pltpu.roll(value, W * zi, 1), low)
+            high = jnp.where(mine, pltpu.roll(value, (W * zi + W) % lanes, 1), high)
+        lo_ref[field] = low
+        hi_ref[field] = high
 
 
 def stencil(u, coefs, ups, downs, speeds):
@@ -170,9 +174,9 @@
 
 def main_kernel(
     flags_ref, courant_ref, center_ref, sharp_ref, gain_ref, color_ref, mask_ref, order_ref,
-    pad_ref, xlo_ref, xhi_ref, ownlo_ref, ownhi_ref,
+    fields_ref, kappa_ref, zlo_ref, zhi_ref, ylo_ref, yhi_ref, xlo_ref, xhi_ref, ownlo_ref, ownhi_ref,
     state_ref, out_ref,
-    next_ref, last_ref, side_ref, edge_ref, base_ref, tile_ref,
+    pad_ref, next_ref, last_ref, side_ref, edge_ref, base_ref, tile_ref,
 ):
     nfield, depth_len, rows, lanes = state_ref.shape
     planes, pitch = depth_len + 2 * W, rows + SUB
@@ -249,6 +253,7 @@
     def depth_mask(zi):
         return jnp.where(zi < W, flag[0], jnp.where(zi >= W + depth_len, flag[1], 1.0))
 
+    assemble((fields_ref, kappa_ref, zlo_ref, zhi_ref), ylo_ref, yhi_ref, flags_ref, pad_ref)
     for field in range(nfield + 1):
         edges(0, field)
     side_step(0, nfield)
@@ -257,19 +262,19 @@
     side_step(1, 1)
     edges(2, 0)
 
-    @pl.loop(1, planes - 1)
+    @pl.loop(1, planes - 1, unroll=steps(planes - 2, 4))
     def _(zi):
         mask = row_mask * depth_mask(zi)
         coefs = weights(*around(pad_ref, 0, nfield, zi, pitch))
         for field in range(nfield):
             next_ref[field * planes + zi] = mask * step_value(pad_ref, 0, field, zi, pitch, coefs)
 
-    @pl.loop(2, planes - 2)
+    @pl.loop(2, planes - 2, unroll=steps(planes - 4, 4))
     def _(zi):
         coefs = weights(*around(pad_ref, 0, nfield, zi, pitch))
         last_ref[zi] = step_value(next_ref, 1, 0, zi, pitch, coefs) * (row_mask * depth_mask(zi))
 
-    @pl.loop(0, depth_len)
+    @pl.loop(0, depth_len, unroll=steps(depth_len, 4))
     def _(z):
         zi = z + W
         coefs = weights(*around(pad_ref, 0, nfield, zi, rows))
@@ -383,8 +388,9 @@
     face_lo, face_hi = pl.pallas_call(
         pack_planes_kernel,
         out_shape=(array(faces, rows_len, cols_len),) * 2,
-        in_specs=[vmem] * 2,
+        in_specs=[pl.BlockSpec(memory_space=pl.ANY)] * 2,
         out_specs=(vmem, vmem),
+        scratch_shapes=[pltpu.SemaphoreType.DMA((2 * nfield + 2,))],
         compiler_params=params,
         name="pack_planes",
     )(fields, diffusivity)
@@ -405,12 +411,13 @@
     else:
         ylo = shift(send_hi, "gy", True)
         yhi = shift(send_lo, "gy", False)
-    own_lo, own_hi, pad = pl.pallas_call(
+    pad = pltpu.VMEM(((nfield + 1) * planes, pitch, cols_len), F32)
+    own_lo, own_hi = pl.pallas_call(
         pack_columns_kernel,
-        out_shape=(array(nfield + 1, pitch, cols_len),) * 2
-        + (array((nfield + 1) * planes, pitch, cols_len),),
+        out_shape=(array(nfield + 1, pitch, cols_len),) * 2,
         in_specs=[smem] + [vmem] * 6,
-        out_specs=(vmem,) * 3,
+        out_specs=(vmem,) * 2,
+        scratch_shapes=[pad],
         compiler_params=params,
         name="pack_columns",
     )(flags, fields, diffusivity, zlo, zhi, ylo, yhi)
@@ -422,9 +429,10 @@
     state, tiles = pl.pallas_call(
         main_kernel,
         out_shape=(array(*fields.shape), array(order.shape[0], 4, cols_len)),
-        in_specs=[smem] * 8 + [vmem] * 5,
+        in_specs=[smem] * 8 + [vmem] * 10,
         out_specs=(vmem, vmem),
         scratch_shapes=[
+            pad,
             pltpu.VMEM((nfield * planes, pitch, cols_len), F32),
             pltpu.VMEM((planes, pitch, cols_len), F32),
             pltpu.VMEM((2, 2, 2, nfield, pitch, cols_len), F32),
@@ -436,7 +444,7 @@
         name="step_and_march",
     )(
         flags, courant, tf_center, tf_sharp, tf_gain, tf_color, tile_mask[0].reshape(-1), order,
-        pad, xlo, xhi, own_lo, own_hi,
+        fields, diffusivity, zlo, zhi, ylo, yhi, xlo, xhi, own_lo, own_hi,
     )
     grouped = tiles.reshape(count, per_owner * 4, cols_len)
     composed = compose(lax.all_to_all(grouped, "gz", split_axis=0, concat_axis=0, tiled=True))

time: 75 us -> 62.4 us (0.83)
  Pallas kernels: 25.1 us -> 15.9 us
  local copies, waits for them, and re-layouts: 6.44 us -> 3.1 us
    pallas_call x1, Pallas kernels: 16.7 us -> 11.9 us  [shards(): pl.pallas_call(main_kernel, out_shape=(array(*fields.shape), array(order....]
    pallas_call x1, Pallas kernels: 7.46 us -> 2.66 us  [shards(): pl.pallas_call(pack_columns_kernel, out_shape=(array(nfield + 1, pitch, c...]
    unnamed x28 -> x24, local copies, waits for them, and re-layouts: 6.26 us -> 2.91 us
where the time goes in v4:
time: 62.4 us; the launch traced here: 61.4 us
  blocking collectives  18.2 us (29%)
  Pallas kernels  15.9 us (25%)
  waiting for transfers between devices  12.2 us (20%)
  starting transfers between devices  10.5 us (17%)
  local copies, waits for them, and re-layouts  3.1 us (5%)
  between operations  0.8 us (1%)
  other arithmetic  0.71 us (1%)
    all_to_all x1, blocking collectives, shards(): lax.all_to_all(grouped, 'gz', split_axis=0, concat_axis=0, tiled=True)  18.2 us
    pallas_call x1, Pallas kernels, shards(): pl.pallas_call(main_kernel, out_shape=(array(*fields.shape), array(order....  11.9 us
    ppermute x4, starting transfers between devices, shift(): return lax.ppermute(message, axis, pairs)  8.94 us
    ppermute x4, waiting for transfers between devices, shift(): return lax.ppermute(message, axis, pairs)  7.61 us
    ppermute x1, waiting for transfers between devices, shards(): ylo = yhi = lax.ppermute(mine, 'gy', [(0, 1), (1, 0)])  4.57 us
    unnamed x24, local copies, waits for them, and re-layouts  2.91 us
    pallas_call x1, Pallas kernels, shards(): pl.pallas_call(pack_columns_kernel, out_shape=(array(nfield + 1, pitch, c...  2.66 us
    ppermute x1, starting transfers between devices, shards(): ylo = yhi = lax.ppermute(mine, 'gy', [(0, 1), (1, 0)])  1.56 us
  transfers between devices with their start and end apart: 5, of which 4 were waited for; matrix products, arithmetic and copies ran while one was open for 2% of the time, Pallas kernels for 0%

profile of v4, /device:TPU:0, one launch (start us, length us, event | category | flops | bytes accessed | tf_op | source)
XLA Modules:
  0.0 61.4 jit_solution(17923855826210698455)
XLA Ops:
  0.6 0.0 copy-start
  0.6 1.3 %copy-done = f32[5,32,16,128]{3,2,1,0:T(8,128)S(1)} copy-done((f32[5,32,16,128]{3,2,1,0:T(8,128)S(1)}, f32[5,32,16,128]{3,2,1,0:T(8,128)}, u32[]{:S(2)}) %copy-start) | copy-done | bytes 1310744
  1.9 0.0 copy-start.2
  1.9 0.9 %copy-done.2 = f32[32,16,128]{2,1,0:T(8,128)S(1)} copy-done((f32[32,16,128]{2,1,0:T(8,128)S(1)}, f32[32,16,128]{2,1,0:T(8,128)}, u32[]{:S(2)}) %copy-start.2) | copy-done | bytes 262168
  2.9 0.0 copy-start.1
  2.9 0.0 copy-start.3
  2.9 0.4 pack_planes.1
  3.3 5.1 %collective-permute-start = (f32[14,16,128]{2,1,0:T(8,128)S(1)}, f32[14,16,128]{2,1,0:T(8,128)S(1)}, u32[]{:S(2)}, u32[]{:S(2)}) collective-permute-start(f32[14,16,128]{2,1,0:T(8,128)S(1)} %get-tuple-element.10), channel_id=1, source_target_pairs={{0,8},{8,16},{16,24},{1,9},{9,17},{17,25},{2,10},{10,18},{18,26},{... | collective-permute-start | bytes 344072 | tf_op jit(solution)/shard_map/ppermute | solution.py:365
  8.4 1.3 %collective-permute-start.1 = (f32[14,16,128]{2,1,0:T(8,128)S(1)}, f32[14,16,128]{2,1,0:T(8,128)S(1)}, u32[]{:S(2)}, u32[]{:S(2)}) collective-permute-start(f32[14,16,128]{2,1,0:T(8,128)S(1)} %get-tuple-element.11), channel_id=1, source_target_pairs={{8,0},{16,8},{24,16},{9,1},{17,9},{25,17},{10,2},{18,10},{26,18},{... | collective-permute-start | bytes 344072 | tf_op jit(solution)/shard_map/ppermute | solution.py:365
  9.7 1.1 %collective-permute-done.zlo_ref = f32[14,16,128]{2,1,0:T(8,128)S(1)} collective-permute-done((f32[14,16,128]{2,1,0:T(8,128)S(1)}, f32[14,16,128]{2,1,0:T(8,128)S(1)}, u32[]{:S(2)}, u32[]{:S(2)}) %collective-permute-start) | collective-permute-done | bytes 114720 | tf_op jit(solution)/shard_map/ppermute | solution.py:365
  10.8 4.3 %collective-permute-done.1.zhi_ref = f32[14,16,128]{2,1,0:T(8,128)S(1)} collective-permute-done((f32[14,16,128]{2,1,0:T(8,128)S(1)}, f32[14,16,128]{2,1,0:T(8,128)S(1)}, u32[]{:S(2)}, u32[]{:S(2)}) %collective-permute-start.1) | collective-permute-done | bytes 114720 | tf_op jit(solution)/shard_map/ppermute | solution.py:365
  15.1 0.0 copy-done.1
  15.1 0.0 copy-done.3
  15.1 0.2 pack_rows.1
  15.3 0.0 copy-start.10
  15.3 0.0 copy-start.9
  15.3 0.0 copy-start.4
  15.3 0.0 copy-start.5
  15.3 0.0 copy-start.6
  15.3 0.0 copy-start.7
  15.4 0.0 copy-start.8
  15.4 1.6 %collective-permute-start.2 = (f32[472,128]{1,0:T(8,128)S(1)}, f32[472,128]{1,0:T(8,128)S(1)}, u32[]{:S(2)}, u32[]{:S(2)}) collective-permute-start(f32[472,128]{1,0:T(8,128)S(1)} %broadcast_select_fusion), channel_id=1, source_target_pairs={{0,4},{4,0},{1,5},{5,1},{2,6},{6,2},{3,7},{7,3},{8,12},{12,8},{9,1... | collective-permute-start | bytes 725000 | tf_op jit(solution)/shard_map/ppermute | solution.py:410
  16.9 0.1 stack.35
  17.0 4.6 %collective-permute-done.2.ylo_ref.yhi_ref = f32[472,128]{1,0:T(8,128)S(1)} collective-permute-done((f32[472,128]{1,0:T(8,128)S(1)}, f32[472,128]{1,0:T(8,128)S(1)}, u32[]{:S(2)}, u32[]{:S(2)}) %collective-permute-start.2) | collective-permute-done | bytes 241696 | tf_op jit(solution)/shard_map/ppermute | solution.py:410
  21.6 2.7 %pack_columns.1 = (f32[6,24,128]{2,1,0:T(8,128)S(1)}, f32[6,24,128]{2,1,0:T(8,128)S(1)}) custom-call(f32[6]{0:T(128)S(1)} %stack.36.flags_ref, f32[5,32,16,128]{3,2,1,0:T(8,128)S(1)} %copy-done.1, f32[32,16,128]{2,1,0:T(8,128)S(1)} %copy-done.3, f32[14,16,128]{2,1,0:T(8,128)S(1)} %collective-permute-done.zlo_ref, ...), custom_call_target="tpu_custom_call" | custom-call | tf_op jit(solution)/shard_map/pack_columns/pallas_call | solution.py:415
  24.3 1.3 %collective-permute-start.3 = (f32[6,24,128]{2,1,0:T(8,128)S(1)}, f32[6,24,128]{2,1,0:T(8,128)S(1)}, u32[]{:S(2)}, u32[]{:S(2)}) collective-permute-start(f32[6,24,128]{2,1,0:T(8,128)S(1)} %get-tuple-element.14.ownhi_ref), channel_id=1, source_target_pairs={{0,1},{1,2},{2,3},{4,5},{5,6},{6,7},{8,9},{9,10},{10,11},{12,13},{... | collective-permute-start | bytes 221192 | tf_op jit(solution)/shard_map/ppermute | solution.py:365
  25.6 1.3 %collective-permute-start.4 = (f32[6,24,128]{2,1,0:T(8,128)S(1)}, f32[6,24,128]{2,1,0:T(8,128)S(1)}, u32[]{:S(2)}, u32[]{:S(2)}) collective-permute-start(f32[6,24,128]{2,1,0:T(8,128)S(1)} %get-tuple-element.15.ownlo_ref), channel_id=1, source_target_pairs={{1,0},{2,1},{3,2},{5,4},{6,5},{7,6},{9,8},{10,9},{11,10},{13,12},{... | collective-permute-start | bytes 221192 | tf_op jit(solution)/shard_map/ppermute | solution.py:365
  26.9 0.0 copy-done.10
  26.9 0.1 copy.11.courant_ref
  27.0 0.5 broadcast.3
  27.5 0.0 copy-done.9
  27.5 0.7 %reduce.3 = s32[16,16]{1,0:T(8,128)S(1)} reduce(s32[1,16,16,1]{2,3,1,0:T(1,128)S(1)} %copy-done.9, s32[]{:T(128)} %broadcast.3), dimensions={0,3}, to_apply=%param.16.reduce_sub_computation.3 | reduce | bytes 2052 | tf_op args[7]
  28.2 0.1 reshape_squeeze.3.mask_ref
  28.3 0.0 collective-permute-done.3.xlo_ref
  28.3 2.2 %collective-permute-done.4.xhi_ref = f32[6,24,128]{2,1,0:T(8,128)S(1)} collective-permute-done((f32[6,24,128]{2,1,0:T(8,128)S(1)}, f32[6,24,128]{2,1,0:T(8,128)S(1)}, u32[]{:S(2)}, u32[]{:S(2)}) %collective-permute-start.4) | collective-permute-done | bytes 73760 | tf_op jit(solution)/shard_map/ppermute | solution.py:365
  30.5 0.0 copy-done.4
  30.5 0.0 copy-done.5
  30.5 0.0 copy-done.6
  30.5 0.0 copy-done.7
  30.5 0.0 copy-done.8
  30.5 11.9 %step_and_march.1 = (f32[5,32,16,128]{3,2,1,0:T(8,128)}, f32[256,4,128]{2,1,0:T(4,128)S(1)}) custom-call(f32[6]{0:T(128)S(1)} %stack.36.flags_ref, f32[5,3]{1,0:T(8,128)S(1)} %copy.11.courant_ref, f32[16]{0:T(128)S(1)} %copy-done.6, f32[16]{0:T(128)S(1)} %copy-done.7, f32[16]{0:T(128)S(1)} %copy-done.8, f32[3,16]{1,0:T(4,128)S(1)} %copy-done.4, ...), custom_call_target="tpu_custom_call" | custom-call | tf_op jit(solution)/shard_map/step_and_march/pallas_call | solution.py:429
  42.4 18.2 %all_to_all.5.part_ref = f32[4,256,128]{2,1,0:T(8,128)S(1)} all-to-all(f32[4,256,128]{2,1,0:T(8,128)S(1)} %bitcast.10), channel_id=1, replica_groups=mesh['gz'=4,'gy'=2,'gx'=4] {'gz'}, dimensions={0} | all-to-all | bytes 1048576 | tf_op jit(solution)/shard_map/all_to_all | solution.py:450
  60.7 0.7 %compose.1 = f32[256,128]{1,0:T(8,128)} custom-call(f32[4,256,128]{2,1,0:T(8,128)S(1)} %all_to_all.5.part_ref), custom_call_target="tpu_custom_call" | custom-call | tf_op jit(solution)/shard_map/compose/pallas_call | solution.py:352
  (2 shorter events, 0.0 us)
Async XLA Ops:
  0.6 1.3 %copy-start = (f32[5,32,16,128]{3,2,1,0:T(8,128)S(1)}, f32[5,32,16,128]{3,2,1,0:T(8,128)}, u32[]{:S(2)}) copy-start(f32[5,32,16,128]{3,2,1,0:T(8,128)} %fields_ref.7) | copy-start | bytes 3932164
  1.9 0.9 %copy-start.2 = (f32[32,16,128]{2,1,0:T(8,128)S(1)}, f32[32,16,128]{2,1,0:T(8,128)}, u32[]{:S(2)}) copy-start(f32[32,16,128]{2,1,0:T(8,128)} %kappa_ref.7) | copy-start | bytes 786436
  2.9 12.2 %copy-start.1 = (f32[5,32,16,128]{3,2,1,0:T(8,128)S(1)}, f32[5,32,16,128]{3,2,1,0:T(8,128)}, u32[]{:S(2)}) copy-start(f32[5,32,16,128]{3,2,1,0:T(8,128)} %fields_ref.7) | copy-start | bytes 3932164
  2.9 12.2 %copy-start.3 = (f32[32,16,128]{2,1,0:T(8,128)S(1)}, f32[32,16,128]{2,1,0:T(8,128)}, u32[]{:S(2)}) copy-start(f32[32,16,128]{2,1,0:T(8,128)} %kappa_ref.7) | copy-start | bytes 786436
  3.3 7.5 %collective-permute-start = (f32[14,16,128]{2,1,0:T(8,128)S(1)}, f32[14,16,128]{2,1,0:T(8,128)S(1)}, u32[]{:S(2)}, u32[]{:S(2)}) collective-permute-start(f32[14,16,128]{2,1,0:T(8,128)S(1)} %get-tuple-element.10), channel_id=1, source_target_pairs={{0,8},{8,16},{16,24},{1,9},{9,17},{17,25},{2,10},{10,18},{18,26},{... | collective-permute-start | bytes 344072 | tf_op jit(solution)/shard_map/ppermute | solution.py:365
  8.4 6.7 %collective-permute-start.1 = (f32[14,16,128]{2,1,0:T(8,128)S(1)}, f32[14,16,128]{2,1,0:T(8,128)S(1)}, u32[]{:S(2)}, u32[]{:S(2)}) collective-permute-start(f32[14,16,128]{2,1,0:T(8,128)S(1)} %get-tuple-element.11), channel_id=1, source_target_pairs={{8,0},{16,8},{24,16},{9,1},{17,9},{25,17},{10,2},{18,10},{26,18},{... | collective-permute-start | bytes 344072 | tf_op jit(solution)/shard_map/ppermute | solution.py:365
  15.3 11.6 %copy-start.10 = (f32[5,3]{0,1:T(4,128)S(1)}, f32[5,3]{0,1:T(4,128)}, u32[]{:S(2)}) copy-start(f32[5,3]{0,1:T(4,128)} %param.11) | copy-start | bytes 184
  15.3 12.2 %copy-start.9 = (s32[1,16,16,1]{2,3,1,0:T(1,128)S(1)}, s32[1,16,16,1]{2,3,1,0:T(1,128)}, u32[]{:S(2)}) copy-start(s32[1,16,16,1]{2,3,1,0:T(1,128)} %param.16) | copy-start | bytes 3076
  15.3 15.2 %copy-start.4 = (f32[3,16]{1,0:T(4,128)S(1)}, f32[3,16]{1,0:T(4,128)}, u32[]{:S(2)}) copy-start(f32[3,16]{1,0:T(4,128)} %color_ref.1) | copy-start | bytes 580
  15.3 15.2 %copy-start.5 = (s32[1,1,256]{2,1,0:T(1,128)S(1)}, s32[1,1,256]{2,1,0:T(1,128)}, u32[]{:S(2)}) copy-start(s32[1,1,256]{2,1,0:T(1,128)} %param.17) | copy-start | bytes 3076
  15.3 15.2 %copy-start.6 = (f32[16]{0:T(128)S(1)}, f32[16]{0:T(128)}, u32[]{:S(2)}) copy-start(f32[16]{0:T(128)} %center_ref.1) | copy-start | bytes 196
  15.3 15.2 %copy-start.7 = (f32[16]{0:T(128)S(1)}, f32[16]{0:T(128)}, u32[]{:S(2)}) copy-start(f32[16]{0:T(128)} %sharp_ref.1) | copy-start | bytes 196
  15.4 15.2 %copy-start.8 = (f32[16]{0:T(128)S(1)}, f32[16]{0:T(128)}, u32[]{:S(2)}) copy-start(f32[16]{0:T(128)} %gain_ref.1) | copy-start | bytes 196
  15.4 6.2 %collective-permute-start.2 = (f32[472,128]{1,0:T(8,128)S(1)}, f32[472,128]{1,0:T(8,128)S(1)}, u32[]{:S(2)}, u32[]{:S(2)}) collective-permute-start(f32[472,128]{1,0:T(8,128)S(1)} %broadcast_select_fusion), channel_id=1, source_target_pairs={{0,4},{4,0},{1,5},{5,1},{2,6},{6,2},{3,7},{7,3},{8,12},{12,8},{9,1... | collective-permute-start | bytes 725000 | tf_op jit(solution)/shard_map/ppermute | solution.py:410
  24.3 4.0 %collective-permute-start.3 = (f32[6,24,128]{2,1,0:T(8,128)S(1)}, f32[6,24,128]{2,1,0:T(8,128)S(1)}, u32[]{:S(2)}, u32[]{:S(2)}) collective-permute-start(f32[6,24,128]{2,1,0:T(8,128)S(1)} %get-tuple-element.14.ownhi_ref), channel_id=1, source_target_pairs={{0,1},{1,2},{2,3},{4,5},{5,6},{6,7},{8,9},{9,10},{10,11},{12,13},{... | collective-permute-start | bytes 221192 | tf_op jit(solution)/shard_map/ppermute | solution.py:365
  25.6 4.9 %collective-permute-start.4 = (f32[6,24,128]{2,1,0:T(8,128)S(1)}, f32[6,24,128]{2,1,0:T(8,128)S(1)}, u32[]{:S(2)}, u32[]{:S(2)}) collective-permute-start(f32[6,24,128]{2,1,0:T(8,128)S(1)} %get-tuple-element.15.ownlo_ref), channel_id=1, source_target_pairs={{1,0},{2,1},{3,2},{5,4},{6,5},{7,6},{9,8},{10,9},{11,10},{13,12},{... | collective-permute-start | bytes 221192 | tf_op jit(solution)/shard_map/ppermute | solution.py:365

commit v5 on v4

--- a/solution.py
+++ b/solution.py
@@ -114,35 +114,62 @@
                 if k >= wide:
                     pad_ref[plane, :rows, :] = jnp.zeros((rows, lanes), F32)
                 pad_ref[plane, rows:, :] = halo
-    flat = pad_ref.reshape((nfield + 1) * planes * pitch, lanes)
+    place_rows(pad_ref, depth_len, rows, ylo_ref, yhi_ref, flags_ref)
+
+
+def place_rows(pad_ref, depth_len, first_row, ylo_ref, yhi_ref, flags_ref):
+    planes = depth_len + 2 * W
+    pitch, lanes = pad_ref.shape[1:]
+    flat = pad_ref.reshape(pad_ref.shape[0] * pitch, lanes)
     low, high = flags_ref[2], flags_ref[3]
-    for field, away, first, length, at in y_plan(nfield, depth_len)[0]:
-        for ref, flag, row in ((ylo_ref, low, pitch - away), (yhi_ref, high, rows + away - 1)):
+    for field, away, first, length, at in y_plan(pad_ref.shape[0] // planes - 1, depth_len)[0]:
+        for ref, flag, row in ((ylo_ref, low, pitch - away), (yhi_ref, high, first_row + away - 1)):
             for start in tiles_of(0, length):
                 flat[pl.ds((field * planes + W + first + start) * pitch + row, SUB, stride=pitch), :] = (
                     ref[pl.ds(at + start, SUB), :] * flag
                 )
 
 
-def pack_columns_kernel(
-    flags_ref, fields_ref, kappa_ref, zlo_ref, zhi_ref, ylo_ref, yhi_ref, lo_ref, hi_ref, pad_ref
-):
+def take_columns(value, zi, lane, low, high):
+    lanes = value.shape[-1]
+    mine = (lane >= W * zi) & (lane < W * zi + W)
+    low = jnp.where(mine, pltpu.roll(value, W * zi, 1), low)
+    high = jnp.where(mine, pltpu.roll(value, (W * zi + W) % lanes, 1), high)
+    return low, high
+
+
+def pack_own_kernel(fields_ref, kappa_ref, zlo_ref, zhi_ref, lo_ref, hi_ref):
     refs = (fields_ref, kappa_ref, zlo_ref, zhi_ref)
     nfield, depth_len, rows, lanes = fields_ref.shape
-    planes, pitch = depth_len + 2 * W, rows + SUB
-    assemble(refs, ylo_ref, yhi_ref, flags_ref, pad_ref)
     lane = lax.broadcasted_iota(jnp.int32, (1, lanes), 1)
-
-    @pl.loop(0, nfield + 1)
-    def _(field):
-        low = high = jnp.zeros((pitch, lanes), F32)
-        for zi in range(planes):
-            mine = (lane >= W * zi) & (lane < W * zi + W)
-            value = pad_ref[field * planes + zi]
-            low = jnp.where(mine, pltpu.roll(value, W * zi, 1), low)
-            high = jnp.where(mine, pltpu.roll(value, (W * zi + W) % lanes, 1), high)
+    for field in range(nfield + 1):
+        wide = reach(field, nfield)
+        low = high = jnp.zeros((rows, lanes), F32)
+        for z in range(-wide, depth_len + wide):
+            low, high = take_columns(source_plane(refs, field, z)[...], z + W, lane, low, high)
         lo_ref[field] = low
         hi_ref[field] = high
+
+
+def pack_columns_kernel(
+    flags_ref, ylo_ref, yhi_ref, mainlo_ref, mainhi_ref, lo_ref, hi_ref, halo_ref
+):
+    nplane, _, lanes = halo_ref.shape
+    nfield, rows = mainlo_ref.shape[0] - 1, mainlo_ref.shape[1]
+    planes = nplane // (nfield + 1)
+    lane = lax.broadcasted_iota(jnp.int32, (1, lanes), 1)
+    zero = jnp.zeros((SUB, lanes), F32)
+    for plane in range(nplane):
+        halo_ref[plane] = zero
+    place_rows(halo_ref, planes - 2 * W, 0, ylo_ref, yhi_ref, flags_ref)
+    for field in range(nfield + 1):
+        low = high = zero
+        for zi in range(planes):
+            low, high = take_columns(halo_ref[field * planes + zi], zi, lane, low, high)
+        lo_ref[field, :rows, :] = mainlo_ref[field]
+        hi_ref[field, :rows, :] = mainhi_ref[field]
+        lo_ref[field, rows:, :] = low
+        hi_ref[field, rows:, :] = high
 
 
 def stencil(u, coefs, ups, downs, speeds):
@@ -176,7 +203,7 @@
     flags_ref, courant_ref, center_ref, sharp_ref, gain_ref, color_ref, mask_ref, order_ref,
     fields_ref, kappa_ref, zlo_ref, zhi_ref, ylo_ref, yhi_ref, xlo_ref, xhi_ref, ownlo_ref, ownhi_ref,
     state_ref, out_ref,
-    pad_ref, next_ref, last_ref, side_ref, edge_ref, base_ref, tile_ref,
+    pad_ref, next_ref, last_ref, side_ref, edge_ref, base_ref, tile_ref, coef_ref, held_ref, sem,
 ):
     nfield, depth_len, rows, lanes = state_ref.shape
     planes, pitch = depth_len + 2 * W, rows + SUB
@@ -250,6 +277,10 @@
         u, ups, downs = around(src_ref, level, field, zi, n)
         return stencil(u, coefs, ups, downs, speed[field])
 
+    def kept(zi, n):
+        found = [coef_ref[i, zi, :n, :] for i in range(7)]
+        return [found[0:2], found[2:4], found[4:6], found[6]]
+
     def depth_mask(zi):
         return jnp.where(zi < W, flag[0], jnp.where(zi >= W + depth_len, flag[1], 1.0))
 
@@ -266,32 +297,36 @@
     def _(zi):
         mask = row_mask * depth_mask(zi)
         coefs = weights(*around(pad_ref, 0, nfield, zi, pitch))
+        for i, value in enumerate(sum(coefs[:3], ()) + (coefs[3],)):
+            coef_ref[i, zi] = value
         for field in range(nfield):
             next_ref[field * planes + zi] = mask * step_value(pad_ref, 0, field, zi, pitch, coefs)
 
     @pl.loop(2, planes - 2, unroll=steps(planes - 4, 4))
     def _(zi):
-        coefs = weights(*around(pad_ref, 0, nfield, zi, pitch))
+        coefs = kept(zi, pitch)
         last_ref[zi] = step_value(next_ref, 1, 0, zi, pitch, coefs) * (row_mask * depth_mask(zi))
 
     @pl.loop(0, depth_len, unroll=steps(depth_len, 4))
     def _(z):
         zi = z + W
-        coefs = weights(*around(pad_ref, 0, nfield, zi, rows))
+        coefs = kept(zi, rows)
         s, ups, downs = around(last_ref, 2, 0, zi, rows)
-        state_ref[0, z] = s
+        held_ref[0, z] = s
         g_z, g_y, g_x = [0.5 * (ups[a] - downs[a]) for a in range(3)]
         shade = 0.35 + 0.65 * jnp.abs(0.64 * g_z + 0.6 * g_y + 0.48 * g_x) * lax.rsqrt(
             g_z * g_z + g_y * g_y + g_x * g_x + 1.0
         )
         for field in range(1, nfield):
             value = step_value(next_ref, 1, field, zi, rows, coefs)
-            state_ref[field, z] = value
+            held_ref[field, z] = value
             if field <= 3:
                 base_ref[field, z] = shade * (0.5 + 0.5 * jnp.tanh(0.5 * value))
             if field == 4:
                 base_ref[0, z] = 1.0 + 0.5 * jnp.tanh(value)
 
+    keep = pltpu.make_async_copy(held_ref, state_ref, sem)
+    keep.start()
     ntf = center_ref.shape[0]
     chunk = 4 if ntf % 4 == 0 else 1
     halves = rows // SUB
@@ -308,7 +343,7 @@
         total = [jnp.zeros(shape, jnp.float32)] * chunk
         acc = [[jnp.zeros(shape, jnp.float32)] * 3 for _ in range(chunk)]
         for z in range(depth_len):
-            s = state_ref[0, z, pl.ds(row, SUB), :]
+            s = held_ref[0, z, pl.ds(row, SUB), :]
             modul = base_ref[0, z, pl.ds(row, SUB), :]
             base = [base_ref[k + 1, z, pl.ds(row, SUB), :] for k in range(3)]
             for j in range(chunk):
@@ -329,12 +364,13 @@
         tile = order_ref[slot]
         cover = mask_ref[tile].astype(jnp.float32)
         out_ref[slot] = tile_ref[pl.ds(pl.multiple_of(tile * 4, 4), 4), :] * cover
+    keep.wait()
 
 
 def compose_kernel(part_ref, out_ref):
     slabs, rows, _ = part_ref.shape
 
-    @pl.loop(0, rows // 32)
+    @pl.loop(0, rows // 32, unroll=rows // 32)
     def _(step):
         def load(slab, k):
             return part_ref[slab, pl.ds(step * 32 + k, 8, stride=4), :]
@@ -391,7 +427,7 @@
         in_specs=[pl.BlockSpec(memory_space=pl.ANY)] * 2,
         out_specs=(vmem, vmem),
         scratch_shapes=[pltpu.SemaphoreType.DMA((2 * nfield + 2,))],
-        compiler_params=params,
+        compiler_params=pltpu.CompilerParams(vmem_limit_bytes=60 * 1024 * 1024),
         name="pack_planes",
     )(fields, diffusivity)
     zlo = shift(face_hi, "gz", True)
@@ -405,6 +441,15 @@
         compiler_params=params,
         name="pack_rows",
     )(fields, diffusivity, zlo, zhi)
+    main_lo, main_hi = pl.pallas_call(
+        pack_own_kernel,
+        out_shape=(array(nfield + 1, rows_len, cols_len),) * 2,
+        in_specs=[vmem] * 4,
+        out_specs=(vmem,) * 2,
+        compiler_params=params,
+        cost_estimate=pl.CostEstimate(flops=10**7, bytes_accessed=4 * 10**6, transcendentals=0),
+        name="pack_own",
+    )(fields, diffusivity, zlo, zhi)
     if lax.axis_size("gy") == 2:
         mine = jnp.where(lax.axis_index("gy") == 0, send_hi, send_lo)
         ylo = yhi = lax.ppermute(mine, "gy", [(0, 1), (1, 0)])
@@ -415,12 +460,12 @@
     own_lo, own_hi = pl.pallas_call(
         pack_columns_kernel,
         out_shape=(array(nfield + 1, pitch, cols_len),) * 2,
-        in_specs=[smem] + [vmem] * 6,
+        in_specs=[smem] + [vmem] * 4,
         out_specs=(vmem,) * 2,
-        scratch_shapes=[pad],
+        scratch_shapes=[pltpu.VMEM(((nfield + 1) * planes, SUB, cols_len), F32)],
         compiler_params=params,
         name="pack_columns",
-    )(flags, fields, diffusivity, zlo, zhi, ylo, yhi)
+    )(flags, ylo, yhi, main_lo, main_hi)
     xlo = shift(own_hi, "gx", True)
     xhi = shift(own_lo, "gx", False)
     count = lax.axis_size("gz")
@@ -430,7 +475,7 @@
         main_kernel,
         out_shape=(array(*fields.shape), array(order.shape[0], 4, cols_len)),
         in_specs=[smem] * 8 + [vmem] * 10,
-        out_specs=(vmem, vmem),
+        out_specs=(pl.BlockSpec(memory_space=pl.ANY), vmem),
         scratch_shapes=[
             pad,
             pltpu.VMEM((nfield * planes, pitch, cols_len), F32),
@@ -439,8 +484,11 @@
             pltpu.VMEM((3, nfield + 1, pitch, cols_len), F32),
             pltpu.VMEM((4, depth_len, rows_len, cols_len), F32),
             pltpu.VMEM((order.shape[0] * 4, cols_len), F32),
+            pltpu.VMEM((7, planes, pitch, cols_len), F32),
+            pltpu.VMEM(fields.shape, F32),
+            pltpu.SemaphoreType.DMA(()),
         ],
-        compiler_params=params,
+        compiler_params=pltpu.CompilerParams(vmem_limit_bytes=24 * 1024 * 1024),
         name="step_and_march",
     )(
         flags, courant, tf_center, tf_sharp, tf_gain, tf_color, tile_mask[0].reshape(-1), order,

time: 62.4 us -> 58.6 us (0.939)
  local copies, waits for them, and re-layouts: 3.1 us -> 0.84 us
  waiting for transfers between devices: 12.2 us -> 11.3 us
    unnamed x24 -> x20, local copies, waits for them, and re-layouts: 2.91 us -> 0.66 us
    pallas_call x1, Pallas kernels: 2.66 us -> 1.13 us  [shards(): pl.pallas_call(pack_columns_kernel, out_shape=(array(nfield + 1, pitch, c...]
    pallas_call x1, Pallas kernels: 0.41 us -> 1.77 us  [shards(): pl.pallas_call(pack_planes_kernel, out_shape=(array(faces, rows_len, cols...]
    pallas_call x1, Pallas kernels: 11.9 us -> 10.6 us  [shards(): pl.pallas_call(main_kernel, out_shape=(array(*fields.shape), array(order....]
    ppermute x1, waiting for transfers between devices: 4.57 us -> 3.51 us  [shards(): ylo = yhi = lax.ppermute(mine, 'gy', [(0, 1), (1, 0)])]
    pallas_call x0 -> x1, Pallas kernels: none -> 1.06 us  [shards(): pl.pallas_call(pack_own_kernel, out_shape=(array(nfield + 1, rows_len, co...]
  transfers between devices with their start and end apart: 5 -> 5, of which waited for: 4 -> 4; matrix products, arithmetic and copies ran while one was open for 2% -> 3% of each run, Pallas kernels for 0% -> 2%
where the time goes in v5:
time: 58.6 us; the launch traced here: 57.7 us
  blocking collectives  18.2 us (31%)
  Pallas kernels  15.4 us (26%)
  waiting for transfers between devices  11.3 us (19%)
  starting transfers between devices  10.4 us (18%)
  local copies, waits for them, and re-layouts  0.84 us (1%)
  between operations  0.82 us (1%)
  other arithmetic  0.71 us (1%)
    all_to_all x1, blocking collectives, shards(): lax.all_to_all(grouped, 'gz', split_axis=0, concat_axis=0, tiled=True)  18.2 us
    pallas_call x1, Pallas kernels, shards(): pl.pallas_call(main_kernel, out_shape=(array(*fields.shape), array(order....  10.6 us
    ppermute x4, starting transfers between devices, shift(): return lax.ppermute(message, axis, pairs)  8.81 us
    ppermute x4, waiting for transfers between devices, shift(): return lax.ppermute(message, axis, pairs)  7.82 us
    ppermute x1, waiting for transfers between devices, shards(): ylo = yhi = lax.ppermute(mine, 'gy', [(0, 1), (1, 0)])  3.51 us
    pallas_call x1, Pallas kernels, shards(): pl.pallas_call(pack_planes_kernel, out_shape=(array(faces, rows_len, cols...  1.77 us
    ppermute x1, starting transfers between devices, shards(): ylo = yhi = lax.ppermute(mine, 'gy', [(0, 1), (1, 0)])  1.56 us
  transfers between devices with their start and end apart: 5, of which 4 were waited for; matrix products, arithmetic and copies ran while one was open for 3% of the time, Pallas kernels for 2%

profile of v5, /device:TPU:0, one launch (start us, length us, event | category | flops | bytes accessed | tf_op | source)
XLA Modules:
  0.0 57.7 jit_solution(14420950742456109107)
XLA Ops:
  0.6 0.0 copy-start.1
  0.6 0.0 copy-start
  0.6 1.8 %pack_planes.1 = (f32[14,16,128]{2,1,0:T(8,128)}, f32[14,16,128]{2,1,0:T(8,128)}) custom-call(f32[5,32,16,128]{3,2,1,0:T(8,128)} %fields_ref.7, f32[32,16,128]{2,1,0:T(8,128)} %kappa_ref.7), custom_call_target="tpu_custom_call" | custom-call | tf_op jit(solution)/shard_map/pack_planes/pallas_call | solution.py:424
  2.4 4.9 %collective-permute-start = (f32[14,16,128]{2,1,0:T(8,128)}, f32[14,16,128]{2,1,0:T(8,128)S(1)}, u32[]{:S(2)}, u32[]{:S(2)}) collective-permute-start(f32[14,16,128]{2,1,0:T(8,128)} %get-tuple-element.12), channel_id=1, source_target_pairs={{0,8},{8,16},{16,24},{1,9},{9,17},{17,25},{2,10},{10,18},{18,26},{... | collective-permute-start | bytes 344072 | tf_op jit(solution)/shard_map/ppermute | solution.py:401
  7.4 1.3 %collective-permute-start.1 = (f32[14,16,128]{2,1,0:T(8,128)}, f32[14,16,128]{2,1,0:T(8,128)S(1)}, u32[]{:S(2)}, u32[]{:S(2)}) collective-permute-start(f32[14,16,128]{2,1,0:T(8,128)} %get-tuple-element.13), channel_id=1, source_target_pairs={{8,0},{16,8},{24,16},{9,1},{17,9},{25,17},{10,2},{18,10},{26,18},{... | collective-permute-start | bytes 344072 | tf_op jit(solution)/shard_map/ppermute | solution.py:401
  8.7 1.4 %collective-permute-done.zlo_ref = f32[14,16,128]{2,1,0:T(8,128)S(1)} collective-permute-done((f32[14,16,128]{2,1,0:T(8,128)}, f32[14,16,128]{2,1,0:T(8,128)S(1)}, u32[]{:S(2)}, u32[]{:S(2)}) %collective-permute-start) | collective-permute-done | bytes 114720 | tf_op jit(solution)/shard_map/ppermute | solution.py:401
  10.1 4.2 %collective-permute-done.1.zhi_ref = f32[14,16,128]{2,1,0:T(8,128)S(1)} collective-permute-done((f32[14,16,128]{2,1,0:T(8,128)}, f32[14,16,128]{2,1,0:T(8,128)S(1)}, u32[]{:S(2)}, u32[]{:S(2)}) %collective-permute-start.1) | collective-permute-done | bytes 114720 | tf_op jit(solution)/shard_map/ppermute | solution.py:401
  14.3 0.0 copy-done.1
  14.3 0.0 copy-done
  14.3 0.2 pack_rows.1
  14.5 0.0 copy-start.8
  14.5 0.0 copy-start.7
  14.5 0.0 copy-start.2
  14.5 0.0 copy-start.3
  14.5 0.0 copy-start.4
  14.5 0.0 copy-start.5
  14.5 0.0 copy-start.6
  14.6 1.6 %collective-permute-start.2 = (f32[472,128]{1,0:T(8,128)S(1)}, f32[472,128]{1,0:T(8,128)S(1)}, u32[]{:S(2)}, u32[]{:S(2)}) collective-permute-start(f32[472,128]{1,0:T(8,128)S(1)} %broadcast_select_fusion), channel_id=1, source_target_pairs={{0,4},{4,0},{1,5},{5,1},{2,6},{6,2},{3,7},{7,3},{8,12},{12,8},{9,1... | collective-permute-start | bytes 725000 | tf_op jit(solution)/shard_map/ppermute | solution.py:455
  16.1 0.1 stack.35
  16.2 1.1 %pack_own.1 = (f32[6,16,128]{2,1,0:T(8,128)S(1)}, f32[6,16,128]{2,1,0:T(8,128)S(1)}) custom-call(f32[5,32,16,128]{3,2,1,0:T(8,128)S(1)} %copy-done, f32[32,16,128]{2,1,0:T(8,128)S(1)} %copy-done.1, f32[14,16,128]{2,1,0:T(8,128)S(1)} %collective-permute-done.zlo_ref, f32[14,16,128]{2,1,0:T(8,128)S(1)} %collective-permute-done.1.zhi_ref), custom_call_target="tpu_custom_call" | custom-call | flops 10000000 | bytes 4000000 | tf_op jit(solution)/shard_map/pack_own/pallas_call | solution.py:444
  17.3 3.5 %collective-permute-done.2.ylo_ref.yhi_ref = f32[472,128]{1,0:T(8,128)S(1)} collective-permute-done((f32[472,128]{1,0:T(8,128)S(1)}, f32[472,128]{1,0:T(8,128)S(1)}, u32[]{:S(2)}, u32[]{:S(2)}) %collective-permute-start.2) | collective-permute-done | bytes 241696 | tf_op jit(solution)/shard_map/ppermute | solution.py:455
  20.8 1.1 %pack_columns.1 = (f32[6,24,128]{2,1,0:T(8,128)S(1)}, f32[6,24,128]{2,1,0:T(8,128)S(1)}) custom-call(f32[6]{0:T(128)S(1)} %stack.36.flags_ref, f32[472,128]{1,0:T(8,128)S(1)} %collective-permute-done.2.ylo_ref.yhi_ref, f32[472,128]{1,0:T(8,128)S(1)} %collective-permute-done.2.ylo_ref.yhi_ref, f32[6,16,128]{2,1,0:T(8,128)S(1)} %get-tuple-element.16.mainlo_ref, ...), custom_call_target="tpu_custom_call" | custom-call | tf_op jit(solution)/shard_map/pack_columns/pallas_call | solution.py:460
  21.9 1.3 %collective-permute-start.3 = (f32[6,24,128]{2,1,0:T(8,128)S(1)}, f32[6,24,128]{2,1,0:T(8,128)S(1)}, u32[]{:S(2)}, u32[]{:S(2)}) collective-permute-start(f32[6,24,128]{2,1,0:T(8,128)S(1)} %get-tuple-element.18.ownhi_ref), channel_id=1, source_target_pairs={{0,1},{1,2},{2,3},{4,5},{5,6},{6,7},{8,9},{9,10},{10,11},{12,13},{... | collective-permute-start | bytes 221192 | tf_op jit(solution)/shard_map/ppermute | solution.py:401
  23.2 1.3 %collective-permute-start.4 = (f32[6,24,128]{2,1,0:T(8,128)S(1)}, f32[6,24,128]{2,1,0:T(8,128)S(1)}, u32[]{:S(2)}, u32[]{:S(2)}) collective-permute-start(f32[6,24,128]{2,1,0:T(8,128)S(1)} %get-tuple-element.19.ownlo_ref), channel_id=1, source_target_pairs={{1,0},{2,1},{3,2},{5,4},{6,5},{7,6},{9,8},{10,9},{11,10},{13,12},{... | collective-permute-start | bytes 221192 | tf_op jit(solution)/shard_map/ppermute | solution.py:401
  24.5 0.0 copy-done.8
  24.5 0.1 copy.11.courant_ref
  24.6 0.5 broadcast.3
  25.1 0.0 copy-done.7
  25.2 0.7 %reduce.3 = s32[16,16]{1,0:T(8,128)S(1)} reduce(s32[1,16,16,1]{2,3,1,0:T(1,128)S(1)} %copy-done.7, s32[]{:T(128)} %broadcast.3), dimensions={0,3}, to_apply=%param.16.reduce_sub_computation.3 | reduce | bytes 2052 | tf_op args[7]
  25.8 0.1 reshape_squeeze.3.mask_ref
  25.9 0.0 collective-permute-done.3.xlo_ref
  25.9 2.2 %collective-permute-done.4.xhi_ref = f32[6,24,128]{2,1,0:T(8,128)S(1)} collective-permute-done((f32[6,24,128]{2,1,0:T(8,128)S(1)}, f32[6,24,128]{2,1,0:T(8,128)S(1)}, u32[]{:S(2)}, u32[]{:S(2)}) %collective-permute-start.4) | collective-permute-done | bytes 73760 | tf_op jit(solution)/shard_map/ppermute | solution.py:401
  28.1 0.0 copy-done.2
  28.1 0.0 copy-done.3
  28.2 0.0 copy-done.4
  28.2 0.0 copy-done.5
  28.2 0.0 copy-done.6
  28.2 10.6 %step_and_march.1 = (f32[5,32,16,128]{3,2,1,0:T(8,128)}, f32[256,4,128]{2,1,0:T(4,128)S(1)}) custom-call(f32[6]{0:T(128)S(1)} %stack.36.flags_ref, f32[5,3]{1,0:T(8,128)S(1)} %copy.11.courant_ref, f32[16]{0:T(128)S(1)} %copy-done.4, f32[16]{0:T(128)S(1)} %copy-done.5, f32[16]{0:T(128)S(1)} %copy-done.6, f32[3,16]{1,0:T(4,128)S(1)} %copy-done.2, ...), custom_call_target="tpu_custom_call" | custom-call | tf_op jit(solution)/shard_map/step_and_march/pallas_call | solution.py:474
  38.7 18.2 %all_to_all.5.part_ref = f32[4,256,128]{2,1,0:T(8,128)S(1)} all-to-all(f32[4,256,128]{2,1,0:T(8,128)S(1)} %bitcast.10), channel_id=1, replica_groups=mesh['gz'=4,'gy'=2,'gx'=4] {'gz'}, dimensions={0} | all-to-all | bytes 1048576 | tf_op jit(solution)/shard_map/all_to_all | solution.py:498
  57.0 0.7 %compose.1 = f32[256,128]{1,0:T(8,128)} custom-call(f32[4,256,128]{2,1,0:T(8,128)S(1)} %all_to_all.5.part_ref), custom_call_target="tpu_custom_call" | custom-call | tf_op jit(solution)/shard_map/compose/pallas_call | solution.py:388
  (2 shorter events, 0.0 us)
Async XLA Ops:
  0.6 13.6 %copy-start.1 = (f32[32,16,128]{2,1,0:T(8,128)S(1)}, f32[32,16,128]{2,1,0:T(8,128)}, u32[]{:S(2)}) copy-start(f32[32,16,128]{2,1,0:T(8,128)} %kappa_ref.7) | copy-start | bytes 786436
  0.6 13.6 %copy-start = (f32[5,32,16,128]{3,2,1,0:T(8,128)S(1)}, f32[5,32,16,128]{3,2,1,0:T(8,128)}, u32[]{:S(2)}) copy-start(f32[5,32,16,128]{3,2,1,0:T(8,128)} %fields_ref.7) | copy-start | bytes 3932164
  2.4 7.6 %collective-permute-start = (f32[14,16,128]{2,1,0:T(8,128)}, f32[14,16,128]{2,1,0:T(8,128)S(1)}, u32[]{:S(2)}, u32[]{:S(2)}) collective-permute-start(f32[14,16,128]{2,1,0:T(8,128)} %get-tuple-element.12), channel_id=1, source_target_pairs={{0,8},{8,16},{16,24},{1,9},{9,17},{17,25},{2,10},{10,18},{18,26},{... | collective-permute-start | bytes 344072 | tf_op jit(solution)/shard_map/ppermute | solution.py:401
  7.4 6.9 %collective-permute-start.1 = (f32[14,16,128]{2,1,0:T(8,128)}, f32[14,16,128]{2,1,0:T(8,128)S(1)}, u32[]{:S(2)}, u32[]{:S(2)}) collective-permute-start(f32[14,16,128]{2,1,0:T(8,128)} %get-tuple-element.13), channel_id=1, source_target_pairs={{8,0},{16,8},{24,16},{9,1},{17,9},{25,17},{10,2},{18,10},{26,18},{... | collective-permute-start | bytes 344072 | tf_op jit(solution)/shard_map/ppermute | solution.py:401
  14.5 10.1 %copy-start.8 = (f32[5,3]{0,1:T(4,128)S(1)}, f32[5,3]{0,1:T(4,128)}, u32[]{:S(2)}) copy-start(f32[5,3]{0,1:T(4,128)} %param.11) | copy-start | bytes 184
  14.5 10.7 %copy-start.7 = (s32[1,16,16,1]{2,3,1,0:T(1,128)S(1)}, s32[1,16,16,1]{2,3,1,0:T(1,128)}, u32[]{:S(2)}) copy-start(s32[1,16,16,1]{2,3,1,0:T(1,128)} %param.16) | copy-start | bytes 3076
  14.5 13.7 %copy-start.2 = (f32[3,16]{1,0:T(4,128)S(1)}, f32[3,16]{1,0:T(4,128)}, u32[]{:S(2)}) copy-start(f32[3,16]{1,0:T(4,128)} %color_ref.1) | copy-start | bytes 580
  14.5 13.6 %copy-start.3 = (s32[1,1,256]{2,1,0:T(1,128)S(1)}, s32[1,1,256]{2,1,0:T(1,128)}, u32[]{:S(2)}) copy-start(s32[1,1,256]{2,1,0:T(1,128)} %param.17) | copy-start | bytes 3076
  14.5 13.6 %copy-start.4 = (f32[16]{0:T(128)S(1)}, f32[16]{0:T(128)}, u32[]{:S(2)}) copy-start(f32[16]{0:T(128)} %center_ref.1) | copy-start | bytes 196
  14.5 13.6 %copy-start.5 = (f32[16]{0:T(128)S(1)}, f32[16]{0:T(128)}, u32[]{:S(2)}) copy-start(f32[16]{0:T(128)} %sharp_ref.1) | copy-start | bytes 196
  14.5 13.6 %copy-start.6 = (f32[16]{0:T(128)S(1)}, f32[16]{0:T(128)}, u32[]{:S(2)}) copy-start(f32[16]{0:T(128)} %gain_ref.1) | copy-start | bytes 196
  14.6 6.2 %collective-permute-start.2 = (f32[472,128]{1,0:T(8,128)S(1)}, f32[472,128]{1,0:T(8,128)S(1)}, u32[]{:S(2)}, u32[]{:S(2)}) collective-permute-start(f32[472,128]{1,0:T(8,128)S(1)} %broadcast_select_fusion), channel_id=1, source_target_pairs={{0,4},{4,0},{1,5},{5,1},{2,6},{6,2},{3,7},{7,3},{8,12},{12,8},{9,1... | collective-permute-start | bytes 725000 | tf_op jit(solution)/shard_map/ppermute | solution.py:455
  21.9 4.0 %collective-permute-start.3 = (f32[6,24,128]{2,1,0:T(8,128)S(1)}, f32[6,24,128]{2,1,0:T(8,128)S(1)}, u32[]{:S(2)}, u32[]{:S(2)}) collective-permute-start(f32[6,24,128]{2,1,0:T(8,128)S(1)} %get-tuple-element.18.ownhi_ref), channel_id=1, source_target_pairs={{0,1},{1,2},{2,3},{4,5},{5,6},{6,7},{8,9},{9,10},{10,11},{12,13},{... | collective-permute-start | bytes 221192 | tf_op jit(solution)/shard_map/ppermute | solution.py:401
  23.2 4.9 %collective-permute-start.4 = (f32[6,24,128]{2,1,0:T(8,128)S(1)}, f32[6,24,128]{2,1,0:T(8,128)S(1)}, u32[]{:S(2)}, u32[]{:S(2)}) collective-permute-start(f32[6,24,128]{2,1,0:T(8,128)S(1)} %get-tuple-element.19.ownlo_ref), channel_id=1, source_target_pairs={{1,0},{2,1},{3,2},{5,4},{6,5},{7,6},{9,8},{10,9},{11,10},{13,12},{... | collective-permute-start | bytes 221192 | tf_op jit(solution)/shard_map/ppermute | solution.py:401

commit v6 on v5

--- a/solution.py
+++ b/solution.py
@@ -27,26 +27,28 @@
     return plan, at
 
 
-def y_plan(nfield, depth_len):
-    plan, at = [], 0
+def y_plan(nfield):
+    kinds, edges = [], []
     for field in range(nfield + 1):
         wide = reach(field, nfield)
         for away in range(1, wide + 1):
-            extra = wide - away
-            plan.append((field, away, -extra, depth_len + 2 * extra, at))
-            at += depth_len + 2 * extra
-    return plan, at + (-at) % SUB
-
-
-def pack_planes_kernel(fields_ref, kappa_ref, lo_ref, hi_ref, sems):
+            kinds.append((field, away))
+            for k in range(1, wide - away + 1):
+                edges.append((field, away, -k))
+                edges.append((field, away, k))
+    return kinds, edges
+
+
+def pack_planes_kernel(fields_ref, kappa_ref, first_ref, second_ref, sems):
     nfield, depth_len = fields_ref.shape[:2]
+    odd = lax.rem(lax.axis_index("gz"), 2)
     copies = []
     for field, at, wide in z_plan(nfield)[0]:
         source = kappa_ref if field == nfield else fields_ref.at[field]
-        for first, target in ((0, lo_ref), (depth_len - wide, hi_ref)):
+        for place, target in ((1 - odd, first_ref), (odd, second_ref)):
             copies.append(
                 pltpu.make_async_copy(
-                    source.at[pl.ds(first, wide)], target.at[pl.ds(at, wide)], sems.at[len(copies)]
+                    source.at[pl.ds(place * (depth_len - wide), wide)], target.at[pl.ds(at, wide)], sems.at[len(copies)]
                 )
             )
     for copy in copies:
@@ -70,28 +72,28 @@
     return kappa_ref.at[z] if field == nfield else fields_ref.at[field, z]
 
 
-def pack_rows_kernel(fields_ref, kappa_ref, zlo_ref, zhi_ref, lo_ref, hi_ref):
-    refs = (fields_ref, kappa_ref, zlo_ref, zhi_ref)
+def pack_rows_kernel(fields_ref, kappa_ref, lo_ref, hi_ref):
     nfield, depth_len, rows, lanes = fields_ref.shape
     flat_fields = fields_ref.reshape(nfield * depth_len * rows, lanes)
     flat_kappa = kappa_ref.reshape(depth_len * rows, lanes)
-    plan, used = y_plan(nfield, depth_len)
     for out_ref, top in ((lo_ref, True), (hi_ref, False)):
-        for field, away, first, length, at in plan:
+        for i, (field, away) in enumerate(y_plan(nfield)[0]):
             row = away - 1 if top else rows - away
-            for z in list(range(first, 0)) + list(range(depth_len, first + length)):
-                out_ref[at + z - first, :] = source_plane(refs, field, z)[row, :]
             flat, base = (flat_kappa, 0) if field == nfield else (flat_fields, field * depth_len * rows)
             for z in range(0, depth_len, SUB):
-                out_ref[pl.ds(at - first + z, SUB), :] = flat[
-                    pl.ds(base + z * rows + row, SUB, stride=rows), :
-                ]
-        spare = plan[-1][3] + plan[-1][4]
-        if used > spare:
-            out_ref[spare:used, :] = jnp.zeros((used - spare, lanes), F32)
-
-
-def assemble(refs, ylo_ref, yhi_ref, flags_ref, pad_ref):
+                out_ref[i, z : z + SUB, :] = flat[pl.ds(base + z * rows + row, SUB, stride=rows), :]
+
+
+def pack_edges_kernel(fields_ref, kappa_ref, zlo_ref, zhi_ref, lo_ref, hi_ref):
+    refs = (fields_ref, kappa_ref, zlo_ref, zhi_ref)
+    nfield, depth_len, rows, _ = fields_ref.shape
+    for i, (field, away, k) in enumerate(y_plan(nfield)[1]):
+        plane = source_plane(refs, field, k if k < 0 else depth_len - 1 + k)
+        lo_ref[i : i + 1, :] = plane[away - 1 : away, :]
+        hi_ref[i : i + 1, :] = plane[rows - away : rows - away + 1, :]
+
+
+def assemble(refs, halo_rows, flags_ref, pad_ref):
     fields_ref, kappa_ref, zlo_ref, zhi_ref = refs
     nfield, depth_len, rows, lanes = fields_ref.shape
     planes, pitch = depth_len + 2 * W, rows + SUB
@@ -114,20 +116,26 @@
                 if k >= wide:
                     pad_ref[plane, :rows, :] = jnp.zeros((rows, lanes), F32)
                 pad_ref[plane, rows:, :] = halo
-    place_rows(pad_ref, depth_len, rows, ylo_ref, yhi_ref, flags_ref)
-
-
-def place_rows(pad_ref, depth_len, first_row, ylo_ref, yhi_ref, flags_ref):
+    place_rows(pad_ref, depth_len, rows, halo_rows, flags_ref)
+
+
+def place_rows(pad_ref, depth_len, first_row, halo_rows, flags_ref):
     planes = depth_len + 2 * W
     pitch, lanes = pad_ref.shape[1:]
     flat = pad_ref.reshape(pad_ref.shape[0] * pitch, lanes)
-    low, high = flags_ref[2], flags_ref[3]
-    for field, away, first, length, at in y_plan(pad_ref.shape[0] // planes - 1, depth_len)[0]:
-        for ref, flag, row in ((ylo_ref, low, pitch - away), (yhi_ref, high, first_row + away - 1)):
-            for start in tiles_of(0, length):
-                flat[pl.ds((field * planes + W + first + start) * pitch + row, SUB, stride=pitch), :] = (
-                    ref[pl.ds(at + start, SUB), :] * flag
+    kinds, edges = y_plan(pad_ref.shape[0] // planes - 1)
+    for low, (ref, edge_ref) in ((True, halo_rows[:2]), (False, halo_rows[2:])):
+        flag = flags_ref[2] if low else flags_ref[3]
+        for i, (field, away) in enumerate(kinds):
+            row = pitch - away if low else first_row + away - 1
+            for z in range(0, depth_len, SUB):
+                flat[pl.ds((field * planes + W + z) * pitch + row, SUB, stride=pitch), :] = (
+                    ref[i, z : z + SUB, :] * flag
                 )
+        for i, (field, away, k) in enumerate(edges):
+            row = pitch - away if low else first_row + away - 1
+            plane = field * planes + W + (k if k < 0 else depth_len - 1 + k)
+            pad_ref[plane, row : row + 1, :] = edge_ref[i : i + 1, :] * flag
 
 
 def take_columns(value, zi, lane, low, high):
@@ -152,7 +160,7 @@
 
 
 def pack_columns_kernel(
-    flags_ref, ylo_ref, yhi_ref, mainlo_ref, mainhi_ref, lo_ref, hi_ref, halo_ref
+    flags_ref, ylo_ref, elo_ref, yhi_ref, ehi_ref, mainlo_ref, mainhi_ref, lo_ref, hi_ref, halo_ref
 ):
     nplane, _, lanes = halo_ref.shape
     nfield, rows = mainlo_ref.shape[0] - 1, mainlo_ref.shape[1]
@@ -161,7 +169,7 @@
     zero = jnp.zeros((SUB, lanes), F32)
     for plane in range(nplane):
         halo_ref[plane] = zero
-    place_rows(halo_ref, planes - 2 * W, 0, ylo_ref, yhi_ref, flags_ref)
+    place_rows(halo_ref, planes - 2 * W, 0, (ylo_ref, elo_ref, yhi_ref, ehi_ref), flags_ref)
     for field in range(nfield + 1):
         low = high = zero
         for zi in range(planes):
@@ -201,7 +209,8 @@
 
 def main_kernel(
     flags_ref, courant_ref, center_ref, sharp_ref, gain_ref, color_ref, mask_ref, order_ref,
-    fields_ref, kappa_ref, zlo_ref, zhi_ref, ylo_ref, yhi_ref, xlo_ref, xhi_ref, ownlo_ref, ownhi_ref,
+    fields_ref, kappa_ref, zlo_ref, zhi_ref,
+    ylo_ref, elo_ref, yhi_ref, ehi_ref, xlo_ref, xhi_ref, ownlo_ref, ownhi_ref,
     state_ref, out_ref,
     pad_ref, next_ref, last_ref, side_ref, edge_ref, base_ref, tile_ref, coef_ref, held_ref, sem,
 ):
@@ -284,7 +293,8 @@
     def depth_mask(zi):
         return jnp.where(zi < W, flag[0], jnp.where(zi >= W + depth_len, flag[1], 1.0))
 
-    assemble((fields_ref, kappa_ref, zlo_ref, zhi_ref), ylo_ref, yhi_ref, flags_ref, pad_ref)
+    halo_rows = (ylo_ref, elo_ref, yhi_ref, ehi_ref)
+    assemble((fields_ref, kappa_ref, zlo_ref, zhi_ref), halo_rows, flags_ref, pad_ref)
     for field in range(nfield + 1):
         edges(0, field)
     side_step(0, nfield)
@@ -359,7 +369,7 @@
                 tile_ref[pl.ds(start + k, SUB, stride=4), :] = acc[j][k] * color_ref[k, first + j]
             tile_ref[pl.ds(start + 3, SUB, stride=4), :] = 1.0 - passed[j]
 
-    @pl.loop(0, order_ref.shape[0], unroll=8)
+    @pl.loop(0, order_ref.shape[0], unroll=steps(order_ref.shape[0], 64))
     def _(slot):
         tile = order_ref[slot]
         cover = mask_ref[tile].astype(jnp.float32)
@@ -395,10 +405,29 @@
     )(parts)
 
 
-def shift(message, axis, up):
+def is_odd(axis):
+    return lax.rem(lax.axis_index(axis), 2) == 1
+
+
+def swap_pairs(first, second, axis):
     count = lax.axis_size(axis)
-    pairs = [(i, i + 1) if up else (i + 1, i) for i in range(count - 1)]
-    return lax.ppermute(message, axis, pairs)
+    came = []
+    for start, message in ((0, first), (1, second)):
+        pairs = []
+        for i in range(start, count - 1, 2):
+            pairs += [(i, i + 1), (i + 1, i)]
+        came.append(lax.ppermute(message, axis, pairs) if pairs else jnp.zeros_like(message))
+    odd = is_odd(axis)
+    return jnp.where(odd, came[0], came[1]), jnp.where(odd, came[1], came[0])
+
+
+def swap_rows(low, high, axis):
+    odd = is_odd(axis)
+    first = jnp.where(odd, low, high)
+    if lax.axis_size(axis) == 2:
+        came = lax.ppermute(first, axis, [(0, 1), (1, 0)])
+        return came, came
+    return swap_pairs(first, jnp.where(odd, high, low), axis)
 
 
 def present(axis):
@@ -421,7 +450,7 @@
     flags = jnp.stack(present("gz") + present("gy") + present("gx"))
 
     faces = z_plan(nfield)[1]
-    face_lo, face_hi = pl.pallas_call(
+    first, second = pl.pallas_call(
         pack_planes_kernel,
         out_shape=(array(faces, rows_len, cols_len),) * 2,
         in_specs=[pl.BlockSpec(memory_space=pl.ANY)] * 2,
@@ -430,17 +459,26 @@
         compiler_params=pltpu.CompilerParams(vmem_limit_bytes=60 * 1024 * 1024),
         name="pack_planes",
     )(fields, diffusivity)
-    zlo = shift(face_hi, "gz", True)
-    zhi = shift(face_lo, "gz", False)
-    used = y_plan(nfield, depth_len)[1]
+    zlo, zhi = swap_pairs(first, second, "gz")
+    kinds, outer = y_plan(nfield)
     send_lo, send_hi = pl.pallas_call(
         pack_rows_kernel,
-        out_shape=(array(used, cols_len), array(used, cols_len)),
+        out_shape=(array(len(kinds), depth_len, cols_len),) * 2,
+        in_specs=[vmem] * 2,
+        out_specs=(vmem, vmem),
+        compiler_params=params,
+        name="pack_rows",
+    )(fields, diffusivity)
+    ylo, yhi = swap_rows(send_lo, send_hi, "gy")
+    send_lo, send_hi = pl.pallas_call(
+        pack_edges_kernel,
+        out_shape=(array(len(outer), cols_len),) * 2,
         in_specs=[vmem] * 4,
         out_specs=(vmem, vmem),
         compiler_params=params,
-        name="pack_rows",
+        name="pack_edges",
     )(fields, diffusivity, zlo, zhi)
+    elo, ehi = swap_rows(send_lo, send_hi, "gy")
     main_lo, main_hi = pl.pallas_call(
         pack_own_kernel,
         out_shape=(array(nfield + 1, rows_len, cols_len),) * 2,
@@ -450,31 +488,25 @@
         cost_estimate=pl.CostEstimate(flops=10**7, bytes_accessed=4 * 10**6, transcendentals=0),
         name="pack_own",
     )(fields, diffusivity, zlo, zhi)
-    if lax.axis_size("gy") == 2:
-        mine = jnp.where(lax.axis_index("gy") == 0, send_hi, send_lo)
-        ylo = yhi = lax.ppermute(mine, "gy", [(0, 1), (1, 0)])
-    else:
-        ylo = shift(send_hi, "gy", True)
-        yhi = shift(send_lo, "gy", False)
     pad = pltpu.VMEM(((nfield + 1) * planes, pitch, cols_len), F32)
     own_lo, own_hi = pl.pallas_call(
         pack_columns_kernel,
         out_shape=(array(nfield + 1, pitch, cols_len),) * 2,
-        in_specs=[smem] + [vmem] * 4,
+        in_specs=[smem] + [vmem] * 6,
         out_specs=(vmem,) * 2,
         scratch_shapes=[pltpu.VMEM(((nfield + 1) * planes, SUB, cols_len), F32)],
         compiler_params=params,
         name="pack_columns",
-    )(flags, ylo, yhi, main_lo, main_hi)
-    xlo = shift(own_hi, "gx", True)
-    xhi = shift(own_lo, "gx", False)
+    )(flags, ylo, elo, yhi, ehi, main_lo, main_hi)
+    odd = is_odd("gx")
+    xlo, xhi = swap_pairs(jnp.where(odd, own_lo, own_hi), jnp.where(odd, own_hi, own_lo), "gx")
     count = lax.axis_size("gz")
     order = tile_perm[0, 0]
     per_owner = order.shape[0] // count
     state, tiles = pl.pallas_call(
         main_kernel,
         out_shape=(array(*fields.shape), array(order.shape[0], 4, cols_len)),
-        in_specs=[smem] * 8 + [vmem] * 10,
+        in_specs=[smem] * 8 + [vmem] * 12,
         out_specs=(pl.BlockSpec(memory_space=pl.ANY), vmem),
         scratch_shapes=[
             pad,
@@ -492,7 +524,7 @@
         name="step_and_march",
     )(
         flags, courant, tf_center, tf_sharp, tf_gain, tf_color, tile_mask[0].reshape(-1), order,
-        fields, diffusivity, zlo, zhi, ylo, yhi, xlo, xhi, own_lo, own_hi,
+        fields, diffusivity, zlo, zhi, ylo, elo, yhi, ehi, xlo, xhi, own_lo, own_hi,
     )
     grouped = tiles.reshape(count, per_owner * 4, cols_len)
     composed = compose(lax.all_to_all(grouped, "gz", split_axis=0, concat_axis=0, tiled=True))

time: 58.6 us -> 52.6 us (0.90); the launches traced: 57.7 us -> 52.4 us
  waiting for transfers between devices: 11.3 us -> 2.82 us
  blocking collectives: 18.2 us -> 21.3 us
    ppermute x5 -> x6, waiting for transfers between devices: 11.3 us -> 2.82 us  [the longest x2 1.89 us: swap_rows(): came = lax.ppermute(first, axis, [(0, 1), (1, 0)])]
    all_to_all x1, blocking collectives: 18.2 us -> 21.3 us  [shards(): lax.all_to_all(grouped, 'gz', split_axis=0, concat_axis=0, tiled=True)]
    ppermute x5 -> x6, starting transfers between devices: 10.4 us -> 10.6 us  [the longest x4 7.35 us: swap_pairs(): lax.ppermute(message, axis, pairs)]
  transfers between devices with their start and end apart: 5 -> 6, of which waited for: 4 -> 2; matrix products, arithmetic and copies ran while one was open for 3% -> 3% of each run, Pallas kernels for 2% -> 2%
where the time goes in v6:
time: 52.6 us; the launch traced here: 52.4 us
  blocking collectives  21.3 us (40%)
  Pallas kernels  15.2 us (29%)
  starting transfers between devices  10.6 us (20%)
  waiting for transfers between devices  2.82 us (5%)
  between operations  0.86 us (2%)
  local copies, waits for them, and re-layouts  0.83 us (2%)
  other arithmetic  0.77 us (1%)
    all_to_all x1, blocking collectives, shards(): lax.all_to_all(grouped, 'gz', split_axis=0, concat_axis=0, tiled=True)  21.3 us
    pallas_call x1, Pallas kernels, shards(): pl.pallas_call(main_kernel, out_shape=(array(*fields.shape), array(order....  10.4 us
    ppermute x4, starting transfers between devices, swap_pairs(): lax.ppermute(message, axis, pairs)  7.35 us
    ppermute x2, starting transfers between devices, swap_rows(): came = lax.ppermute(first, axis, [(0, 1), (1, 0)])  3.28 us
    ppermute x2, waiting for transfers between devices, swap_rows(): came = lax.ppermute(first, axis, [(0, 1), (1, 0)])  1.89 us
    pallas_call x1, Pallas kernels, shards(): pl.pallas_call(pack_planes_kernel, out_shape=(array(faces, rows_len, cols...  1.78 us
    pallas_call x1, Pallas kernels, shards(): pl.pallas_call(pack_columns_kernel, out_shape=(array(nfield + 1, pitch, c...  1.13 us
    pallas_call x1, Pallas kernels, shards(): pl.pallas_call(pack_own_kernel, out_shape=(array(nfield + 1, rows_len, co...  1.06 us
  transfers between devices with their start and end apart: 6, of which 2 were waited for; matrix products, arithmetic and copies ran while one was open for 3% of the time, Pallas kernels for 2%

profile of v6, /device:TPU:0, one launch (start us, length us, event | category | flops | bytes accessed | tf_op | source)
XLA Modules:
  0.0 52.4 jit_solution(2827467332655253004)
XLA Ops:
  0.6 0.0 copy-start.1
  0.6 0.0 copy-start
  0.6 1.8 %pack_planes.1 = (f32[14,16,128]{2,1,0:T(8,128)}, f32[14,16,128]{2,1,0:T(8,128)}) custom-call(f32[5,32,16,128]{3,2,1,0:T(8,128)} %fields_ref.9, f32[32,16,128]{2,1,0:T(8,128)} %kappa_ref.9), custom_call_target="tpu_custom_call" | custom-call | tf_op jit(solution)/shard_map/pack_planes/pallas_call | solution.py:453
  2.4 3.1 %collective-permute-start = (f32[14,16,128]{2,1,0:T(8,128)}, f32[14,16,128]{2,1,0:T(8,128)S(1)}, u32[]{:S(2)}, u32[]{:S(2)}) collective-permute-start(f32[14,16,128]{2,1,0:T(8,128)} %get-tuple-element.14), channel_id=1, source_target_pairs={{0,8},{8,0},{16,24},{24,16},{1,9},{9,1},{17,25},{25,17},{2,10},{10... | collective-permute-start | bytes 344072 | tf_op jit(solution)/shard_map/ppermute | solution.py:419
  5.5 0.7 %collective-permute-start.1 = (f32[14,16,128]{2,1,0:T(8,128)}, f32[14,16,128]{2,1,0:T(8,128)S(1)}, u32[]{:S(2)}, u32[]{:S(2)}) collective-permute-start(f32[14,16,128]{2,1,0:T(8,128)} %get-tuple-element.15), channel_id=1, source_target_pairs={{8,16},{16,8},{9,17},{17,9},{10,18},{18,10},{11,19},{19,11},{12,20... | collective-permute-start | bytes 344072 | tf_op jit(solution)/shard_map/ppermute | solution.py:419
  6.2 0.0 copy-done.1
  6.2 0.0 copy-done
  6.2 0.1 pack_rows.1
  6.4 1.6 %collective-permute-start.2 = (f32[14,32,128]{2,1,0:T(8,128)S(1)}, f32[14,32,128]{2,1,0:T(8,128)S(1)}, u32[]{:S(2)}, u32[]{:S(2)}) collective-permute-start(f32[14,32,128]{2,1,0:T(8,128)S(1)} %broadcast_select_fusion), channel_id=1, source_target_pairs={{0,4},{4,0},{1,5},{5,1},{2,6},{6,2},{3,7},{7,3},{8,12},{12,8},{9,1... | collective-permute-start | bytes 688136 | tf_op jit(solution)/shard_map/ppermute | solution.py:428
  8.0 0.9 %collective-permute-done = f32[14,16,128]{2,1,0:T(8,128)S(1)} collective-permute-done((f32[14,16,128]{2,1,0:T(8,128)}, f32[14,16,128]{2,1,0:T(8,128)S(1)}, u32[]{:S(2)}, u32[]{:S(2)}) %collective-permute-start) | collective-permute-done | bytes 114720 | tf_op jit(solution)/shard_map/ppermute | solution.py:419
  8.9 0.0 collective-permute-done.1
  8.9 1.7 %collective-permute-start.3 = (f32[20,128]{1,0:T(8,128)S(1)}, f32[20,128]{1,0:T(8,128)S(1)}, u32[]{:S(2)}, u32[]{:S(2)}) collective-permute-start(f32[20,128]{1,0:T(8,128)S(1)} %broadcast_select_fusion.7), channel_id=1, source_target_pairs={{0,4},{4,0},{1,5},{5,1},{2,6},{6,2},{3,7},{7,3},{8,12},{12,8},{9,1... | collective-permute-start | bytes 30728 | tf_op jit(solution)/shard_map/ppermute | solution.py:428
  10.7 0.1 stack.35
  10.8 0.0 copy-start.8
  10.8 0.0 copy-start.7
  10.8 0.0 copy-start.2
  10.8 0.0 copy-start.3
  10.8 0.0 copy-start.4
  10.8 0.0 copy-start.5
  10.8 0.0 copy-start.6
  10.8 1.1 %pack_own.1 = (f32[6,16,128]{2,1,0:T(8,128)S(1)}, f32[6,16,128]{2,1,0:T(8,128)S(1)}) custom-call(f32[5,32,16,128]{3,2,1,0:T(8,128)S(1)} %copy-done, f32[32,16,128]{2,1,0:T(8,128)S(1)} %copy-done.1, f32[14,16,128]{2,1,0:T(8,128)S(1)} %get-tuple-element.27.zlo_ref, f32[14,16,128]{2,1,0:T(8,128)S(1)} %get-tuple-element.26.zhi_ref), custom_call_target="tpu_custom_call" | custom-call | flops 10000000 | bytes 4000000 | tf_op jit(solution)/shard_map/pack_own/pallas_call | solution.py:482
  11.9 1.9 %collective-permute-done.3.elo_ref.ehi_ref = f32[20,128]{1,0:T(8,128)S(1)} collective-permute-done((f32[20,128]{1,0:T(8,128)S(1)}, f32[20,128]{1,0:T(8,128)S(1)}, u32[]{:S(2)}, u32[]{:S(2)}) %collective-permute-start.3) | collective-permute-done | bytes 10272 | tf_op jit(solution)/shard_map/ppermute | solution.py:428
  13.8 0.0 collective-permute-done.2.ylo_ref.yhi_ref
  13.8 1.1 %pack_columns.1 = (f32[6,24,128]{2,1,0:T(8,128)S(1)}, f32[6,24,128]{2,1,0:T(8,128)S(1)}) custom-call(f32[6]{0:T(128)S(1)} %stack.36.flags_ref, f32[14,32,128]{2,1,0:T(8,128)S(1)} %collective-permute-done.2.ylo_ref.yhi_ref, f32[20,128]{1,0:T(8,128)S(1)} %collective-permute-done.3.elo_ref.ehi_ref, f32[14,32,128]{2,1,0:T(8,128)S(1)} %collective-permute-done.2.ylo_ref.yhi_ref, ...), custom_call_target="tpu_custom_call" | custom-call | tf_op jit(solution)/shard_map/pack_columns/pallas_call | solution.py:492
  15.0 0.7 %collective-permute-start.5 = (f32[6,24,128]{2,1,0:T(8,128)S(1)}, f32[6,24,128]{2,1,0:T(8,128)S(1)}, u32[]{:S(2)}, u32[]{:S(2)}) collective-permute-start(f32[6,24,128]{2,1,0:T(8,128)S(1)} %get-tuple-element.30), channel_id=1, source_target_pairs={{1,2},{2,1},{5,6},{6,5},{9,10},{10,9},{13,14},{14,13},{17,18},{18,... | collective-permute-start | bytes 221192 | tf_op jit(solution)/shard_map/ppermute | solution.py:419
  15.6 2.9 %collective-permute-start.4 = (f32[6,24,128]{2,1,0:T(8,128)S(1)}, f32[6,24,128]{2,1,0:T(8,128)S(1)}, u32[]{:S(2)}, u32[]{:S(2)}) collective-permute-start(f32[6,24,128]{2,1,0:T(8,128)S(1)} %get-tuple-element.31), channel_id=1, source_target_pairs={{0,1},{1,0},{2,3},{3,2},{4,5},{5,4},{6,7},{7,6},{8,9},{9,8},{10,11... | collective-permute-start | bytes 221192 | tf_op jit(solution)/shard_map/ppermute | solution.py:419
  18.6 0.0 copy-done.8
  18.6 0.1 copy.11.courant_ref
  18.7 0.5 broadcast.6
  19.2 0.0 copy-done.7
  19.2 0.7 %reduce.3 = s32[16,16]{1,0:T(8,128)S(1)} reduce(s32[1,16,16,1]{2,3,1,0:T(1,128)S(1)} %copy-done.7, s32[]{:T(128)} %broadcast.6), dimensions={0,3}, to_apply=%param.16.reduce_sub_computation.3 | reduce | bytes 2052 | tf_op args[7]
  19.9 0.1 reshape_squeeze.3.mask_ref
  19.9 0.0 collective-permute-done.5
  20.0 0.0 collective-permute-done.4
  20.0 0.0 copy-done.2
  20.0 0.0 copy-done.3
  20.0 0.0 copy-done.4
  20.0 0.0 copy-done.5
  20.0 0.0 copy-done.6
  20.0 10.4 %step_and_march.1 = (f32[5,32,16,128]{3,2,1,0:T(8,128)}, f32[256,4,128]{2,1,0:T(4,128)S(1)}) custom-call(f32[6]{0:T(128)S(1)} %stack.36.flags_ref, f32[5,3]{1,0:T(8,128)S(1)} %copy.11.courant_ref, f32[16]{0:T(128)S(1)} %copy-done.4, f32[16]{0:T(128)S(1)} %copy-done.5, f32[16]{0:T(128)S(1)} %copy-done.6, f32[3,16]{1,0:T(4,128)S(1)} %copy-done.2, ...), custom_call_target="tpu_custom_call" | custom-call | tf_op jit(solution)/shard_map/step_and_march/pallas_call | solution.py:506
  30.4 21.3 %all_to_all.5.part_ref = f32[4,256,128]{2,1,0:T(8,128)S(1)} all-to-all(f32[4,256,128]{2,1,0:T(8,128)S(1)} %bitcast.10), channel_id=1, replica_groups=mesh['gz'=4,'gy'=2,'gx'=4] {'gz'}, dimensions={0} | all-to-all | bytes 1048576 | tf_op jit(solution)/shard_map/all_to_all | solution.py:530
  51.7 0.7 %compose.1 = f32[256,128]{1,0:T(8,128)} custom-call(f32[4,256,128]{2,1,0:T(8,128)S(1)} %all_to_all.5.part_ref), custom_call_target="tpu_custom_call" | custom-call | tf_op jit(solution)/shard_map/compose/pallas_call | solution.py:398
  (7 shorter events, 0.1 us)
Async XLA Ops:
  0.6 5.6 %copy-start.1 = (f32[32,16,128]{2,1,0:T(8,128)S(1)}, f32[32,16,128]{2,1,0:T(8,128)}, u32[]{:S(2)}) copy-start(f32[32,16,128]{2,1,0:T(8,128)} %kappa_ref.9) | copy-start | bytes 786436
  0.6 5.6 %copy-start = (f32[5,32,16,128]{3,2,1,0:T(8,128)S(1)}, f32[5,32,16,128]{3,2,1,0:T(8,128)}, u32[]{:S(2)}) copy-start(f32[5,32,16,128]{3,2,1,0:T(8,128)} %fields_ref.9) | copy-start | bytes 3932164
  2.4 6.4 %collective-permute-start = (f32[14,16,128]{2,1,0:T(8,128)}, f32[14,16,128]{2,1,0:T(8,128)S(1)}, u32[]{:S(2)}, u32[]{:S(2)}) collective-permute-start(f32[14,16,128]{2,1,0:T(8,128)} %get-tuple-element.14), channel_id=1, source_target_pairs={{0,8},{8,0},{16,24},{24,16},{1,9},{9,1},{17,25},{25,17},{2,10},{10... | collective-permute-start | bytes 344072 | tf_op jit(solution)/shard_map/ppermute | solution.py:419
  5.5 3.4 %collective-permute-start.1 = (f32[14,16,128]{2,1,0:T(8,128)}, f32[14,16,128]{2,1,0:T(8,128)S(1)}, u32[]{:S(2)}, u32[]{:S(2)}) collective-permute-start(f32[14,16,128]{2,1,0:T(8,128)} %get-tuple-element.15), channel_id=1, source_target_pairs={{8,16},{16,8},{9,17},{17,9},{10,18},{18,10},{11,19},{19,11},{12,20... | collective-permute-start | bytes 344072 | tf_op jit(solution)/shard_map/ppermute | solution.py:419
  6.4 7.4 %collective-permute-start.2 = (f32[14,32,128]{2,1,0:T(8,128)S(1)}, f32[14,32,128]{2,1,0:T(8,128)S(1)}, u32[]{:S(2)}, u32[]{:S(2)}) collective-permute-start(f32[14,32,128]{2,1,0:T(8,128)S(1)} %broadcast_select_fusion), channel_id=1, source_target_pairs={{0,4},{4,0},{1,5},{5,1},{2,6},{6,2},{3,7},{7,3},{8,12},{12,8},{9,1... | collective-permute-start | bytes 688136 | tf_op jit(solution)/shard_map/ppermute | solution.py:428
  8.9 4.9 %collective-permute-start.3 = (f32[20,128]{1,0:T(8,128)S(1)}, f32[20,128]{1,0:T(8,128)S(1)}, u32[]{:S(2)}, u32[]{:S(2)}) collective-permute-start(f32[20,128]{1,0:T(8,128)S(1)} %broadcast_select_fusion.7), channel_id=1, source_target_pairs={{0,4},{4,0},{1,5},{5,1},{2,6},{6,2},{3,7},{7,3},{8,12},{12,8},{9,1... | collective-permute-start | bytes 30728 | tf_op jit(solution)/shard_map/ppermute | solution.py:428
  10.8 7.8 %copy-start.8 = (f32[5,3]{0,1:T(4,128)S(1)}, f32[5,3]{0,1:T(4,128)}, u32[]{:S(2)}) copy-start(f32[5,3]{0,1:T(4,128)} %param.11) | copy-start | bytes 184
  10.8 8.4 %copy-start.7 = (s32[1,16,16,1]{2,3,1,0:T(1,128)S(1)}, s32[1,16,16,1]{2,3,1,0:T(1,128)}, u32[]{:S(2)}) copy-start(s32[1,16,16,1]{2,3,1,0:T(1,128)} %param.16) | copy-start | bytes 3076
  10.8 9.2 %copy-start.2 = (f32[3,16]{1,0:T(4,128)S(1)}, f32[3,16]{1,0:T(4,128)}, u32[]{:S(2)}) copy-start(f32[3,16]{1,0:T(4,128)} %color_ref.1) | copy-start | bytes 580
  10.8 9.2 %copy-start.3 = (s32[1,1,256]{2,1,0:T(1,128)S(1)}, s32[1,1,256]{2,1,0:T(1,128)}, u32[]{:S(2)}) copy-start(s32[1,1,256]{2,1,0:T(1,128)} %param.17) | copy-start | bytes 3076
  10.8 9.2 %copy-start.4 = (f32[16]{0:T(128)S(1)}, f32[16]{0:T(128)}, u32[]{:S(2)}) copy-start(f32[16]{0:T(128)} %center_ref.1) | copy-start | bytes 196
  10.8 9.2 %copy-start.5 = (f32[16]{0:T(128)S(1)}, f32[16]{0:T(128)}, u32[]{:S(2)}) copy-start(f32[16]{0:T(128)} %sharp_ref.1) | copy-start | bytes 196
  10.8 9.2 %copy-start.6 = (f32[16]{0:T(128)S(1)}, f32[16]{0:T(128)}, u32[]{:S(2)}) copy-start(f32[16]{0:T(128)} %gain_ref.1) | copy-start | bytes 196
  15.0 5.0 %collective-permute-start.5 = (f32[6,24,128]{2,1,0:T(8,128)S(1)}, f32[6,24,128]{2,1,0:T(8,128)S(1)}, u32[]{:S(2)}, u32[]{:S(2)}) collective-permute-start(f32[6,24,128]{2,1,0:T(8,128)S(1)} %get-tuple-element.30), channel_id=1, source_target_pairs={{1,2},{2,1},{5,6},{6,5},{9,10},{10,9},{13,14},{14,13},{17,18},{18,... | collective-permute-start | bytes 221192 | tf_op jit(solution)/shard_map/ppermute | solution.py:419
  15.6 4.3 %collective-permute-start.4 = (f32[6,24,128]{2,1,0:T(8,128)S(1)}, f32[6,24,128]{2,1,0:T(8,128)S(1)}, u32[]{:S(2)}, u32[]{:S(2)}) collective-permute-start(f32[6,24,128]{2,1,0:T(8,128)S(1)} %get-tuple-element.31), channel_id=1, source_target_pairs={{0,1},{1,0},{2,3},{3,2},{4,5},{5,4},{6,7},{7,6},{8,9},{9,8},{10,11... | collective-permute-start | bytes 221192 | tf_op jit(solution)/shard_map/ppermute | solution.py:419

commit v7 on v6

--- a/solution.py
+++ b/solution.py
@@ -84,13 +84,27 @@
                 out_ref[i, z : z + SUB, :] = flat[pl.ds(base + z * rows + row, SUB, stride=rows), :]
 
 
-def pack_edges_kernel(fields_ref, kappa_ref, zlo_ref, zhi_ref, lo_ref, hi_ref):
+def pack_edges_kernel(
+    fields_ref, kappa_ref, zlo_ref, zhi_ref, ownlo_ref, ownhi_ref, lo_ref, hi_ref, mainlo_ref, mainhi_ref
+):
     refs = (fields_ref, kappa_ref, zlo_ref, zhi_ref)
-    nfield, depth_len, rows, _ = fields_ref.shape
-    for i, (field, away, k) in enumerate(y_plan(nfield)[1]):
+    nfield, depth_len, rows, lanes = fields_ref.shape
+    lane = lax.broadcasted_iota(jnp.int32, (1, lanes), 1)
+    edges = y_plan(nfield)[1]
+    for i, (field, away, k) in enumerate(edges):
         plane = source_plane(refs, field, k if k < 0 else depth_len - 1 + k)
         lo_ref[i : i + 1, :] = plane[away - 1 : away, :]
         hi_ref[i : i + 1, :] = plane[rows - away : rows - away + 1, :]
+    for field in range(nfield + 1):
+        wide = reach(field, nfield)
+        pair = (ownlo_ref[field], ownhi_ref[field])
+        for z in list(range(-wide, 0)) + list(range(depth_len, depth_len + wide)):
+            pair = take_columns(source_plane(refs, field, z)[...], z + W, lane, *pair)
+        mainlo_ref[field], mainhi_ref[field] = pair
+        for side in range(2):
+            at = len(edges) + (side * (nfield + 1) + field) * W
+            lo_ref[at : at + W, :] = pair[side][:W]
+            hi_ref[at : at + W, :] = pair[side][rows - W :]
 
 
 def assemble(refs, halo_rows, flags_ref, pad_ref):
@@ -146,38 +160,31 @@
     return low, high
 
 
-def pack_own_kernel(fields_ref, kappa_ref, zlo_ref, zhi_ref, lo_ref, hi_ref):
-    refs = (fields_ref, kappa_ref, zlo_ref, zhi_ref)
+def pack_own_kernel(fields_ref, kappa_ref, lo_ref, hi_ref):
     nfield, depth_len, rows, lanes = fields_ref.shape
     lane = lax.broadcasted_iota(jnp.int32, (1, lanes), 1)
     for field in range(nfield + 1):
-        wide = reach(field, nfield)
         low = high = jnp.zeros((rows, lanes), F32)
-        for z in range(-wide, depth_len + wide):
-            low, high = take_columns(source_plane(refs, field, z)[...], z + W, lane, low, high)
+        for z in range(depth_len):
+            value = kappa_ref[z] if field == nfield else fields_ref[field, z]
+            low, high = take_columns(value, z + W, lane, low, high)
         lo_ref[field] = low
         hi_ref[field] = high
 
 
 def pack_columns_kernel(
-    flags_ref, ylo_ref, elo_ref, yhi_ref, ehi_ref, mainlo_ref, mainhi_ref, lo_ref, hi_ref, halo_ref
+    flags_ref, elo_ref, ehi_ref, mainlo_ref, mainhi_ref, rows_ref, lo_ref, hi_ref
 ):
-    nplane, _, lanes = halo_ref.shape
-    nfield, rows = mainlo_ref.shape[0] - 1, mainlo_ref.shape[1]
-    planes = nplane // (nfield + 1)
-    lane = lax.broadcasted_iota(jnp.int32, (1, lanes), 1)
-    zero = jnp.zeros((SUB, lanes), F32)
-    for plane in range(nplane):
-        halo_ref[plane] = zero
-    place_rows(halo_ref, planes - 2 * W, 0, (ylo_ref, elo_ref, yhi_ref, ehi_ref), flags_ref)
-    for field in range(nfield + 1):
-        low = high = zero
-        for zi in range(planes):
-            low, high = take_columns(halo_ref[field * planes + zi], zi, lane, low, high)
-        lo_ref[field, :rows, :] = mainlo_ref[field]
-        hi_ref[field, :rows, :] = mainhi_ref[field]
-        lo_ref[field, rows:, :] = low
-        hi_ref[field, rows:, :] = high
+    del rows_ref
+    count, rows, lanes = mainlo_ref.shape
+    at = len(y_plan(count - 1)[1])
+    for main_ref, out_ref in ((mainlo_ref, lo_ref), (mainhi_ref, hi_ref)):
+        for field in range(count):
+            out_ref[field, :rows, :] = main_ref[field]
+            out_ref[field, rows:, :] = jnp.zeros((SUB, lanes), F32)
+            out_ref[field, rows : rows + W, :] = ehi_ref[at : at + W, :] * flags_ref[3]
+            out_ref[field, rows + SUB - W :, :] = elo_ref[at : at + W, :] * flags_ref[2]
+            at += W
 
 
 def stencil(u, coefs, ups, downs, speeds):
@@ -303,7 +310,7 @@
     side_step(1, 1)
     edges(2, 0)
 
-    @pl.loop(1, planes - 1, unroll=steps(planes - 2, 4))
+    @pl.loop(1, planes - 1, unroll=steps(planes - 2, 6))
     def _(zi):
         mask = row_mask * depth_mask(zi)
         coefs = weights(*around(pad_ref, 0, nfield, zi, pitch))
@@ -312,12 +319,12 @@
         for field in range(nfield):
             next_ref[field * planes + zi] = mask * step_value(pad_ref, 0, field, zi, pitch, coefs)
 
-    @pl.loop(2, planes - 2, unroll=steps(planes - 4, 4))
+    @pl.loop(2, planes - 2, unroll=steps(planes - 4, 17))
     def _(zi):
         coefs = kept(zi, pitch)
         last_ref[zi] = step_value(next_ref, 1, 0, zi, pitch, coefs) * (row_mask * depth_mask(zi))
 
-    @pl.loop(0, depth_len, unroll=steps(depth_len, 4))
+    @pl.loop(0, depth_len, unroll=steps(depth_len, 8))
     def _(z):
         zi = z + W
         coefs = kept(zi, rows)
@@ -372,7 +379,7 @@
     @pl.loop(0, order_ref.shape[0], unroll=steps(order_ref.shape[0], 64))
     def _(slot):
         tile = order_ref[slot]
-        cover = mask_ref[tile].astype(jnp.float32)
+        cover = mask_ref[lax.div(tile, rows), lax.rem(tile, rows)].astype(F32)
         out_ref[slot] = tile_ref[pl.ds(pl.multiple_of(tile * 4, 4), 4), :] * cover
     keep.wait()
 
@@ -454,7 +461,7 @@
         pack_planes_kernel,
         out_shape=(array(faces, rows_len, cols_len),) * 2,
         in_specs=[pl.BlockSpec(memory_space=pl.ANY)] * 2,
-        out_specs=(vmem, vmem),
+        out_specs=(pl.BlockSpec(memory_space=pl.ANY),) * 2,
         scratch_shapes=[pltpu.SemaphoreType.DMA((2 * nfield + 2,))],
         compiler_params=pltpu.CompilerParams(vmem_limit_bytes=60 * 1024 * 1024),
         name="pack_planes",
@@ -470,34 +477,34 @@
         name="pack_rows",
     )(fields, diffusivity)
     ylo, yhi = swap_rows(send_lo, send_hi, "gy")
-    send_lo, send_hi = pl.pallas_call(
-        pack_edges_kernel,
-        out_shape=(array(len(outer), cols_len),) * 2,
-        in_specs=[vmem] * 4,
-        out_specs=(vmem, vmem),
-        compiler_params=params,
-        name="pack_edges",
-    )(fields, diffusivity, zlo, zhi)
-    elo, ehi = swap_rows(send_lo, send_hi, "gy")
-    main_lo, main_hi = pl.pallas_call(
+    part_lo, part_hi = pl.pallas_call(
         pack_own_kernel,
         out_shape=(array(nfield + 1, rows_len, cols_len),) * 2,
-        in_specs=[vmem] * 4,
+        in_specs=[vmem] * 2,
         out_specs=(vmem,) * 2,
         compiler_params=params,
         cost_estimate=pl.CostEstimate(flops=10**7, bytes_accessed=4 * 10**6, transcendentals=0),
         name="pack_own",
-    )(fields, diffusivity, zlo, zhi)
+    )(fields, diffusivity)
+    extra = len(outer) + 2 * (nfield + 1) * W
+    send_lo, send_hi, main_lo, main_hi = pl.pallas_call(
+        pack_edges_kernel,
+        out_shape=(array(extra, cols_len),) * 2 + (array(nfield + 1, rows_len, cols_len),) * 2,
+        in_specs=[vmem] * 6,
+        out_specs=(vmem,) * 4,
+        compiler_params=params,
+        name="pack_edges",
+    )(fields, diffusivity, zlo, zhi, part_lo, part_hi)
+    elo, ehi = swap_rows(send_lo, send_hi, "gy")
     pad = pltpu.VMEM(((nfield + 1) * planes, pitch, cols_len), F32)
     own_lo, own_hi = pl.pallas_call(
         pack_columns_kernel,
         out_shape=(array(nfield + 1, pitch, cols_len),) * 2,
-        in_specs=[smem] + [vmem] * 6,
+        in_specs=[smem] + [vmem] * 4 + [pl.BlockSpec(memory_space=pl.ANY)],
         out_specs=(vmem,) * 2,
-        scratch_shapes=[pltpu.VMEM(((nfield + 1) * planes, SUB, cols_len), F32)],
         compiler_params=params,
         name="pack_columns",
-    )(flags, ylo, elo, yhi, ehi, main_lo, main_hi)
+    )(flags, elo, ehi, main_lo, main_hi, ylo)
     odd = is_odd("gx")
     xlo, xhi = swap_pairs(jnp.where(odd, own_lo, own_hi), jnp.where(odd, own_hi, own_lo), "gx")
     count = lax.axis_size("gz")
@@ -523,7 +530,7 @@
         compiler_params=pltpu.CompilerParams(vmem_limit_bytes=24 * 1024 * 1024),
         name="step_and_march",
     )(
-        flags, courant, tf_center, tf_sharp, tf_gain, tf_color, tile_mask[0].reshape(-1), order,
+        flags, courant, tf_center, tf_sharp, tf_gain, tf_color, tile_mask[0, :, :, 0], order,
         fields, diffusivity, zlo, zhi, ylo, elo, yhi, ehi, xlo, xhi, own_lo, own_hi,
     )
     grouped = tiles.reshape(count, per_owner * 4, cols_len)

time: 52.6 us -> 58.5 us (1.11)
  Pallas kernels: 15.2 us -> 20.6 us
  waiting for transfers between devices: 2.82 us -> 3.95 us
  other arithmetic: 0.77 us -> 0.1 us
  blocking collectives: 21.3 us -> 21.9 us
    pallas_call x1, Pallas kernels: 1.78 us -> 8.17 us  [shards(): pl.pallas_call(pack_planes_kernel, out_shape=(array(faces, rows_len, cols...]
    ppermute x2, waiting for transfers between devices: 1.89 us -> 3.13 us  [swap_rows(): came = lax.ppermute(first, axis, [(0, 1), (1, 0)])]
    unnamed x1 -> x0, other arithmetic: 0.67 us -> none
    all_to_all x1, blocking collectives: 21.3 us -> 21.9 us  [shards(): lax.all_to_all(grouped, 'gz', split_axis=0, concat_axis=0, tiled=True)]
  transfers between devices with their start and end apart: 6 -> 6, of which waited for: 2 -> 2; matrix products, arithmetic and copies ran while one was open for 3% -> 0% of each run, Pallas kernels for 2% -> 2%
where the time goes in v7:
time: 58.5 us; the launch traced here: 58.3 us
  blocking collectives  21.9 us (37%)
  Pallas kernels  20.6 us (35%)
  starting transfers between devices  10.6 us (18%)
  waiting for transfers between devices  3.95 us (7%)
  between operations  0.89 us (2%)
    all_to_all x1, blocking collectives, shards(): lax.all_to_all(grouped, 'gz', split_axis=0, concat_axis=0, tiled=True)  21.9 us
    pallas_call x1, Pallas kernels, shards(): pl.pallas_call(main_kernel, out_shape=(array(*fields.shape), array(order....  9.96 us
    pallas_call x1, Pallas kernels, shards(): pl.pallas_call(pack_planes_kernel, out_shape=(array(faces, rows_len, cols...  8.17 us
    ppermute x4, starting transfers between devices, swap_pairs(): lax.ppermute(message, axis, pairs)  7.35 us
    ppermute x2, starting transfers between devices, swap_rows(): came = lax.ppermute(first, axis, [(0, 1), (1, 0)])  3.25 us
    ppermute x2, waiting for transfers between devices, swap_rows(): came = lax.ppermute(first, axis, [(0, 1), (1, 0)])  3.13 us
  transfers between devices with their start and end apart: 6, of which 2 were waited for; matrix products, arithmetic and copies ran while one was open for 0% of the time, Pallas kernels for 2%

profile of v7, /device:TPU:0, one launch (start us, length us, event | category | flops | bytes accessed | tf_op | source)
XLA Modules:
  0.0 58.3 jit_solution(11371873818964732776)
XLA Ops:
  0.6 0.0 copy-start.1
  0.6 0.0 copy-start
  0.6 8.2 %pack_planes.1 = (f32[14,16,128]{2,1,0:T(8,128)}, f32[14,16,128]{2,1,0:T(8,128)}) custom-call(f32[5,32,16,128]{3,2,1,0:T(8,128)} %fields_ref.9, f32[32,16,128]{2,1,0:T(8,128)} %kappa_ref.9), custom_call_target="tpu_custom_call" | custom-call | tf_op jit(solution)/shard_map/pack_planes/pallas_call | solution.py:460
  8.8 3.1 %collective-permute-start = (f32[14,16,128]{2,1,0:T(8,128)}, f32[14,16,128]{2,1,0:T(8,128)S(1)}, u32[]{:S(2)}, u32[]{:S(2)}) collective-permute-start(f32[14,16,128]{2,1,0:T(8,128)} %get-tuple-element.16), channel_id=1, source_target_pairs={{0,8},{8,0},{16,24},{24,16},{1,9},{9,1},{17,25},{25,17},{2,10},{10... | collective-permute-start | bytes 344072 | tf_op jit(solution)/shard_map/ppermute | solution.py:426
  11.9 0.7 %collective-permute-start.1 = (f32[14,16,128]{2,1,0:T(8,128)}, f32[14,16,128]{2,1,0:T(8,128)S(1)}, u32[]{:S(2)}, u32[]{:S(2)}) collective-permute-start(f32[14,16,128]{2,1,0:T(8,128)} %get-tuple-element.17), channel_id=1, source_target_pairs={{8,16},{16,8},{9,17},{17,9},{10,18},{18,10},{11,19},{19,11},{12,20... | collective-permute-start | bytes 344072 | tf_op jit(solution)/shard_map/ppermute | solution.py:426
  12.6 0.0 copy-done.1
  12.6 0.0 copy-done
  12.6 0.1 pack_rows.1
  12.8 1.6 %collective-permute-start.2 = (f32[14,32,128]{2,1,0:T(8,128)S(1)}, f32[14,32,128]{2,1,0:T(8,128)S(1)}, u32[]{:S(2)}, u32[]{:S(2)}) collective-permute-start(f32[14,32,128]{2,1,0:T(8,128)S(1)} %broadcast_select_fusion), channel_id=1, source_target_pairs={{0,4},{4,0},{1,5},{5,1},{2,6},{6,2},{3,7},{7,3},{8,12},{12,8},{9,1... | collective-permute-start | bytes 688136 | tf_op jit(solution)/shard_map/ppermute | solution.py:435
  14.4 0.9 %pack_own.1 = (f32[6,16,128]{2,1,0:T(8,128)S(1)}, f32[6,16,128]{2,1,0:T(8,128)S(1)}) custom-call(f32[5,32,16,128]{3,2,1,0:T(8,128)S(1)} %copy-done, f32[32,16,128]{2,1,0:T(8,128)S(1)} %copy-done.1), custom_call_target="tpu_custom_call" | custom-call | flops 10000000 | bytes 4000000 | tf_op jit(solution)/shard_map/pack_own/pallas_call | solution.py:480
  15.3 0.0 collective-permute-done
  15.3 0.0 collective-permute-done.1
  15.3 0.0 copy-start.8
  15.3 0.0 copy-start.2
  15.4 0.0 copy-start.3
  15.4 0.0 copy-start.4
  15.4 0.0 copy-start.5
  15.4 0.0 copy-start.6
  15.4 0.0 copy-start.7
  15.4 0.2 pack_edges.1
  15.6 1.7 %collective-permute-start.3 = (f32[56,128]{1,0:T(8,128)S(1)}, f32[56,128]{1,0:T(8,128)S(1)}, u32[]{:S(2)}, u32[]{:S(2)}) collective-permute-start(f32[56,128]{1,0:T(8,128)S(1)} %broadcast_select_fusion.7), channel_id=1, source_target_pairs={{0,4},{4,0},{1,5},{5,1},{2,6},{6,2},{3,7},{7,3},{8,12},{12,8},{9,1... | collective-permute-start | bytes 86024 | tf_op jit(solution)/shard_map/ppermute | solution.py:435
  17.3 0.1 stack.35
  17.4 3.1 %collective-permute-done.3.elo_ref.ehi_ref = f32[56,128]{1,0:T(8,128)S(1)} collective-permute-done((f32[56,128]{1,0:T(8,128)S(1)}, f32[56,128]{1,0:T(8,128)S(1)}, u32[]{:S(2)}, u32[]{:S(2)}) %collective-permute-start.3) | collective-permute-done | bytes 28704 | tf_op jit(solution)/shard_map/ppermute | solution.py:435
  20.5 0.0 collective-permute-done.2.rows_ref.ylo_ref.yhi_ref
  20.5 0.6 pack_columns.1
  21.1 0.7 %collective-permute-start.5 = (f32[6,24,128]{2,1,0:T(8,128)S(1)}, f32[6,24,128]{2,1,0:T(8,128)S(1)}, u32[]{:S(2)}, u32[]{:S(2)}) collective-permute-start(f32[6,24,128]{2,1,0:T(8,128)S(1)} %get-tuple-element.34), channel_id=1, source_target_pairs={{1,2},{2,1},{5,6},{6,5},{9,10},{10,9},{13,14},{14,13},{17,18},{18,... | collective-permute-start | bytes 221192 | tf_op jit(solution)/shard_map/ppermute | solution.py:426
  21.8 2.9 %collective-permute-start.4 = (f32[6,24,128]{2,1,0:T(8,128)S(1)}, f32[6,24,128]{2,1,0:T(8,128)S(1)}, u32[]{:S(2)}, u32[]{:S(2)}) collective-permute-start(f32[6,24,128]{2,1,0:T(8,128)S(1)} %get-tuple-element.35), channel_id=1, source_target_pairs={{0,1},{1,0},{2,3},{3,2},{4,5},{5,4},{6,7},{7,6},{8,9},{9,8},{10,11... | collective-permute-start | bytes 221192 | tf_op jit(solution)/shard_map/ppermute | solution.py:426
  24.8 0.0 copy-done.8
  24.8 0.1 copy.11.courant_ref
  24.9 0.0 collective-permute-done.5
  24.9 0.8 %collective-permute-done.4 = f32[6,24,128]{2,1,0:T(8,128)S(1)} collective-permute-done((f32[6,24,128]{2,1,0:T(8,128)S(1)}, f32[6,24,128]{2,1,0:T(8,128)S(1)}, u32[]{:S(2)}, u32[]{:S(2)}) %collective-permute-start.4) | collective-permute-done | bytes 73760 | tf_op jit(solution)/shard_map/ppermute | solution.py:426
  25.7 0.0 copy-done.2
  25.7 0.0 copy-done.3
  25.7 0.0 copy-done.4
  25.7 0.0 copy-done.5
  25.7 0.0 copy-done.6
  25.7 0.0 copy-done.7
  25.7 10.0 %step_and_march.1 = (f32[5,32,16,128]{3,2,1,0:T(8,128)}, f32[256,4,128]{2,1,0:T(4,128)S(1)}) custom-call(f32[6]{0:T(128)S(1)} %stack.36.flags_ref, f32[5,3]{1,0:T(8,128)S(1)} %copy.11.courant_ref, f32[16]{0:T(128)S(1)} %copy-done.5, f32[16]{0:T(128)S(1)} %copy-done.6, f32[16]{0:T(128)S(1)} %copy-done.7, f32[3,16]{1,0:T(4,128)S(1)} %copy-done.3, ...), custom_call_target="tpu_custom_call" | custom-call | tf_op jit(solution)/shard_map/step_and_march/pallas_call | solution.py:513
  35.7 21.9 %all_to_all.5.part_ref = f32[4,256,128]{2,1,0:T(8,128)S(1)} all-to-all(f32[4,256,128]{2,1,0:T(8,128)S(1)} %bitcast.10), channel_id=1, replica_groups=mesh['gz'=4,'gy'=2,'gx'=4] {'gz'}, dimensions={0} | all-to-all | bytes 1048576 | tf_op jit(solution)/shard_map/all_to_all | solution.py:537
  57.6 0.7 %compose.1 = f32[256,128]{1,0:T(8,128)} custom-call(f32[4,256,128]{2,1,0:T(8,128)S(1)} %all_to_all.5.part_ref), custom_call_target="tpu_custom_call" | custom-call | tf_op jit(solution)/shard_map/compose/pallas_call | solution.py:405
  (6 shorter events, 0.1 us)
Async XLA Ops:
  0.6 12.0 %copy-start.1 = (f32[32,16,128]{2,1,0:T(8,128)S(1)}, f32[32,16,128]{2,1,0:T(8,128)}, u32[]{:S(2)}) copy-start(f32[32,16,128]{2,1,0:T(8,128)} %kappa_ref.9) | copy-start | bytes 786436
  0.6 12.0 %copy-start = (f32[5,32,16,128]{3,2,1,0:T(8,128)S(1)}, f32[5,32,16,128]{3,2,1,0:T(8,128)}, u32[]{:S(2)}) copy-start(f32[5,32,16,128]{3,2,1,0:T(8,128)} %fields_ref.9) | copy-start | bytes 3932164
  8.8 6.5 %collective-permute-start = (f32[14,16,128]{2,1,0:T(8,128)}, f32[14,16,128]{2,1,0:T(8,128)S(1)}, u32[]{:S(2)}, u32[]{:S(2)}) collective-permute-start(f32[14,16,128]{2,1,0:T(8,128)} %get-tuple-element.16), channel_id=1, source_target_pairs={{0,8},{8,0},{16,24},{24,16},{1,9},{9,1},{17,25},{25,17},{2,10},{10... | collective-permute-start | bytes 344072 | tf_op jit(solution)/shard_map/ppermute | solution.py:426
  11.9 3.4 %collective-permute-start.1 = (f32[14,16,128]{2,1,0:T(8,128)}, f32[14,16,128]{2,1,0:T(8,128)S(1)}, u32[]{:S(2)}, u32[]{:S(2)}) collective-permute-start(f32[14,16,128]{2,1,0:T(8,128)} %get-tuple-element.17), channel_id=1, source_target_pairs={{8,16},{16,8},{9,17},{17,9},{10,18},{18,10},{11,19},{19,11},{12,20... | collective-permute-start | bytes 344072 | tf_op jit(solution)/shard_map/ppermute | solution.py:426
  12.8 7.7 %collective-permute-start.2 = (f32[14,32,128]{2,1,0:T(8,128)S(1)}, f32[14,32,128]{2,1,0:T(8,128)S(1)}, u32[]{:S(2)}, u32[]{:S(2)}) collective-permute-start(f32[14,32,128]{2,1,0:T(8,128)S(1)} %broadcast_select_fusion), channel_id=1, source_target_pairs={{0,4},{4,0},{1,5},{5,1},{2,6},{6,2},{3,7},{7,3},{8,12},{12,8},{9,1... | collective-permute-start | bytes 688136 | tf_op jit(solution)/shard_map/ppermute | solution.py:435
  15.3 9.4 %copy-start.8 = (f32[5,3]{0,1:T(4,128)S(1)}, f32[5,3]{0,1:T(4,128)}, u32[]{:S(2)}) copy-start(f32[5,3]{0,1:T(4,128)} %param.11) | copy-start | bytes 184
  15.3 10.3 %copy-start.2 = (s32[1,16,16,1]{2,3,1,0:T(1,128)S(1)}, s32[1,16,16,1]{2,3,1,0:T(1,128)}, u32[]{:S(2)}) copy-start(s32[1,16,16,1]{2,3,1,0:T(1,128)} %param.16) | copy-start | bytes 3076
  15.4 10.3 %copy-start.3 = (f32[3,16]{1,0:T(4,128)S(1)}, f32[3,16]{1,0:T(4,128)}, u32[]{:S(2)}) copy-start(f32[3,16]{1,0:T(4,128)} %color_ref.1) | copy-start | bytes 580
  15.4 10.3 %copy-start.4 = (s32[1,1,256]{2,1,0:T(1,128)S(1)}, s32[1,1,256]{2,1,0:T(1,128)}, u32[]{:S(2)}) copy-start(s32[1,1,256]{2,1,0:T(1,128)} %param.17) | copy-start | bytes 3076
  15.4 10.3 %copy-start.5 = (f32[16]{0:T(128)S(1)}, f32[16]{0:T(128)}, u32[]{:S(2)}) copy-start(f32[16]{0:T(128)} %center_ref.1) | copy-start | bytes 196
  15.4 10.3 %copy-start.6 = (f32[16]{0:T(128)S(1)}, f32[16]{0:T(128)}, u32[]{:S(2)}) copy-start(f32[16]{0:T(128)} %sharp_ref.1) | copy-start | bytes 196
  15.4 10.3 %copy-start.7 = (f32[16]{0:T(128)S(1)}, f32[16]{0:T(128)}, u32[]{:S(2)}) copy-start(f32[16]{0:T(128)} %gain_ref.1) | copy-start | bytes 196
  15.6 4.9 %collective-permute-start.3 = (f32[56,128]{1,0:T(8,128)S(1)}, f32[56,128]{1,0:T(8,128)S(1)}, u32[]{:S(2)}, u32[]{:S(2)}) collective-permute-start(f32[56,128]{1,0:T(8,128)S(1)} %broadcast_select_fusion.7), channel_id=1, source_target_pairs={{0,4},{4,0},{1,5},{5,1},{2,6},{6,2},{3,7},{7,3},{8,12},{12,8},{9,1... | collective-permute-start | bytes 86024 | tf_op jit(solution)/shard_map/ppermute | solution.py:435
  21.1 3.7 %collective-permute-start.5 = (f32[6,24,128]{2,1,0:T(8,128)S(1)}, f32[6,24,128]{2,1,0:T(8,128)S(1)}, u32[]{:S(2)}, u32[]{:S(2)}) collective-permute-start(f32[6,24,128]{2,1,0:T(8,128)S(1)} %get-tuple-element.34), channel_id=1, source_target_pairs={{1,2},{2,1},{5,6},{6,5},{9,10},{10,9},{13,14},{14,13},{17,18},{18,... | collective-permute-start | bytes 221192 | tf_op jit(solution)/shard_map/ppermute | solution.py:426
  21.8 3.9 %collective-permute-start.4 = (f32[6,24,128]{2,1,0:T(8,128)S(1)}, f32[6,24,128]{2,1,0:T(8,128)S(1)}, u32[]{:S(2)}, u32[]{:S(2)}) collective-permute-start(f32[6,24,128]{2,1,0:T(8,128)S(1)} %get-tuple-element.35), channel_id=1, source_target_pairs={{0,1},{1,0},{2,3},{3,2},{4,5},{5,4},{6,7},{7,6},{8,9},{9,8},{10,11... | collective-permute-start | bytes 221192 | tf_op jit(solution)/shard_map/ppermute | solution.py:426

commit v8 on v7

--- a/solution.py
+++ b/solution.py
@@ -55,6 +55,11 @@
         copy.start()
     for copy in copies:
         copy.wait()
+
+
+def present(axis):
+    here = lax.axis_index(axis)
+    return jnp.where(here > 0, 1.0, 0.0), jnp.where(here < lax.axis_size(axis) - 1, 1.0, 0.0)
 
 
 def steps(count, most):
@@ -107,7 +112,7 @@
             hi_ref[at : at + W, :] = pair[side][rows - W :]
 
 
-def assemble(refs, halo_rows, flags_ref, pad_ref):
+def assemble(refs, halo_rows, pad_ref):
     fields_ref, kappa_ref, zlo_ref, zhi_ref = refs
     nfield, depth_len, rows, lanes = fields_ref.shape
     planes, pitch = depth_len + 2 * W, rows + SUB
@@ -130,16 +135,16 @@
                 if k >= wide:
                     pad_ref[plane, :rows, :] = jnp.zeros((rows, lanes), F32)
                 pad_ref[plane, rows:, :] = halo
-    place_rows(pad_ref, depth_len, rows, halo_rows, flags_ref)
-
-
-def place_rows(pad_ref, depth_len, first_row, halo_rows, flags_ref):
+    place_rows(pad_ref, depth_len, rows, halo_rows)
+
+
+def place_rows(pad_ref, depth_len, first_row, halo_rows):
     planes = depth_len + 2 * W
     pitch, lanes = pad_ref.shape[1:]
     flat = pad_ref.reshape(pad_ref.shape[0] * pitch, lanes)
     kinds, edges = y_plan(pad_ref.shape[0] // planes - 1)
     for low, (ref, edge_ref) in ((True, halo_rows[:2]), (False, halo_rows[2:])):
-        flag = flags_ref[2] if low else flags_ref[3]
+        flag = present("gy")[0 if low else 1]
         for i, (field, away) in enumerate(kinds):
             row = pitch - away if low else first_row + away - 1
             for z in range(0, depth_len, SUB):
@@ -173,17 +178,18 @@
 
 
 def pack_columns_kernel(
-    flags_ref, elo_ref, ehi_ref, mainlo_ref, mainhi_ref, rows_ref, lo_ref, hi_ref
+    elo_ref, ehi_ref, mainlo_ref, mainhi_ref, rows_ref, lo_ref, hi_ref
 ):
     del rows_ref
     count, rows, lanes = mainlo_ref.shape
+    low, high = present("gy")
     at = len(y_plan(count - 1)[1])
     for main_ref, out_ref in ((mainlo_ref, lo_ref), (mainhi_ref, hi_ref)):
         for field in range(count):
             out_ref[field, :rows, :] = main_ref[field]
             out_ref[field, rows:, :] = jnp.zeros((SUB, lanes), F32)
-            out_ref[field, rows : rows + W, :] = ehi_ref[at : at + W, :] * flags_ref[3]
-            out_ref[field, rows + SUB - W :, :] = elo_ref[at : at + W, :] * flags_ref[2]
+            out_ref[field, rows : rows + W, :] = ehi_ref[at : at + W, :] * high
+            out_ref[field, rows + SUB - W :, :] = elo_ref[at : at + W, :] * low
             at += W
 
 
@@ -215,7 +221,7 @@
 
 
 def main_kernel(
-    flags_ref, courant_ref, center_ref, sharp_ref, gain_ref, color_ref, mask_ref, order_ref,
+    courant_ref, center_ref, sharp_ref, gain_ref, color_ref, mask_ref, order_ref,
     fields_ref, kappa_ref, zlo_ref, zhi_ref,
     ylo_ref, elo_ref, yhi_ref, ehi_ref, xlo_ref, xhi_ref, ownlo_ref, ownhi_ref,
     state_ref, out_ref,
@@ -227,7 +233,7 @@
     r = lax.broadcasted_iota(jnp.int32, (pitch, lanes), 0)
     zi_of = lane // W
     col = lane - zi_of * W
-    flag = [flags_ref[i] for i in range(6)]
+    flag = present("gz") + present("gy") + present("gx")
     speed = [[courant_ref[f, a] for a in range(3)] for f in range(nfield)]
     row_mask = jnp.where(r < rows, 1.0, jnp.where(r < rows + SUB // 2, flag[3], flag[2]))
 
@@ -301,7 +307,7 @@
         return jnp.where(zi < W, flag[0], jnp.where(zi >= W + depth_len, flag[1], 1.0))
 
     halo_rows = (ylo_ref, elo_ref, yhi_ref, ehi_ref)
-    assemble((fields_ref, kappa_ref, zlo_ref, zhi_ref), halo_rows, flags_ref, pad_ref)
+    assemble((fields_ref, kappa_ref, zlo_ref, zhi_ref), halo_rows, pad_ref)
     for field in range(nfield + 1):
         edges(0, field)
     side_step(0, nfield)
@@ -437,11 +443,6 @@
     return swap_pairs(first, jnp.where(odd, high, low), axis)
 
 
-def present(axis):
-    here = lax.axis_index(axis)
-    return [(here > 0).astype(F32), (here < lax.axis_size(axis) - 1).astype(F32)]
-
-
 def shards(
     fields, diffusivity, courant, tf_center, tf_sharp, tf_gain, tf_color, tile_mask, tile_perm
 ):
@@ -454,14 +455,12 @@
     def array(*shape):
         return jax.ShapeDtypeStruct(shape, F32)
 
-    flags = jnp.stack(present("gz") + present("gy") + present("gx"))
-
     faces = z_plan(nfield)[1]
     first, second = pl.pallas_call(
         pack_planes_kernel,
         out_shape=(array(faces, rows_len, cols_len),) * 2,
         in_specs=[pl.BlockSpec(memory_space=pl.ANY)] * 2,
-        out_specs=(pl.BlockSpec(memory_space=pl.ANY),) * 2,
+        out_specs=(vmem, vmem),
         scratch_shapes=[pltpu.SemaphoreType.DMA((2 * nfield + 2,))],
         compiler_params=pltpu.CompilerParams(vmem_limit_bytes=60 * 1024 * 1024),
         name="pack_planes",
@@ -500,11 +499,11 @@
     own_lo, own_hi = pl.pallas_call(
         pack_columns_kernel,
         out_shape=(array(nfield + 1, pitch, cols_len),) * 2,
-        in_specs=[smem] + [vmem] * 4 + [pl.BlockSpec(memory_space=pl.ANY)],
+        in_specs=[vmem] * 4 + [pl.BlockSpec(memory_space=pl.ANY)],
         out_specs=(vmem,) * 2,
         compiler_params=params,
         name="pack_columns",
-    )(flags, elo, ehi, main_lo, main_hi, ylo)
+    )(elo, ehi, main_lo, main_hi, ylo)
     odd = is_odd("gx")
     xlo, xhi = swap_pairs(jnp.where(odd, own_lo, own_hi), jnp.where(odd, own_hi, own_lo), "gx")
     count = lax.axis_size("gz")
@@ -513,7 +512,7 @@
     state, tiles = pl.pallas_call(
         main_kernel,
         out_shape=(array(*fields.shape), array(order.shape[0], 4, cols_len)),
-        in_specs=[smem] * 8 + [vmem] * 12,
+        in_specs=[smem] * 7 + [vmem] * 12,
         out_specs=(pl.BlockSpec(memory_space=pl.ANY), vmem),
         scratch_shapes=[
             pad,
@@ -530,7 +529,7 @@
         compiler_params=pltpu.CompilerParams(vmem_limit_bytes=24 * 1024 * 1024),
         name="step_and_march",
     )(
-        flags, courant, tf_center, tf_sharp, tf_gain, tf_color, tile_mask[0, :, :, 0], order,
+        courant, tf_center, tf_sharp, tf_gain, tf_color, tile_mask[0, :, :, 0], order,
         fields, diffusivity, zlo, zhi, ylo, elo, yhi, ehi, xlo, xhi, own_lo, own_hi,
     )
     grouped = tiles.reshape(count, per_owner * 4, cols_len)

time: 58.5 us -> 51.6 us (0.88)
  Pallas kernels: 20.6 us -> 13.7 us
    pallas_call x1, Pallas kernels: 8.17 us -> 1.78 us  [shards(): pl.pallas_call(pack_planes_kernel, out_shape=(array(faces, rows_len, cols...]
where the time goes in v8:
time: 51.6 us; the launch traced here: 51.4 us
  blocking collectives  21.9 us (42%)
  Pallas kernels  13.7 us (27%)
  starting transfers between devices  10.6 us (21%)
  waiting for transfers between devices  4.06 us (8%)
  between operations  0.88 us (2%)
    all_to_all x1, blocking collectives, shards(): lax.all_to_all(grouped, 'gz', split_axis=0, concat_axis=0, tiled=True)  21.9 us
    pallas_call x1, Pallas kernels, shards(): pl.pallas_call(main_kernel, out_shape=(array(*fields.shape), array(order....  9.97 us
    ppermute x4, starting transfers between devices, swap_pairs(): lax.ppermute(message, axis, pairs)  7.35 us
    ppermute x2, starting transfers between devices, swap_rows(): came = lax.ppermute(first, axis, [(0, 1), (1, 0)])  3.25 us
    ppermute x2, waiting for transfers between devices, swap_rows(): came = lax.ppermute(first, axis, [(0, 1), (1, 0)])  3.24 us
    pallas_call x1, Pallas kernels, shards(): pl.pallas_call(pack_planes_kernel, out_shape=(array(faces, rows_len, cols...  1.78 us
  transfers between devices with their start and end apart: 6, of which 2 were waited for; matrix products, arithmetic and copies ran while one was open for 0% of the time, Pallas kernels for 2%

profile of v8, /device:TPU:0, one launch (start us, length us, event | category | flops | bytes accessed | tf_op | source)
XLA Modules:
  0.0 51.4 jit_solution(9516500597437130385)
XLA Ops:
  0.6 0.0 copy-start.1
  0.6 0.0 copy-start
  0.6 1.8 %pack_planes.1 = (f32[14,16,128]{2,1,0:T(8,128)}, f32[14,16,128]{2,1,0:T(8,128)}) custom-call(f32[5,32,16,128]{3,2,1,0:T(8,128)} %fields_ref.9, f32[32,16,128]{2,1,0:T(8,128)} %kappa_ref.9), custom_call_target="tpu_custom_call" | custom-call | tf_op jit(solution)/shard_map/pack_planes/pallas_call | solution.py:459
  2.4 3.1 %collective-permute-start = (f32[14,16,128]{2,1,0:T(8,128)}, f32[14,16,128]{2,1,0:T(8,128)S(1)}, u32[]{:S(2)}, u32[]{:S(2)}) collective-permute-start(f32[14,16,128]{2,1,0:T(8,128)} %get-tuple-element.16), channel_id=1, source_target_pairs={{0,8},{8,0},{16,24},{24,16},{1,9},{9,1},{17,25},{25,17},{2,10},{10... | collective-permute-start | bytes 344072 | tf_op jit(solution)/shard_map/ppermute | solution.py:432
  5.5 0.7 %collective-permute-start.1 = (f32[14,16,128]{2,1,0:T(8,128)}, f32[14,16,128]{2,1,0:T(8,128)S(1)}, u32[]{:S(2)}, u32[]{:S(2)}) collective-permute-start(f32[14,16,128]{2,1,0:T(8,128)} %get-tuple-element.17), channel_id=1, source_target_pairs={{8,16},{16,8},{9,17},{17,9},{10,18},{18,10},{11,19},{19,11},{12,20... | collective-permute-start | bytes 344072 | tf_op jit(solution)/shard_map/ppermute | solution.py:432
  6.2 0.0 copy-done.1
  6.2 0.0 copy-done
  6.2 0.1 pack_rows.1
  6.4 1.6 %collective-permute-start.2 = (f32[14,32,128]{2,1,0:T(8,128)S(1)}, f32[14,32,128]{2,1,0:T(8,128)S(1)}, u32[]{:S(2)}, u32[]{:S(2)}) collective-permute-start(f32[14,32,128]{2,1,0:T(8,128)S(1)} %broadcast_select_fusion), channel_id=1, source_target_pairs={{0,4},{4,0},{1,5},{5,1},{2,6},{6,2},{3,7},{7,3},{8,12},{12,8},{9,1... | collective-permute-start | bytes 688136 | tf_op jit(solution)/shard_map/ppermute | solution.py:441
  8.0 0.9 %pack_own.1 = (f32[6,16,128]{2,1,0:T(8,128)S(1)}, f32[6,16,128]{2,1,0:T(8,128)S(1)}) custom-call(f32[5,32,16,128]{3,2,1,0:T(8,128)S(1)} %copy-done, f32[32,16,128]{2,1,0:T(8,128)S(1)} %copy-done.1), custom_call_target="tpu_custom_call" | custom-call | flops 10000000 | bytes 4000000 | tf_op jit(solution)/shard_map/pack_own/pallas_call | solution.py:479
  8.9 0.0 collective-permute-done
  8.9 0.0 collective-permute-done.1
  8.9 0.0 copy-start.8
  9.0 0.0 copy-start.2
  9.0 0.0 copy-start.3
  9.0 0.0 copy-start.4
  9.0 0.0 copy-start.5
  9.0 0.0 copy-start.6
  9.0 0.0 copy-start.7
  9.0 0.2 pack_edges.1
  9.2 1.7 %collective-permute-start.3 = (f32[56,128]{1,0:T(8,128)S(1)}, f32[56,128]{1,0:T(8,128)S(1)}, u32[]{:S(2)}, u32[]{:S(2)}) collective-permute-start(f32[56,128]{1,0:T(8,128)S(1)} %broadcast_select_fusion.7), channel_id=1, source_target_pairs={{0,4},{4,0},{1,5},{5,1},{2,6},{6,2},{3,7},{7,3},{8,12},{12,8},{9,1... | collective-permute-start | bytes 86024 | tf_op jit(solution)/shard_map/ppermute | solution.py:441
  10.9 3.2 %collective-permute-done.3.elo_ref.ehi_ref = f32[56,128]{1,0:T(8,128)S(1)} collective-permute-done((f32[56,128]{1,0:T(8,128)S(1)}, f32[56,128]{1,0:T(8,128)S(1)}, u32[]{:S(2)}, u32[]{:S(2)}) %collective-permute-start.3) | collective-permute-done | bytes 28704 | tf_op jit(solution)/shard_map/ppermute | solution.py:441
  14.2 0.0 collective-permute-done.2.rows_ref.ylo_ref.yhi_ref
  14.2 0.7 %collective-permute-start.5 = (f32[6,24,128]{2,1,0:T(8,128)S(1)}, f32[6,24,128]{2,1,0:T(8,128)S(1)}, u32[]{:S(2)}, u32[]{:S(2)}) collective-permute-start(f32[6,24,128]{2,1,0:T(8,128)S(1)} %get-tuple-element.34), channel_id=1, source_target_pairs={{1,2},{2,1},{5,6},{6,5},{9,10},{10,9},{13,14},{14,13},{17,18},{18,... | collective-permute-start | bytes 221192 | tf_op jit(solution)/shard_map/ppermute | solution.py:432
  14.9 2.9 %collective-permute-start.4 = (f32[6,24,128]{2,1,0:T(8,128)S(1)}, f32[6,24,128]{2,1,0:T(8,128)S(1)}, u32[]{:S(2)}, u32[]{:S(2)}) collective-permute-start(f32[6,24,128]{2,1,0:T(8,128)S(1)} %get-tuple-element.35), channel_id=1, source_target_pairs={{0,1},{1,0},{2,3},{3,2},{4,5},{5,4},{6,7},{7,6},{8,9},{9,8},{10,11... | collective-permute-start | bytes 221192 | tf_op jit(solution)/shard_map/ppermute | solution.py:432
  17.8 0.0 copy-done.8
  17.8 0.1 copy.11.courant_ref
  17.9 0.0 collective-permute-done.5
  17.9 0.8 %collective-permute-done.4 = f32[6,24,128]{2,1,0:T(8,128)S(1)} collective-permute-done((f32[6,24,128]{2,1,0:T(8,128)S(1)}, f32[6,24,128]{2,1,0:T(8,128)S(1)}, u32[]{:S(2)}, u32[]{:S(2)}) %collective-permute-start.4) | collective-permute-done | bytes 73760 | tf_op jit(solution)/shard_map/ppermute | solution.py:432
  18.7 0.0 copy-done.2
  18.8 0.0 copy-done.3
  18.8 0.0 copy-done.4
  18.8 0.0 copy-done.5
  18.8 0.0 copy-done.6
  18.8 0.0 copy-done.7
  18.8 10.0 %step_and_march.1 = (f32[5,32,16,128]{3,2,1,0:T(8,128)}, f32[256,4,128]{2,1,0:T(4,128)S(1)}) custom-call(f32[5,3]{1,0:T(8,128)S(1)} %copy.11.courant_ref, f32[16]{0:T(128)S(1)} %copy-done.5, f32[16]{0:T(128)S(1)} %copy-done.6, f32[16]{0:T(128)S(1)} %copy-done.7, f32[3,16]{1,0:T(4,128)S(1)} %copy-done.3, s32[16,16]{1,0:T(8,128)S(1)} %bitcast.5, ...), custom_call_target="tpu_custom_call" | custom-call | tf_op jit(solution)/shard_map/step_and_march/pallas_call | solution.py:512
  28.8 21.9 %all_to_all.5.part_ref = f32[4,256,128]{2,1,0:T(8,128)S(1)} all-to-all(f32[4,256,128]{2,1,0:T(8,128)S(1)} %bitcast.4), channel_id=1, replica_groups=mesh['gz'=4,'gy'=2,'gx'=4] {'gz'}, dimensions={0} | all-to-all | bytes 1048576 | tf_op jit(solution)/shard_map/all_to_all | solution.py:536
  50.7 0.7 %compose.1 = f32[256,128]{1,0:T(8,128)} custom-call(f32[4,256,128]{2,1,0:T(8,128)S(1)} %all_to_all.5.part_ref), custom_call_target="tpu_custom_call" | custom-call | tf_op jit(solution)/shard_map/compose/pallas_call | solution.py:411
  (6 shorter events, 0.1 us)
Async XLA Ops:
  0.6 5.6 %copy-start.1 = (f32[32,16,128]{2,1,0:T(8,128)S(1)}, f32[32,16,128]{2,1,0:T(8,128)}, u32[]{:S(2)}) copy-start(f32[32,16,128]{2,1,0:T(8,128)} %kappa_ref.9) | copy-start | bytes 786436
  0.6 5.6 %copy-start = (f32[5,32,16,128]{3,2,1,0:T(8,128)S(1)}, f32[5,32,16,128]{3,2,1,0:T(8,128)}, u32[]{:S(2)}) copy-start(f32[5,32,16,128]{3,2,1,0:T(8,128)} %fields_ref.9) | copy-start | bytes 3932164
  2.4 6.5 %collective-permute-start = (f32[14,16,128]{2,1,0:T(8,128)}, f32[14,16,128]{2,1,0:T(8,128)S(1)}, u32[]{:S(2)}, u32[]{:S(2)}) collective-permute-start(f32[14,16,128]{2,1,0:T(8,128)} %get-tuple-element.16), channel_id=1, source_target_pairs={{0,8},{8,0},{16,24},{24,16},{1,9},{9,1},{17,25},{25,17},{2,10},{10... | collective-permute-start | bytes 344072 | tf_op jit(solution)/shard_map/ppermute | solution.py:432
  5.5 3.4 %collective-permute-start.1 = (f32[14,16,128]{2,1,0:T(8,128)}, f32[14,16,128]{2,1,0:T(8,128)S(1)}, u32[]{:S(2)}, u32[]{:S(2)}) collective-permute-start(f32[14,16,128]{2,1,0:T(8,128)} %get-tuple-element.17), channel_id=1, source_target_pairs={{8,16},{16,8},{9,17},{17,9},{10,18},{18,10},{11,19},{19,11},{12,20... | collective-permute-start | bytes 344072 | tf_op jit(solution)/shard_map/ppermute | solution.py:432
  6.4 7.7 %collective-permute-start.2 = (f32[14,32,128]{2,1,0:T(8,128)S(1)}, f32[14,32,128]{2,1,0:T(8,128)S(1)}, u32[]{:S(2)}, u32[]{:S(2)}) collective-permute-start(f32[14,32,128]{2,1,0:T(8,128)S(1)} %broadcast_select_fusion), channel_id=1, source_target_pairs={{0,4},{4,0},{1,5},{5,1},{2,6},{6,2},{3,7},{7,3},{8,12},{12,8},{9,1... | collective-permute-start | bytes 688136 | tf_op jit(solution)/shard_map/ppermute | solution.py:441
  8.9 8.9 %copy-start.8 = (f32[5,3]{0,1:T(4,128)S(1)}, f32[5,3]{0,1:T(4,128)}, u32[]{:S(2)}) copy-start(f32[5,3]{0,1:T(4,128)} %param.11) | copy-start | bytes 184
  9.0 9.8 %copy-start.2 = (s32[1,16,16,1]{2,3,1,0:T(1,128)S(1)}, s32[1,16,16,1]{2,3,1,0:T(1,128)}, u32[]{:S(2)}) copy-start(s32[1,16,16,1]{2,3,1,0:T(1,128)} %param.16) | copy-start | bytes 3076
  9.0 9.8 %copy-start.3 = (f32[3,16]{1,0:T(4,128)S(1)}, f32[3,16]{1,0:T(4,128)}, u32[]{:S(2)}) copy-start(f32[3,16]{1,0:T(4,128)} %color_ref.1) | copy-start | bytes 580
  9.0 9.8 %copy-start.4 = (s32[1,1,256]{2,1,0:T(1,128)S(1)}, s32[1,1,256]{2,1,0:T(1,128)}, u32[]{:S(2)}) copy-start(s32[1,1,256]{2,1,0:T(1,128)} %param.17) | copy-start | bytes 3076
  9.0 9.8 %copy-start.5 = (f32[16]{0:T(128)S(1)}, f32[16]{0:T(128)}, u32[]{:S(2)}) copy-start(f32[16]{0:T(128)} %center_ref.1) | copy-start | bytes 196
  9.0 9.8 %copy-start.6 = (f32[16]{0:T(128)S(1)}, f32[16]{0:T(128)}, u32[]{:S(2)}) copy-start(f32[16]{0:T(128)} %sharp_ref.1) | copy-start | bytes 196
  9.0 9.8 %copy-start.7 = (f32[16]{0:T(128)S(1)}, f32[16]{0:T(128)}, u32[]{:S(2)}) copy-start(f32[16]{0:T(128)} %gain_ref.1) | copy-start | bytes 196
  9.2 4.9 %collective-permute-start.3 = (f32[56,128]{1,0:T(8,128)S(1)}, f32[56,128]{1,0:T(8,128)S(1)}, u32[]{:S(2)}, u32[]{:S(2)}) collective-permute-start(f32[56,128]{1,0:T(8,128)S(1)} %broadcast_select_fusion.7), channel_id=1, source_target_pairs={{0,4},{4,0},{1,5},{5,1},{2,6},{6,2},{3,7},{7,3},{8,12},{12,8},{9,1... | collective-permute-start | bytes 86024 | tf_op jit(solution)/shard_map/ppermute | solution.py:441
  14.2 3.7 %collective-permute-start.5 = (f32[6,24,128]{2,1,0:T(8,128)S(1)}, f32[6,24,128]{2,1,0:T(8,128)S(1)}, u32[]{:S(2)}, u32[]{:S(2)}) collective-permute-start(f32[6,24,128]{2,1,0:T(8,128)S(1)} %get-tuple-element.34), channel_id=1, source_target_pairs={{1,2},{2,1},{5,6},{6,5},{9,10},{10,9},{13,14},{14,13},{17,18},{18,... | collective-permute-start | bytes 221192 | tf_op jit(solution)/shard_map/ppermute | solution.py:432
  14.9 3.9 %collective-permute-start.4 = (f32[6,24,128]{2,1,0:T(8,128)S(1)}, f32[6,24,128]{2,1,0:T(8,128)S(1)}, u32[]{:S(2)}, u32[]{:S(2)}) collective-permute-start(f32[6,24,128]{2,1,0:T(8,128)S(1)} %get-tuple-element.35), channel_id=1, source_target_pairs={{0,1},{1,0},{2,3},{3,2},{4,5},{5,4},{6,7},{7,6},{8,9},{9,8},{10,11... | collective-permute-start | bytes 221192 | tf_op jit(solution)/shard_map/ppermute | solution.py:432

commit v9 on v8

--- a/solution.py
+++ b/solution.py
@@ -112,7 +112,7 @@
             hi_ref[at : at + W, :] = pair[side][rows - W :]
 
 
-def assemble(refs, halo_rows, pad_ref):
+def assemble(refs, halo_rows, pad_ref, chosen):
     fields_ref, kappa_ref, zlo_ref, zhi_ref = refs
     nfield, depth_len, rows, lanes = fields_ref.shape
     planes, pitch = depth_len + 2 * W, rows + SUB
@@ -120,14 +120,15 @@
 
     @pl.loop(0, depth_len, unroll=steps(depth_len, 4))
     def _(z):
-        for field in range(nfield + 1):
-            plane = field * planes + W + z
+        for slot, field in enumerate(chosen):
+            plane = slot * planes + W + z
             pad_ref[plane, :rows, :] = kappa_ref[z] if field == nfield else fields_ref[field, z]
             pad_ref[plane, rows:, :] = halo
 
-    for field, at, wide in z_plan(nfield)[0]:
+    for slot, field in enumerate(chosen):
+        _, at, wide = z_plan(nfield)[0][field]
         for k in range(W):
-            below, above = field * planes + W - 1 - k, field * planes + W + depth_len + k
+            below, above = slot * planes + W - 1 - k, slot * planes + W + depth_len + k
             if k < wide:
                 pad_ref[below, :rows, :] = zlo_ref[at + wide - 1 - k]
                 pad_ref[above, :rows, :] = zhi_ref[at + k]
@@ -135,25 +136,24 @@
                 if k >= wide:
                     pad_ref[plane, :rows, :] = jnp.zeros((rows, lanes), F32)
                 pad_ref[plane, rows:, :] = halo
-    place_rows(pad_ref, depth_len, rows, halo_rows)
-
-
-def place_rows(pad_ref, depth_len, first_row, halo_rows):
-    planes = depth_len + 2 * W
     pitch, lanes = pad_ref.shape[1:]
     flat = pad_ref.reshape(pad_ref.shape[0] * pitch, lanes)
-    kinds, edges = y_plan(pad_ref.shape[0] // planes - 1)
+    kinds, edges = y_plan(nfield)
     for low, (ref, edge_ref) in ((True, halo_rows[:2]), (False, halo_rows[2:])):
         flag = present("gy")[0 if low else 1]
         for i, (field, away) in enumerate(kinds):
-            row = pitch - away if low else first_row + away - 1
+            if field not in chosen:
+                continue
+            row = pitch - away if low else rows + away - 1
             for z in range(0, depth_len, SUB):
-                flat[pl.ds((field * planes + W + z) * pitch + row, SUB, stride=pitch), :] = (
+                flat[pl.ds((chosen.index(field) * planes + W + z) * pitch + row, SUB, stride=pitch), :] = (
                     ref[i, z : z + SUB, :] * flag
                 )
         for i, (field, away, k) in enumerate(edges):
-            row = pitch - away if low else first_row + away - 1
-            plane = field * planes + W + (k if k < 0 else depth_len - 1 + k)
+            if field not in chosen:
+                continue
+            row = pitch - away if low else rows + away - 1
+            plane = chosen.index(field) * planes + W + (k if k < 0 else depth_len - 1 + k)
             pad_ref[plane, row : row + 1, :] = edge_ref[i : i + 1, :] * flag
 
 
@@ -210,6 +210,47 @@
     return coefs + [rest]
 
 
+def row_flags(shape, rows):
+    r = lax.broadcasted_iota(jnp.int32, shape, 0)
+    low, high = present("gy")
+    return jnp.where(r < rows, 1.0, jnp.where(r < rows + SUB // 2, high, low))
+
+
+def plane_flag(zi, depth_len):
+    low, high = present("gz")
+    return jnp.where(zi < W, low, jnp.where(zi >= W + depth_len, high, 1.0))
+
+
+def first_step_kernel(
+    courant_ref, fields_ref, kappa_ref, zlo_ref, zhi_ref, ylo_ref, elo_ref, yhi_ref, ehi_ref, *rest
+):
+    out_refs, pad_ref = rest[:-1], rest[-1]
+    nfield, depth_len, rows, lanes = fields_ref.shape
+    planes, pitch = depth_len + 2 * W, rows + SUB
+    refs, halo_rows = (fields_ref, kappa_ref, zlo_ref, zhi_ref), (ylo_ref, elo_ref, yhi_ref, ehi_ref)
+    assemble(refs, halo_rows, pad_ref, list(range(nfield + 1)))
+    lane = lax.broadcasted_iota(jnp.int32, (pitch, lanes), 1)
+    row_mask = row_flags((pitch, lanes), rows)
+    speed = [[courant_ref[f, a] for a in range(3)] for f in range(nfield)]
+
+    def around(field, zi):
+        plane = field * planes + zi
+        value = pad_ref[plane]
+        x_up = jnp.where(lane == lanes - 1, value, pltpu.roll(value, lanes - 1, 1))
+        x_down = jnp.where(lane == 0, value, pltpu.roll(value, 1, 1))
+        ups = (pad_ref[plane + 1], pltpu.roll(value, pitch - 1, 0), x_up)
+        downs = (pad_ref[plane - 1], pltpu.roll(value, 1, 0), x_down)
+        return value, ups, downs
+
+    @pl.loop(1, planes - 1, unroll=steps(planes - 2, 6))
+    def _(zi):
+        mask = row_mask * plane_flag(zi, depth_len)
+        coefs = weights(*around(nfield, zi))
+        for field in range(nfield):
+            u, ups, downs = around(field, zi)
+            out_refs[field][zi] = mask * stencil(u, coefs, ups, downs, speed[field])
+
+
 def side_neighbours(near, own, is_left, lanes, col):
     first, second = (near, own) if is_left else (own, near)
     first_up = jnp.where(col == W - 1, pltpu.roll(second, W - 1, 1), pltpu.roll(first, lanes - 1, 1))
@@ -223,19 +264,22 @@
 def main_kernel(
     courant_ref, center_ref, sharp_ref, gain_ref, color_ref, mask_ref, order_ref,
     fields_ref, kappa_ref, zlo_ref, zhi_ref,
-    ylo_ref, elo_ref, yhi_ref, ehi_ref, xlo_ref, xhi_ref, ownlo_ref, ownhi_ref,
-    state_ref, out_ref,
-    pad_ref, next_ref, last_ref, side_ref, edge_ref, base_ref, tile_ref, coef_ref, held_ref, sem,
+    ylo_ref, elo_ref, yhi_ref, ehi_ref, xlo_ref, xhi_ref, ownlo_ref, ownhi_ref, *rest,
 ):
+    nfield, depth_len, rows, lanes = fields_ref.shape
+    step_refs = rest[:nfield]
+    (
+        state_ref, out_ref, kpad_ref, next_ref, last_ref, side_ref, edge_ref, base_ref,
+        tile_ref, coef_ref, held_ref, flux_ref, sem,
+    ) = rest[nfield:]
     nfield, depth_len, rows, lanes = state_ref.shape
     planes, pitch = depth_len + 2 * W, rows + SUB
     lane = lax.broadcasted_iota(jnp.int32, (pitch, lanes), 1)
-    r = lax.broadcasted_iota(jnp.int32, (pitch, lanes), 0)
     zi_of = lane // W
     col = lane - zi_of * W
     flag = present("gz") + present("gy") + present("gx")
     speed = [[courant_ref[f, a] for a in range(3)] for f in range(nfield)]
-    row_mask = jnp.where(r < rows, 1.0, jnp.where(r < rows + SUB // 2, flag[3], flag[2]))
+    row_mask = row_flags((pitch, lanes), rows)
 
     def along_y(value):
         return pltpu.roll(value, pitch - 1, 0), pltpu.roll(value, 1, 0)
@@ -283,8 +327,8 @@
         down = jnp.where(lane[:n] == 0, turned, pltpu.roll(value, 1, 1))
         return up, down
 
-    def around(src_ref, level, field, zi, n):
-        plane = field * planes + zi
+    def around(src_ref, level, field, zi, n, slot=None):
+        plane = (field if slot is None else slot) * planes + zi
         whole = src_ref[plane]
         value = whole[:n]
         y_up, y_down = along_y(whole)
@@ -303,13 +347,18 @@
         found = [coef_ref[i, zi, :n, :] for i in range(7)]
         return [found[0:2], found[2:4], found[4:6], found[6]]
 
-    def depth_mask(zi):
-        return jnp.where(zi < W, flag[0], jnp.where(zi >= W + depth_len, flag[1], 1.0))
-
     halo_rows = (ylo_ref, elo_ref, yhi_ref, ehi_ref)
-    assemble((fields_ref, kappa_ref, zlo_ref, zhi_ref), halo_rows, pad_ref)
-    for field in range(nfield + 1):
-        edges(0, field)
+    assemble((fields_ref, kappa_ref, zlo_ref, zhi_ref), halo_rows, kpad_ref, [nfield])
+    edges(0, nfield)
+    lane_mask = row_mask * jnp.where(
+        zi_of < W, flag[0], jnp.where(zi_of >= W + depth_len, flag[1], 1.0)
+    )
+    k_left = 0.5 * (xlo_ref[nfield] + pltpu.roll(ownlo_ref[nfield], W - 1, 1))
+    k_right = 0.5 * (xhi_ref[nfield] + pltpu.roll(ownhi_ref[nfield], lanes - (W - 1), 1))
+    for field in range(nfield):
+        left = (k_left + speed[field][2]) * (xlo_ref[field] - pltpu.roll(ownlo_ref[field], W - 1, 1))
+        right = k_right * (xhi_ref[field] - pltpu.roll(ownhi_ref[field], lanes - (W - 1), 1))
+        flux_ref[field] = lane_mask * jnp.where(col == W - 1, left, pltpu.roll(right, 1, 1))
     side_step(0, nfield)
     for field in range(nfield):
         edges(1, field)
@@ -318,17 +367,18 @@
 
     @pl.loop(1, planes - 1, unroll=steps(planes - 2, 6))
     def _(zi):
-        mask = row_mask * depth_mask(zi)
-        coefs = weights(*around(pad_ref, 0, nfield, zi, pitch))
+        coefs = weights(*around(kpad_ref, 0, nfield, zi, pitch, 0))
         for i, value in enumerate(sum(coefs[:3], ()) + (coefs[3],)):
             coef_ref[i, zi] = value
+        outer = (lane == 0) | (lane == lanes - 1)
         for field in range(nfield):
-            next_ref[field * planes + zi] = mask * step_value(pad_ref, 0, field, zi, pitch, coefs)
+            turned = pltpu.roll(flux_ref[field], lax.rem(2 * lanes - 2 - W * zi, lanes), 1)
+            next_ref[field * planes + zi] = step_refs[field][zi] + jnp.where(outer, turned, 0.0)
 
     @pl.loop(2, planes - 2, unroll=steps(planes - 4, 17))
     def _(zi):
         coefs = kept(zi, pitch)
-        last_ref[zi] = step_value(next_ref, 1, 0, zi, pitch, coefs) * (row_mask * depth_mask(zi))
+        last_ref[zi] = step_value(next_ref, 1, 0, zi, pitch, coefs) * (row_mask * plane_flag(zi, depth_len))
 
     @pl.loop(0, depth_len, unroll=steps(depth_len, 8))
     def _(z):
@@ -506,16 +556,26 @@
     )(elo, ehi, main_lo, main_hi, ylo)
     odd = is_odd("gx")
     xlo, xhi = swap_pairs(jnp.where(odd, own_lo, own_hi), jnp.where(odd, own_hi, own_lo), "gx")
+    stepped = pl.pallas_call(
+        first_step_kernel,
+        out_shape=(array(planes, pitch, cols_len),) * nfield,
+        in_specs=[smem] + [vmem] * 8,
+        out_specs=(vmem,) * nfield,
+        scratch_shapes=[pad],
+        compiler_params=params,
+        cost_estimate=pl.CostEstimate(flops=10**8, bytes_accessed=8 * 10**6, transcendentals=0),
+        name="first_step",
+    )(courant, fields, diffusivity, zlo, zhi, ylo, elo, yhi, ehi)
     count = lax.axis_size("gz")
     order = tile_perm[0, 0]
     per_owner = order.shape[0] // count
     state, tiles = pl.pallas_call(
         main_kernel,
         out_shape=(array(*fields.shape), array(order.shape[0], 4, cols_len)),
-        in_specs=[smem] * 7 + [vmem] * 12,
+        in_specs=[smem] * 7 + [vmem] * (12 + nfield),
         out_specs=(pl.BlockSpec(memory_space=pl.ANY), vmem),
         scratch_shapes=[
-            pad,
+            pltpu.VMEM((planes, pitch, cols_len), F32),
             pltpu.VMEM((nfield * planes, pitch, cols_len), F32),
             pltpu.VMEM((planes, pitch, cols_len), F32),
             pltpu.VMEM((2, 2, 2, nfield, pitch, cols_len), F32),
@@ -524,6 +584,7 @@
             pltpu.VMEM((order.shape[0] * 4, cols_len), F32),
             pltpu.VMEM((7, planes, pitch, cols_len), F32),
             pltpu.VMEM(fields.shape, F32),
+            pltpu.VMEM((nfield, pitch, cols_len), F32),
             pltpu.SemaphoreType.DMA(()),
         ],
         compiler_params=pltpu.CompilerParams(vmem_limit_bytes=24 * 1024 * 1024),
@@ -531,6 +592,7 @@
     )(
         courant, tf_center, tf_sharp, tf_gain, tf_color, tile_mask[0, :, :, 0], order,
         fields, diffusivity, zlo, zhi, ylo, elo, yhi, ehi, xlo, xhi, own_lo, own_hi,
+        *stepped,
     )
     grouped = tiles.reshape(count, per_owner * 4, cols_len)
     composed = compose(lax.all_to_all(grouped, "gz", split_axis=0, concat_axis=0, tiled=True))

time: 51.6 us -> 51.4 us (level)
  Pallas kernels: 13.7 us -> 15.4 us
  blocking collectives: 21.9 us -> 20.8 us
  waiting for transfers between devices: 4.06 us -> 3.32 us
    pallas_call x0 -> x1, Pallas kernels: none -> 3.25 us  [shards(): pl.pallas_call(first_step_kernel, out_shape=(array(planes, pitch, cols_le...]
    pallas_call x1, Pallas kernels: 9.97 us -> 8.47 us  [shards(): pl.pallas_call(main_kernel, out_shape=(array(*fields.shape), array(order....]
    all_to_all x1, blocking collectives: 21.9 us -> 20.8 us  [shards(): lax.all_to_all(grouped, 'gz', split_axis=0, concat_axis=0, tiled=True)]
    ppermute x4, waiting for transfers between devices: 0.82 us -> 0.01 us  [swap_pairs(): lax.ppermute(message, axis, pairs)]
  transfers between devices with their start and end apart: 6 -> 6, of which waited for: 2 -> 1; matrix products, arithmetic and copies ran while one was open for 0% -> 0% of each run, Pallas kernels for 2% -> 9%
where the time goes in v9:
time: 51.4 us; the launch traced here: 51.2 us
  blocking collectives  20.8 us (40%)
  Pallas kernels  15.4 us (30%)
  starting transfers between devices  10.6 us (21%)
  waiting for transfers between devices  3.32 us (6%)
  between operations  0.88 us (2%)
    all_to_all x1, blocking collectives, shards(): lax.all_to_all(grouped, 'gz', split_axis=0, concat_axis=0, tiled=True)  20.8 us
    pallas_call x1, Pallas kernels, shards(): pl.pallas_call(main_kernel, out_shape=(array(*fields.shape), array(order....  8.47 us
    ppermute x4, starting transfers between devices, swap_pairs(): lax.ppermute(message, axis, pairs)  7.35 us
    ppermute x2, waiting for transfers between devices, swap_rows(): came = lax.ppermute(first, axis, [(0, 1), (1, 0)])  3.31 us
    pallas_call x1, Pallas kernels, shards(): pl.pallas_call(first_step_kernel, out_shape=(array(planes, pitch, cols_le...  3.25 us
    ppermute x2, starting transfers between devices, swap_rows(): came = lax.ppermute(first, axis, [(0, 1), (1, 0)])  3.25 us
    pallas_call x1, Pallas kernels, shards(): pl.pallas_call(pack_planes_kernel, out_shape=(array(faces, rows_len, cols...  1.78 us
  transfers between devices with their start and end apart: 6, of which 1 were waited for; matrix products, arithmetic and copies ran while one was open for 0% of the time, Pallas kernels for 9%

profile of v9, /device:TPU:0, one launch (start us, length us, event | category | flops | bytes accessed | tf_op | source)
XLA Modules:
  0.0 51.2 jit_solution(8971346287706234299)
XLA Ops:
  0.6 0.0 copy-start.1
  0.6 0.0 copy-start
  0.6 1.8 %pack_planes.1 = (f32[14,16,128]{2,1,0:T(8,128)}, f32[14,16,128]{2,1,0:T(8,128)}) custom-call(f32[5,32,16,128]{3,2,1,0:T(8,128)} %fields_ref.11, f32[32,16,128]{2,1,0:T(8,128)} %kappa_ref.11), custom_call_target="tpu_custom_call" | custom-call | tf_op jit(solution)/shard_map/pack_planes/pallas_call | solution.py:509
  2.4 3.1 %collective-permute-start = (f32[14,16,128]{2,1,0:T(8,128)}, f32[14,16,128]{2,1,0:T(8,128)S(1)}, u32[]{:S(2)}, u32[]{:S(2)}) collective-permute-start(f32[14,16,128]{2,1,0:T(8,128)} %get-tuple-element.21), channel_id=1, source_target_pairs={{0,8},{8,0},{16,24},{24,16},{1,9},{9,1},{17,25},{25,17},{2,10},{10... | collective-permute-start | bytes 344072 | tf_op jit(solution)/shard_map/ppermute | solution.py:482
  5.5 0.7 %collective-permute-start.1 = (f32[14,16,128]{2,1,0:T(8,128)}, f32[14,16,128]{2,1,0:T(8,128)S(1)}, u32[]{:S(2)}, u32[]{:S(2)}) collective-permute-start(f32[14,16,128]{2,1,0:T(8,128)} %get-tuple-element.22), channel_id=1, source_target_pairs={{8,16},{16,8},{9,17},{17,9},{10,18},{18,10},{11,19},{19,11},{12,20... | collective-permute-start | bytes 344072 | tf_op jit(solution)/shard_map/ppermute | solution.py:482
  6.2 0.0 copy-done.1
  6.2 0.0 copy-done
  6.2 0.1 pack_rows.1
  6.4 1.6 %collective-permute-start.2 = (f32[14,32,128]{2,1,0:T(8,128)S(1)}, f32[14,32,128]{2,1,0:T(8,128)S(1)}, u32[]{:S(2)}, u32[]{:S(2)}) collective-permute-start(f32[14,32,128]{2,1,0:T(8,128)S(1)} %broadcast_select_fusion), channel_id=1, source_target_pairs={{0,4},{4,0},{1,5},{5,1},{2,6},{6,2},{3,7},{7,3},{8,12},{12,8},{9,1... | collective-permute-start | bytes 688136 | tf_op jit(solution)/shard_map/ppermute | solution.py:491
  8.0 0.9 %pack_own.1 = (f32[6,16,128]{2,1,0:T(8,128)S(1)}, f32[6,16,128]{2,1,0:T(8,128)S(1)}) custom-call(f32[5,32,16,128]{3,2,1,0:T(8,128)S(1)} %copy-done, f32[32,16,128]{2,1,0:T(8,128)S(1)} %copy-done.1), custom_call_target="tpu_custom_call" | custom-call | flops 10000000 | bytes 4000000 | tf_op jit(solution)/shard_map/pack_own/pallas_call | solution.py:529
  8.9 0.0 collective-permute-done
  8.9 0.0 collective-permute-done.1
  8.9 0.0 copy-start.8
  9.0 0.2 pack_edges.1
  9.2 1.7 %collective-permute-start.3 = (f32[56,128]{1,0:T(8,128)S(1)}, f32[56,128]{1,0:T(8,128)S(1)}, u32[]{:S(2)}, u32[]{:S(2)}) collective-permute-start(f32[56,128]{1,0:T(8,128)S(1)} %broadcast_select_fusion.7), channel_id=1, source_target_pairs={{0,4},{4,0},{1,5},{5,1},{2,6},{6,2},{3,7},{7,3},{8,12},{12,8},{9,1... | collective-permute-start | bytes 86024 | tf_op jit(solution)/shard_map/ppermute | solution.py:491
  10.8 3.3 %collective-permute-done.3.elo_ref.ehi_ref = f32[56,128]{1,0:T(8,128)S(1)} collective-permute-done((f32[56,128]{1,0:T(8,128)S(1)}, f32[56,128]{1,0:T(8,128)S(1)}, u32[]{:S(2)}, u32[]{:S(2)}) %collective-permute-start.3) | collective-permute-done | bytes 28704 | tf_op jit(solution)/shard_map/ppermute | solution.py:491
  14.2 0.0 collective-permute-done.2.rows_ref.ylo_ref.yhi_ref
  14.2 0.7 %collective-permute-start.5 = (f32[6,24,128]{2,1,0:T(8,128)S(1)}, f32[6,24,128]{2,1,0:T(8,128)S(1)}, u32[]{:S(2)}, u32[]{:S(2)}) collective-permute-start(f32[6,24,128]{2,1,0:T(8,128)S(1)} %get-tuple-element.44), channel_id=1, source_target_pairs={{1,2},{2,1},{5,6},{6,5},{9,10},{10,9},{13,14},{14,13},{17,18},{18,... | collective-permute-start | bytes 221192 | tf_op jit(solution)/shard_map/ppermute | solution.py:482
  14.9 2.9 %collective-permute-start.4 = (f32[6,24,128]{2,1,0:T(8,128)S(1)}, f32[6,24,128]{2,1,0:T(8,128)S(1)}, u32[]{:S(2)}, u32[]{:S(2)}) collective-permute-start(f32[6,24,128]{2,1,0:T(8,128)S(1)} %get-tuple-element.45), channel_id=1, source_target_pairs={{0,1},{1,0},{2,3},{3,2},{4,5},{5,4},{6,7},{7,6},{8,9},{9,8},{10,11... | collective-permute-start | bytes 221192 | tf_op jit(solution)/shard_map/ppermute | solution.py:482
  17.8 0.0 copy-done.8
  17.8 0.1 copy.12.courant_ref
  17.9 0.0 copy-start.2
  17.9 0.0 copy-start.3
  17.9 0.0 copy-start.4
  17.9 0.0 copy-start.5
  17.9 0.0 copy-start.6
  17.9 0.0 copy-start.7
  17.9 3.2 %first_step.1 = (f32[38,24,128]{2,1,0:T(8,128)S(1)}, f32[38,24,128]{2,1,0:T(8,128)S(1)}, f32[38,24,128]{2,1,0:T(8,128)S(1)}, f32[38,24,128]{2,1,0:T(8,128)S(1)}, f32[38,24,128]{2,1,0:T(8,128)S(1)}) custom-call(f32[5,3]{1,0:T(8,128)S(1)} %copy.12.courant_ref, f32[5,32,16,128]{3,2,1,0:T(8,128)S(1)} %copy-done, f32[32,16,128]{2,1,0:T(8,128)S(1)} %copy-done.1, ...), custom_call_target="tpu_custom_call" | custom-call | flops 100000000 | bytes 8000000 | tf_op jit(solution)/shard_map/first_step/pallas_call | solution.py:559
  21.2 0.0 collective-permute-done.5
  21.2 0.0 collective-permute-done.4
  21.2 0.0 copy-done.2
  21.3 0.0 copy-done.3
  21.3 0.0 copy-done.4
  21.3 0.0 copy-done.5
  21.3 0.0 copy-done.6
  21.3 0.0 copy-done.7
  21.3 8.5 %step_and_march.1 = (f32[5,32,16,128]{3,2,1,0:T(8,128)}, f32[256,4,128]{2,1,0:T(4,128)S(1)}) custom-call(f32[5,3]{1,0:T(8,128)S(1)} %copy.12.courant_ref, f32[16]{0:T(128)S(1)} %copy-done.5, f32[16]{0:T(128)S(1)} %copy-done.6, f32[16]{0:T(128)S(1)} %copy-done.7, f32[3,16]{1,0:T(4,128)S(1)} %copy-done.3, s32[16,16]{1,0:T(8,128)S(1)} %bitcast.5, ...), custom_call_target="tpu_custom_call" | custom-call | tf_op jit(solution)/shard_map/step_and_march/pallas_call | solution.py:572
  29.8 20.8 %all_to_all.5.part_ref = f32[4,256,128]{2,1,0:T(8,128)S(1)} all-to-all(f32[4,256,128]{2,1,0:T(8,128)S(1)} %bitcast.4), channel_id=1, replica_groups=mesh['gz'=4,'gy'=2,'gx'=4] {'gz'}, dimensions={0} | all-to-all | bytes 1048576 | tf_op jit(solution)/shard_map/all_to_all | solution.py:598
  50.6 0.7 %compose.1 = f32[256,128]{1,0:T(8,128)} custom-call(f32[4,256,128]{2,1,0:T(8,128)S(1)} %all_to_all.5.part_ref), custom_call_target="tpu_custom_call" | custom-call | tf_op jit(solution)/shard_map/compose/pallas_call | solution.py:461
  (6 shorter events, 0.1 us)
Async XLA Ops:
  0.6 5.6 %copy-start.1 = (f32[32,16,128]{2,1,0:T(8,128)S(1)}, f32[32,16,128]{2,1,0:T(8,128)}, u32[]{:S(2)}) copy-start(f32[32,16,128]{2,1,0:T(8,128)} %kappa_ref.11) | copy-start | bytes 786436
  0.6 5.6 %copy-start = (f32[5,32,16,128]{3,2,1,0:T(8,128)S(1)}, f32[5,32,16,128]{3,2,1,0:T(8,128)}, u32[]{:S(2)}) copy-start(f32[5,32,16,128]{3,2,1,0:T(8,128)} %fields_ref.11) | copy-start | bytes 3932164
  2.4 6.5 %collective-permute-start = (f32[14,16,128]{2,1,0:T(8,128)}, f32[14,16,128]{2,1,0:T(8,128)S(1)}, u32[]{:S(2)}, u32[]{:S(2)}) collective-permute-start(f32[14,16,128]{2,1,0:T(8,128)} %get-tuple-element.21), channel_id=1, source_target_pairs={{0,8},{8,0},{16,24},{24,16},{1,9},{9,1},{17,25},{25,17},{2,10},{10... | collective-permute-start | bytes 344072 | tf_op jit(solution)/shard_map/ppermute | solution.py:482
  5.5 3.4 %collective-permute-start.1 = (f32[14,16,128]{2,1,0:T(8,128)}, f32[14,16,128]{2,1,0:T(8,128)S(1)}, u32[]{:S(2)}, u32[]{:S(2)}) collective-permute-start(f32[14,16,128]{2,1,0:T(8,128)} %get-tuple-element.22), channel_id=1, source_target_pairs={{8,16},{16,8},{9,17},{17,9},{10,18},{18,10},{11,19},{19,11},{12,20... | collective-permute-start | bytes 344072 | tf_op jit(solution)/shard_map/ppermute | solution.py:482
  6.4 7.7 %collective-permute-start.2 = (f32[14,32,128]{2,1,0:T(8,128)S(1)}, f32[14,32,128]{2,1,0:T(8,128)S(1)}, u32[]{:S(2)}, u32[]{:S(2)}) collective-permute-start(f32[14,32,128]{2,1,0:T(8,128)S(1)} %broadcast_select_fusion), channel_id=1, source_target_pairs={{0,4},{4,0},{1,5},{5,1},{2,6},{6,2},{3,7},{7,3},{8,12},{12,8},{9,1... | collective-permute-start | bytes 688136 | tf_op jit(solution)/shard_map/ppermute | solution.py:491
  8.9 8.9 %copy-start.8 = (f32[5,3]{0,1:T(4,128)S(1)}, f32[5,3]{0,1:T(4,128)}, u32[]{:S(2)}) copy-start(f32[5,3]{0,1:T(4,128)} %param.11) | copy-start | bytes 184
  9.2 5.0 %collective-permute-start.3 = (f32[56,128]{1,0:T(8,128)S(1)}, f32[56,128]{1,0:T(8,128)S(1)}, u32[]{:S(2)}, u32[]{:S(2)}) collective-permute-start(f32[56,128]{1,0:T(8,128)S(1)} %broadcast_select_fusion.7), channel_id=1, source_target_pairs={{0,4},{4,0},{1,5},{5,1},{2,6},{6,2},{3,7},{7,3},{8,12},{12,8},{9,1... | collective-permute-start | bytes 86024 | tf_op jit(solution)/shard_map/ppermute | solution.py:491
  14.2 7.0 %collective-permute-start.5 = (f32[6,24,128]{2,1,0:T(8,128)S(1)}, f32[6,24,128]{2,1,0:T(8,128)S(1)}, u32[]{:S(2)}, u32[]{:S(2)}) collective-permute-start(f32[6,24,128]{2,1,0:T(8,128)S(1)} %get-tuple-element.44), channel_id=1, source_target_pairs={{1,2},{2,1},{5,6},{6,5},{9,10},{10,9},{13,14},{14,13},{17,18},{18,... | collective-permute-start | bytes 221192 | tf_op jit(solution)/shard_map/ppermute | solution.py:482
  14.9 6.3 %collective-permute-start.4 = (f32[6,24,128]{2,1,0:T(8,128)S(1)}, f32[6,24,128]{2,1,0:T(8,128)S(1)}, u32[]{:S(2)}, u32[]{:S(2)}) collective-permute-start(f32[6,24,128]{2,1,0:T(8,128)S(1)} %get-tuple-element.45), channel_id=1, source_target_pairs={{0,1},{1,0},{2,3},{3,2},{4,5},{5,4},{6,7},{7,6},{8,9},{9,8},{10,11... | collective-permute-start | bytes 221192 | tf_op jit(solution)/shard_map/ppermute | solution.py:482
  17.9 3.3 %copy-start.2 = (s32[1,16,16,1]{2,3,1,0:T(1,128)S(1)}, s32[1,16,16,1]{2,3,1,0:T(1,128)}, u32[]{:S(2)}) copy-start(s32[1,16,16,1]{2,3,1,0:T(1,128)} %param.16) | copy-start | bytes 3076
  17.9 3.3 %copy-start.3 = (f32[3,16]{1,0:T(4,128)S(1)}, f32[3,16]{1,0:T(4,128)}, u32[]{:S(2)}) copy-start(f32[3,16]{1,0:T(4,128)} %color_ref.1) | copy-start | bytes 580
  17.9 3.4 %copy-start.4 = (s32[1,1,256]{2,1,0:T(1,128)S(1)}, s32[1,1,256]{2,1,0:T(1,128)}, u32[]{:S(2)}) copy-start(s32[1,1,256]{2,1,0:T(1,128)} %param.17) | copy-start | bytes 3076
  17.9 3.4 %copy-start.5 = (f32[16]{0:T(128)S(1)}, f32[16]{0:T(128)}, u32[]{:S(2)}) copy-start(f32[16]{0:T(128)} %center_ref.1) | copy-start | bytes 196
  17.9 3.4 %copy-start.6 = (f32[16]{0:T(128)S(1)}, f32[16]{0:T(128)}, u32[]{:S(2)}) copy-start(f32[16]{0:T(128)} %sharp_ref.1) | copy-start | bytes 196
  17.9 3.4 %copy-start.7 = (f32[16]{0:T(128)S(1)}, f32[16]{0:T(128)}, u32[]{:S(2)}) copy-start(f32[16]{0:T(128)} %gain_ref.1) | copy-start | bytes 196

commit v10 on v9

--- a/solution.py
+++ b/solution.py
@@ -224,7 +224,7 @@
 def first_step_kernel(
     courant_ref, fields_ref, kappa_ref, zlo_ref, zhi_ref, ylo_ref, elo_ref, yhi_ref, ehi_ref, *rest
 ):
-    out_refs, pad_ref = rest[:-1], rest[-1]
+    out_refs, coef_ref, pad_ref = rest[:-2], rest[-2], rest[-1]
     nfield, depth_len, rows, lanes = fields_ref.shape
     planes, pitch = depth_len + 2 * W, rows + SUB
     refs, halo_rows = (fields_ref, kappa_ref, zlo_ref, zhi_ref), (ylo_ref, elo_ref, yhi_ref, ehi_ref)
@@ -246,6 +246,8 @@
     def _(zi):
         mask = row_mask * plane_flag(zi, depth_len)
         coefs = weights(*around(nfield, zi))
+        for i, value in enumerate(sum(coefs[:3], ()) + (coefs[3],)):
+            coef_ref[i, zi] = value
         for field in range(nfield):
             u, ups, downs = around(field, zi)
             out_refs[field][zi] = mask * stencil(u, coefs, ups, downs, speed[field])
@@ -263,16 +265,15 @@
 
 def main_kernel(
     courant_ref, center_ref, sharp_ref, gain_ref, color_ref, mask_ref, order_ref,
-    fields_ref, kappa_ref, zlo_ref, zhi_ref,
-    ylo_ref, elo_ref, yhi_ref, ehi_ref, xlo_ref, xhi_ref, ownlo_ref, ownhi_ref, *rest,
+    xlo_ref, xhi_ref, ownlo_ref, ownhi_ref, coef_ref, *rest,
 ):
-    nfield, depth_len, rows, lanes = fields_ref.shape
+    nfield = courant_ref.shape[0]
     step_refs = rest[:nfield]
     (
-        state_ref, out_ref, kpad_ref, next_ref, last_ref, side_ref, edge_ref, base_ref,
-        tile_ref, coef_ref, held_ref, flux_ref, sem,
+        state_ref, out_ref, next_ref, last_ref, side_ref, edge_ref, base_ref, tile_ref, held_ref,
+        flux_ref, sem,
     ) = rest[nfield:]
-    nfield, depth_len, rows, lanes = state_ref.shape
+    _, depth_len, rows, lanes = held_ref.shape
     planes, pitch = depth_len + 2 * W, rows + SUB
     lane = lax.broadcasted_iota(jnp.int32, (pitch, lanes), 1)
     zi_of = lane // W
@@ -291,9 +292,11 @@
             return sides[side][block][field]
         return side_ref[level - 1, side, block, field]
 
-    def edges(level, field):
-        left, right = block_of(level, 0, 0, field), block_of(level, 1, 0, field)
-        edge_ref[level, field] = jnp.where(col == W - 1, left, pltpu.roll(right, 1, 1))
+    def fluxes(level, field, masks):
+        near, own = [[block_of(level, side, block, field) for side in (0, 1)] for block in (0, 1)]
+        left = (k_left + speed[field][2]) * (near[0] - pltpu.roll(own[0], W - 1, 1))
+        right = k_right * (near[1] - pltpu.roll(own[1], lanes - (W - 1), 1))
+        flux_ref[level, field] = masks * jnp.where(col == W - 1, left, pltpu.roll(right, 1, 1))
 
     def side_step(level, count):
         zmask = row_mask * jnp.where(
@@ -320,78 +323,71 @@
                     value = stencil(u, coefs[block], ups, downs, speed[field])
                     side_ref[level, side, block, field] = value * (zmask * present if block == 0 else zmask)
 
-    def along_x(value, zi, edge):
-        n = value.shape[0]
-        turned = pltpu.roll(edge, lax.rem(2 * lanes - 2 - W * zi, lanes), 1)
-        up = jnp.where(lane[:n] == lanes - 1, turned, pltpu.roll(value, lanes - 1, 1))
-        down = jnp.where(lane[:n] == 0, turned, pltpu.roll(value, 1, 1))
-        return up, down
-
-    def around(src_ref, level, field, zi, n, slot=None):
-        plane = (field if slot is None else slot) * planes + zi
-        whole = src_ref[plane]
-        value = whole[:n]
+    def turned(packed, zi, n):
+        return pltpu.roll(packed[:n], lax.rem(2 * lanes - 2 - W * zi, lanes), 1)
+
+    def step_value(field, zi, n, coefs):
+        plane = field * planes + zi
+        whole = next_ref[plane]
+        u = whole[:n]
         y_up, y_down = along_y(whole)
-        x_up, x_down = along_x(value, zi, edge_ref[level, field, :n, :])
-        return (
-            value,
-            (src_ref[plane + 1, :n, :], y_up[:n], x_up),
-            (src_ref[plane - 1, :n, :], y_down[:n], x_down),
-        )
-
-    def step_value(src_ref, level, field, zi, n, coefs):
-        u, ups, downs = around(src_ref, level, field, zi, n)
-        return stencil(u, coefs, ups, downs, speed[field])
+        x_up = jnp.where(lane[:n] == lanes - 1, u, pltpu.roll(u, lanes - 1, 1))
+        x_down = jnp.where(lane[:n] == 0, u, pltpu.roll(u, 1, 1))
+        ups = (next_ref[plane + 1, :n, :], y_up[:n], x_up)
+        downs = (next_ref[plane - 1, :n, :], y_down[:n], x_down)
+        inner = stencil(u, coefs, ups, downs, speed[field])
+        return inner + jnp.where(outer[:n], turned(flux_ref[1, field], zi, n), 0.0)
 
     def kept(zi, n):
         found = [coef_ref[i, zi, :n, :] for i in range(7)]
         return [found[0:2], found[2:4], found[4:6], found[6]]
 
-    halo_rows = (ylo_ref, elo_ref, yhi_ref, ehi_ref)
-    assemble((fields_ref, kappa_ref, zlo_ref, zhi_ref), halo_rows, kpad_ref, [nfield])
-    edges(0, nfield)
+    outer = (lane == 0) | (lane == lanes - 1)
     lane_mask = row_mask * jnp.where(
         zi_of < W, flag[0], jnp.where(zi_of >= W + depth_len, flag[1], 1.0)
     )
     k_left = 0.5 * (xlo_ref[nfield] + pltpu.roll(ownlo_ref[nfield], W - 1, 1))
     k_right = 0.5 * (xhi_ref[nfield] + pltpu.roll(ownhi_ref[nfield], lanes - (W - 1), 1))
     for field in range(nfield):
-        left = (k_left + speed[field][2]) * (xlo_ref[field] - pltpu.roll(ownlo_ref[field], W - 1, 1))
-        right = k_right * (xhi_ref[field] - pltpu.roll(ownhi_ref[field], lanes - (W - 1), 1))
-        flux_ref[field] = lane_mask * jnp.where(col == W - 1, left, pltpu.roll(right, 1, 1))
+        fluxes(0, field, lane_mask)
     side_step(0, nfield)
     for field in range(nfield):
-        edges(1, field)
+        fluxes(1, field, lane_mask)
     side_step(1, 1)
-    edges(2, 0)
+    left, right = block_of(2, 0, 0, 0), block_of(2, 1, 0, 0)
+    edge_ref[...] = jnp.where(col == W - 1, left, pltpu.roll(right, 1, 1))
 
     @pl.loop(1, planes - 1, unroll=steps(planes - 2, 6))
     def _(zi):
-        coefs = weights(*around(kpad_ref, 0, nfield, zi, pitch, 0))
-        for i, value in enumerate(sum(coefs[:3], ()) + (coefs[3],)):
-            coef_ref[i, zi] = value
-        outer = (lane == 0) | (lane == lanes - 1)
         for field in range(nfield):
-            turned = pltpu.roll(flux_ref[field], lax.rem(2 * lanes - 2 - W * zi, lanes), 1)
-            next_ref[field * planes + zi] = step_refs[field][zi] + jnp.where(outer, turned, 0.0)
+            next_ref[field * planes + zi] = step_refs[field][zi] + jnp.where(
+                outer, turned(flux_ref[0, field], zi, pitch), 0.0
+            )
 
     @pl.loop(2, planes - 2, unroll=steps(planes - 4, 17))
     def _(zi):
         coefs = kept(zi, pitch)
-        last_ref[zi] = step_value(next_ref, 1, 0, zi, pitch, coefs) * (row_mask * plane_flag(zi, depth_len))
+        last_ref[zi] = step_value(0, zi, pitch, coefs) * (row_mask * plane_flag(zi, depth_len))
 
     @pl.loop(0, depth_len, unroll=steps(depth_len, 8))
     def _(z):
         zi = z + W
         coefs = kept(zi, rows)
-        s, ups, downs = around(last_ref, 2, 0, zi, rows)
+        whole = last_ref[zi]
+        s = whole[:rows]
         held_ref[0, z] = s
-        g_z, g_y, g_x = [0.5 * (ups[a] - downs[a]) for a in range(3)]
+        y_up, y_down = along_y(whole)
+        beside = turned(edge_ref[...], zi, rows)
+        x_up = jnp.where(lane[:rows] == lanes - 1, beside, pltpu.roll(s, lanes - 1, 1))
+        x_down = jnp.where(lane[:rows] == 0, beside, pltpu.roll(s, 1, 1))
+        g_z = 0.5 * (last_ref[zi + 1, :rows, :] - last_ref[zi - 1, :rows, :])
+        g_y = 0.5 * (y_up[:rows] - y_down[:rows])
+        g_x = 0.5 * (x_up - x_down)
         shade = 0.35 + 0.65 * jnp.abs(0.64 * g_z + 0.6 * g_y + 0.48 * g_x) * lax.rsqrt(
             g_z * g_z + g_y * g_y + g_x * g_x + 1.0
         )
         for field in range(1, nfield):
-            value = step_value(next_ref, 1, field, zi, rows, coefs)
+            value = step_value(field, zi, rows, coefs)
             held_ref[field, z] = value
             if field <= 3:
                 base_ref[field, z] = shade * (0.5 + 0.5 * jnp.tanh(0.5 * value))
@@ -556,11 +552,11 @@
     )(elo, ehi, main_lo, main_hi, ylo)
     odd = is_odd("gx")
     xlo, xhi = swap_pairs(jnp.where(odd, own_lo, own_hi), jnp.where(odd, own_hi, own_lo), "gx")
-    stepped = pl.pallas_call(
+    *stepped, coefs = pl.pallas_call(
         first_step_kernel,
-        out_shape=(array(planes, pitch, cols_len),) * nfield,
+        out_shape=(array(planes, pitch, cols_len),) * nfield + (array(7, planes, pitch, cols_len),),
         in_specs=[smem] + [vmem] * 8,
-        out_specs=(vmem,) * nfield,
+        out_specs=(vmem,) * (nfield + 1),
         scratch_shapes=[pad],
         compiler_params=params,
         cost_estimate=pl.CostEstimate(flops=10**8, bytes_accessed=8 * 10**6, transcendentals=0),
@@ -572,26 +568,24 @@
     state, tiles = pl.pallas_call(
         main_kernel,
         out_shape=(array(*fields.shape), array(order.shape[0], 4, cols_len)),
-        in_specs=[smem] * 7 + [vmem] * (12 + nfield),
+        in_specs=[smem] * 7 + [vmem] * (5 + nfield),
         out_specs=(pl.BlockSpec(memory_space=pl.ANY), vmem),
         scratch_shapes=[
-            pltpu.VMEM((planes, pitch, cols_len), F32),
             pltpu.VMEM((nfield * planes, pitch, cols_len), F32),
             pltpu.VMEM((planes, pitch, cols_len), F32),
             pltpu.VMEM((2, 2, 2, nfield, pitch, cols_len), F32),
-            pltpu.VMEM((3, nfield + 1, pitch, cols_len), F32),
+            pltpu.VMEM((pitch, cols_len), F32),
             pltpu.VMEM((4, depth_len, rows_len, cols_len), F32),
             pltpu.VMEM((order.shape[0] * 4, cols_len), F32),
-            pltpu.VMEM((7, planes, pitch, cols_len), F32),
             pltpu.VMEM(fields.shape, F32),
-            pltpu.VMEM((nfield, pitch, cols_len), F32),
+            pltpu.VMEM((2, nfield, pitch, cols_len), F32),
             pltpu.SemaphoreType.DMA(()),
         ],
         compiler_params=pltpu.CompilerParams(vmem_limit_bytes=24 * 1024 * 1024),
         name="step_and_march",
     )(
         courant, tf_center, tf_sharp, tf_gain, tf_color, tile_mask[0, :, :, 0], order,
-        fields, diffusivity, zlo, zhi, ylo, elo, yhi, ehi, xlo, xhi, own_lo, own_hi,
+        xlo, xhi, own_lo, own_hi, coefs,
         *stepped,
     )
     grouped = tiles.reshape(count, per_owner * 4, cols_len)

time: 51.4 us -> 51.3 us (level)
  no operation moved by 1% of the time
where the time goes in v10:
time: 51.3 us; the launch traced here: 51.1 us
  blocking collectives  20.8 us (41%)
  Pallas kernels  15.3 us (30%)
  starting transfers between devices  10.6 us (21%)
  waiting for transfers between devices  3.32 us (6%)
  between operations  0.88 us (2%)
    all_to_all x1, blocking collectives, shards(): lax.all_to_all(grouped, 'gz', split_axis=0, concat_axis=0, tiled=True)  20.8 us
    pallas_call x1, Pallas kernels, shards(): pl.pallas_call(main_kernel, out_shape=(array(*fields.shape), array(order....  8.31 us
    ppermute x4, starting transfers between devices, swap_pairs(): lax.ppermute(message, axis, pairs)  7.35 us
    ppermute x2, waiting for transfers between devices, swap_rows(): came = lax.ppermute(first, axis, [(0, 1), (1, 0)])  3.31 us
    pallas_call x1, Pallas kernels, shards(): pl.pallas_call(first_step_kernel, out_shape=(array(planes, pitch, cols_le...  3.27 us
    ppermute x2, starting transfers between devices, swap_rows(): came = lax.ppermute(first, axis, [(0, 1), (1, 0)])  3.25 us
    pallas_call x1, Pallas kernels, shards(): pl.pallas_call(pack_planes_kernel, out_shape=(array(faces, rows_len, cols...  1.78 us
  transfers between devices with their start and end apart: 6, of which 1 were waited for; matrix products, arithmetic and copies ran while one was open for 0% of the time, Pallas kernels for 9%

profile of v10, /device:TPU:0, one launch (start us, length us, event | category | flops | bytes accessed | tf_op | source)
XLA Modules:
  0.0 51.1 jit_solution(15498173517078818727)
XLA Ops:
  0.6 0.0 copy-start.1
  0.6 0.0 copy-start
  0.6 1.8 %pack_planes.1 = (f32[14,16,128]{2,1,0:T(8,128)}, f32[14,16,128]{2,1,0:T(8,128)}) custom-call(f32[5,32,16,128]{3,2,1,0:T(8,128)} %fields_ref.9, f32[32,16,128]{2,1,0:T(8,128)} %kappa_ref.9), custom_call_target="tpu_custom_call" | custom-call | tf_op jit(solution)/shard_map/pack_planes/pallas_call | solution.py:505
  2.4 3.1 %collective-permute-start = (f32[14,16,128]{2,1,0:T(8,128)}, f32[14,16,128]{2,1,0:T(8,128)S(1)}, u32[]{:S(2)}, u32[]{:S(2)}) collective-permute-start(f32[14,16,128]{2,1,0:T(8,128)} %get-tuple-element.22), channel_id=1, source_target_pairs={{0,8},{8,0},{16,24},{24,16},{1,9},{9,1},{17,25},{25,17},{2,10},{10... | collective-permute-start | bytes 344072 | tf_op jit(solution)/shard_map/ppermute | solution.py:478
  5.5 0.7 %collective-permute-start.1 = (f32[14,16,128]{2,1,0:T(8,128)}, f32[14,16,128]{2,1,0:T(8,128)S(1)}, u32[]{:S(2)}, u32[]{:S(2)}) collective-permute-start(f32[14,16,128]{2,1,0:T(8,128)} %get-tuple-element.23), channel_id=1, source_target_pairs={{8,16},{16,8},{9,17},{17,9},{10,18},{18,10},{11,19},{19,11},{12,20... | collective-permute-start | bytes 344072 | tf_op jit(solution)/shard_map/ppermute | solution.py:478
  6.2 0.0 copy-done.1
  6.2 0.0 copy-done
  6.2 0.1 pack_rows.1
  6.4 1.6 %collective-permute-start.3 = (f32[14,32,128]{2,1,0:T(8,128)S(1)}, f32[14,32,128]{2,1,0:T(8,128)S(1)}, u32[]{:S(2)}, u32[]{:S(2)}) collective-permute-start(f32[14,32,128]{2,1,0:T(8,128)S(1)} %broadcast_select_fusion), channel_id=1, source_target_pairs={{0,4},{4,0},{1,5},{5,1},{2,6},{6,2},{3,7},{7,3},{8,12},{12,8},{9,1... | collective-permute-start | bytes 688136 | tf_op jit(solution)/shard_map/ppermute | solution.py:487
  8.0 0.9 %pack_own.1 = (f32[6,16,128]{2,1,0:T(8,128)S(1)}, f32[6,16,128]{2,1,0:T(8,128)S(1)}) custom-call(f32[5,32,16,128]{3,2,1,0:T(8,128)S(1)} %copy-done, f32[32,16,128]{2,1,0:T(8,128)S(1)} %copy-done.1), custom_call_target="tpu_custom_call" | custom-call | flops 10000000 | bytes 4000000 | tf_op jit(solution)/shard_map/pack_own/pallas_call | solution.py:525
  8.9 0.0 collective-permute-done
  8.9 0.0 collective-permute-done.1
  8.9 0.0 copy-start.8
  9.0 0.2 pack_edges.1
  9.2 1.7 %collective-permute-start.2 = (f32[56,128]{1,0:T(8,128)S(1)}, f32[56,128]{1,0:T(8,128)S(1)}, u32[]{:S(2)}, u32[]{:S(2)}) collective-permute-start(f32[56,128]{1,0:T(8,128)S(1)} %broadcast_select_fusion.7), channel_id=1, source_target_pairs={{0,4},{4,0},{1,5},{5,1},{2,6},{6,2},{3,7},{7,3},{8,12},{12,8},{9,1... | collective-permute-start | bytes 86024 | tf_op jit(solution)/shard_map/ppermute | solution.py:487
  10.8 3.3 %collective-permute-done.2.elo_ref.ehi_ref = f32[56,128]{1,0:T(8,128)S(1)} collective-permute-done((f32[56,128]{1,0:T(8,128)S(1)}, f32[56,128]{1,0:T(8,128)S(1)}, u32[]{:S(2)}, u32[]{:S(2)}) %collective-permute-start.2) | collective-permute-done | bytes 28704 | tf_op jit(solution)/shard_map/ppermute | solution.py:487
  14.2 0.0 collective-permute-done.3.rows_ref.ylo_ref.yhi_ref
  14.2 0.7 %collective-permute-start.5 = (f32[6,24,128]{2,1,0:T(8,128)S(1)}, f32[6,24,128]{2,1,0:T(8,128)S(1)}, u32[]{:S(2)}, u32[]{:S(2)}) collective-permute-start(f32[6,24,128]{2,1,0:T(8,128)S(1)} %get-tuple-element.46), channel_id=1, source_target_pairs={{1,2},{2,1},{5,6},{6,5},{9,10},{10,9},{13,14},{14,13},{17,18},{18,... | collective-permute-start | bytes 221192 | tf_op jit(solution)/shard_map/ppermute | solution.py:478
  14.9 2.9 %collective-permute-start.4 = (f32[6,24,128]{2,1,0:T(8,128)S(1)}, f32[6,24,128]{2,1,0:T(8,128)S(1)}, u32[]{:S(2)}, u32[]{:S(2)}) collective-permute-start(f32[6,24,128]{2,1,0:T(8,128)S(1)} %get-tuple-element.47), channel_id=1, source_target_pairs={{0,1},{1,0},{2,3},{3,2},{4,5},{5,4},{6,7},{7,6},{8,9},{9,8},{10,11... | collective-permute-start | bytes 221192 | tf_op jit(solution)/shard_map/ppermute | solution.py:478
  17.8 0.0 copy-done.8
  17.8 0.1 copy.12.courant_ref
  17.9 0.0 copy-start.2
  17.9 0.0 copy-start.3
  17.9 0.0 copy-start.4
  17.9 0.0 copy-start.5
  17.9 0.0 copy-start.6
  17.9 0.0 copy-start.7
  17.9 3.3 %first_step.1 = (f32[38,24,128]{2,1,0:T(8,128)S(1)}, f32[38,24,128]{2,1,0:T(8,128)S(1)}, f32[38,24,128]{2,1,0:T(8,128)S(1)}, f32[38,24,128]{2,1,0:T(8,128)S(1)},...) custom-call(f32[5,3]{1,0:T(8,128)S(1)} %copy.12.courant_ref, f32[5,32,16,128]{3,2,1,0:T(8,128)S(1)} %copy-done, ...), custom_call_target="tpu_custom_call" | custom-call | flops 100000000 | bytes 8000000 | tf_op jit(solution)/shard_map/first_step/pallas_call | solution.py:555
  21.2 0.0 collective-permute-done.5
  21.2 0.0 collective-permute-done.4
  21.3 0.0 copy-done.2
  21.3 0.0 copy-done.3
  21.3 0.0 copy-done.4
  21.3 0.0 copy-done.5
  21.3 0.0 copy-done.6
  21.3 0.0 copy-done.7
  21.3 8.3 %step_and_march.1 = (f32[5,32,16,128]{3,2,1,0:T(8,128)}, f32[256,4,128]{2,1,0:T(4,128)S(1)}) custom-call(f32[5,3]{1,0:T(8,128)S(1)} %copy.12.courant_ref, f32[16]{0:T(128)S(1)} %copy-done.5, f32[16]{0:T(128)S(1)} %copy-done.6, f32[16]{0:T(128)S(1)} %copy-done.7, f32[3,16]{1,0:T(4,128)S(1)} %copy-done.3, s32[16,16]{1,0:T(8,128)S(1)} %bitcast.5, ...), custom_call_target="tpu_custom_call" | custom-call | tf_op jit(solution)/shard_map/step_and_march/pallas_call | solution.py:568
  29.6 20.8 %all_to_all.5.part_ref = f32[4,256,128]{2,1,0:T(8,128)S(1)} all-to-all(f32[4,256,128]{2,1,0:T(8,128)S(1)} %bitcast.4), channel_id=1, replica_groups=mesh['gz'=4,'gy'=2,'gx'=4] {'gz'}, dimensions={0} | all-to-all | bytes 1048576 | tf_op jit(solution)/shard_map/all_to_all | solution.py:592
  50.4 0.7 %compose.1 = f32[256,128]{1,0:T(8,128)} custom-call(f32[4,256,128]{2,1,0:T(8,128)S(1)} %all_to_all.5.part_ref), custom_call_target="tpu_custom_call" | custom-call | tf_op jit(solution)/shard_map/compose/pallas_call | solution.py:457
  (6 shorter events, 0.1 us)
Async XLA Ops:
  0.6 5.6 %copy-start.1 = (f32[32,16,128]{2,1,0:T(8,128)S(1)}, f32[32,16,128]{2,1,0:T(8,128)}, u32[]{:S(2)}) copy-start(f32[32,16,128]{2,1,0:T(8,128)} %kappa_ref.9) | copy-start | bytes 786436
  0.6 5.6 %copy-start = (f32[5,32,16,128]{3,2,1,0:T(8,128)S(1)}, f32[5,32,16,128]{3,2,1,0:T(8,128)}, u32[]{:S(2)}) copy-start(f32[5,32,16,128]{3,2,1,0:T(8,128)} %fields_ref.9) | copy-start | bytes 3932164
  2.4 6.5 %collective-permute-start = (f32[14,16,128]{2,1,0:T(8,128)}, f32[14,16,128]{2,1,0:T(8,128)S(1)}, u32[]{:S(2)}, u32[]{:S(2)}) collective-permute-start(f32[14,16,128]{2,1,0:T(8,128)} %get-tuple-element.22), channel_id=1, source_target_pairs={{0,8},{8,0},{16,24},{24,16},{1,9},{9,1},{17,25},{25,17},{2,10},{10... | collective-permute-start | bytes 344072 | tf_op jit(solution)/shard_map/ppermute | solution.py:478
  5.5 3.4 %collective-permute-start.1 = (f32[14,16,128]{2,1,0:T(8,128)}, f32[14,16,128]{2,1,0:T(8,128)S(1)}, u32[]{:S(2)}, u32[]{:S(2)}) collective-permute-start(f32[14,16,128]{2,1,0:T(8,128)} %get-tuple-element.23), channel_id=1, source_target_pairs={{8,16},{16,8},{9,17},{17,9},{10,18},{18,10},{11,19},{19,11},{12,20... | collective-permute-start | bytes 344072 | tf_op jit(solution)/shard_map/ppermute | solution.py:478
  6.4 7.7 %collective-permute-start.3 = (f32[14,32,128]{2,1,0:T(8,128)S(1)}, f32[14,32,128]{2,1,0:T(8,128)S(1)}, u32[]{:S(2)}, u32[]{:S(2)}) collective-permute-start(f32[14,32,128]{2,1,0:T(8,128)S(1)} %broadcast_select_fusion), channel_id=1, source_target_pairs={{0,4},{4,0},{1,5},{5,1},{2,6},{6,2},{3,7},{7,3},{8,12},{12,8},{9,1... | collective-permute-start | bytes 688136 | tf_op jit(solution)/shard_map/ppermute | solution.py:487
  8.9 8.9 %copy-start.8 = (f32[5,3]{0,1:T(4,128)S(1)}, f32[5,3]{0,1:T(4,128)}, u32[]{:S(2)}) copy-start(f32[5,3]{0,1:T(4,128)} %param.11) | copy-start | bytes 184
  9.2 5.0 %collective-permute-start.2 = (f32[56,128]{1,0:T(8,128)S(1)}, f32[56,128]{1,0:T(8,128)S(1)}, u32[]{:S(2)}, u32[]{:S(2)}) collective-permute-start(f32[56,128]{1,0:T(8,128)S(1)} %broadcast_select_fusion.7), channel_id=1, source_target_pairs={{0,4},{4,0},{1,5},{5,1},{2,6},{6,2},{3,7},{7,3},{8,12},{12,8},{9,1... | collective-permute-start | bytes 86024 | tf_op jit(solution)/shard_map/ppermute | solution.py:487
  14.2 7.0 %collective-permute-start.5 = (f32[6,24,128]{2,1,0:T(8,128)S(1)}, f32[6,24,128]{2,1,0:T(8,128)S(1)}, u32[]{:S(2)}, u32[]{:S(2)}) collective-permute-start(f32[6,24,128]{2,1,0:T(8,128)S(1)} %get-tuple-element.46), channel_id=1, source_target_pairs={{1,2},{2,1},{5,6},{6,5},{9,10},{10,9},{13,14},{14,13},{17,18},{18,... | collective-permute-start | bytes 221192 | tf_op jit(solution)/shard_map/ppermute | solution.py:478
  14.9 6.4 %collective-permute-start.4 = (f32[6,24,128]{2,1,0:T(8,128)S(1)}, f32[6,24,128]{2,1,0:T(8,128)S(1)}, u32[]{:S(2)}, u32[]{:S(2)}) collective-permute-start(f32[6,24,128]{2,1,0:T(8,128)S(1)} %get-tuple-element.47), channel_id=1, source_target_pairs={{0,1},{1,0},{2,3},{3,2},{4,5},{5,4},{6,7},{7,6},{8,9},{9,8},{10,11... | collective-permute-start | bytes 221192 | tf_op jit(solution)/shard_map/ppermute | solution.py:478
  17.9 3.4 %copy-start.2 = (s32[1,16,16,1]{2,3,1,0:T(1,128)S(1)}, s32[1,16,16,1]{2,3,1,0:T(1,128)}, u32[]{:S(2)}) copy-start(s32[1,16,16,1]{2,3,1,0:T(1,128)} %param.16) | copy-start | bytes 3076
  17.9 3.4 %copy-start.3 = (f32[3,16]{1,0:T(4,128)S(1)}, f32[3,16]{1,0:T(4,128)}, u32[]{:S(2)}) copy-start(f32[3,16]{1,0:T(4,128)} %color_ref.1) | copy-start | bytes 580
  17.9 3.4 %copy-start.4 = (s32[1,1,256]{2,1,0:T(1,128)S(1)}, s32[1,1,256]{2,1,0:T(1,128)}, u32[]{:S(2)}) copy-start(s32[1,1,256]{2,1,0:T(1,128)} %param.17) | copy-start | bytes 3076
  17.9 3.4 %copy-start.5 = (f32[16]{0:T(128)S(1)}, f32[16]{0:T(128)}, u32[]{:S(2)}) copy-start(f32[16]{0:T(128)} %center_ref.1) | copy-start | bytes 196
  17.9 3.4 %copy-start.6 = (f32[16]{0:T(128)S(1)}, f32[16]{0:T(128)}, u32[]{:S(2)}) copy-start(f32[16]{0:T(128)} %sharp_ref.1) | copy-start | bytes 196
  17.9 3.4 %copy-start.7 = (f32[16]{0:T(128)S(1)}, f32[16]{0:T(128)}, u32[]{:S(2)}) copy-start(f32[16]{0:T(128)} %gain_ref.1) | copy-start | bytes 196

commit v11 on v9

--- a/solution.py
+++ b/solution.py
@@ -268,10 +268,12 @@
 ):
     nfield, depth_len, rows, lanes = fields_ref.shape
     step_refs = rest[:nfield]
+    count = lax.axis_size("gz")
+    state_ref, out_refs = rest[nfield], rest[nfield + 1 : nfield + 1 + count]
     (
-        state_ref, out_ref, kpad_ref, next_ref, last_ref, side_ref, edge_ref, base_ref,
+        kpad_ref, next_ref, last_ref, side_ref, edge_ref, base_ref,
         tile_ref, coef_ref, held_ref, flux_ref, sem,
-    ) = rest[nfield:]
+    ) = rest[nfield + 1 + count :]
     nfield, depth_len, rows, lanes = state_ref.shape
     planes, pitch = depth_len + 2 * W, rows + SUB
     lane = lax.broadcasted_iota(jnp.int32, (pitch, lanes), 1)
@@ -432,26 +434,42 @@
                 tile_ref[pl.ds(start + k, SUB, stride=4), :] = acc[j][k] * color_ref[k, first + j]
             tile_ref[pl.ds(start + 3, SUB, stride=4), :] = 1.0 - passed[j]
 
-    @pl.loop(0, order_ref.shape[0], unroll=steps(order_ref.shape[0], 64))
-    def _(slot):
-        tile = order_ref[slot]
-        cover = mask_ref[lax.div(tile, rows), lax.rem(tile, rows)].astype(F32)
-        out_ref[slot] = tile_ref[pl.ds(pl.multiple_of(tile * 4, 4), 4), :] * cover
+    per_owner = out_refs[0].shape[0]
+    for distance, out_ref in enumerate(out_refs):
+        first_slot = lax.bitwise_xor(lax.axis_index("gz"), distance) * per_owner
+
+        @pl.loop(0, per_owner, unroll=per_owner)
+        def _(place):
+            tile = order_ref[first_slot + place]
+            cover = mask_ref[lax.div(tile, rows), lax.rem(tile, rows)].astype(F32)
+            out_ref[place] = tile_ref[pl.ds(pl.multiple_of(tile * 4, 4), 4), :] * cover
+
     keep.wait()
 
 
-def compose_kernel(part_ref, out_ref):
-    slabs, rows, _ = part_ref.shape
+def compose_kernel(*refs):
+    part_refs, out_ref = refs[:-1], refs[-1]
+    slabs, rows = len(part_refs), out_ref.shape[0]
+    here = lax.axis_index("gz")
 
     @pl.loop(0, rows // 32, unroll=rows // 32)
     def _(step):
-        def load(slab, k):
-            return part_ref[slab, pl.ds(step * 32 + k, 8, stride=4), :]
-
-        acc = [load(0, k) for k in range(4)]
+        def load(k):
+            return [ref[pl.ds(step * 32 + k, 8, stride=4), :] for ref in part_refs]
+
+        parts = [load(k) for k in range(4)]
+
+        def slab_of(slab, k):
+            distance = lax.bitwise_xor(here, slab)
+            value = parts[k][0]
+            for i in range(1, slabs):
+                value = jnp.where(distance == i, parts[k][i], value)
+            return value
+
+        acc = [slab_of(0, k) for k in range(4)]
         for slab in range(1, slabs):
             clear = 1.0 - acc[3]
-            acc = [acc[k] + clear * load(slab, k) for k in range(4)]
+            acc = [acc[k] + clear * slab_of(slab, k) for k in range(4)]
         for k in range(4):
             out_ref[pl.ds(step * 32 + k, 8, stride=4), :] = acc[k]
 
@@ -460,12 +478,12 @@
     vmem = pl.BlockSpec(memory_space=pltpu.VMEM)
     return pl.pallas_call(
         compose_kernel,
-        out_shape=jax.ShapeDtypeStruct(parts.shape[1:], jnp.float32),
-        in_specs=[vmem],
+        out_shape=jax.ShapeDtypeStruct(parts[0].shape, jnp.float32),
+        in_specs=[vmem] * len(parts),
         out_specs=vmem,
         compiler_params=pltpu.CompilerParams(vmem_limit_bytes=16 * 1024 * 1024),
         name="compose",
-    )(parts)
+    )(*parts)
 
 
 def is_odd(axis):
@@ -569,11 +587,11 @@
     count = lax.axis_size("gz")
     order = tile_perm[0, 0]
     per_owner = order.shape[0] // count
-    state, tiles = pl.pallas_call(
+    state, *blocks = pl.pallas_call(
         main_kernel,
-        out_shape=(array(*fields.shape), array(order.shape[0], 4, cols_len)),
+        out_shape=(array(*fields.shape),) + (array(per_owner, 4, cols_len),) * count,
         in_specs=[smem] * 7 + [vmem] * (12 + nfield),
-        out_specs=(pl.BlockSpec(memory_space=pl.ANY), vmem),
+        out_specs=(pl.BlockSpec(memory_space=pl.ANY),) + (vmem,) * count,
         scratch_shapes=[
             pltpu.VMEM((planes, pitch, cols_len), F32),
             pltpu.VMEM((nfield * planes, pitch, cols_len), F32),
@@ -594,8 +612,10 @@
         fields, diffusivity, zlo, zhi, ylo, elo, yhi, ehi, xlo, xhi, own_lo, own_hi,
         *stepped,
     )
-    grouped = tiles.reshape(count, per_owner * 4, cols_len)
-    composed = compose(lax.all_to_all(grouped, "gz", split_axis=0, concat_axis=0, tiled=True))
+    parts = [blocks[0]]
+    for distance in range(1, count):
+        parts.append(lax.ppermute(blocks[distance], "gz", [(i, i ^ distance) for i in range(count)]))
+    composed = compose([part.reshape(per_owner * 4, cols_len) for part in parts])
     picture = composed.reshape(1, 1, per_owner, 4, cols_len)
     return (state, picture)
 

time: 51.4 us -> 47.8 us (0.930)
  blocking collectives: 20.8 us -> 0 us
  waiting for transfers between devices: 3.32 us -> 13.8 us
  starting transfers between devices: 10.6 us -> 17.2 us
    all_to_all x1 -> x0, blocking collectives: 20.8 us -> none  [shards(): lax.all_to_all(grouped, 'gz', split_axis=0, concat_axis=0, tiled=True)]
    ppermute x0 -> x3, waiting for transfers between devices: none -> 10.5 us  [shards(): lax.ppermute(blocks[distance], 'gz', [(i, i ^ distance) for i in range(co...]
    ppermute x0 -> x3, starting transfers between devices: none -> 6.62 us  [shards(): lax.ppermute(blocks[distance], 'gz', [(i, i ^ distance) for i in range(co...]
  transfers between devices with their start and end apart: 6 -> 9, of which waited for: 1 -> 3; matrix products, arithmetic and copies ran while one was open for 0% -> 0% of each run, Pallas kernels for 9% -> 9%
where the time goes in v11:
time: 47.8 us; the launch traced here: 47.6 us
  starting transfers between devices  17.2 us (36%)
  Pallas kernels  15.5 us (32%)
  waiting for transfers between devices  13.8 us (29%)
  between operations  0.89 us (2%)
    ppermute x3, waiting for transfers between devices, shards(): lax.ppermute(blocks[distance], 'gz', [(i, i ^ distance) for i in range(co...  10.5 us
    pallas_call x1, Pallas kernels, shards(): pl.pallas_call(main_kernel, out_shape=(array(*fields.shape),) + (array(pe...  8.45 us
    ppermute x4, starting transfers between devices, swap_pairs(): lax.ppermute(message, axis, pairs)  7.35 us
    ppermute x3, starting transfers between devices, shards(): lax.ppermute(blocks[distance], 'gz', [(i, i ^ distance) for i in range(co...  6.62 us
    ppermute x2, waiting for transfers between devices, swap_rows(): came = lax.ppermute(first, axis, [(0, 1), (1, 0)])  3.31 us
    pallas_call x1, Pallas kernels, shards(): pl.pallas_call(first_step_kernel, out_shape=(array(planes, pitch, cols_le...  3.25 us
    ppermute x2, starting transfers between devices, swap_rows(): came = lax.ppermute(first, axis, [(0, 1), (1, 0)])  3.25 us
    pallas_call x1, Pallas kernels, shards(): pl.pallas_call(pack_planes_kernel, out_shape=(array(faces, rows_len, cols...  1.78 us
  transfers between devices with their start and end apart: 9, of which 3 were waited for; matrix products, arithmetic and copies ran while one was open for 0% of the time, Pallas kernels for 9%

profile of v11, /device:TPU:0, one launch (start us, length us, event | category | flops | bytes accessed | tf_op | source)
XLA Modules:
  0.0 47.6 jit_solution(17089596765399891477)
XLA Ops:
  0.6 0.0 copy-start.1
  0.6 0.0 copy-start
  0.6 1.8 %pack_planes.1 = (f32[14,16,128]{2,1,0:T(8,128)}, f32[14,16,128]{2,1,0:T(8,128)}) custom-call(f32[5,32,16,128]{3,2,1,0:T(8,128)} %fields_ref.11, f32[32,16,128]{2,1,0:T(8,128)} %kappa_ref.11), custom_call_target="tpu_custom_call" | custom-call | tf_op jit(solution)/shard_map/pack_planes/pallas_call | solution.py:527
  2.4 3.1 %collective-permute-start = (f32[14,16,128]{2,1,0:T(8,128)}, f32[14,16,128]{2,1,0:T(8,128)S(1)}, u32[]{:S(2)}, u32[]{:S(2)}) collective-permute-start(f32[14,16,128]{2,1,0:T(8,128)} %get-tuple-element.24), channel_id=1, source_target_pairs={{0,8},{8,0},{16,24},{24,16},{1,9},{9,1},{17,25},{25,17},{2,10},{10... | collective-permute-start | bytes 344072 | tf_op jit(solution)/shard_map/ppermute | solution.py:500
  5.5 0.7 %collective-permute-start.1 = (f32[14,16,128]{2,1,0:T(8,128)}, f32[14,16,128]{2,1,0:T(8,128)S(1)}, u32[]{:S(2)}, u32[]{:S(2)}) collective-permute-start(f32[14,16,128]{2,1,0:T(8,128)} %get-tuple-element.25), channel_id=1, source_target_pairs={{8,16},{16,8},{9,17},{17,9},{10,18},{18,10},{11,19},{19,11},{12,20... | collective-permute-start | bytes 344072 | tf_op jit(solution)/shard_map/ppermute | solution.py:500
  6.2 0.0 copy-done.1
  6.2 0.0 copy-done
  6.2 0.1 pack_rows.1
  6.4 1.6 %collective-permute-start.2 = (f32[14,32,128]{2,1,0:T(8,128)S(1)}, f32[14,32,128]{2,1,0:T(8,128)S(1)}, u32[]{:S(2)}, u32[]{:S(2)}) collective-permute-start(f32[14,32,128]{2,1,0:T(8,128)S(1)} %broadcast_select_fusion), channel_id=1, source_target_pairs={{0,4},{4,0},{1,5},{5,1},{2,6},{6,2},{3,7},{7,3},{8,12},{12,8},{9,1... | collective-permute-start | bytes 688136 | tf_op jit(solution)/shard_map/ppermute | solution.py:509
  8.0 0.9 %pack_own.1 = (f32[6,16,128]{2,1,0:T(8,128)S(1)}, f32[6,16,128]{2,1,0:T(8,128)S(1)}) custom-call(f32[5,32,16,128]{3,2,1,0:T(8,128)S(1)} %copy-done, f32[32,16,128]{2,1,0:T(8,128)S(1)} %copy-done.1), custom_call_target="tpu_custom_call" | custom-call | flops 10000000 | bytes 4000000 | tf_op jit(solution)/shard_map/pack_own/pallas_call | solution.py:547
  8.9 0.0 collective-permute-done
  8.9 0.0 collective-permute-done.1
  8.9 0.0 copy-start.8
  9.0 0.2 pack_edges.1
  9.2 1.7 %collective-permute-start.3 = (f32[56,128]{1,0:T(8,128)S(1)}, f32[56,128]{1,0:T(8,128)S(1)}, u32[]{:S(2)}, u32[]{:S(2)}) collective-permute-start(f32[56,128]{1,0:T(8,128)S(1)} %broadcast_select_fusion.7), channel_id=1, source_target_pairs={{0,4},{4,0},{1,5},{5,1},{2,6},{6,2},{3,7},{7,3},{8,12},{12,8},{9,1... | collective-permute-start | bytes 86024 | tf_op jit(solution)/shard_map/ppermute | solution.py:509
  10.8 3.3 %collective-permute-done.3.elo_ref.ehi_ref = f32[56,128]{1,0:T(8,128)S(1)} collective-permute-done((f32[56,128]{1,0:T(8,128)S(1)}, f32[56,128]{1,0:T(8,128)S(1)}, u32[]{:S(2)}, u32[]{:S(2)}) %collective-permute-start.3) | collective-permute-done | bytes 28704 | tf_op jit(solution)/shard_map/ppermute | solution.py:509
  14.2 0.0 collective-permute-done.2.rows_ref.ylo_ref.yhi_ref
  14.2 0.7 %collective-permute-start.5 = (f32[6,24,128]{2,1,0:T(8,128)S(1)}, f32[6,24,128]{2,1,0:T(8,128)S(1)}, u32[]{:S(2)}, u32[]{:S(2)}) collective-permute-start(f32[6,24,128]{2,1,0:T(8,128)S(1)} %get-tuple-element.50), channel_id=1, source_target_pairs={{1,2},{2,1},{5,6},{6,5},{9,10},{10,9},{13,14},{14,13},{17,18},{18,... | collective-permute-start | bytes 221192 | tf_op jit(solution)/shard_map/ppermute | solution.py:500
  14.9 2.9 %collective-permute-start.4 = (f32[6,24,128]{2,1,0:T(8,128)S(1)}, f32[6,24,128]{2,1,0:T(8,128)S(1)}, u32[]{:S(2)}, u32[]{:S(2)}) collective-permute-start(f32[6,24,128]{2,1,0:T(8,128)S(1)} %get-tuple-element.51), channel_id=1, source_target_pairs={{0,1},{1,0},{2,3},{3,2},{4,5},{5,4},{6,7},{7,6},{8,9},{9,8},{10,11... | collective-permute-start | bytes 221192 | tf_op jit(solution)/shard_map/ppermute | solution.py:500
  17.8 0.0 copy-done.8
  17.8 0.1 copy.12.courant_ref
  17.9 0.0 copy-start.2
  17.9 0.0 copy-start.3
  17.9 0.0 copy-start.4
  17.9 0.0 copy-start.5
  17.9 0.0 copy-start.6
  17.9 0.0 copy-start.7
  17.9 3.2 %first_step.1 = (f32[38,24,128]{2,1,0:T(8,128)S(1)}, f32[38,24,128]{2,1,0:T(8,128)S(1)}, f32[38,24,128]{2,1,0:T(8,128)S(1)}, f32[38,24,128]{2,1,0:T(8,128)S(1)}, f32[38,24,128]{2,1,0:T(8,128)S(1)}) custom-call(f32[5,3]{1,0:T(8,128)S(1)} %copy.12.courant_ref, f32[5,32,16,128]{3,2,1,0:T(8,128)S(1)} %copy-done, f32[32,16,128]{2,1,0:T(8,128)S(1)} %copy-done.1, ...), custom_call_target="tpu_custom_call" | custom-call | flops 100000000 | bytes 8000000 | tf_op jit(solution)/shard_map/first_step/pallas_call | solution.py:577
  21.2 0.0 collective-permute-done.5
  21.2 0.0 collective-permute-done.4
  21.2 0.0 copy-done.2
  21.3 0.0 copy-done.3
  21.3 0.0 copy-done.4
  21.3 0.0 copy-done.5
  21.3 0.0 copy-done.6
  21.3 0.0 copy-done.7
  21.3 8.5 %step_and_march.1 = (f32[5,32,16,128]{3,2,1,0:T(8,128)}, f32[64,4,128]{2,1,0:T(4,128)S(1)}, f32[64,4,128]{2,1,0:T(4,128)S(1)}, f32[64,4,128]{2,1,0:T(4,128)S(1)}, f32[64,4,128]{2,1,0:T(4,128)S(1)}) custom-call(f32[5,3]{1,0:T(8,128)S(1)} %copy.12.courant_ref, f32[16]{0:T(128)S(1)} %copy-done.5, f32[16]{0:T(128)S(1)} %copy-done.6, f32[16]{0:T(128)S(1)} %copy-done.7, ...), custom_call_target="tpu_custom_call" | custom-call | tf_op jit(solution)/shard_map/step_and_march/pallas_call | solution.py:590
  29.8 4.2 %collective-permute-start.6 = (f32[64,4,128]{2,1,0:T(4,128)S(1)}, f32[64,4,128]{2,1,0:T(4,128)S(1)}, u32[]{:S(2)}, u32[]{:S(2)}) collective-permute-start(f32[64,4,128]{2,1,0:T(4,128)S(1)} %get-tuple-element.43), channel_id=1, source_target_pairs={{0,8},{8,0},{16,24},{24,16},{1,9},{9,1},{17,25},{25,17},{2,10},{10... | collective-permute-start | bytes 393224 | tf_op jit(solution)/shard_map/ppermute | solution.py:617
  33.9 1.0 %collective-permute-start.7 = (f32[64,4,128]{2,1,0:T(4,128)S(1)}, f32[64,4,128]{2,1,0:T(4,128)S(1)}, u32[]{:S(2)}, u32[]{:S(2)}) collective-permute-start(f32[64,4,128]{2,1,0:T(4,128)S(1)} %get-tuple-element.44), channel_id=1, source_target_pairs={{0,16},{8,24},{16,0},{24,8},{1,17},{9,25},{17,1},{25,9},{2,18},{10... | collective-permute-start | bytes 393224 | tf_op jit(solution)/shard_map/ppermute | solution.py:617
  34.9 1.5 %collective-permute-start.8 = (f32[64,4,128]{2,1,0:T(4,128)S(1)}, f32[64,4,128]{2,1,0:T(4,128)S(1)}, u32[]{:S(2)}, u32[]{:S(2)}) collective-permute-start(f32[64,4,128]{2,1,0:T(4,128)S(1)} %get-tuple-element.45), channel_id=1, source_target_pairs={{0,24},{8,16},{16,8},{24,0},{1,25},{9,17},{17,9},{25,1},{2,26},{10... | collective-permute-start | bytes 393224 | tf_op jit(solution)/shard_map/ppermute | solution.py:617
  36.4 3.0 %collective-permute-done.6 = f32[64,4,128]{2,1,0:T(4,128)S(1)} collective-permute-done((f32[64,4,128]{2,1,0:T(4,128)S(1)}, f32[64,4,128]{2,1,0:T(4,128)S(1)}, u32[]{:S(2)}, u32[]{:S(2)}) %collective-permute-start.6) | collective-permute-done | bytes 131104 | tf_op jit(solution)/shard_map/ppermute | solution.py:617
  39.3 7.5 %collective-permute-done.7 = f32[64,4,128]{2,1,0:T(4,128)S(1)} collective-permute-done((f32[64,4,128]{2,1,0:T(4,128)S(1)}, f32[64,4,128]{2,1,0:T(4,128)S(1)}, u32[]{:S(2)}, u32[]{:S(2)}) %collective-permute-start.7) | collective-permute-done | bytes 131104 | tf_op jit(solution)/shard_map/ppermute | solution.py:617
  46.9 0.0 collective-permute-done.8
  46.9 0.7 %compose.1 = f32[256,128]{1,0:T(8,128)} custom-call(f32[256,128]{1,0:T(8,128)S(1)} %bitcast.7, f32[256,128]{1,0:T(8,128)S(1)} %bitcast.8, f32[256,128]{1,0:T(8,128)S(1)} %bitcast.9, f32[256,128]{1,0:T(8,128)S(1)} %bitcast.10), custom_call_target="tpu_custom_call" | custom-call | tf_op jit(solution)/shard_map/compose/pallas_call | solution.py:479
  (6 shorter events, 0.1 us)
Async XLA Ops:
  0.6 5.6 %copy-start.1 = (f32[32,16,128]{2,1,0:T(8,128)S(1)}, f32[32,16,128]{2,1,0:T(8,128)}, u32[]{:S(2)}) copy-start(f32[32,16,128]{2,1,0:T(8,128)} %kappa_ref.11) | copy-start | bytes 786436
  0.6 5.6 %copy-start = (f32[5,32,16,128]{3,2,1,0:T(8,128)S(1)}, f32[5,32,16,128]{3,2,1,0:T(8,128)}, u32[]{:S(2)}) copy-start(f32[5,32,16,128]{3,2,1,0:T(8,128)} %fields_ref.11) | copy-start | bytes 3932164
  2.4 6.5 %collective-permute-start = (f32[14,16,128]{2,1,0:T(8,128)}, f32[14,16,128]{2,1,0:T(8,128)S(1)}, u32[]{:S(2)}, u32[]{:S(2)}) collective-permute-start(f32[14,16,128]{2,1,0:T(8,128)} %get-tuple-element.24), channel_id=1, source_target_pairs={{0,8},{8,0},{16,24},{24,16},{1,9},{9,1},{17,25},{25,17},{2,10},{10... | collective-permute-start | bytes 344072 | tf_op jit(solution)/shard_map/ppermute | solution.py:500
  5.5 3.4 %collective-permute-start.1 = (f32[14,16,128]{2,1,0:T(8,128)}, f32[14,16,128]{2,1,0:T(8,128)S(1)}, u32[]{:S(2)}, u32[]{:S(2)}) collective-permute-start(f32[14,16,128]{2,1,0:T(8,128)} %get-tuple-element.25), channel_id=1, source_target_pairs={{8,16},{16,8},{9,17},{17,9},{10,18},{18,10},{11,19},{19,11},{12,20... | collective-permute-start | bytes 344072 | tf_op jit(solution)/shard_map/ppermute | solution.py:500
  6.4 7.7 %collective-permute-start.2 = (f32[14,32,128]{2,1,0:T(8,128)S(1)}, f32[14,32,128]{2,1,0:T(8,128)S(1)}, u32[]{:S(2)}, u32[]{:S(2)}) collective-permute-start(f32[14,32,128]{2,1,0:T(8,128)S(1)} %broadcast_select_fusion), channel_id=1, source_target_pairs={{0,4},{4,0},{1,5},{5,1},{2,6},{6,2},{3,7},{7,3},{8,12},{12,8},{9,1... | collective-permute-start | bytes 688136 | tf_op jit(solution)/shard_map/ppermute | solution.py:509
  8.9 8.9 %copy-start.8 = (f32[5,3]{0,1:T(4,128)S(1)}, f32[5,3]{0,1:T(4,128)}, u32[]{:S(2)}) copy-start(f32[5,3]{0,1:T(4,128)} %param.11) | copy-start | bytes 184
  9.2 5.0 %collective-permute-start.3 = (f32[56,128]{1,0:T(8,128)S(1)}, f32[56,128]{1,0:T(8,128)S(1)}, u32[]{:S(2)}, u32[]{:S(2)}) collective-permute-start(f32[56,128]{1,0:T(8,128)S(1)} %broadcast_select_fusion.7), channel_id=1, source_target_pairs={{0,4},{4,0},{1,5},{5,1},{2,6},{6,2},{3,7},{7,3},{8,12},{12,8},{9,1... | collective-permute-start | bytes 86024 | tf_op jit(solution)/shard_map/ppermute | solution.py:509
  14.2 7.0 %collective-permute-start.5 = (f32[6,24,128]{2,1,0:T(8,128)S(1)}, f32[6,24,128]{2,1,0:T(8,128)S(1)}, u32[]{:S(2)}, u32[]{:S(2)}) collective-permute-start(f32[6,24,128]{2,1,0:T(8,128)S(1)} %get-tuple-element.50), channel_id=1, source_target_pairs={{1,2},{2,1},{5,6},{6,5},{9,10},{10,9},{13,14},{14,13},{17,18},{18,... | collective-permute-start | bytes 221192 | tf_op jit(solution)/shard_map/ppermute | solution.py:500
  14.9 6.3 %collective-permute-start.4 = (f32[6,24,128]{2,1,0:T(8,128)S(1)}, f32[6,24,128]{2,1,0:T(8,128)S(1)}, u32[]{:S(2)}, u32[]{:S(2)}) collective-permute-start(f32[6,24,128]{2,1,0:T(8,128)S(1)} %get-tuple-element.51), channel_id=1, source_target_pairs={{0,1},{1,0},{2,3},{3,2},{4,5},{5,4},{6,7},{7,6},{8,9},{9,8},{10,11... | collective-permute-start | bytes 221192 | tf_op jit(solution)/shard_map/ppermute | solution.py:500
  17.9 3.3 %copy-start.2 = (s32[1,16,16,1]{2,3,1,0:T(1,128)S(1)}, s32[1,16,16,1]{2,3,1,0:T(1,128)}, u32[]{:S(2)}) copy-start(s32[1,16,16,1]{2,3,1,0:T(1,128)} %param.16) | copy-start | bytes 3076
  17.9 3.3 %copy-start.3 = (f32[3,16]{1,0:T(4,128)S(1)}, f32[3,16]{1,0:T(4,128)}, u32[]{:S(2)}) copy-start(f32[3,16]{1,0:T(4,128)} %color_ref.1) | copy-start | bytes 580
  17.9 3.4 %copy-start.4 = (s32[1,1,256]{2,1,0:T(1,128)S(1)}, s32[1,1,256]{2,1,0:T(1,128)}, u32[]{:S(2)}) copy-start(s32[1,1,256]{2,1,0:T(1,128)} %param.17) | copy-start | bytes 3076
  17.9 3.4 %copy-start.5 = (f32[16]{0:T(128)S(1)}, f32[16]{0:T(128)}, u32[]{:S(2)}) copy-start(f32[16]{0:T(128)} %center_ref.1) | copy-start | bytes 196
  17.9 3.4 %copy-start.6 = (f32[16]{0:T(128)S(1)}, f32[16]{0:T(128)}, u32[]{:S(2)}) copy-start(f32[16]{0:T(128)} %sharp_ref.1) | copy-start | bytes 196
  17.9 3.4 %copy-start.7 = (f32[16]{0:T(128)S(1)}, f32[16]{0:T(128)}, u32[]{:S(2)}) copy-start(f32[16]{0:T(128)} %gain_ref.1) | copy-start | bytes 196
  29.8 9.6 %collective-permute-start.6 = (f32[64,4,128]{2,1,0:T(4,128)S(1)}, f32[64,4,128]{2,1,0:T(4,128)S(1)}, u32[]{:S(2)}, u32[]{:S(2)}) collective-permute-start(f32[64,4,128]{2,1,0:T(4,128)S(1)} %get-tuple-element.43), channel_id=1, source_target_pairs={{0,8},{8,0},{16,24},{24,16},{1,9},{9,1},{17,25},{25,17},{2,10},{10... | collective-permute-start | bytes 393224 | tf_op jit(solution)/shard_map/ppermute | solution.py:617
  33.9 12.9 %collective-permute-start.7 = (f32[64,4,128]{2,1,0:T(4,128)S(1)}, f32[64,4,128]{2,1,0:T(4,128)S(1)}, u32[]{:S(2)}, u32[]{:S(2)}) collective-permute-start(f32[64,4,128]{2,1,0:T(4,128)S(1)} %get-tuple-element.44), channel_id=1, source_target_pairs={{0,16},{8,24},{16,0},{24,8},{1,17},{9,25},{17,1},{25,9},{2,18},{10... | collective-permute-start | bytes 393224 | tf_op jit(solution)/shard_map/ppermute | solution.py:617
  34.9 11.9 %collective-permute-start.8 = (f32[64,4,128]{2,1,0:T(4,128)S(1)}, f32[64,4,128]{2,1,0:T(4,128)S(1)}, u32[]{:S(2)}, u32[]{:S(2)}) collective-permute-start(f32[64,4,128]{2,1,0:T(4,128)S(1)} %get-tuple-element.45), channel_id=1, source_target_pairs={{0,24},{8,16},{16,8},{24,0},{1,25},{9,17},{17,9},{25,1},{2,26},{10... | collective-permute-start | bytes 393224 | tf_op jit(solution)/shard_map/ppermute | solution.py:617

commit v12 on v11

--- a/solution.py
+++ b/solution.py
@@ -448,7 +448,7 @@
 
 
 def compose_kernel(*refs):
-    part_refs, out_ref = refs[:-1], refs[-1]
+    part_refs, out_ref = refs[:1] + refs[-2:0:-1], refs[-1]
     slabs, rows = len(part_refs), out_ref.shape[0]
     here = lax.axis_index("gz")
 
@@ -612,10 +612,11 @@
         fields, diffusivity, zlo, zhi, ylo, elo, yhi, ehi, xlo, xhi, own_lo, own_hi,
         *stepped,
     )
-    parts = [blocks[0]]
-    for distance in range(1, count):
-        parts.append(lax.ppermute(blocks[distance], "gz", [(i, i ^ distance) for i in range(count)]))
-    composed = compose([part.reshape(per_owner * 4, cols_len) for part in parts])
+    parts = [blocks[0]] * count
+    for distance in reversed(range(1, count)):
+        parts[distance] = lax.ppermute(blocks[distance], "gz", [(i, i ^ distance) for i in range(count)])
+    farthest_first = parts[:1] + parts[:0:-1]
+    composed = compose([part.reshape(per_owner * 4, cols_len) for part in farthest_first])
     picture = composed.reshape(1, 1, per_owner, 4, cols_len)
     return (state, picture)
 

time: 47.8 us -> 46.4 us (0.971)
  starting transfers between devices: 17.2 us -> 16.2 us
    ppermute x3, starting transfers between devices: 6.62 us -> 5.65 us  [shards(): lax.ppermute(blocks[distance], 'gz', [(i, i ^ distance) for i in range(co...]
  transfers between devices with their start and end apart: 9 -> 9, of which waited for: 3 -> 3; matrix products, arithmetic and copies ran while one was open for 0% -> 0% of each run, Pallas kernels for 9% -> 10%
where the time goes in v12:
time: 46.4 us; the launch traced here: 46.2 us
  starting transfers between devices  16.2 us (35%)
  Pallas kernels  15.5 us (33%)
  waiting for transfers between devices  13.4 us (29%)
  between operations  0.89 us (2%)
    ppermute x3, waiting for transfers between devices, shards(): lax.ppermute(blocks[distance], 'gz', [(i, i ^ distance) for i in range(co...  10.1 us
    pallas_call x1, Pallas kernels, shards(): pl.pallas_call(main_kernel, out_shape=(array(*fields.shape),) + (array(pe...  8.45 us
    ppermute x4, starting transfers between devices, swap_pairs(): lax.ppermute(message, axis, pairs)  7.35 us
    ppermute x3, starting transfers between devices, shards(): lax.ppermute(blocks[distance], 'gz', [(i, i ^ distance) for i in range(co...  5.65 us
    ppermute x2, waiting for transfers between devices, swap_rows(): came = lax.ppermute(first, axis, [(0, 1), (1, 0)])  3.31 us
    pallas_call x1, Pallas kernels, shards(): pl.pallas_call(first_step_kernel, out_shape=(array(planes, pitch, cols_le...  3.25 us
    ppermute x2, starting transfers between devices, swap_rows(): came = lax.ppermute(first, axis, [(0, 1), (1, 0)])  3.25 us
    pallas_call x1, Pallas kernels, shards(): pl.pallas_call(pack_planes_kernel, out_shape=(array(faces, rows_len, cols...  1.78 us
  transfers between devices with their start and end apart: 9, of which 3 were waited for; matrix products, arithmetic and copies ran while one was open for 0% of the time, Pallas kernels for 10%

profile of v12, /device:TPU:0, one launch (start us, length us, event | category | flops | bytes accessed | tf_op | source)
XLA Modules:
  0.0 46.2 jit_solution(3903885225227803626)
XLA Ops:
  0.6 0.0 copy-start.1
  0.6 0.0 copy-start
  0.6 1.8 %pack_planes.1 = (f32[14,16,128]{2,1,0:T(8,128)}, f32[14,16,128]{2,1,0:T(8,128)}) custom-call(f32[5,32,16,128]{3,2,1,0:T(8,128)} %fields_ref.11, f32[32,16,128]{2,1,0:T(8,128)} %kappa_ref.11), custom_call_target="tpu_custom_call" | custom-call | tf_op jit(solution)/shard_map/pack_planes/pallas_call | solution.py:527
  2.4 3.1 %collective-permute-start = (f32[14,16,128]{2,1,0:T(8,128)}, f32[14,16,128]{2,1,0:T(8,128)S(1)}, u32[]{:S(2)}, u32[]{:S(2)}) collective-permute-start(f32[14,16,128]{2,1,0:T(8,128)} %get-tuple-element.24), channel_id=1, source_target_pairs={{0,8},{8,0},{16,24},{24,16},{1,9},{9,1},{17,25},{25,17},{2,10},{10... | collective-permute-start | bytes 344072 | tf_op jit(solution)/shard_map/ppermute | solution.py:500
  5.5 0.7 %collective-permute-start.1 = (f32[14,16,128]{2,1,0:T(8,128)}, f32[14,16,128]{2,1,0:T(8,128)S(1)}, u32[]{:S(2)}, u32[]{:S(2)}) collective-permute-start(f32[14,16,128]{2,1,0:T(8,128)} %get-tuple-element.25), channel_id=1, source_target_pairs={{8,16},{16,8},{9,17},{17,9},{10,18},{18,10},{11,19},{19,11},{12,20... | collective-permute-start | bytes 344072 | tf_op jit(solution)/shard_map/ppermute | solution.py:500
  6.2 0.0 copy-done.1
  6.2 0.0 copy-done
  6.2 0.1 pack_rows.1
  6.4 1.6 %collective-permute-start.2 = (f32[14,32,128]{2,1,0:T(8,128)S(1)}, f32[14,32,128]{2,1,0:T(8,128)S(1)}, u32[]{:S(2)}, u32[]{:S(2)}) collective-permute-start(f32[14,32,128]{2,1,0:T(8,128)S(1)} %broadcast_select_fusion), channel_id=1, source_target_pairs={{0,4},{4,0},{1,5},{5,1},{2,6},{6,2},{3,7},{7,3},{8,12},{12,8},{9,1... | collective-permute-start | bytes 688136 | tf_op jit(solution)/shard_map/ppermute | solution.py:509
  8.0 0.9 %pack_own.1 = (f32[6,16,128]{2,1,0:T(8,128)S(1)}, f32[6,16,128]{2,1,0:T(8,128)S(1)}) custom-call(f32[5,32,16,128]{3,2,1,0:T(8,128)S(1)} %copy-done, f32[32,16,128]{2,1,0:T(8,128)S(1)} %copy-done.1), custom_call_target="tpu_custom_call" | custom-call | flops 10000000 | bytes 4000000 | tf_op jit(solution)/shard_map/pack_own/pallas_call | solution.py:547
  8.9 0.0 collective-permute-done
  8.9 0.0 collective-permute-done.1
  8.9 0.0 copy-start.8
  9.0 0.2 pack_edges.1
  9.2 1.7 %collective-permute-start.3 = (f32[56,128]{1,0:T(8,128)S(1)}, f32[56,128]{1,0:T(8,128)S(1)}, u32[]{:S(2)}, u32[]{:S(2)}) collective-permute-start(f32[56,128]{1,0:T(8,128)S(1)} %broadcast_select_fusion.7), channel_id=1, source_target_pairs={{0,4},{4,0},{1,5},{5,1},{2,6},{6,2},{3,7},{7,3},{8,12},{12,8},{9,1... | collective-permute-start | bytes 86024 | tf_op jit(solution)/shard_map/ppermute | solution.py:509
  10.8 3.3 %collective-permute-done.3.elo_ref.ehi_ref = f32[56,128]{1,0:T(8,128)S(1)} collective-permute-done((f32[56,128]{1,0:T(8,128)S(1)}, f32[56,128]{1,0:T(8,128)S(1)}, u32[]{:S(2)}, u32[]{:S(2)}) %collective-permute-start.3) | collective-permute-done | bytes 28704 | tf_op jit(solution)/shard_map/ppermute | solution.py:509
  14.2 0.0 collective-permute-done.2.rows_ref.ylo_ref.yhi_ref
  14.2 0.7 %collective-permute-start.5 = (f32[6,24,128]{2,1,0:T(8,128)S(1)}, f32[6,24,128]{2,1,0:T(8,128)S(1)}, u32[]{:S(2)}, u32[]{:S(2)}) collective-permute-start(f32[6,24,128]{2,1,0:T(8,128)S(1)} %get-tuple-element.50), channel_id=1, source_target_pairs={{1,2},{2,1},{5,6},{6,5},{9,10},{10,9},{13,14},{14,13},{17,18},{18,... | collective-permute-start | bytes 221192 | tf_op jit(solution)/shard_map/ppermute | solution.py:500
  14.9 2.9 %collective-permute-start.4 = (f32[6,24,128]{2,1,0:T(8,128)S(1)}, f32[6,24,128]{2,1,0:T(8,128)S(1)}, u32[]{:S(2)}, u32[]{:S(2)}) collective-permute-start(f32[6,24,128]{2,1,0:T(8,128)S(1)} %get-tuple-element.51), channel_id=1, source_target_pairs={{0,1},{1,0},{2,3},{3,2},{4,5},{5,4},{6,7},{7,6},{8,9},{9,8},{10,11... | collective-permute-start | bytes 221192 | tf_op jit(solution)/shard_map/ppermute | solution.py:500
  17.8 0.0 copy-done.8
  17.8 0.1 copy.12.courant_ref
  17.9 0.0 copy-start.2
  17.9 0.0 copy-start.3
  17.9 0.0 copy-start.4
  17.9 0.0 copy-start.5
  17.9 0.0 copy-start.6
  17.9 0.0 copy-start.7
  17.9 3.2 %first_step.1 = (f32[38,24,128]{2,1,0:T(8,128)S(1)}, f32[38,24,128]{2,1,0:T(8,128)S(1)}, f32[38,24,128]{2,1,0:T(8,128)S(1)}, f32[38,24,128]{2,1,0:T(8,128)S(1)}, f32[38,24,128]{2,1,0:T(8,128)S(1)}) custom-call(f32[5,3]{1,0:T(8,128)S(1)} %copy.12.courant_ref, f32[5,32,16,128]{3,2,1,0:T(8,128)S(1)} %copy-done, f32[32,16,128]{2,1,0:T(8,128)S(1)} %copy-done.1, ...), custom_call_target="tpu_custom_call" | custom-call | flops 100000000 | bytes 8000000 | tf_op jit(solution)/shard_map/first_step/pallas_call | solution.py:577
  21.2 0.0 collective-permute-done.5
  21.2 0.0 collective-permute-done.4
  21.2 0.0 copy-done.2
  21.3 0.0 copy-done.3
  21.3 0.0 copy-done.4
  21.3 0.0 copy-done.5
  21.3 0.0 copy-done.6
  21.3 0.0 copy-done.7
  21.3 8.5 %step_and_march.1 = (f32[5,32,16,128]{3,2,1,0:T(8,128)}, f32[64,4,128]{2,1,0:T(4,128)S(1)}, f32[64,4,128]{2,1,0:T(4,128)S(1)}, f32[64,4,128]{2,1,0:T(4,128)S(1)}, f32[64,4,128]{2,1,0:T(4,128)S(1)}) custom-call(f32[5,3]{1,0:T(8,128)S(1)} %copy.12.courant_ref, f32[16]{0:T(128)S(1)} %copy-done.5, f32[16]{0:T(128)S(1)} %copy-done.6, f32[16]{0:T(128)S(1)} %copy-done.7, ...), custom_call_target="tpu_custom_call" | custom-call | tf_op jit(solution)/shard_map/step_and_march/pallas_call | solution.py:590
  29.8 2.7 %collective-permute-start.6 = (f32[64,4,128]{2,1,0:T(4,128)S(1)}, f32[64,4,128]{2,1,0:T(4,128)S(1)}, u32[]{:S(2)}, u32[]{:S(2)}) collective-permute-start(f32[64,4,128]{2,1,0:T(4,128)S(1)} %get-tuple-element.43), channel_id=1, source_target_pairs={{0,24},{8,16},{16,8},{24,0},{1,25},{9,17},{17,9},{25,1},{2,26},{10... | collective-permute-start | bytes 393224 | tf_op jit(solution)/shard_map/ppermute | solution.py:617
  32.5 2.9 %collective-permute-start.7 = (f32[64,4,128]{2,1,0:T(4,128)S(1)}, f32[64,4,128]{2,1,0:T(4,128)S(1)}, u32[]{:S(2)}, u32[]{:S(2)}) collective-permute-start(f32[64,4,128]{2,1,0:T(4,128)S(1)} %get-tuple-element.44), channel_id=1, source_target_pairs={{0,16},{8,24},{16,0},{24,8},{1,17},{9,25},{17,1},{25,9},{2,18},{10... | collective-permute-start | bytes 393224 | tf_op jit(solution)/shard_map/ppermute | solution.py:617
  35.4 0.0 collective-permute-start.8
  35.4 1.7 %collective-permute-done.6 = f32[64,4,128]{2,1,0:T(4,128)S(1)} collective-permute-done((f32[64,4,128]{2,1,0:T(4,128)S(1)}, f32[64,4,128]{2,1,0:T(4,128)S(1)}, u32[]{:S(2)}, u32[]{:S(2)}) %collective-permute-start.6) | collective-permute-done | bytes 131104 | tf_op jit(solution)/shard_map/ppermute | solution.py:617
  37.2 8.3 %collective-permute-done.7 = f32[64,4,128]{2,1,0:T(4,128)S(1)} collective-permute-done((f32[64,4,128]{2,1,0:T(4,128)S(1)}, f32[64,4,128]{2,1,0:T(4,128)S(1)}, u32[]{:S(2)}, u32[]{:S(2)}) %collective-permute-start.7) | collective-permute-done | bytes 131104 | tf_op jit(solution)/shard_map/ppermute | solution.py:617
  45.5 0.0 collective-permute-done.8
  45.5 0.7 %compose.1 = f32[256,128]{1,0:T(8,128)} custom-call(f32[256,128]{1,0:T(8,128)S(1)} %bitcast.7, f32[256,128]{1,0:T(8,128)S(1)} %bitcast.8, f32[256,128]{1,0:T(8,128)S(1)} %bitcast.9, f32[256,128]{1,0:T(8,128)S(1)} %bitcast.10), custom_call_target="tpu_custom_call" | custom-call | tf_op jit(solution)/shard_map/compose/pallas_call | solution.py:479
  (6 shorter events, 0.1 us)
Async XLA Ops:
  0.6 5.6 %copy-start.1 = (f32[32,16,128]{2,1,0:T(8,128)S(1)}, f32[32,16,128]{2,1,0:T(8,128)}, u32[]{:S(2)}) copy-start(f32[32,16,128]{2,1,0:T(8,128)} %kappa_ref.11) | copy-start | bytes 786436
  0.6 5.6 %copy-start = (f32[5,32,16,128]{3,2,1,0:T(8,128)S(1)}, f32[5,32,16,128]{3,2,1,0:T(8,128)}, u32[]{:S(2)}) copy-start(f32[5,32,16,128]{3,2,1,0:T(8,128)} %fields_ref.11) | copy-start | bytes 3932164
  2.4 6.5 %collective-permute-start = (f32[14,16,128]{2,1,0:T(8,128)}, f32[14,16,128]{2,1,0:T(8,128)S(1)}, u32[]{:S(2)}, u32[]{:S(2)}) collective-permute-start(f32[14,16,128]{2,1,0:T(8,128)} %get-tuple-element.24), channel_id=1, source_target_pairs={{0,8},{8,0},{16,24},{24,16},{1,9},{9,1},{17,25},{25,17},{2,10},{10... | collective-permute-start | bytes 344072 | tf_op jit(solution)/shard_map/ppermute | solution.py:500
  5.5 3.4 %collective-permute-start.1 = (f32[14,16,128]{2,1,0:T(8,128)}, f32[14,16,128]{2,1,0:T(8,128)S(1)}, u32[]{:S(2)}, u32[]{:S(2)}) collective-permute-start(f32[14,16,128]{2,1,0:T(8,128)} %get-tuple-element.25), channel_id=1, source_target_pairs={{8,16},{16,8},{9,17},{17,9},{10,18},{18,10},{11,19},{19,11},{12,20... | collective-permute-start | bytes 344072 | tf_op jit(solution)/shard_map/ppermute | solution.py:500
  6.4 7.7 %collective-permute-start.2 = (f32[14,32,128]{2,1,0:T(8,128)S(1)}, f32[14,32,128]{2,1,0:T(8,128)S(1)}, u32[]{:S(2)}, u32[]{:S(2)}) collective-permute-start(f32[14,32,128]{2,1,0:T(8,128)S(1)} %broadcast_select_fusion), channel_id=1, source_target_pairs={{0,4},{4,0},{1,5},{5,1},{2,6},{6,2},{3,7},{7,3},{8,12},{12,8},{9,1... | collective-permute-start | bytes 688136 | tf_op jit(solution)/shard_map/ppermute | solution.py:509
  8.9 8.9 %copy-start.8 = (f32[5,3]{0,1:T(4,128)S(1)}, f32[5,3]{0,1:T(4,128)}, u32[]{:S(2)}) copy-start(f32[5,3]{0,1:T(4,128)} %param.11) | copy-start | bytes 184
  9.2 5.0 %collective-permute-start.3 = (f32[56,128]{1,0:T(8,128)S(1)}, f32[56,128]{1,0:T(8,128)S(1)}, u32[]{:S(2)}, u32[]{:S(2)}) collective-permute-start(f32[56,128]{1,0:T(8,128)S(1)} %broadcast_select_fusion.7), channel_id=1, source_target_pairs={{0,4},{4,0},{1,5},{5,1},{2,6},{6,2},{3,7},{7,3},{8,12},{12,8},{9,1... | collective-permute-start | bytes 86024 | tf_op jit(solution)/shard_map/ppermute | solution.py:509
  14.2 7.0 %collective-permute-start.5 = (f32[6,24,128]{2,1,0:T(8,128)S(1)}, f32[6,24,128]{2,1,0:T(8,128)S(1)}, u32[]{:S(2)}, u32[]{:S(2)}) collective-permute-start(f32[6,24,128]{2,1,0:T(8,128)S(1)} %get-tuple-element.50), channel_id=1, source_target_pairs={{1,2},{2,1},{5,6},{6,5},{9,10},{10,9},{13,14},{14,13},{17,18},{18,... | collective-permute-start | bytes 221192 | tf_op jit(solution)/shard_map/ppermute | solution.py:500
  14.9 6.3 %collective-permute-start.4 = (f32[6,24,128]{2,1,0:T(8,128)S(1)}, f32[6,24,128]{2,1,0:T(8,128)S(1)}, u32[]{:S(2)}, u32[]{:S(2)}) collective-permute-start(f32[6,24,128]{2,1,0:T(8,128)S(1)} %get-tuple-element.51), channel_id=1, source_target_pairs={{0,1},{1,0},{2,3},{3,2},{4,5},{5,4},{6,7},{7,6},{8,9},{9,8},{10,11... | collective-permute-start | bytes 221192 | tf_op jit(solution)/shard_map/ppermute | solution.py:500
  17.9 3.3 %copy-start.2 = (s32[1,16,16,1]{2,3,1,0:T(1,128)S(1)}, s32[1,16,16,1]{2,3,1,0:T(1,128)}, u32[]{:S(2)}) copy-start(s32[1,16,16,1]{2,3,1,0:T(1,128)} %param.16) | copy-start | bytes 3076
  17.9 3.3 %copy-start.3 = (f32[3,16]{1,0:T(4,128)S(1)}, f32[3,16]{1,0:T(4,128)}, u32[]{:S(2)}) copy-start(f32[3,16]{1,0:T(4,128)} %color_ref.1) | copy-start | bytes 580
  17.9 3.4 %copy-start.4 = (s32[1,1,256]{2,1,0:T(1,128)S(1)}, s32[1,1,256]{2,1,0:T(1,128)}, u32[]{:S(2)}) copy-start(s32[1,1,256]{2,1,0:T(1,128)} %param.17) | copy-start | bytes 3076
  17.9 3.4 %copy-start.5 = (f32[16]{0:T(128)S(1)}, f32[16]{0:T(128)}, u32[]{:S(2)}) copy-start(f32[16]{0:T(128)} %center_ref.1) | copy-start | bytes 196
  17.9 3.4 %copy-start.6 = (f32[16]{0:T(128)S(1)}, f32[16]{0:T(128)}, u32[]{:S(2)}) copy-start(f32[16]{0:T(128)} %sharp_ref.1) | copy-start | bytes 196
  17.9 3.4 %copy-start.7 = (f32[16]{0:T(128)S(1)}, f32[16]{0:T(128)}, u32[]{:S(2)}) copy-start(f32[16]{0:T(128)} %gain_ref.1) | copy-start | bytes 196
  29.8 7.4 %collective-permute-start.6 = (f32[64,4,128]{2,1,0:T(4,128)S(1)}, f32[64,4,128]{2,1,0:T(4,128)S(1)}, u32[]{:S(2)}, u32[]{:S(2)}) collective-permute-start(f32[64,4,128]{2,1,0:T(4,128)S(1)} %get-tuple-element.43), channel_id=1, source_target_pairs={{0,24},{8,16},{16,8},{24,0},{1,25},{9,17},{17,9},{25,1},{2,26},{10... | collective-permute-start | bytes 393224 | tf_op jit(solution)/shard_map/ppermute | solution.py:617
  32.5 13.0 %collective-permute-start.7 = (f32[64,4,128]{2,1,0:T(4,128)S(1)}, f32[64,4,128]{2,1,0:T(4,128)S(1)}, u32[]{:S(2)}, u32[]{:S(2)}) collective-permute-start(f32[64,4,128]{2,1,0:T(4,128)S(1)} %get-tuple-element.44), channel_id=1, source_target_pairs={{0,16},{8,24},{16,0},{24,8},{1,17},{9,25},{17,1},{25,9},{2,18},{10... | collective-permute-start | bytes 393224 | tf_op jit(solution)/shard_map/ppermute | solution.py:617
  35.4 10.1 %collective-permute-start.8 = (f32[64,4,128]{2,1,0:T(4,128)S(1)}, f32[64,4,128]{2,1,0:T(4,128)S(1)}, u32[]{:S(2)}, u32[]{:S(2)}) collective-permute-start(f32[64,4,128]{2,1,0:T(4,128)S(1)} %get-tuple-element.45), channel_id=1, source_target_pairs={{0,8},{8,0},{16,24},{24,16},{1,9},{9,1},{17,25},{25,17},{2,10},{10... | collective-permute-start | bytes 393224 | tf_op jit(solution)/shard_map/ppermute | solution.py:617

commit v13 on v12

--- a/solution.py
+++ b/solution.py
@@ -490,7 +490,7 @@
     return lax.rem(lax.axis_index(axis), 2) == 1
 
 
-def swap_pairs(first, second, axis):
+def swap_pairs(first, second, axis, flip=False):
     count = lax.axis_size(axis)
     came = []
     for start, message in ((0, first), (1, second)):
@@ -499,6 +499,9 @@
             pairs += [(i, i + 1), (i + 1, i)]
         came.append(lax.ppermute(message, axis, pairs) if pairs else jnp.zeros_like(message))
     odd = is_odd(axis)
+    if flip:
+        even = jnp.logical_not(odd)
+        return jnp.where(even, came[1], came[0]), jnp.where(even, came[0], came[1])
     return jnp.where(odd, came[0], came[1]), jnp.where(odd, came[1], came[0])
 
 
@@ -573,7 +576,7 @@
         name="pack_columns",
     )(elo, ehi, main_lo, main_hi, ylo)
     odd = is_odd("gx")
-    xlo, xhi = swap_pairs(jnp.where(odd, own_lo, own_hi), jnp.where(odd, own_hi, own_lo), "gx")
+    xlo, xhi = swap_pairs(jnp.where(odd, own_lo, own_hi), jnp.where(odd, own_hi, own_lo), "gx", True)
     stepped = pl.pallas_call(
         first_step_kernel,
         out_shape=(array(planes, pitch, cols_len),) * nfield,

time: 46.4 us -> 44.3 us (0.955)
  starting transfers between devices: 16.2 us -> 13.4 us
  waiting for transfers between devices: 13.4 us -> 14.1 us
    ppermute x4, starting transfers between devices: 7.35 us -> 4.48 us  [swap_pairs(): lax.ppermute(message, axis, pairs)]
    ppermute x3, waiting for transfers between devices: 10.1 us -> 10.8 us  [shards(): lax.ppermute(blocks[distance], 'gz', [(i, i ^ distance) for i in range(co...]
where the time goes in v13:
time: 44.3 us; the launch traced here: 44.1 us
  Pallas kernels  15.5 us (35%)
  waiting for transfers between devices  14.1 us (32%)
  starting transfers between devices  13.4 us (30%)
  between operations  0.9 us (2%)
    ppermute x3, waiting for transfers between devices, shards(): lax.ppermute(blocks[distance], 'gz', [(i, i ^ distance) for i in range(co...  10.8 us
    pallas_call x1, Pallas kernels, shards(): pl.pallas_call(main_kernel, out_shape=(array(*fields.shape),) + (array(pe...  8.45 us
    ppermute x3, starting transfers between devices, shards(): lax.ppermute(blocks[distance], 'gz', [(i, i ^ distance) for i in range(co...  5.65 us
    ppermute x4, starting transfers between devices, swap_pairs(): lax.ppermute(message, axis, pairs)  4.48 us
    ppermute x2, waiting for transfers between devices, swap_rows(): came = lax.ppermute(first, axis, [(0, 1), (1, 0)])  3.31 us
    pallas_call x1, Pallas kernels, shards(): pl.pallas_call(first_step_kernel, out_shape=(array(planes, pitch, cols_le...  3.25 us
    ppermute x2, starting transfers between devices, swap_rows(): came = lax.ppermute(first, axis, [(0, 1), (1, 0)])  3.25 us
    pallas_call x1, Pallas kernels, shards(): pl.pallas_call(pack_planes_kernel, out_shape=(array(faces, rows_len, cols...  1.78 us
  transfers between devices with their start and end apart: 9, of which 3 were waited for; matrix products, arithmetic and copies ran while one was open for 0% of the time, Pallas kernels for 10%

profile of v13, /device:TPU:0, one launch (start us, length us, event | category | flops | bytes accessed | tf_op | source)
XLA Modules:
  0.0 44.1 jit_solution(7527236335630248558)
XLA Ops:
  0.6 0.0 copy-start.1
  0.6 0.0 copy-start
  0.6 1.8 %pack_planes.1 = (f32[14,16,128]{2,1,0:T(8,128)}, f32[14,16,128]{2,1,0:T(8,128)}) custom-call(f32[5,32,16,128]{3,2,1,0:T(8,128)} %fields_ref.11, f32[32,16,128]{2,1,0:T(8,128)} %kappa_ref.11), custom_call_target="tpu_custom_call" | custom-call | tf_op jit(solution)/shard_map/pack_planes/pallas_call | solution.py:530
  2.4 3.1 %collective-permute-start = (f32[14,16,128]{2,1,0:T(8,128)}, f32[14,16,128]{2,1,0:T(8,128)S(1)}, u32[]{:S(2)}, u32[]{:S(2)}) collective-permute-start(f32[14,16,128]{2,1,0:T(8,128)} %get-tuple-element.24), channel_id=1, source_target_pairs={{0,8},{8,0},{16,24},{24,16},{1,9},{9,1},{17,25},{25,17},{2,10},{10... | collective-permute-start | bytes 344072 | tf_op jit(solution)/shard_map/ppermute | solution.py:500
  5.5 0.7 %collective-permute-start.1 = (f32[14,16,128]{2,1,0:T(8,128)}, f32[14,16,128]{2,1,0:T(8,128)S(1)}, u32[]{:S(2)}, u32[]{:S(2)}) collective-permute-start(f32[14,16,128]{2,1,0:T(8,128)} %get-tuple-element.25), channel_id=1, source_target_pairs={{8,16},{16,8},{9,17},{17,9},{10,18},{18,10},{11,19},{19,11},{12,20... | collective-permute-start | bytes 344072 | tf_op jit(solution)/shard_map/ppermute | solution.py:500
  6.2 0.0 copy-done.1
  6.2 0.0 copy-done
  6.2 0.1 pack_rows.1
  6.4 1.6 %collective-permute-start.2 = (f32[14,32,128]{2,1,0:T(8,128)S(1)}, f32[14,32,128]{2,1,0:T(8,128)S(1)}, u32[]{:S(2)}, u32[]{:S(2)}) collective-permute-start(f32[14,32,128]{2,1,0:T(8,128)S(1)} %broadcast_select_fusion), channel_id=1, source_target_pairs={{0,4},{4,0},{1,5},{5,1},{2,6},{6,2},{3,7},{7,3},{8,12},{12,8},{9,1... | collective-permute-start | bytes 688136 | tf_op jit(solution)/shard_map/ppermute | solution.py:512
  8.0 0.9 %pack_own.1 = (f32[6,16,128]{2,1,0:T(8,128)S(1)}, f32[6,16,128]{2,1,0:T(8,128)S(1)}) custom-call(f32[5,32,16,128]{3,2,1,0:T(8,128)S(1)} %copy-done, f32[32,16,128]{2,1,0:T(8,128)S(1)} %copy-done.1), custom_call_target="tpu_custom_call" | custom-call | flops 10000000 | bytes 4000000 | tf_op jit(solution)/shard_map/pack_own/pallas_call | solution.py:550
  8.9 0.0 collective-permute-done
  8.9 0.0 collective-permute-done.1
  8.9 0.0 copy-start.8
  9.0 0.2 pack_edges.1
  9.2 1.7 %collective-permute-start.3 = (f32[56,128]{1,0:T(8,128)S(1)}, f32[56,128]{1,0:T(8,128)S(1)}, u32[]{:S(2)}, u32[]{:S(2)}) collective-permute-start(f32[56,128]{1,0:T(8,128)S(1)} %broadcast_select_fusion.7), channel_id=1, source_target_pairs={{0,4},{4,0},{1,5},{5,1},{2,6},{6,2},{3,7},{7,3},{8,12},{12,8},{9,1... | collective-permute-start | bytes 86024 | tf_op jit(solution)/shard_map/ppermute | solution.py:512
  10.8 3.3 %collective-permute-done.3.elo_ref.ehi_ref = f32[56,128]{1,0:T(8,128)S(1)} collective-permute-done((f32[56,128]{1,0:T(8,128)S(1)}, f32[56,128]{1,0:T(8,128)S(1)}, u32[]{:S(2)}, u32[]{:S(2)}) %collective-permute-start.3) | collective-permute-done | bytes 28704 | tf_op jit(solution)/shard_map/ppermute | solution.py:512
  14.2 0.0 collective-permute-done.2.rows_ref.ylo_ref.yhi_ref
  14.2 0.1 collective-permute-start.5
  14.3 0.7 %collective-permute-start.4 = (f32[6,24,128]{2,1,0:T(8,128)S(1)}, f32[6,24,128]{2,1,0:T(8,128)S(1)}, u32[]{:S(2)}, u32[]{:S(2)}) collective-permute-start(f32[6,24,128]{2,1,0:T(8,128)S(1)} %get-tuple-element.51), channel_id=1, source_target_pairs={{1,2},{2,1},{5,6},{6,5},{9,10},{10,9},{13,14},{14,13},{17,18},{18,... | collective-permute-start | bytes 221192 | tf_op jit(solution)/shard_map/ppermute | solution.py:500
  15.0 0.0 copy-done.8
  15.0 0.1 copy.12.courant_ref
  15.1 0.0 copy-start.2
  15.1 0.0 copy-start.3
  15.1 0.0 copy-start.4
  15.1 0.0 copy-start.5
  15.1 0.0 copy-start.6
  15.1 0.0 copy-start.7
  15.1 3.2 %first_step.1 = (f32[38,24,128]{2,1,0:T(8,128)S(1)}, f32[38,24,128]{2,1,0:T(8,128)S(1)}, f32[38,24,128]{2,1,0:T(8,128)S(1)}, f32[38,24,128]{2,1,0:T(8,128)S(1)}, f32[38,24,128]{2,1,0:T(8,128)S(1)}) custom-call(f32[5,3]{1,0:T(8,128)S(1)} %copy.12.courant_ref, f32[5,32,16,128]{3,2,1,0:T(8,128)S(1)} %copy-done, f32[32,16,128]{2,1,0:T(8,128)S(1)} %copy-done.1, ...), custom_call_target="tpu_custom_call" | custom-call | flops 100000000 | bytes 8000000 | tf_op jit(solution)/shard_map/first_step/pallas_call | solution.py:580
  18.4 0.0 collective-permute-done.5
  18.4 0.0 collective-permute-done.4
  18.4 0.0 copy-done.2
  18.4 0.0 copy-done.3
  18.4 0.0 copy-done.4
  18.4 0.0 copy-done.5
  18.4 0.0 copy-done.6
  18.4 0.0 copy-done.7
  18.5 8.5 %step_and_march.1 = (f32[5,32,16,128]{3,2,1,0:T(8,128)}, f32[64,4,128]{2,1,0:T(4,128)S(1)}, f32[64,4,128]{2,1,0:T(4,128)S(1)}, f32[64,4,128]{2,1,0:T(4,128)S(1)}, f32[64,4,128]{2,1,0:T(4,128)S(1)}) custom-call(f32[5,3]{1,0:T(8,128)S(1)} %copy.12.courant_ref, f32[16]{0:T(128)S(1)} %copy-done.5, f32[16]{0:T(128)S(1)} %copy-done.6, f32[16]{0:T(128)S(1)} %copy-done.7, ...), custom_call_target="tpu_custom_call" | custom-call | tf_op jit(solution)/shard_map/step_and_march/pallas_call | solution.py:593
  26.9 2.7 %collective-permute-start.6 = (f32[64,4,128]{2,1,0:T(4,128)S(1)}, f32[64,4,128]{2,1,0:T(4,128)S(1)}, u32[]{:S(2)}, u32[]{:S(2)}) collective-permute-start(f32[64,4,128]{2,1,0:T(4,128)S(1)} %get-tuple-element.43), channel_id=1, source_target_pairs={{0,24},{8,16},{16,8},{24,0},{1,25},{9,17},{17,9},{25,1},{2,26},{10... | collective-permute-start | bytes 393224 | tf_op jit(solution)/shard_map/ppermute | solution.py:620
  29.7 2.9 %collective-permute-start.7 = (f32[64,4,128]{2,1,0:T(4,128)S(1)}, f32[64,4,128]{2,1,0:T(4,128)S(1)}, u32[]{:S(2)}, u32[]{:S(2)}) collective-permute-start(f32[64,4,128]{2,1,0:T(4,128)S(1)} %get-tuple-element.44), channel_id=1, source_target_pairs={{0,16},{8,24},{16,0},{24,8},{1,17},{9,25},{17,1},{25,9},{2,18},{10... | collective-permute-start | bytes 393224 | tf_op jit(solution)/shard_map/ppermute | solution.py:620
  32.6 0.0 collective-permute-start.8
  32.6 1.2 %collective-permute-done.6 = f32[64,4,128]{2,1,0:T(4,128)S(1)} collective-permute-done((f32[64,4,128]{2,1,0:T(4,128)S(1)}, f32[64,4,128]{2,1,0:T(4,128)S(1)}, u32[]{:S(2)}, u32[]{:S(2)}) %collective-permute-start.6) | collective-permute-done | bytes 131104 | tf_op jit(solution)/shard_map/ppermute | solution.py:620
  33.8 9.6 %collective-permute-done.7 = f32[64,4,128]{2,1,0:T(4,128)S(1)} collective-permute-done((f32[64,4,128]{2,1,0:T(4,128)S(1)}, f32[64,4,128]{2,1,0:T(4,128)S(1)}, u32[]{:S(2)}, u32[]{:S(2)}) %collective-permute-start.7) | collective-permute-done | bytes 131104 | tf_op jit(solution)/shard_map/ppermute | solution.py:620
  43.4 0.0 collective-permute-done.8
  43.4 0.7 %compose.1 = f32[256,128]{1,0:T(8,128)} custom-call(f32[256,128]{1,0:T(8,128)S(1)} %bitcast.7, f32[256,128]{1,0:T(8,128)S(1)} %bitcast.8, f32[256,128]{1,0:T(8,128)S(1)} %bitcast.9, f32[256,128]{1,0:T(8,128)S(1)} %bitcast.10), custom_call_target="tpu_custom_call" | custom-call | tf_op jit(solution)/shard_map/compose/pallas_call | solution.py:479
  (6 shorter events, 0.1 us)
Async XLA Ops:
  0.6 5.6 %copy-start.1 = (f32[32,16,128]{2,1,0:T(8,128)S(1)}, f32[32,16,128]{2,1,0:T(8,128)}, u32[]{:S(2)}) copy-start(f32[32,16,128]{2,1,0:T(8,128)} %kappa_ref.11) | copy-start | bytes 786436
  0.6 5.6 %copy-start = (f32[5,32,16,128]{3,2,1,0:T(8,128)S(1)}, f32[5,32,16,128]{3,2,1,0:T(8,128)}, u32[]{:S(2)}) copy-start(f32[5,32,16,128]{3,2,1,0:T(8,128)} %fields_ref.11) | copy-start | bytes 3932164
  2.4 6.5 %collective-permute-start = (f32[14,16,128]{2,1,0:T(8,128)}, f32[14,16,128]{2,1,0:T(8,128)S(1)}, u32[]{:S(2)}, u32[]{:S(2)}) collective-permute-start(f32[14,16,128]{2,1,0:T(8,128)} %get-tuple-element.24), channel_id=1, source_target_pairs={{0,8},{8,0},{16,24},{24,16},{1,9},{9,1},{17,25},{25,17},{2,10},{10... | collective-permute-start | bytes 344072 | tf_op jit(solution)/shard_map/ppermute | solution.py:500
  5.5 3.4 %collective-permute-start.1 = (f32[14,16,128]{2,1,0:T(8,128)}, f32[14,16,128]{2,1,0:T(8,128)S(1)}, u32[]{:S(2)}, u32[]{:S(2)}) collective-permute-start(f32[14,16,128]{2,1,0:T(8,128)} %get-tuple-element.25), channel_id=1, source_target_pairs={{8,16},{16,8},{9,17},{17,9},{10,18},{18,10},{11,19},{19,11},{12,20... | collective-permute-start | bytes 344072 | tf_op jit(solution)/shard_map/ppermute | solution.py:500
  6.4 7.7 %collective-permute-start.2 = (f32[14,32,128]{2,1,0:T(8,128)S(1)}, f32[14,32,128]{2,1,0:T(8,128)S(1)}, u32[]{:S(2)}, u32[]{:S(2)}) collective-permute-start(f32[14,32,128]{2,1,0:T(8,128)S(1)} %broadcast_select_fusion), channel_id=1, source_target_pairs={{0,4},{4,0},{1,5},{5,1},{2,6},{6,2},{3,7},{7,3},{8,12},{12,8},{9,1... | collective-permute-start | bytes 688136 | tf_op jit(solution)/shard_map/ppermute | solution.py:512
  8.9 6.0 %copy-start.8 = (f32[5,3]{0,1:T(4,128)S(1)}, f32[5,3]{0,1:T(4,128)}, u32[]{:S(2)}) copy-start(f32[5,3]{0,1:T(4,128)} %param.11) | copy-start | bytes 184
  9.2 5.0 %collective-permute-start.3 = (f32[56,128]{1,0:T(8,128)S(1)}, f32[56,128]{1,0:T(8,128)S(1)}, u32[]{:S(2)}, u32[]{:S(2)}) collective-permute-start(f32[56,128]{1,0:T(8,128)S(1)} %broadcast_select_fusion.7), channel_id=1, source_target_pairs={{0,4},{4,0},{1,5},{5,1},{2,6},{6,2},{3,7},{7,3},{8,12},{12,8},{9,1... | collective-permute-start | bytes 86024 | tf_op jit(solution)/shard_map/ppermute | solution.py:512
  14.2 4.2 %collective-permute-start.5 = (f32[6,24,128]{2,1,0:T(8,128)S(1)}, f32[6,24,128]{2,1,0:T(8,128)S(1)}, u32[]{:S(2)}, u32[]{:S(2)}) collective-permute-start(f32[6,24,128]{2,1,0:T(8,128)S(1)} %get-tuple-element.50), channel_id=1, source_target_pairs={{0,1},{1,0},{2,3},{3,2},{4,5},{5,4},{6,7},{7,6},{8,9},{9,8},{10,11... | collective-permute-start | bytes 221192 | tf_op jit(solution)/shard_map/ppermute | solution.py:500
  14.3 4.1 %collective-permute-start.4 = (f32[6,24,128]{2,1,0:T(8,128)S(1)}, f32[6,24,128]{2,1,0:T(8,128)S(1)}, u32[]{:S(2)}, u32[]{:S(2)}) collective-permute-start(f32[6,24,128]{2,1,0:T(8,128)S(1)} %get-tuple-element.51), channel_id=1, source_target_pairs={{1,2},{2,1},{5,6},{6,5},{9,10},{10,9},{13,14},{14,13},{17,18},{18,... | collective-permute-start | bytes 221192 | tf_op jit(solution)/shard_map/ppermute | solution.py:500
  15.1 3.3 %copy-start.2 = (s32[1,16,16,1]{2,3,1,0:T(1,128)S(1)}, s32[1,16,16,1]{2,3,1,0:T(1,128)}, u32[]{:S(2)}) copy-start(s32[1,16,16,1]{2,3,1,0:T(1,128)} %param.16) | copy-start | bytes 3076
  15.1 3.3 %copy-start.3 = (f32[3,16]{1,0:T(4,128)S(1)}, f32[3,16]{1,0:T(4,128)}, u32[]{:S(2)}) copy-start(f32[3,16]{1,0:T(4,128)} %color_ref.1) | copy-start | bytes 580
  15.1 3.4 %copy-start.4 = (s32[1,1,256]{2,1,0:T(1,128)S(1)}, s32[1,1,256]{2,1,0:T(1,128)}, u32[]{:S(2)}) copy-start(s32[1,1,256]{2,1,0:T(1,128)} %param.17) | copy-start | bytes 3076
  15.1 3.4 %copy-start.5 = (f32[16]{0:T(128)S(1)}, f32[16]{0:T(128)}, u32[]{:S(2)}) copy-start(f32[16]{0:T(128)} %center_ref.1) | copy-start | bytes 196
  15.1 3.4 %copy-start.6 = (f32[16]{0:T(128)S(1)}, f32[16]{0:T(128)}, u32[]{:S(2)}) copy-start(f32[16]{0:T(128)} %sharp_ref.1) | copy-start | bytes 196
  15.1 3.4 %copy-start.7 = (f32[16]{0:T(128)S(1)}, f32[16]{0:T(128)}, u32[]{:S(2)}) copy-start(f32[16]{0:T(128)} %gain_ref.1) | copy-start | bytes 196
  26.9 6.8 %collective-permute-start.6 = (f32[64,4,128]{2,1,0:T(4,128)S(1)}, f32[64,4,128]{2,1,0:T(4,128)S(1)}, u32[]{:S(2)}, u32[]{:S(2)}) collective-permute-start(f32[64,4,128]{2,1,0:T(4,128)S(1)} %get-tuple-element.43), channel_id=1, source_target_pairs={{0,24},{8,16},{16,8},{24,0},{1,25},{9,17},{17,9},{25,1},{2,26},{10... | collective-permute-start | bytes 393224 | tf_op jit(solution)/shard_map/ppermute | solution.py:620
  29.7 13.7 %collective-permute-start.7 = (f32[64,4,128]{2,1,0:T(4,128)S(1)}, f32[64,4,128]{2,1,0:T(4,128)S(1)}, u32[]{:S(2)}, u32[]{:S(2)}) collective-permute-start(f32[64,4,128]{2,1,0:T(4,128)S(1)} %get-tuple-element.44), channel_id=1, source_target_pairs={{0,16},{8,24},{16,0},{24,8},{1,17},{9,25},{17,1},{25,9},{2,18},{10... | collective-permute-start | bytes 393224 | tf_op jit(solution)/shard_map/ppermute | solution.py:620
  32.6 10.8 %collective-permute-start.8 = (f32[64,4,128]{2,1,0:T(4,128)S(1)}, f32[64,4,128]{2,1,0:T(4,128)S(1)}, u32[]{:S(2)}, u32[]{:S(2)}) collective-permute-start(f32[64,4,128]{2,1,0:T(4,128)S(1)} %get-tuple-element.45), channel_id=1, source_target_pairs={{0,8},{8,0},{16,24},{24,16},{1,9},{9,1},{17,25},{25,17},{2,10},{10... | collective-permute-start | bytes 393224 | tf_op jit(solution)/shard_map/ppermute | solution.py:620
